TPU v7x, 32 devices: a whole 2x2x4 slice. The times are simulated.
32 devices in a mesh: grp: 2 (over x), gx: 16 (over z, y, core).
Axes of the slice: x: 2, y: 2, z: 4, core: 2. Of those that a mesh axis runs over, the one named last changes fastest.
Arguments:
- phase_lin: float32 [64, 128, 512], P(('grp', 'gx')), parts along dimension 0, may hold values from -1.1 to 1.1
- phase_state: float32 [64, 128, 512], P(('grp', 'gx')), parts along dimension 0, may hold values from -1 to 1
- cotangent: float32 [2, 64, 128, 512], P(None, ('grp', 'gx')), parts along dimension 1, may hold values from -4 to 4
- warm_start: float32 [2, 64, 128, 512], P(None, ('grp', 'gx')), parts along dimension 1, may hold values from -3 to 3
Outputs:
- adjoint: float32 [2, 64, 128, 512], P(None, ('grp', 'gx')), parts along dimension 1
- design_grad: float32 [64, 128, 512], P(('grp', 'gx')), parts along dimension 0
There are 2 independent parts, one for each index of `grp`. A program takes and returns all parts, laid end to end along the dimension named above; each array names one. Nothing has to cross between parts.
All inputs are finite; a program needn't handle non-finite values.
Results may differ from a plain program's by a relative error of at most 0.0001.
Values sent between devices are 32-bit elements; how exact they have to be, the bound alone decides.
No kernel may reach another device: no remote copies, remote signals or barrier semaphores. Data moves between devices by JAX's collectives and lax.ppermute only.
A program may use at most 192 MiB of HBM per device.

v0:
```python
import jax
import jax.numpy as jnp
from jax import lax
from jax.sharding import PartitionSpec as P

SWEEPS = 2
COARSE_SWEEPS = 4


GRADIENT_ENERGY = 1.0
TIME_STEP = 0.02
DAMPING = 0.8


def with_halo(x, sides, width):
    for axis, dim in sides:
        count, length = (lax.axis_size(axis), x.shape[dim])
        up = [(i, (i + 1) % count) for i in range(count - 1)]
        down = [(j, i) for i, j in up]
        last = lax.slice_in_dim(x, length - width, length, axis=dim)
        first = lax.slice_in_dim(x, 0, width, axis=dim)
        before = lax.ppermute(last, axis, up)
        after = lax.ppermute(first, axis, down)
        x = jnp.concatenate([before, x, after], axis=dim)
    return x


def neighbours(extended):
    centre = extended[:, 1:-1]
    padded = jnp.pad(centre, ((0, 0), (0, 0), (1, 1), (1, 1)))
    total = extended[:, 2:] + extended[:, :-2]
    total = total + padded[:, :, 2:, 1:-1] + padded[:, :, :-2, 1:-1]
    total = total + padded[:, :, 1:-1, 2:] + padded[:, :, 1:-1, :-2]
    return total


def defect_cells(extended, curvature, source, energy, step):
    centre = extended[:, 1:-1]
    laplace = neighbours(extended) - 6.0 * centre
    resid_phase = source[0] - (centre[0] - curvature * centre[1] + energy * laplace[1])
    resid_chem = source[1] - (-step * laplace[0] + centre[1])
    return (resid_phase, resid_chem)


def relax_cells(extended, curvature, source, energy, step):
    centre = extended[:, 1:-1]
    resid_phase, resid_chem = defect_cells(extended, curvature, source, energy, step)
    coupling = curvature + 6.0 * energy
    determinant = 1.0 + 6.0 * step * coupling
    new_phase = centre[0] + DAMPING * (resid_phase + coupling * resid_chem) / determinant
    new_chem = centre[1] + DAMPING * (resid_chem - 6.0 * step * resid_phase) / determinant
    return jnp.stack([new_phase, new_chem])


def coarsen(field):
    lead = field.shape[:-3]
    planes, rows_y, cols_z = field.shape[-3:]
    blocks = field.reshape(lead + (planes // 2, 2, rows_y // 2, 2, cols_z // 2, 2))
    return jnp.mean(blocks, axis=(-5, -3, -1))


def refine(field):
    return jnp.repeat(jnp.repeat(jnp.repeat(field, 2, -3), 2, -2), 2, -1)


def zero_rim(field):
    return jnp.pad(field, ((0, 0), (1, 1), (0, 0), (0, 0)))


def on_device(phase_lin, phase_state, cotangent, warm_start):
    curvature = 3.0 * phase_lin * phase_lin - 1.0
    coarse_curv = coarsen(curvature)
    coarse_energy = GRADIENT_ENERGY / 4.0
    coarse_step = TIME_STEP / 4.0

    def smooth(state):
        for sweep_index in range(SWEEPS):
            extended = with_halo(state, (("gx", 1),), 1)
            state = relax_cells(extended, curvature, cotangent, GRADIENT_ENERGY, TIME_STEP)
        return state

    state = warm_start
    state = smooth(state)
    extended = with_halo(state, (("gx", 1),), 1)
    resid_phase, resid_chem = defect_cells(
        extended, curvature, cotangent, GRADIENT_ENERGY, TIME_STEP
    )
    coarse_source = coarsen(jnp.stack([resid_phase, resid_chem]))
    correction = jnp.zeros_like(coarse_source)
    correction = relax_cells(
        zero_rim(correction), coarse_curv, coarse_source, coarse_energy, coarse_step
    )
    for sweep_index in range(COARSE_SWEEPS - 1):
        coarse_ext = with_halo(correction, (("gx", 1),), 1)
        correction = relax_cells(coarse_ext, coarse_curv, coarse_source, coarse_energy, coarse_step)
    state = state + refine(correction)
    state = smooth(state)
    design_grad = 6.0 * phase_lin * phase_state * state[1]
    return (state, design_grad)


def solution(mesh):
    in_specs = (
        P(("grp", "gx"), None, None),
        P(("grp", "gx"), None, None),
        P(None, ("grp", "gx"), None, None),
        P(None, ("grp", "gx"), None, None),
    )
    out_specs = (P(None, ("grp", "gx"), None, None), P(("grp", "gx"), None, None))
    return jax.shard_map(
        on_device, mesh=mesh, in_specs=in_specs, out_specs=out_specs, check_vma=False
    )
```

profile of v0, /device:TPU:1, one launch (start us, length us, event | category | flops | bytes accessed | tf_op | source)
XLA Modules:
  0.0 241.1 jit_solution(6472898224971577691)
XLA Ops:
  0.6 1.3 fusion.102
  1.9 2.1 collective-permute-start
  4.0 4.5 %collective-permute-start.1 = (f32[2,1,128,512]{3,2,1,0:T(8,128)S(1)}, f32[2,1,128,512]{3,2,1,0:T(8,128)S(1)}, u32[]{:S(2)}, u32[]{:S(2)}) collective-permute-start(f32[2,1,128,512]{3,2,1,0:T(8,128)S(1)} %get-tuple-element.22), channel_id=1, source_target_pairs={{0,1},{1,2},{2,3},{3,4},{4,5},{5,6},{6,7},{7,8},{8,9},{9,10},{10,1... | collective-permute-start | bytes 1572872 | tf_op jit(solution)/shard_map/ppermute | solution.py:22
  8.5 4.9 %collective-permute-done = f32[2,1,128,512]{3,2,1,0:T(8,128)S(1)} collective-permute-done((f32[2,1,128,512]{3,2,1,0:T(8,128)S(1)}, f32[2,1,128,512]{3,2,1,0:T(8,128)S(1)}, u32[]{:S(2)}, u32[]{:S(2)}) %collective-permute-start) | collective-permute-done | bytes 524320 | tf_op jit(solution)/shard_map/ppermute | solution.py:23
  13.5 5.8 %collective-permute-done.1 = f32[2,1,128,512]{3,2,1,0:T(8,128)S(1)} collective-permute-done((f32[2,1,128,512]{3,2,1,0:T(8,128)S(1)}, f32[2,1,128,512]{3,2,1,0:T(8,128)S(1)}, u32[]{:S(2)}, u32[]{:S(2)}) %collective-permute-start.1) | collective-permute-done | bytes 524320 | tf_op jit(solution)/shard_map/ppermute | solution.py:22
  19.2 4.6 %fusion.4 = f32[2,2,128,512]{3,2,1,0:T(8,128)S(1)} fusion(f32[2,2,128,512]{3,2,1,0:T(8,128)} %param.7, f32[2,1,128,512]{3,2,1,0:T(8,128)S(1)} %collective-permute-done.1, f32[2,1,128,512]{3,2,1,0:T(8,128)S(1)} %collective-permute-done), kind=kLoop, calls=%fused_computation.40 | loop fusion | flops 2359296 | bytes 3145728 | tf_op jit(solution)/shard_map/sub | solution.py:39
  23.8 2.2 bitcast_add_fusion.1
  26.0 1.7 bitcast_add_fusion
  27.7 0.1 fusion.34
  27.7 1.9 collective-permute-start.2
  29.7 4.4 %collective-permute-start.3 = (f32[2,1,128,512]{3,2,1,0:T(8,128)S(1)}, f32[2,1,128,512]{3,2,1,0:T(8,128)S(1)}, u32[]{:S(2)}, u32[]{:S(2)}) collective-permute-start(f32[2,1,128,512]{3,2,1,0:T(8,128)S(1)} %get-tuple-element.20), channel_id=1, source_target_pairs={{0,1},{1,2},{2,3},{3,4},{4,5},{5,6},{6,7},{7,8},{8,9},{9,10},{10,1... | collective-permute-start | bytes 1572872 | tf_op jit(solution)/shard_map/ppermute | solution.py:22
  34.1 0.1 pad_maximum_fusion
  34.2 4.8 %collective-permute-done.2 = f32[2,1,128,512]{3,2,1,0:T(8,128)S(1)} collective-permute-done((f32[2,1,128,512]{3,2,1,0:T(8,128)S(1)}, f32[2,1,128,512]{3,2,1,0:T(8,128)S(1)}, u32[]{:S(2)}, u32[]{:S(2)}) %collective-permute-start.2) | collective-permute-done | bytes 524320 | tf_op jit(solution)/shard_map/ppermute | solution.py:23
  39.0 2.2 collective-permute-done.3
  41.2 0.8 fusion.9
  42.0 1.8 divide_add_fusion.4
  43.8 1.0 fusion.32
  44.9 1.9 collective-permute-start.4
  46.8 4.4 %collective-permute-start.5 = (f32[2,1,128,512]{3,2,1,0:T(8,128)}, f32[2,1,128,512]{3,2,1,0:T(8,128)}, u32[]{:S(2)}, u32[]{:S(2)}) collective-permute-start(f32[2,1,128,512]{3,2,1,0:T(8,128)} %get-tuple-element.18), channel_id=1, source_target_pairs={{0,1},{1,2},{2,3},{3,4},{4,5},{5,6},{6,7},{7,8},{8,9},{9,10},{10,1... | collective-permute-start | bytes 1572872 | tf_op jit(solution)/shard_map/ppermute | solution.py:22
  51.2 18.1 %reduce_sum.27 = f32[64,2,256,2]{3,2,1,0:T(8,128)} reshape(f32[128,512]{1,0:T(8,128)S(1)} %get-tuple-element.23) | data formatting | bytes 524288 | tf_op jit(solution)/shard_map/reduce_sum | solution.py:59
  69.3 8.0 %reduce_sum.28 = f32[64,256]{1,0:T(8,128)S(1)} reduce(f32[64,2,256,2]{3,2,1,0:T(8,128)} %reduce_sum.27, f32[]{:T(128)} %constant.16.clone.1), dimensions={1,3}, to_apply=%region_2.3 | reduce | flops 49152 | bytes 327684 | tf_op jit(solution)/shard_map/reduce_sum | solution.py:59
  77.3 0.1 pad_maximum_fusion.1
  77.4 1.9 fusion.14
  79.4 1.2 fusion.50
  80.6 35.6 %stack.73 = f32[1,1,2,64,2,256,2]{6,5,4,3,2,1,0:T(8,128)} reshape(f32[2,128,512]{2,1,0:T(8,128)} %get-tuple-element.11) | data formatting | bytes 1048576 | tf_op jit(solution)/shard_map/stack | solution.py:88
  116.2 34.8 %stack.74 = f32[1,1,2,64,2,256,2]{6,5,4,3,2,1,0:T(8,128)} reshape(f32[2,128,512]{2,1,0:T(8,128)S(1)} %get-tuple-element.12) | data formatting | bytes 1048576 | tf_op jit(solution)/shard_map/stack | solution.py:88
  151.0 20.9 %maximum_reduce_fusion = f32[2,64,256]{2,1,0:T(8,128)S(1)} fusion(f32[1,1,2,64,2,256,2]{6,5,4,3,2,1,0:T(8,128)} %stack.74, f32[1,1,2,64,2,256,2]{6,5,4,3,2,1,0:T(8,128)} %stack.73), kind=kLoop, calls=%fused_computation | loop fusion | flops 491520 | bytes 1179648 | tf_op jit(solution)/shard_map/reduce_sum | solution.py:59
  172.0 0.1 fusion.97
  172.2 2.4 collective-permute-start.7
  174.6 2.1 collective-permute-start.6
  176.7 4.2 %collective-permute-done.6 = f32[2,1,64,256]{3,2,1,0:T(8,128)S(1)} collective-permute-done((f32[2,1,64,256]{3,2,1,0:T(8,128)S(1)}, f32[2,1,64,256]{3,2,1,0:T(8,128)S(1)}, u32[]{:S(2)}, u32[]{:S(2)}) %collective-permute-start.6) | collective-permute-done | bytes 131104 | tf_op jit(solution)/shard_map/ppermute | solution.py:23
  180.9 0.1 fusion.68
  181.0 0.1 divide_add_fusion.10
  181.1 2.1 collective-permute-start.9
  183.2 2.2 collective-permute-start.8
  185.5 6.7 %collective-permute-done.8 = f32[2,1,64,256]{3,2,1,0:T(8,128)S(1)} collective-permute-done((f32[2,1,64,256]{3,2,1,0:T(8,128)S(1)}, f32[2,1,64,256]{3,2,1,0:T(8,128)S(1)}, u32[]{:S(2)}, u32[]{:S(2)}) %collective-permute-start.8) | collective-permute-done | bytes 131104 | tf_op jit(solution)/shard_map/ppermute | solution.py:23
  192.2 0.1 fusion.73
  192.4 1.9 collective-permute-start.11
  194.3 2.4 collective-permute-start.10
  196.8 4.8 %collective-permute-done.10 = f32[2,1,64,256]{3,2,1,0:T(8,128)S(1)} collective-permute-done((f32[2,1,64,256]{3,2,1,0:T(8,128)S(1)}, f32[2,1,64,256]{3,2,1,0:T(8,128)S(1)}, u32[]{:S(2)}, u32[]{:S(2)}) %collective-permute-start.10) | collective-permute-done | bytes 131104 | tf_op jit(solution)/shard_map/ppermute | solution.py:23
  201.5 0.1 fusion.78
  201.8 0.1 copy.21
  201.9 0.1 broadcast_in_dim.14
  202.0 0.1 copy.22
  202.1 1.0 broadcast_in_dim.16
  203.1 1.2 copy.23
  204.3 0.1 broadcast_add_fusion
  204.5 0.1 fusion.101
  204.5 1.9 collective-permute-start.12
  206.5 3.6 %collective-permute-start.13 = (f32[2,1,128,512]{3,2,1,0:T(8,128)S(1)}, f32[2,1,128,512]{3,2,1,0:T(8,128)S(1)}, u32[]{:S(2)}, u32[]{:S(2)}) collective-permute-start(f32[2,1,128,512]{3,2,1,0:T(8,128)S(1)} %get-tuple-element.16), channel_id=1, source_target_pairs={{0,1},{1,2},{2,3},{3,4},{4,5},{5,6},{6,7},{7,8},{8,9},{9,10},{10,1... | collective-permute-start | bytes 1572872 | tf_op jit(solution)/shard_map/ppermute | solution.py:22
  210.1 4.9 %collective-permute-done.12 = f32[2,1,128,512]{3,2,1,0:T(8,128)S(1)} collective-permute-done((f32[2,1,128,512]{3,2,1,0:T(8,128)S(1)}, f32[2,1,128,512]{3,2,1,0:T(8,128)S(1)}, u32[]{:S(2)}, u32[]{:S(2)}) %collective-permute-start.12) | collective-permute-done | bytes 524320 | tf_op jit(solution)/shard_map/ppermute | solution.py:23
  215.0 6.8 %collective-permute-done.13 = f32[2,1,128,512]{3,2,1,0:T(8,128)S(1)} collective-permute-done((f32[2,1,128,512]{3,2,1,0:T(8,128)S(1)}, f32[2,1,128,512]{3,2,1,0:T(8,128)S(1)}, u32[]{:S(2)}, u32[]{:S(2)}) %collective-permute-start.13) | collective-permute-done | bytes 524320 | tf_op jit(solution)/shard_map/ppermute | solution.py:22
  221.8 0.7 fusion.19
  222.5 0.5 divide_add_fusion.2
  223.0 0.3 divide_add_fusion.1
  223.3 0.1 fusion.30
  223.4 1.9 collective-permute-start.14
  225.3 4.4 %collective-permute-start.15 = (f32[2,1,128,512]{3,2,1,0:T(8,128)S(1)}, f32[2,1,128,512]{3,2,1,0:T(8,128)S(1)}, u32[]{:S(2)}, u32[]{:S(2)}) collective-permute-start(f32[2,1,128,512]{3,2,1,0:T(8,128)S(1)} %get-tuple-element.14), channel_id=1, source_target_pairs={{0,1},{1,2},{2,3},{3,4},{4,5},{5,6},{6,7},{7,8},{8,9},{9,10},{10,1... | collective-permute-start | bytes 1572872 | tf_op jit(solution)/shard_map/ppermute | solution.py:22
  229.7 0.1 pad_maximum_fusion.2
  229.8 4.8 %collective-permute-done.14 = f32[2,1,128,512]{3,2,1,0:T(8,128)S(1)} collective-permute-done((f32[2,1,128,512]{3,2,1,0:T(8,128)S(1)}, f32[2,1,128,512]{3,2,1,0:T(8,128)S(1)}, u32[]{:S(2)}, u32[]{:S(2)}) %collective-permute-start.14) | collective-permute-done | bytes 524320 | tf_op jit(solution)/shard_map/ppermute | solution.py:23
  234.6 2.2 collective-permute-done.15
  236.9 0.8 fusion.24
  237.7 2.4 multiply_multiply_fusion.1
  240.0 1.0 pad_maximum_fusion.19
  (17 shorter events, 0.2 us)
Async XLA Ops:
  1.9 77.5 %copy-start = (f32[2,2,128,512]{3,2,1,0:T(8,128)S(1)}, f32[2,2,128,512]{3,2,1,0:T(8,128)}, u32[]{:S(2)}) copy-start(f32[2,2,128,512]{3,2,1,0:T(8,128)} %param.6) | copy-start | bytes 3145732
  1.9 77.5 %copy-start.1 = (f32[2,128,512]{2,1,0:T(8,128)S(1)}, f32[2,128,512]{2,1,0:T(8,128)}, u32[]{:S(2)}) copy-start(f32[2,128,512]{2,1,0:T(8,128)} %param.4) | copy-start | bytes 1572868
  1.9 11.5 %collective-permute-start = (f32[2,1,128,512]{3,2,1,0:T(8,128)S(1)}, f32[2,1,128,512]{3,2,1,0:T(8,128)S(1)}, u32[]{:S(2)}, u32[]{:S(2)}) collective-permute-start(f32[2,1,128,512]{3,2,1,0:T(8,128)S(1)} %get-tuple-element.21), channel_id=1, source_target_pairs={{1,0},{2,1},{3,2},{4,3},{5,4},{6,5},{7,6},{8,7},{9,8},{10,9},{11,1... | collective-permute-start | bytes 1572872 | tf_op jit(solution)/shard_map/ppermute | solution.py:23
  4.0 15.2 %collective-permute-start.1 = (f32[2,1,128,512]{3,2,1,0:T(8,128)S(1)}, f32[2,1,128,512]{3,2,1,0:T(8,128)S(1)}, u32[]{:S(2)}, u32[]{:S(2)}) collective-permute-start(f32[2,1,128,512]{3,2,1,0:T(8,128)S(1)} %get-tuple-element.22), channel_id=1, source_target_pairs={{0,1},{1,2},{2,3},{3,4},{4,5},{5,6},{6,7},{7,8},{8,9},{9,10},{10,1... | collective-permute-start | bytes 1572872 | tf_op jit(solution)/shard_map/ppermute | solution.py:22
  27.7 11.2 %collective-permute-start.2 = (f32[2,1,128,512]{3,2,1,0:T(8,128)S(1)}, f32[2,1,128,512]{3,2,1,0:T(8,128)S(1)}, u32[]{:S(2)}, u32[]{:S(2)}) collective-permute-start(f32[2,1,128,512]{3,2,1,0:T(8,128)S(1)} %get-tuple-element.19), channel_id=1, source_target_pairs={{1,0},{2,1},{3,2},{4,3},{5,4},{6,5},{7,6},{8,7},{9,8},{10,9},{11,1... | collective-permute-start | bytes 1572872 | tf_op jit(solution)/shard_map/ppermute | solution.py:23
  29.7 11.5 %collective-permute-start.3 = (f32[2,1,128,512]{3,2,1,0:T(8,128)S(1)}, f32[2,1,128,512]{3,2,1,0:T(8,128)S(1)}, u32[]{:S(2)}, u32[]{:S(2)}) collective-permute-start(f32[2,1,128,512]{3,2,1,0:T(8,128)S(1)} %get-tuple-element.20), channel_id=1, source_target_pairs={{0,1},{1,2},{2,3},{3,4},{4,5},{5,6},{6,7},{7,8},{8,9},{9,10},{10,1... | collective-permute-start | bytes 1572872 | tf_op jit(solution)/shard_map/ppermute | solution.py:22
  44.9 32.5 %collective-permute-start.4 = (f32[2,1,128,512]{3,2,1,0:T(8,128)}, f32[2,1,128,512]{3,2,1,0:T(8,128)}, u32[]{:S(2)}, u32[]{:S(2)}) collective-permute-start(f32[2,1,128,512]{3,2,1,0:T(8,128)} %get-tuple-element.17), channel_id=1, source_target_pairs={{1,0},{2,1},{3,2},{4,3},{5,4},{6,5},{7,6},{8,7},{9,8},{10,9},{11,1... | collective-permute-start | bytes 1572872 | tf_op jit(solution)/shard_map/ppermute | solution.py:23
  46.8 30.6 %collective-permute-start.5 = (f32[2,1,128,512]{3,2,1,0:T(8,128)}, f32[2,1,128,512]{3,2,1,0:T(8,128)}, u32[]{:S(2)}, u32[]{:S(2)}) collective-permute-start(f32[2,1,128,512]{3,2,1,0:T(8,128)} %get-tuple-element.18), channel_id=1, source_target_pairs={{0,1},{1,2},{2,3},{3,4},{4,5},{5,6},{6,7},{7,8},{8,9},{9,10},{10,1... | collective-permute-start | bytes 1572872 | tf_op jit(solution)/shard_map/ppermute | solution.py:22
  172.2 4.5 %collective-permute-start.7 = (f32[2,1,64,256]{3,2,1,0:T(8,128)S(1)}, f32[2,1,64,256]{3,2,1,0:T(8,128)S(1)}, u32[]{:S(2)}, u32[]{:S(2)}) collective-permute-start(f32[2,1,64,256]{3,2,1,0:T(8,128)S(1)} %pad_maximum_fusion.20), channel_id=1, source_target_pairs={{0,1},{1,2},{2,3},{3,4},{4,5},{5,6},{6,7},{7,8},{8,9},{9,10},{10,1... | collective-permute-start | bytes 393224 | tf_op jit(solution)/shard_map/ppermute | solution.py:22
  174.6 6.3 %collective-permute-start.6 = (f32[2,1,64,256]{3,2,1,0:T(8,128)S(1)}, f32[2,1,64,256]{3,2,1,0:T(8,128)S(1)}, u32[]{:S(2)}, u32[]{:S(2)}) collective-permute-start(f32[2,1,64,256]{3,2,1,0:T(8,128)S(1)} %pad_maximum_fusion.20), channel_id=1, source_target_pairs={{1,0},{2,1},{3,2},{4,3},{5,4},{6,5},{7,6},{8,7},{9,8},{10,9},{11,1... | collective-permute-start | bytes 393224 | tf_op jit(solution)/shard_map/ppermute | solution.py:23
  181.1 4.3 %collective-permute-start.9 = (f32[2,1,64,256]{3,2,1,0:T(8,128)S(1)}, f32[2,1,64,256]{3,2,1,0:T(8,128)S(1)}, u32[]{:S(2)}, u32[]{:S(2)}) collective-permute-start(f32[2,1,64,256]{3,2,1,0:T(8,128)S(1)} %pad_maximum_fusion.21), channel_id=1, source_target_pairs={{0,1},{1,2},{2,3},{3,4},{4,5},{5,6},{6,7},{7,8},{8,9},{9,10},{10,1... | collective-permute-start | bytes 393224 | tf_op jit(solution)/shard_map/ppermute | solution.py:22
  183.2 9.0 %collective-permute-start.8 = (f32[2,1,64,256]{3,2,1,0:T(8,128)S(1)}, f32[2,1,64,256]{3,2,1,0:T(8,128)S(1)}, u32[]{:S(2)}, u32[]{:S(2)}) collective-permute-start(f32[2,1,64,256]{3,2,1,0:T(8,128)S(1)} %pad_maximum_fusion.21), channel_id=1, source_target_pairs={{1,0},{2,1},{3,2},{4,3},{5,4},{6,5},{7,6},{8,7},{9,8},{10,9},{11,1... | collective-permute-start | bytes 393224 | tf_op jit(solution)/shard_map/ppermute | solution.py:23
  192.4 4.3 %collective-permute-start.11 = (f32[2,1,64,256]{3,2,1,0:T(8,128)S(1)}, f32[2,1,64,256]{3,2,1,0:T(8,128)S(1)}, u32[]{:S(2)}, u32[]{:S(2)}) collective-permute-start(f32[2,1,64,256]{3,2,1,0:T(8,128)S(1)} %pad_maximum_fusion.22), channel_id=1, source_target_pairs={{0,1},{1,2},{2,3},{3,4},{4,5},{5,6},{6,7},{7,8},{8,9},{9,10},{10,1... | collective-permute-start | bytes 393224 | tf_op jit(solution)/shard_map/ppermute | solution.py:22
  194.3 7.2 %collective-permute-start.10 = (f32[2,1,64,256]{3,2,1,0:T(8,128)S(1)}, f32[2,1,64,256]{3,2,1,0:T(8,128)S(1)}, u32[]{:S(2)}, u32[]{:S(2)}) collective-permute-start(f32[2,1,64,256]{3,2,1,0:T(8,128)S(1)} %pad_maximum_fusion.22), channel_id=1, source_target_pairs={{1,0},{2,1},{3,2},{4,3},{5,4},{6,5},{7,6},{8,7},{9,8},{10,9},{11,1... | collective-permute-start | bytes 393224 | tf_op jit(solution)/shard_map/ppermute | solution.py:23
  204.5 10.5 %collective-permute-start.12 = (f32[2,1,128,512]{3,2,1,0:T(8,128)S(1)}, f32[2,1,128,512]{3,2,1,0:T(8,128)S(1)}, u32[]{:S(2)}, u32[]{:S(2)}) collective-permute-start(f32[2,1,128,512]{3,2,1,0:T(8,128)S(1)} %get-tuple-element.15), channel_id=1, source_target_pairs={{1,0},{2,1},{3,2},{4,3},{5,4},{6,5},{7,6},{8,7},{9,8},{10,9},{11,1... | collective-permute-start | bytes 1572872 | tf_op jit(solution)/shard_map/ppermute | solution.py:23
  206.5 15.4 %collective-permute-start.13 = (f32[2,1,128,512]{3,2,1,0:T(8,128)S(1)}, f32[2,1,128,512]{3,2,1,0:T(8,128)S(1)}, u32[]{:S(2)}, u32[]{:S(2)}) collective-permute-start(f32[2,1,128,512]{3,2,1,0:T(8,128)S(1)} %get-tuple-element.16), channel_id=1, source_target_pairs={{0,1},{1,2},{2,3},{3,4},{4,5},{5,6},{6,7},{7,8},{8,9},{9,10},{10,1... | collective-permute-start | bytes 1572872 | tf_op jit(solution)/shard_map/ppermute | solution.py:22
  223.4 11.2 %collective-permute-start.14 = (f32[2,1,128,512]{3,2,1,0:T(8,128)S(1)}, f32[2,1,128,512]{3,2,1,0:T(8,128)S(1)}, u32[]{:S(2)}, u32[]{:S(2)}) collective-permute-start(f32[2,1,128,512]{3,2,1,0:T(8,128)S(1)} %get-tuple-element.13), channel_id=1, source_target_pairs={{1,0},{2,1},{3,2},{4,3},{5,4},{6,5},{7,6},{8,7},{9,8},{10,9},{11,1... | collective-permute-start | bytes 1572872 | tf_op jit(solution)/shard_map/ppermute | solution.py:23
  225.3 11.6 %collective-permute-start.15 = (f32[2,1,128,512]{3,2,1,0:T(8,128)S(1)}, f32[2,1,128,512]{3,2,1,0:T(8,128)S(1)}, u32[]{:S(2)}, u32[]{:S(2)}) collective-permute-start(f32[2,1,128,512]{3,2,1,0:T(8,128)S(1)} %get-tuple-element.14), channel_id=1, source_target_pairs={{0,1},{1,2},{2,3},{3,4},{4,5},{5,6},{6,7},{7,8},{8,9},{9,10},{10,1... | collective-permute-start | bytes 1572872 | tf_op jit(solution)/shard_map/ppermute | solution.py:22
where the time goes:
time: 244 us; the launch traced here: 241 us
  local copies, waits for them, and re-layouts  92.4 us (38%)
  waiting for transfers between devices  52.2 us (21%)
  other arithmetic  51.2 us (21%)
  starting transfers between devices  44.2 us (18%)
    another operation x2, local copies, waits for them, and re-layouts, on_device(): coarse_source = coarsen(jnp.stack([resid_phase, resid_chem]))  70.4 us
    ppermute x8, waiting for transfers between devices, with_halo(): after = lax.ppermute(first, axis, down)  35.2 us
    reduce_sum x2, other arithmetic, coarsen(): return jnp.mean(blocks, axis=(-5, -3, -1))  28.9 us
    ppermute x8, starting transfers between devices, with_halo(): before = lax.ppermute(last, axis, up)  27.7 us
    reduce_sum x1, local copies, waits for them, and re-layouts, coarsen(): return jnp.mean(blocks, axis=(-5, -3, -1))  18.1 us
    ppermute x8, waiting for transfers between devices, with_halo(): before = lax.ppermute(last, axis, up)  17 us
    ppermute x8, starting transfers between devices, with_halo(): after = lax.ppermute(first, axis, down)  16.5 us
    sub x8, other arithmetic, defect_cells(): laplace = neighbours(extended) - 6.0 * centre  9.15 us
  transfers between devices with their start and end apart: 16, of which 11 were waited for; matrix products, arithmetic and copies ran while one was open for 11% of the time, Pallas kernels for 0%

commit v1 on v0

v1 whole, which is shorter than its diff:
```python
import jax
import jax.numpy as jnp
from jax import lax
from jax.sharding import PartitionSpec as P

SWEEPS = 2
COARSE_SWEEPS = 4

GRADIENT_ENERGY = 1.0
TIME_STEP = 0.02
DAMPING = 0.8


def chip_pairs(count):
    return [(i, i ^ 1) for i in range(count)]


def cross_pairs(groups, count):
    pairs = []
    for g in range(groups):
        pairs += [(g * count + i, g * count + i + 1) for i in range(1, count - 1, 2)]
    for g in range(0, groups - 1, 2):
        pairs += [(g * count + i, (g + 1) * count + i) for i in (0, count - 1)]
    swaps = pairs + [(b, a) for a, b in pairs]
    if groups % 2 == 1:
        swaps += [((groups - 1) * count + i,) * 2 for i in (0, count - 1)]
    return swaps


def in_plane(x):
    lead = ((0, 0),) * (x.ndim - 2)
    rows = jnp.pad(x, lead + ((1, 1), (0, 0)))
    cols = jnp.pad(x, lead + ((0, 0), (1, 1)))
    return rows[..., 2:, :] + rows[..., :-2, :] + cols[..., 2:] + cols[..., :-2]


def pair_matrix(size):
    row = lax.broadcasted_iota(jnp.int32, (size, size // 2), 0)
    col = lax.broadcasted_iota(jnp.int32, (size, size // 2), 1)
    return (row // 2 == col).astype(jnp.float32)


def pooled(x):
    rows, cols = x.shape[-2:]
    lead = x.shape[:-2]
    flat = x.reshape((-1, cols))
    half = jnp.dot(flat, pair_matrix(cols), precision=lax.Precision.HIGHEST)
    half = half.reshape((-1, rows, cols // 2))
    out = jnp.einsum("ry,nyc->nrc", pair_matrix(rows).T, half, precision=lax.Precision.HIGHEST)
    return out.reshape(lead + (rows // 2, cols // 2))


def spread(x):
    rows, cols = x.shape[-2:]
    lead = x.shape[:-2]
    tall = jnp.einsum("ry,nyc->nrc", pair_matrix(2 * rows), x.reshape((-1, rows, cols)), precision=lax.Precision.HIGHEST)
    wide = jnp.dot(tall.reshape((-1, cols)), pair_matrix(2 * cols).T, precision=lax.Precision.HIGHEST)
    return wide.reshape(lead + (2 * rows, 2 * cols))


class Level:
    def __init__(self, curvature, source, energy, step):
        self.energy, self.step = energy, step
        coupling = curvature + 6.0 * energy
        self.gain = DAMPING / (1.0 + 6.0 * step * coupling)
        self.gain_coupling = self.gain * coupling * step
        self.own = (
            self.gain * (source[0] + coupling * source[1]),
            self.gain * (source[1] - 6.0 * step * source[0]),
        )

    def add(self, base, nb):
        phase = base[0] - self.gain * (self.energy * nb[1]) + self.gain_coupling * nb[0]
        chem = base[1] + self.gain * (self.step * (nb[0] + 6.0 * self.energy * nb[1]))
        return jnp.stack([phase, chem])

    def begin(self, state, nb):
        keep = 1.0 - DAMPING
        return self.add((keep * state[0] + self.own[0], keep * state[1] + self.own[1]), nb)


def on_device(phase_lin, phase_state, cotangent, warm_start):
    groups, count = lax.axis_size("grp"), lax.axis_size("gx")
    me = lax.axis_index("gx")
    cross = me % 2
    inner = 1 - cross
    at_end = (me == 0) | (me == count - 1)
    across = cross_pairs(groups, count)
    on_chip = chip_pairs(count)

    def swap_cross(x):
        return lax.ppermute(x, ("grp", "gx"), across)

    def swap_chip(x):
        return lax.ppermute(x, "gx", on_chip)

    def masked(x):
        return jnp.where(at_end, 0.0, x)

    def plane(x, which, axis):
        return lax.dynamic_index_in_dim(x, which, axis, keepdims=False)

    fence = lax.optimization_barrier

    state = (plane(warm_start, cross, 1), plane(warm_start, inner, 1))
    phi = (plane(phase_lin, cross, 0), plane(phase_lin, inner, 0))
    cot = (plane(cotangent, cross, 1), plane(cotangent, inner, 1))
    curvature = tuple(3.0 * v * v - 1.0 for v in phi)
    fine = tuple(Level(c, s, GRADIENT_ENERGY, TIME_STEP) for c, s in zip(curvature, cot))

    def sweep(state, halo):
        part = fence(tuple(fine[i].begin(state[i], in_plane(state[i]) + state[1 - i]) for i in range(2)))
        return tuple(fine[i].add(part[i], halo[i]) for i in range(2))

    def halos(state):
        far = swap_cross(state[0])
        near = swap_chip(state[1])
        return (masked(far), near)

    for sweep_index in range(SWEEPS):
        state = sweep(state, halos(state))
    state = fence(state)

    coarse_halos = halos(tuple(pooled(v) for v in state))
    state_halos = halos(state)

    def local_defect(i):
        own, nb = state[i], in_plane(state[i]) + state[1 - i]
        lap = nb - 6.0 * own
        r0 = cot[i][0] - (own[0] - curvature[i] * own[1] + GRADIENT_ENERGY * lap[1])
        r1 = cot[i][1] - (-TIME_STEP * lap[0] + own[1])
        return jnp.stack([r0, r1])

    coarse_curv = pooled(curvature[0] + curvature[1]) / 8.0
    local = fence(pooled(local_defect(0) + local_defect(1)) / 8.0)
    both = (coarse_halos[0] + coarse_halos[1]) / 8.0
    source = (local[0] - GRADIENT_ENERGY * both[1], local[1] + TIME_STEP * both[0])

    coarse = Level(coarse_curv, source, GRADIENT_ENERGY / 4.0, TIME_STEP / 4.0)
    fix = jnp.stack(coarse.own)
    for sweep_index in range(COARSE_SWEEPS - 1):
        far, near = halos((fix, fix))
        part = fence(coarse.begin(fix, in_plane(fix)))
        fix = coarse.add(part, far + near)

    fix_halos = halos((fix, fix))
    fine_fix = spread(fix)
    state = tuple(v + fine_fix for v in state)
    part = fence(tuple(fine[i].begin(state[i], in_plane(state[i]) + state[1 - i]) for i in range(2)))
    part = fence(tuple(fine[i].add(part[i], state_halos[i]) for i in range(2)))
    state = tuple(fine[i].add(part[i], spread(fix_halos[i])) for i in range(2))
    for sweep_index in range(SWEEPS - 1):
        state = sweep(state, halos(state))

    first = jnp.where(cross == 0, state[0], state[1])
    second = jnp.where(cross == 0, state[1], state[0])
    adjoint = jnp.stack([first, second], axis=1)
    design_grad = 6.0 * phase_lin * phase_state * adjoint[1]
    return (adjoint, design_grad)


def solution(mesh):
    in_specs = (
        P(("grp", "gx"), None, None),
        P(("grp", "gx"), None, None),
        P(None, ("grp", "gx"), None, None),
        P(None, ("grp", "gx"), None, None),
    )
    out_specs = (P(None, ("grp", "gx"), None, None), P(("grp", "gx"), None, None))
    return jax.shard_map(
        on_device, mesh=mesh, in_specs=in_specs, out_specs=out_specs, check_vma=False
    )
```

time: 244 us -> 103 us (0.42)
  local copies, waits for them, and re-layouts: 92.4 us -> 2.11 us
  other arithmetic: 51.2 us -> 20 us
  starting transfers between devices: 44.2 us -> 23.6 us
  matrix products: 0 us -> 7.55 us
  waiting for transfers between devices: 52.2 us -> 47.1 us
    another operation x3 -> x0, local copies, waits for them, and re-layouts: 70.5 us -> none  [the longest x2 70.4 us: on_device(): coarse_source = coarsen(jnp.stack([resid_phase, resid_chem]))]
    reduce_sum x2 -> x0, other arithmetic: 28.9 us -> none  [coarsen(): return jnp.mean(blocks, axis=(-5, -3, -1))]
    ppermute x16 -> x18, starting transfers between devices: 44.2 us -> 23.6 us  [the longest x9 22.8 us: swap_cross(): return lax.ppermute(x, ('grp', 'gx'), across)]
    reduce_sum x1 -> x0, local copies, waits for them, and re-layouts: 18.1 us -> none  [coarsen(): return jnp.mean(blocks, axis=(-5, -3, -1))]
    sub x9 -> x2, other arithmetic: 10.4 us -> 1.05 us  [the longest x1 0.61 us: local_defect(): lap = nb - 6.0 * own]
    dot_general x0 -> x14, matrix products: none -> 7.55 us  [the longest x3 3.35 us: spread(): jnp.dot(tall.reshape((-1, cols)), pair_matrix(2 * cols).T, precision=lax....]
    add x9 -> x27, other arithmetic: 6.81 us -> 14 us  [the longest x6 7.42 us: sweep(): in_plane(state[i]) + state[1 - i]]
    ppermute x16 -> x18, waiting for transfers between devices: 52.2 us -> 47.1 us  [the longest x9 47.1 us: swap_cross(): return lax.ppermute(x, ('grp', 'gx'), across)]
  transfers between devices with their start and end apart: 16 -> 18, of which waited for: 11 -> 7; matrix products, arithmetic and copies ran while one was open for 11% -> 19% of each run, Pallas kernels for 0% -> 0%
where the time goes in v1:
time: 103 us; the launch traced here: 102 us
  waiting for transfers between devices  47.1 us (46%)
  starting transfers between devices  23.6 us (23%)
  other arithmetic  20 us (19%)
  matrix products  7.55 us (7%)
  local copies, waits for them, and re-layouts  2.11 us (2%)
  between operations  1.28 us (1%)
    ppermute x9, waiting for transfers between devices, swap_cross(): return lax.ppermute(x, ('grp', 'gx'), across)  47.1 us
    ppermute x9, starting transfers between devices, swap_cross(): return lax.ppermute(x, ('grp', 'gx'), across)  22.8 us
    add x6, other arithmetic, sweep(): in_plane(state[i]) + state[1 - i]  7.42 us
    add x12, other arithmetic, add(): base[0] - self.gain * (self.energy * nb[1]) + self.gain_coupling * nb[0]  4.9 us
    dot_general x3, matrix products, spread(): jnp.dot(tall.reshape((-1, cols)), pair_matrix(2 * cols).T, precision=lax....  3.35 us
    dot_general x4, matrix products, pooled(): half = jnp.dot(flat, pair_matrix(cols), precision=lax.Precision.HIGHEST)  2.33 us
  transfers between devices with their start and end apart: 18, of which 7 were waited for; matrix products, arithmetic and copies ran while one was open for 19% of the time, Pallas kernels for 0%

profile of v1, /device:TPU:1, one launch (start us, length us, event | category | flops | bytes accessed | tf_op | source)
XLA Modules:
  0.0 101.6 jit_solution(3983660458365292612)
XLA Ops:
  0.7 2.0 %dynamic-slice_bitcast_fusion = f32[2,128,512]{2,1,0:T(8,128)} fusion(f32[2,2,128,512]{3,2,1,0:T(8,128)} %param.7, s32[]{:T(128)S(6)} %select_n.138), kind=kLoop, calls=%fused_computation.126 | loop fusion | bytes 1048580 | tf_op jit(solution)/shard_map/jit(dynamic_index_in_dim)/squeeze | solution.py:101
  2.7 3.0 %fusion.10 = (f32[2,128,512]{2,1,0:T(8,128)}, f32[2,128,512]{2,1,0:T(8,128)}) fusion(f32[2,128,512]{2,1,0:T(8,128)} %dynamic-slice_bitcast_fusion, f32[2,2,128,512]{3,2,1,0:T(8,128)S(1)} %copy-done.2, s32[]{:T(128)S(6)} %select_n.137), kind=kLoop, calls=%fused_computation.58 | loop fusion | flops 524288 | bytes 2097156 | tf_op jit(solution)/shard_map/add | solution.py:112
  5.7 2.6 %collective-permute-start = (f32[2,128,512]{2,1,0:T(8,128)}, f32[2,128,512]{2,1,0:T(8,128)}, u32[]{:S(2)}, u32[]{:S(2)}) collective-permute-start(f32[2,128,512]{2,1,0:T(8,128)} %get-tuple-element.31), channel_id=1, source_target_pairs={{1,2},{3,4},{5,6},{7,8},{9,10},{11,12},{13,14},{17,18},{19,20},{21... | collective-permute-start | bytes 1572872 | tf_op jit(solution)/shard_map/ppermute | solution.py:92
  8.3 3.0 %fusion.6 = f32[2,128,512]{2,1,0:T(8,128)} fusion(f32[2,128,512]{2,1,0:T(8,128)} %get-tuple-element.31, f32[2,2,128,512]{3,2,1,0:T(8,128)S(1)} %copy-done.2, s32[]{:T(128)S(6)} %select_n.138), kind=kLoop, calls=%fused_computation.54 | loop fusion | flops 524288 | bytes 1572868 | tf_op jit(solution)/shard_map/add | solution.py:112
  11.3 1.7 %fusion.82 = (f32[1,128,512]{2,1,0:T(8,128)S(1)}, f32[1,128,512]{2,1,0:T(8,128)S(1)}, f32[1,128,512]{2,1,0:T(8,128)S(1)}, f32[1,128,512]{2,1,0:T(8,128)S(1)}, f3...) fusion(f32[2,2,128,512]{3,2,1,0:T(8,128)S(1)} %copy-done.2, s32[]{:T(128)S(6)} %select_n.138, ...), kind=kLoop, calls=%fused_computation.170 | loop fusion | flops 3538944 | bytes 5242892 | tf_op jit(solution)/shard_map/add | solution.py:73
  13.1 0.5 fusion.57
  13.7 6.7 %collective-permute-done = f32[2,128,512]{2,1,0:T(8,128)} collective-permute-done((f32[2,128,512]{2,1,0:T(8,128)}, f32[2,128,512]{2,1,0:T(8,128)}, u32[]{:S(2)}, u32[]{:S(2)}) %collective-permute-start) | collective-permute-done | bytes 524320 | tf_op jit(solution)/shard_map/ppermute | solution.py:92
  20.3 1.1 %broadcast_select_fusion.3 = f32[2,128,512]{2,1,0:T(8,128)S(1)} fusion(f32[2,128,512]{2,1,0:T(8,128)} %collective-permute-done, pred[]{:T(512)S(6)} %or.3), kind=kLoop, calls=%fused_computation.260 | loop fusion | flops 131072 | bytes 1048577 | tf_op jit(solution)/shard_map/jit(_where)/select_n | solution.py:98
  21.4 1.4 %multiply_add_fusion.13 = (f32[1,128,512]{2,1,0:T(8,128)S(1)}, f32[1,128,512]{2,1,0:T(8,128)S(1)}, f32[1,128,512]{2,1,0:T(8,128)S(1)}, f32[1,128,512]{2,1,0:T(8,128)S(1)}) fusion(f32[2,128,512]{2,1,0:T(8,128)S(1)} %get-tuple-element.15, f32[2,128,512]{2,1,0:T(8,128)} %collective-permute-done.1, f32[2,128,512]{2,1,0:T(8,128)S(1)} %copy-done, ...), kind=kLoop, calls=%fused_computation.254 | loop fusion | flops 2228224 | bytes 3670024 | tf_op jit(solution)/shard_map/add | solution.py:73
  22.8 0.1 collective-permute-start.3
  22.9 0.3 fusion.18
  23.3 0.3 fusion.14
  23.6 2.5 %collective-permute-start.2 = (f32[2,128,512]{2,1,0:T(8,128)S(1)}, f32[2,128,512]{2,1,0:T(8,128)S(1)}, u32[]{:S(2)}, u32[]{:S(2)}) collective-permute-start(f32[2,128,512]{2,1,0:T(8,128)S(1)} %get-tuple-element.92), channel_id=1, source_target_pairs={{1,2},{3,4},{5,6},{7,8},{9,10},{11,12},{13,14},{17,18},{19,20},{21... | collective-permute-start | bytes 1572872 | tf_op jit(solution)/shard_map/ppermute | solution.py:92
  26.2 0.5 multiply_add_fusion.8
  26.8 11.1 %collective-permute-done.2 = f32[2,128,512]{2,1,0:T(8,128)S(1)} collective-permute-done((f32[2,128,512]{2,1,0:T(8,128)S(1)}, f32[2,128,512]{2,1,0:T(8,128)S(1)}, u32[]{:S(2)}, u32[]{:S(2)}) %collective-permute-start.2) | collective-permute-done | bytes 524320 | tf_op jit(solution)/shard_map/ppermute | solution.py:92
  38.0 0.3 multiply_add_fusion.5
  38.4 0.6 fusion.174
  39.0 0.6 fusion.176
  39.6 0.6 fusion.28
  40.3 2.5 %collective-permute-start.12 = (f32[2,128,512]{2,1,0:T(8,128)S(1)}, f32[2,128,512]{2,1,0:T(8,128)S(1)}, u32[]{:S(2)}, u32[]{:S(2)}) collective-permute-start(f32[2,128,512]{2,1,0:T(8,128)S(1)} %pad_maximum_fusion.7), channel_id=1, source_target_pairs={{1,2},{3,4},{5,6},{7,8},{9,10},{11,12},{13,14},{17,18},{19,20},{21... | collective-permute-start | bytes 1572872 | tf_op jit(solution)/shard_map/ppermute | solution.py:92
  42.9 0.2 convolution_bitcast_fusion.1
  43.1 0.1 collective-permute-start.5
  43.2 0.2 convolution_bitcast_fusion.2
  43.4 2.1 %collective-permute-start.4 = (f32[2,64,256]{2,1,0:T(8,128)S(1)}, f32[2,64,256]{2,1,0:T(8,128)S(1)}, u32[]{:S(2)}, u32[]{:S(2)}) collective-permute-start(f32[2,64,256]{2,1,0:T(8,128)S(1)} %convolution_bitcast_fusion.2), channel_id=1, source_target_pairs={{1,2},{3,4},{5,6},{7,8},{9,10},{11,12},{13,14},{17,18},{19,20},{21... | collective-permute-start | bytes 393224 | tf_op jit(solution)/shard_map/ppermute | solution.py:92
  45.5 0.4 fusion.72
  46.0 0.6 fusion.48
  46.6 0.2 fusion
  46.9 10.5 %collective-permute-done.4 = f32[2,64,256]{2,1,0:T(8,128)S(1)} collective-permute-done((f32[2,64,256]{2,1,0:T(8,128)S(1)}, f32[2,64,256]{2,1,0:T(8,128)S(1)}, u32[]{:S(2)}, u32[]{:S(2)}) %collective-permute-start.4) | collective-permute-done | bytes 131104 | tf_op jit(solution)/shard_map/ppermute | solution.py:92
  57.4 0.2 add_multiply_fusion.1
  57.7 0.1 fusion.132
  57.8 0.1 collective-permute-start.7
  57.9 2.5 %collective-permute-start.6 = (f32[2,64,256]{2,1,0:T(8,128)S(1)}, f32[2,64,256]{2,1,0:T(8,128)S(1)}, u32[]{:S(2)}, u32[]{:S(2)}) collective-permute-start(f32[2,64,256]{2,1,0:T(8,128)S(1)} %pad_maximum_fusion.19), channel_id=1, source_target_pairs={{1,2},{3,4},{5,6},{7,8},{9,10},{11,12},{13,14},{17,18},{19,20},{21... | collective-permute-start | bytes 393224 | tf_op jit(solution)/shard_map/ppermute | solution.py:92
  60.5 2.6 %collective-permute-done.6 = f32[2,64,256]{2,1,0:T(8,128)S(1)} collective-permute-done((f32[2,64,256]{2,1,0:T(8,128)S(1)}, f32[2,64,256]{2,1,0:T(8,128)S(1)}, u32[]{:S(2)}, u32[]{:S(2)}) %collective-permute-start.6) | collective-permute-done | bytes 131104 | tf_op jit(solution)/shard_map/ppermute | solution.py:92
  63.2 0.1 fusion.135
  63.3 0.3 collective-permute-start.9
  63.6 2.8 %collective-permute-start.8 = (f32[2,64,256]{2,1,0:T(8,128)S(1)}, f32[2,64,256]{2,1,0:T(8,128)S(1)}, u32[]{:S(2)}, u32[]{:S(2)}) collective-permute-start(f32[2,64,256]{2,1,0:T(8,128)S(1)} %pad_maximum_fusion.21), channel_id=1, source_target_pairs={{1,2},{3,4},{5,6},{7,8},{9,10},{11,12},{13,14},{17,18},{19,20},{21... | collective-permute-start | bytes 393224 | tf_op jit(solution)/shard_map/ppermute | solution.py:92
  66.5 2.6 %collective-permute-done.8 = f32[2,64,256]{2,1,0:T(8,128)S(1)} collective-permute-done((f32[2,64,256]{2,1,0:T(8,128)S(1)}, f32[2,64,256]{2,1,0:T(8,128)S(1)}, u32[]{:S(2)}, u32[]{:S(2)}) %collective-permute-start.8) | collective-permute-done | bytes 131104 | tf_op jit(solution)/shard_map/ppermute | solution.py:92
  69.2 0.1 fusion.138
  69.4 3.2 %collective-permute-start.10 = (f32[2,64,256]{2,1,0:T(8,128)S(1)}, f32[2,64,256]{2,1,0:T(8,128)S(1)}, u32[]{:S(2)}, u32[]{:S(2)}) collective-permute-start(f32[2,64,256]{2,1,0:T(8,128)S(1)} %pad_maximum_fusion.23), channel_id=1, source_target_pairs={{1,2},{3,4},{5,6},{7,8},{9,10},{11,12},{13,14},{17,18},{19,20},{21... | collective-permute-start | bytes 393224 | tf_op jit(solution)/shard_map/ppermute | solution.py:92
  72.7 2.6 %collective-permute-done.10 = f32[2,64,256]{2,1,0:T(8,128)S(1)} collective-permute-done((f32[2,64,256]{2,1,0:T(8,128)S(1)}, f32[2,64,256]{2,1,0:T(8,128)S(1)}, u32[]{:S(2)}, u32[]{:S(2)}) %collective-permute-start.10) | collective-permute-done | bytes 131104 | tf_op jit(solution)/shard_map/ppermute | solution.py:92
  75.3 0.3 convolution_bitcast_fusion
  75.7 0.1 collective-permute-start.15
  75.8 3.1 %collective-permute-start.14 = (f32[2,64,256]{2,1,0:T(8,128)S(1)}, f32[2,64,256]{2,1,0:T(8,128)S(1)}, u32[]{:S(2)}, u32[]{:S(2)}) collective-permute-start(f32[2,64,256]{2,1,0:T(8,128)S(1)} %pad_maximum_fusion.25), channel_id=1, source_target_pairs={{1,2},{3,4},{5,6},{7,8},{9,10},{11,12},{13,14},{17,18},{19,20},{21... | collective-permute-start | bytes 393224 | tf_op jit(solution)/shard_map/ppermute | solution.py:92
  78.8 1.1 %fusion.181 = (f32[2,128,512]{2,1,0:T(8,128)S(1)}, f32[2,128,512]{2,1,0:T(8,128)S(1)}) fusion(f32[2,128,512]{2,1,0:T(8,128)S(1)} %pad_maximum_fusion.8, f32[2,128,256]{2,1,0:T(8,128)S(1)} %convolution_bitcast_fusion, s32[512]{0:T(512)S(1)} %get-tuple-element.114, s32[512]{0:T(512)S(1)} %get-tuple-element.115, pred[512]{0:T(512)(128)(4,1)S(1)} %fusion.158), kind=kOutput, calls=%fused_computation.358 | convolution fusion | flops 403046400 | bytes 1839616 | tf_op jit(solution)/shard_map/dot_general | solution.py:57
  79.9 0.4 fusion.36
  80.3 0.3 fusion.32
  80.7 0.5 fusion.64
  81.4 0.3 multiply_add_fusion.1
  81.8 0.3 fusion.163
  82.1 1.1 %fusion.55 = f32[256,512]{1,0:T(8,128)S(1)} fusion(f32[256,256]{1,0:T(8,128)S(1)} %bitcast.307, s32[512]{0:T(512)S(1)} %get-tuple-element.114, s32[512]{0:T(512)S(1)} %get-tuple-element.115, pred[512]{0:T(512)(128)(4,1)S(1)} %fusion.158), kind=kOutput, calls=%fused_computation.123 | convolution fusion | flops 402915328 | bytes 791040 | tf_op jit(solution)/shard_map/dot_general | solution.py:57
  83.3 0.3 fusion.139
  83.6 1.1 %fusion.54 = f32[256,512]{1,0:T(8,128)S(1)} fusion(f32[256,256]{1,0:T(8,128)S(1)} %bitcast.306, s32[512]{0:T(512)S(1)} %get-tuple-element.114, s32[512]{0:T(512)S(1)} %get-tuple-element.115, pred[512]{0:T(512)(128)(4,1)S(1)} %fusion.158), kind=kOutput, calls=%fused_computation.122 | convolution fusion | flops 402915328 | bytes 791040 | tf_op jit(solution)/shard_map/dot_general | solution.py:57
  84.7 0.3 fusion.100
  85.1 0.3 fusion.44
  85.5 0.3 fusion.40
  85.8 1.4 %collective-permute-start.16 = (f32[2,128,512]{2,1,0:T(8,128)S(1)}, f32[2,128,512]{2,1,0:T(8,128)S(1)}, u32[]{:S(2)}, u32[]{:S(2)}) collective-permute-start(f32[2,128,512]{2,1,0:T(8,128)S(1)} %get-tuple-element.84), channel_id=1, source_target_pairs={{1,2},{3,4},{5,6},{7,8},{9,10},{11,12},{13,14},{17,18},{19,20},{21... | collective-permute-start | bytes 1572872 | tf_op jit(solution)/shard_map/ppermute | solution.py:92
  87.2 0.3 fusion.106
  87.5 0.3 fusion.95
  87.9 11.0 %collective-permute-done.16 = f32[2,128,512]{2,1,0:T(8,128)S(1)} collective-permute-done((f32[2,128,512]{2,1,0:T(8,128)S(1)}, f32[2,128,512]{2,1,0:T(8,128)S(1)}, u32[]{:S(2)}, u32[]{:S(2)}) %collective-permute-start.16) | collective-permute-done | bytes 524320 | tf_op jit(solution)/shard_map/ppermute | solution.py:92
  99.0 0.3 add_bitcast_fusion.3
  99.4 0.1 fusion.59
  99.5 1.0 %pad_maximum_fusion = f32[2,2,128,512]{3,2,1,0:T(8,128)} fusion(f32[2,1,128,512]{3,2,1,0:T(8,128)S(1)} %get-tuple-element.77, f32[2,1,128,512]{3,2,1,0:T(8,128)S(1)} %get-tuple-element.76), kind=kLoop, calls=%fused_computation.1 | loop fusion | flops 262144 | bytes 2097152 | tf_op jit(solution)/shard_map/stack | solution.py:157
  100.5 0.1 copy-done.3
  100.7 0.9 fusion.47
  (59 shorter events, 1.3 us)
Async XLA Ops:
  0.6 2.0 %copy-start.2 = (f32[2,2,128,512]{3,2,1,0:T(8,128)S(1)}, f32[2,2,128,512]{3,2,1,0:T(8,128)}, u32[]{:S(2)}) copy-start(f32[2,2,128,512]{3,2,1,0:T(8,128)} %param.7) | copy-start | bytes 3145732
  2.6 18.8 %collective-permute-start.1 = (f32[2,128,512]{2,1,0:T(8,128)}, f32[2,128,512]{2,1,0:T(8,128)}, u32[]{:S(2)}, u32[]{:S(2)}) collective-permute-start(f32[2,128,512]{2,1,0:T(8,128)} %dynamic-slice_bitcast_fusion), channel_id=1, source_target_pairs={{0,1},{1,0},{2,3},{3,2},{4,5},{5,4},{6,7},{7,6},{8,9},{9,8},{10,11... | collective-permute-start | bytes 1572872 | tf_op jit(solution)/shard_map/ppermute | solution.py:95
  5.7 5.6 %copy-start.1 = (f32[2,2,128,512]{3,2,1,0:T(8,128)S(1)}, f32[2,2,128,512]{3,2,1,0:T(8,128)}, u32[]{:S(2)}) copy-start(f32[2,2,128,512]{3,2,1,0:T(8,128)} %param.6) | copy-start | bytes 3145732
  5.7 5.6 %copy-start = (f32[2,128,512]{2,1,0:T(8,128)S(1)}, f32[2,128,512]{2,1,0:T(8,128)}, u32[]{:S(2)}) copy-start(f32[2,128,512]{2,1,0:T(8,128)} %param.4) | copy-start | bytes 1572868
  5.7 14.6 %collective-permute-start = (f32[2,128,512]{2,1,0:T(8,128)}, f32[2,128,512]{2,1,0:T(8,128)}, u32[]{:S(2)}, u32[]{:S(2)}) collective-permute-start(f32[2,128,512]{2,1,0:T(8,128)} %get-tuple-element.31), channel_id=1, source_target_pairs={{1,2},{3,4},{5,6},{7,8},{9,10},{11,12},{13,14},{17,18},{19,20},{21... | collective-permute-start | bytes 1572872 | tf_op jit(solution)/shard_map/ppermute | solution.py:92
  22.8 15.1 %collective-permute-start.3 = (f32[2,128,512]{2,1,0:T(8,128)S(1)}, f32[2,128,512]{2,1,0:T(8,128)S(1)}, u32[]{:S(2)}, u32[]{:S(2)}) collective-permute-start(f32[2,128,512]{2,1,0:T(8,128)S(1)} %pad_maximum_fusion.4), channel_id=1, source_target_pairs={{0,1},{1,0},{2,3},{3,2},{4,5},{5,4},{6,7},{7,6},{8,9},{9,8},{10,11... | collective-permute-start | bytes 1572872 | tf_op jit(solution)/shard_map/ppermute | solution.py:95
  23.6 14.3 %collective-permute-start.2 = (f32[2,128,512]{2,1,0:T(8,128)S(1)}, f32[2,128,512]{2,1,0:T(8,128)S(1)}, u32[]{:S(2)}, u32[]{:S(2)}) collective-permute-start(f32[2,128,512]{2,1,0:T(8,128)S(1)} %get-tuple-element.92), channel_id=1, source_target_pairs={{1,2},{3,4},{5,6},{7,8},{9,10},{11,12},{13,14},{17,18},{19,20},{21... | collective-permute-start | bytes 1572872 | tf_op jit(solution)/shard_map/ppermute | solution.py:92
  40.2 41.1 %collective-permute-start.13 = (f32[2,128,512]{2,1,0:T(8,128)S(1)}, f32[2,128,512]{2,1,0:T(8,128)S(1)}, u32[]{:S(2)}, u32[]{:S(2)}) collective-permute-start(f32[2,128,512]{2,1,0:T(8,128)S(1)} %pad_maximum_fusion.8), channel_id=1, source_target_pairs={{0,1},{1,0},{2,3},{3,2},{4,5},{5,4},{6,7},{7,6},{8,9},{9,8},{10,11... | collective-permute-start | bytes 1572872 | tf_op jit(solution)/shard_map/ppermute | solution.py:95
  40.3 41.0 %collective-permute-start.12 = (f32[2,128,512]{2,1,0:T(8,128)S(1)}, f32[2,128,512]{2,1,0:T(8,128)S(1)}, u32[]{:S(2)}, u32[]{:S(2)}) collective-permute-start(f32[2,128,512]{2,1,0:T(8,128)S(1)} %pad_maximum_fusion.7), channel_id=1, source_target_pairs={{1,2},{3,4},{5,6},{7,8},{9,10},{11,12},{13,14},{17,18},{19,20},{21... | collective-permute-start | bytes 1572872 | tf_op jit(solution)/shard_map/ppermute | solution.py:92
  43.1 3.8 %collective-permute-start.5 = (f32[2,64,256]{2,1,0:T(8,128)S(1)}, f32[2,64,256]{2,1,0:T(8,128)S(1)}, u32[]{:S(2)}, u32[]{:S(2)}) collective-permute-start(f32[2,64,256]{2,1,0:T(8,128)S(1)} %convolution_bitcast_fusion.1), channel_id=1, source_target_pairs={{0,1},{1,0},{2,3},{3,2},{4,5},{5,4},{6,7},{7,6},{8,9},{9,8},{10,11... | collective-permute-start | bytes 393224 | tf_op jit(solution)/shard_map/ppermute | solution.py:95
  43.4 14.0 %collective-permute-start.4 = (f32[2,64,256]{2,1,0:T(8,128)S(1)}, f32[2,64,256]{2,1,0:T(8,128)S(1)}, u32[]{:S(2)}, u32[]{:S(2)}) collective-permute-start(f32[2,64,256]{2,1,0:T(8,128)S(1)} %convolution_bitcast_fusion.2), channel_id=1, source_target_pairs={{1,2},{3,4},{5,6},{7,8},{9,10},{11,12},{13,14},{17,18},{19,20},{21... | collective-permute-start | bytes 393224 | tf_op jit(solution)/shard_map/ppermute | solution.py:92
  57.8 2.7 %collective-permute-start.7 = (f32[2,64,256]{2,1,0:T(8,128)S(1)}, f32[2,64,256]{2,1,0:T(8,128)S(1)}, u32[]{:S(2)}, u32[]{:S(2)}) collective-permute-start(f32[2,64,256]{2,1,0:T(8,128)S(1)} %pad_maximum_fusion.19), channel_id=1, source_target_pairs={{0,1},{1,0},{2,3},{3,2},{4,5},{5,4},{6,7},{7,6},{8,9},{9,8},{10,11... | collective-permute-start | bytes 393224 | tf_op jit(solution)/shard_map/ppermute | solution.py:95
  57.9 5.2 %collective-permute-start.6 = (f32[2,64,256]{2,1,0:T(8,128)S(1)}, f32[2,64,256]{2,1,0:T(8,128)S(1)}, u32[]{:S(2)}, u32[]{:S(2)}) collective-permute-start(f32[2,64,256]{2,1,0:T(8,128)S(1)} %pad_maximum_fusion.19), channel_id=1, source_target_pairs={{1,2},{3,4},{5,6},{7,8},{9,10},{11,12},{13,14},{17,18},{19,20},{21... | collective-permute-start | bytes 393224 | tf_op jit(solution)/shard_map/ppermute | solution.py:92
  63.3 3.2 %collective-permute-start.9 = (f32[2,64,256]{2,1,0:T(8,128)S(1)}, f32[2,64,256]{2,1,0:T(8,128)S(1)}, u32[]{:S(2)}, u32[]{:S(2)}) collective-permute-start(f32[2,64,256]{2,1,0:T(8,128)S(1)} %pad_maximum_fusion.21), channel_id=1, source_target_pairs={{0,1},{1,0},{2,3},{3,2},{4,5},{5,4},{6,7},{7,6},{8,9},{9,8},{10,11... | collective-permute-start | bytes 393224 | tf_op jit(solution)/shard_map/ppermute | solution.py:95
  63.6 5.5 %collective-permute-start.8 = (f32[2,64,256]{2,1,0:T(8,128)S(1)}, f32[2,64,256]{2,1,0:T(8,128)S(1)}, u32[]{:S(2)}, u32[]{:S(2)}) collective-permute-start(f32[2,64,256]{2,1,0:T(8,128)S(1)} %pad_maximum_fusion.21), channel_id=1, source_target_pairs={{1,2},{3,4},{5,6},{7,8},{9,10},{11,12},{13,14},{17,18},{19,20},{21... | collective-permute-start | bytes 393224 | tf_op jit(solution)/shard_map/ppermute | solution.py:92
  69.3 3.4 %collective-permute-start.11 = (f32[2,64,256]{2,1,0:T(8,128)S(1)}, f32[2,64,256]{2,1,0:T(8,128)S(1)}, u32[]{:S(2)}, u32[]{:S(2)}) collective-permute-start(f32[2,64,256]{2,1,0:T(8,128)S(1)} %pad_maximum_fusion.23), channel_id=1, source_target_pairs={{0,1},{1,0},{2,3},{3,2},{4,5},{5,4},{6,7},{7,6},{8,9},{9,8},{10,11... | collective-permute-start | bytes 393224 | tf_op jit(solution)/shard_map/ppermute | solution.py:95
  69.4 5.9 %collective-permute-start.10 = (f32[2,64,256]{2,1,0:T(8,128)S(1)}, f32[2,64,256]{2,1,0:T(8,128)S(1)}, u32[]{:S(2)}, u32[]{:S(2)}) collective-permute-start(f32[2,64,256]{2,1,0:T(8,128)S(1)} %pad_maximum_fusion.23), channel_id=1, source_target_pairs={{1,2},{3,4},{5,6},{7,8},{9,10},{11,12},{13,14},{17,18},{19,20},{21... | collective-permute-start | bytes 393224 | tf_op jit(solution)/shard_map/ppermute | solution.py:92
  75.7 6.1 %collective-permute-start.15 = (f32[2,64,256]{2,1,0:T(8,128)S(1)}, f32[2,64,256]{2,1,0:T(8,128)S(1)}, u32[]{:S(2)}, u32[]{:S(2)}) collective-permute-start(f32[2,64,256]{2,1,0:T(8,128)S(1)} %pad_maximum_fusion.25), channel_id=1, source_target_pairs={{0,1},{1,0},{2,3},{3,2},{4,5},{5,4},{6,7},{7,6},{8,9},{9,8},{10,11... | collective-permute-start | bytes 393224 | tf_op jit(solution)/shard_map/ppermute | solution.py:95
  75.8 7.5 %collective-permute-start.14 = (f32[2,64,256]{2,1,0:T(8,128)S(1)}, f32[2,64,256]{2,1,0:T(8,128)S(1)}, u32[]{:S(2)}, u32[]{:S(2)}) collective-permute-start(f32[2,64,256]{2,1,0:T(8,128)S(1)} %pad_maximum_fusion.25), channel_id=1, source_target_pairs={{1,2},{3,4},{5,6},{7,8},{9,10},{11,12},{13,14},{17,18},{19,20},{21... | collective-permute-start | bytes 393224 | tf_op jit(solution)/shard_map/ppermute | solution.py:92
  85.8 13.1 %collective-permute-start.16 = (f32[2,128,512]{2,1,0:T(8,128)S(1)}, f32[2,128,512]{2,1,0:T(8,128)S(1)}, u32[]{:S(2)}, u32[]{:S(2)}) collective-permute-start(f32[2,128,512]{2,1,0:T(8,128)S(1)} %get-tuple-element.84), channel_id=1, source_target_pairs={{1,2},{3,4},{5,6},{7,8},{9,10},{11,12},{13,14},{17,18},{19,20},{21... | collective-permute-start | bytes 1572872 | tf_op jit(solution)/shard_map/ppermute | solution.py:92
  87.2 11.8 %collective-permute-start.17 = (f32[2,128,512]{2,1,0:T(8,128)S(1)}, f32[2,128,512]{2,1,0:T(8,128)S(1)}, u32[]{:S(2)}, u32[]{:S(2)}) collective-permute-start(f32[2,128,512]{2,1,0:T(8,128)S(1)} %pad_maximum_fusion.14), channel_id=1, source_target_pairs={{0,1},{1,0},{2,3},{3,2},{4,5},{5,4},{6,7},{7,6},{8,9},{9,8},{10,11... | collective-permute-start | bytes 1572872 | tf_op jit(solution)/shard_map/ppermute | solution.py:95
  99.5 1.2 %copy-start.3 = (f32[2,128,512]{2,1,0:T(8,128)S(1)}, f32[2,128,512]{2,1,0:T(8,128)}, u32[]{:S(2)}) copy-start(f32[2,128,512]{2,1,0:T(8,128)} %param.5) | copy-start | bytes 1572868

commit v2 on v0

v2 whole, which is shorter than its diff:
```python
import functools

import jax
import jax.numpy as jnp
from jax import lax
from jax.experimental import pallas as pl
from jax.experimental.pallas import tpu as pltpu
from jax.sharding import PartitionSpec as P

SWEEPS = 2
COARSE_SWEEPS = 4

GRADIENT_ENERGY = 1.0
TIME_STEP = 0.02
DAMPING = 0.8
KEEP = 1.0 - DAMPING
COARSE_ENERGY = GRADIENT_ENERGY / 4.0
COARSE_STEP = TIME_STEP / 4.0


VMEM = pl.BlockSpec(memory_space=pltpu.VMEM)
SMEM = pl.BlockSpec(memory_space=pltpu.SMEM)
ANY = pl.BlockSpec(memory_space=pl.ANY)
BLOCK = 16
F32 = jnp.float32


def chip_pairs(count):
    return [(i, i ^ 1) for i in range(count)]


def cross_pairs(groups, count):
    pairs = []
    for g in range(groups):
        pairs += [(g * count + i, g * count + i + 1) for i in range(1, count - 1, 2)]
    for g in range(0, groups - 1, 2):
        pairs += [(g * count + i, (g + 1) * count + i) for i in (0, count - 1)]
    swaps = pairs + [(b, a) for a, b in pairs]
    if groups % 2 == 1:
        swaps += [((groups - 1) * count + i,) * 2 for i in (0, count - 1)]
    return swaps


def call(body, name, outs, args, in_specs=None, out_specs=None, scratch=(), aliases=None, work=30):
    shapes = [jax.ShapeDtypeStruct(s, F32) for s in outs]
    size = sum(int(a.size) for a in args)
    made = sum(s.size for s in shapes)
    return pl.pallas_call(
        body,
        out_shape=shapes,
        in_specs=in_specs or [VMEM] * len(args),
        out_specs=out_specs or [VMEM] * len(outs),
        scratch_shapes=list(scratch),
        input_output_aliases=aliases or {},
        name=name,
        cost_estimate=pl.CostEstimate(flops=work * made, bytes_accessed=4 * (size + made), transcendentals=0),
        compiler_params=pltpu.CompilerParams(vmem_limit_bytes=24 * 1024 * 1024),
    )(*args)


def blocks(rows):
    return range(0, rows, BLOCK)


def around(read, r, rows):
    x = read(r, r + BLOCK)
    cols = x.shape[-1]
    row = lax.broadcasted_iota(jnp.int32, x.shape, 0)
    col = lax.broadcasted_iota(jnp.int32, x.shape, 1)
    up = read(r - 1, r - 1 + BLOCK) if r > 0 else jnp.where(row == 0, 0.0, pltpu.roll(x, 1, 0))
    if r + BLOCK < rows:
        down = read(r + 1, r + 1 + BLOCK)
    else:
        down = jnp.where(row == BLOCK - 1, 0.0, pltpu.roll(x, BLOCK - 1, 0))
    left = jnp.where(col == 0, 0.0, pltpu.roll(x, 1, 1))
    right = jnp.where(col == cols - 1, 0.0, pltpu.roll(x, cols - 1, 1))
    return x, (up + down) + (left + right)


def reader(ref, *lead):
    return lambda lo, hi: ref[(*lead, slice(lo, hi))]


def add_terms(base_p, base_m, gain, gain_kt, nb_p, nb_m, energy, step):
    new_p = base_p - gain * (energy * nb_m) + gain_kt * nb_p
    new_m = base_m + gain * (step * nb_p + (6.0 * step * energy) * nb_m)
    return new_p, new_m


def parts3(x):
    high = x.astype(jnp.bfloat16)
    rest = x - high.astype(F32)
    middle = rest.astype(jnp.bfloat16)
    low = (rest - middle.astype(F32)).astype(jnp.bfloat16)
    return high, middle, low


def pair_cols(x, pair):
    return sum(jnp.dot(v, pair, preferred_element_type=F32) for v in parts3(x))


def copy_cols(x, pair):
    dims = (((1,), (1,)), ((), ()))
    return sum(lax.dot_general(v, pair, dims, preferred_element_type=F32) for v in parts3(x))


LANES = 128


def tiles(rows, cols):
    return pltpu.VMEM((cols // LANES, rows, LANES), F32)


def put_rows(ref, rows, x):
    for j in range(ref.shape[0]):
        ref[j, rows] = x[:, j * LANES : (j + 1) * LANES]


def get_rows(ref, rows):
    return jnp.concatenate([ref[j, rows] for j in range(ref.shape[0])], axis=1)


def even_odd(ref):
    half = ref.shape[1] // 2
    return pl.ds(0, half, stride=2), pl.ds(1, half, stride=2)


def pair_rows(ref):
    even, odd = even_odd(ref)
    return get_rows(ref, even) + get_rows(ref, odd)


def split_body(where, warm, far, near, sems):
    c = where[0]
    first = pltpu.make_async_copy(warm.at[:, c], far, sems.at[0])
    second = pltpu.make_async_copy(warm.at[:, 1 - c], near, sems.at[1])
    first.start()
    second.start()
    first.wait()
    second.wait()


def setup_body(where, phi, cot, gain, gain_kt, own):
    c = where[0]
    for i in range(2):
        plane = c if i == 0 else 1 - c
        for r in blocks(phi.shape[1]):
            rows = slice(r, r + BLOCK)
            v = phi[plane, rows]
            k = 3.0 * v * v - 1.0 + 6.0 * GRADIENT_ENERGY
            g = DAMPING / (1.0 + 6.0 * TIME_STEP * k)
            s0, s1 = cot[0, plane, rows], cot[1, plane, rows]
            gain[i, rows] = g
            gain_kt[i, rows] = g * k * TIME_STEP
            own[i, 0, rows] = g * (s0 + k * s1)
            own[i, 1, rows] = g * (s1 - 6.0 * TIME_STEP * s0)


def coarse_setup_body(phi, pair, gain, gain_kt, both):
    for r in blocks(phi.shape[1]):
        rows = slice(r, r + BLOCK)
        a, b = phi[0, rows], phi[1, rows]
        put_rows(both, rows, (3.0 * a * a - 1.0) + (3.0 * b * b - 1.0))
    k = pair_cols(pair_rows(both), pair[...]) / 8.0 + 6.0 * COARSE_ENERGY
    g = DAMPING / (1.0 + 6.0 * COARSE_STEP * k)
    gain[...] = g
    gain_kt[...] = g * k * COARSE_STEP


def part_body(far, near, gain, gain_kt, own, far_out, near_out):
    rows_all = far.shape[1]
    for i, (mine, other, out) in enumerate(((far, near, far_out), (near, far, near_out))):
        for r in blocks(rows_all):
            rows = slice(r, r + BLOCK)
            p, nb_p = around(reader(mine, 0), r, rows_all)
            m, nb_m = around(reader(mine, 1), r, rows_all)
            out[0, rows], out[1, rows] = add_terms(
                KEEP * p + own[i, 0, rows],
                KEEP * m + own[i, 1, rows],
                gain[i, rows],
                gain_kt[i, rows],
                nb_p + other[0, rows],
                nb_m + other[1, rows],
                GRADIENT_ENERGY,
                TIME_STEP,
            )


def finish_body(i, keep, part, halo, gain, gain_kt, out):
    for r in blocks(part.shape[1]):
        rows = slice(r, r + BLOCK)
        hp, hm = halo[0, rows], halo[1, rows]
        if i == 0:
            hp, hm = hp * keep[0], hm * keep[0]
        out[0, rows], out[1, rows] = add_terms(
            part[0, rows], part[1, rows], gain[i, rows], gain_kt[i, rows], hp, hm, GRADIENT_ENERGY, TIME_STEP
        )


def finish_pool_body(i, keep, part, halo, gain, gain_kt, pair, pool, out, tile):
    finish_body(i, keep, part, halo, gain, gain_kt, out)
    for f in range(2):
        for r in blocks(part.shape[1]):
            rows = slice(r, r + BLOCK)
            put_rows(tile, rows, out[f, rows])
        pool[f] = pair_cols(pair_rows(tile), pair[...])


def defect_body(where, far, near, phi, cot, pair, out, total, tile):
    c = where[0]
    rows_all = far.shape[1]
    for i, (mine, other) in enumerate(((far, near), (near, far))):
        plane = c if i == 0 else 1 - c
        for r in blocks(rows_all):
            rows = slice(r, r + BLOCK)
            p, nb_p = around(reader(mine, 0), r, rows_all)
            m, nb_m = around(reader(mine, 1), r, rows_all)
            v = phi[plane, rows]
            lap_p = nb_p + other[0, rows] - 6.0 * p
            lap_m = nb_m + other[1, rows] - 6.0 * m
            r0 = cot[0, plane, rows] - (p - (3.0 * v * v - 1.0) * m + GRADIENT_ENERGY * lap_m)
            r1 = cot[1, plane, rows] - (m - TIME_STEP * lap_p)
            total[0, rows] = r0 if i == 0 else total[0, rows] + r0
            total[1, rows] = r1 if i == 0 else total[1, rows] + r1
    for f in range(2):
        for r in blocks(rows_all):
            rows = slice(r, r + BLOCK)
            put_rows(tile, rows, total[f, rows])
        out[f] = pair_cols(pair_rows(tile), pair[...]) / 8.0


def coarse_first_body(keep, local, far, near, gain, gain_kt, out):
    for r in blocks(local.shape[1]):
        rows = slice(r, r + BLOCK)
        s0 = local[0, rows] - (GRADIENT_ENERGY / 8.0) * (far[1, rows] * keep[0] + near[1, rows])
        s1 = local[1, rows] + (TIME_STEP / 8.0) * (far[0, rows] * keep[0] + near[0, rows])
        g = gain[rows]
        out[0, rows] = g * s0 + (gain_kt[rows] / COARSE_STEP) * s1
        out[1, rows] = g * (s1 - 6.0 * COARSE_STEP * s0)


def coarse_part_body(fix, own, gain, gain_kt, out):
    rows_all = fix.shape[1]
    for r in blocks(rows_all):
        rows = slice(r, r + BLOCK)
        p, nb_p = around(reader(fix, 0), r, rows_all)
        m, nb_m = around(reader(fix, 1), r, rows_all)
        out[0, rows], out[1, rows] = add_terms(
            KEEP * p + own[0, rows],
            KEEP * m + own[1, rows],
            gain[rows],
            gain_kt[rows],
            nb_p,
            nb_m,
            COARSE_ENERGY,
            COARSE_STEP,
        )


def coarse_finish_body(keep, part, far, near, gain, gain_kt, out):
    for r in blocks(part.shape[1]):
        rows = slice(r, r + BLOCK)
        out[0, rows], out[1, rows] = add_terms(
            part[0, rows],
            part[1, rows],
            gain[rows],
            gain_kt[rows],
            far[0, rows] * keep[0] + near[0, rows],
            far[1, rows] * keep[0] + near[1, rows],
            COARSE_ENERGY,
            COARSE_STEP,
        )


def spread_into(tile, fix, pair):
    wide = copy_cols(fix, pair)
    for rows in even_odd(tile):
        put_rows(tile, rows, wide)


def correct_body(far, near, fix, pair, far_out, near_out, tile):
    for f in range(2):
        spread_into(tile, fix[f], pair[...])
        for r in blocks(far.shape[1]):
            rows = slice(r, r + BLOCK)
            wide = get_rows(tile, rows)
            far_out[f, rows] = far[f, rows] + wide
            near_out[f, rows] = near[f, rows] + wide


def finish_fix_body(i, keep, part, halo, pair, gain, gain_kt, out, phase, chem):
    spread_into(phase, halo[0], pair[...])
    spread_into(chem, halo[1], pair[...])
    for r in blocks(part.shape[1]):
        rows = slice(r, r + BLOCK)
        hp, hm = get_rows(phase, rows), get_rows(chem, rows)
        if i == 0:
            hp, hm = hp * keep[0], hm * keep[0]
        out[0, rows], out[1, rows] = add_terms(
            part[0, rows], part[1, rows], gain[i, rows], gain_kt[i, rows], hp, hm, GRADIENT_ENERGY, TIME_STEP
        )


def final_plane(i, where, keep, part, halo, gain, gain_kt, phi, psi, adjoint, design, plane_out, grad_out, sems):
    c = where[0]
    plane = c if i == 0 else 1 - c
    rows_all = part.shape[1]
    step = rows_all // 2
    copies = []
    for n, lo in enumerate(range(0, rows_all, step)):
        for r in range(lo, lo + step, BLOCK):
            rows = slice(r, r + BLOCK)
            hp, hm = halo[0, rows], halo[1, rows]
            if i == 0:
                hp, hm = hp * keep[0], hm * keep[0]
            p, m = add_terms(
                part[0, rows], part[1, rows], gain[i, rows], gain_kt[i, rows], hp, hm, GRADIENT_ENERGY, TIME_STEP
            )
            plane_out[0, rows] = p
            plane_out[1, rows] = m
            grad_out[rows] = 6.0 * phi[plane, rows] * psi[plane, rows] * m
        rows = pl.ds(lo, step)
        copies.append(pltpu.make_async_copy(plane_out.at[:, rows], adjoint.at[:, plane, rows], sems.at[2 * n]))
        copies.append(pltpu.make_async_copy(grad_out.at[rows], design.at[plane, rows], sems.at[2 * n + 1]))
        copies[-2].start()
        copies[-1].start()
    for copy in copies:
        copy.wait()


def last_near_body(where, keep, part, halo, gain, gain_kt, phi, psi, adjoint, design, plane_out, grad_out, sems):
    final_plane(1, where, keep, part, halo, gain, gain_kt, phi, psi, adjoint, design, plane_out, grad_out, sems)


def last_far_body(
    where, keep, part, halo, gain, gain_kt, phi, psi, a_in, d_in, adjoint, design, plane_out, grad_out, sems
):
    final_plane(0, where, keep, part, halo, gain, gain_kt, phi, psi, adjoint, design, plane_out, grad_out, sems)


def on_device(phase_lin, phase_state, cotangent, warm_start):
    groups, count = lax.axis_size("grp"), lax.axis_size("gx")
    me = lax.axis_index("gx")
    where = jnp.reshape(me % 2, (1,)).astype(jnp.int32)
    keep = jnp.reshape(((me > 0) & (me < count - 1)).astype(F32), (1,))
    across, on_chip = cross_pairs(groups, count), chip_pairs(count)
    rows, cols = phase_lin.shape[1:]
    full, half = (2, rows, cols), (2, rows // 2, cols // 2)
    pair = lax.broadcasted_iota(jnp.int32, (cols, cols // 2), 0) // 2
    pair = (pair == lax.broadcasted_iota(jnp.int32, (cols, cols // 2), 1)).astype(jnp.bfloat16)

    def swap_far(x):
        return lax.ppermute(x, ("grp", "gx"), across)

    def swap_near(x):
        return lax.ppermute(x, "gx", on_chip)

    def finish(i, part, halo):
        body = functools.partial(finish_body, i)
        return call(body, "finish", [full], (keep, part, halo, gain, gain_kt), [SMEM] + [VMEM] * 4, work=8)[0]

    far, near = call(
        split_body, "split", [full, full], (where, warm_start), [SMEM, ANY], scratch=[pltpu.SemaphoreType.DMA((2,))]
    )
    far_halo, near_halo = swap_far(far), swap_near(near)
    gain, gain_kt, own = call(
        setup_body, "setup", [full, full, (2, 2, rows, cols)], (where, phase_lin, cotangent), [SMEM, VMEM, VMEM]
    )

    def part_of(far, near):
        return call(part_body, "part", [full, full], (far, near, gain, gain_kt, own))

    far_part, near_part = part_of(far, near)
    far, near = finish(0, far_part, far_halo), finish(1, near_part, near_halo)
    for sweep_index in range(SWEEPS - 2):
        far_halo, near_halo = swap_far(far), swap_near(near)
        far_part, near_part = part_of(far, near)
        far, near = finish(0, far_part, far_halo), finish(1, near_part, near_halo)

    far_halo, near_halo = swap_far(far), swap_near(near)
    far_part, near_part = part_of(far, near)
    coarse_gain, coarse_kt = call(
        coarse_setup_body, "coarse_setup", [half[1:], half[1:]], (phase_lin, pair), scratch=[tiles(rows, cols)]
    )

    def finish_pool(i, part, halo):
        body = functools.partial(finish_pool_body, i)
        specs = [SMEM] + [VMEM] * 5
        args = (keep, part, halo, gain, gain_kt, pair)
        return call(body, "finish_pool", [half, full], args, specs, scratch=[tiles(rows, cols)], work=8)

    near_pool, near = finish_pool(1, near_part, near_halo)
    far_pool, far = finish_pool(0, far_part, far_halo)

    far_sums, near_sums = swap_far(far_pool), swap_near(near_pool)
    near_halo = swap_near(near)
    piece = rows // COARSE_SWEEPS
    far_pieces = [far[:, n * piece : (n + 1) * piece] for n in range(COARSE_SWEEPS)]
    arrived = [swap_far(far_pieces[0])]
    local = call(
        defect_body,
        "defect",
        [half],
        (where, far, near, phase_lin, cotangent, pair),
        [SMEM] + [VMEM] * 5,
        scratch=[pltpu.VMEM(full, F32), tiles(rows, cols)],
    )[0]
    fix = call(
        coarse_first_body,
        "coarse_first",
        [half],
        (keep, local, far_sums, near_sums, coarse_gain, coarse_kt),
        [SMEM] + [VMEM] * 5,
        work=8,
    )[0]
    first = fix
    for sweep_index in range(COARSE_SWEEPS - 1):
        far_sums, near_sums = swap_far(fix), swap_near(fix)
        fix, held = lax.optimization_barrier((fix, far_pieces[sweep_index + 1]))
        arrived.append(swap_far(held))
        part = call(coarse_part_body, "coarse_part", [half], (fix, first, coarse_gain, coarse_kt))[0]
        part, arrived[sweep_index] = lax.optimization_barrier((part, arrived[sweep_index]))
        fix = call(
            coarse_finish_body,
            "coarse_finish",
            [half],
            (keep, part, far_sums, near_sums, coarse_gain, coarse_kt),
            [SMEM] + [VMEM] * 5,
            work=8,
        )[0]

    far_sums, near_sums = swap_far(fix), swap_near(fix)
    far, near = call(
        correct_body, "correct", [full, full], (far, near, fix, pair), scratch=[tiles(rows, cols)], work=4
    )
    far_part, near_part = part_of(far, near)
    far_part = finish(0, far_part, jnp.concatenate(arrived, axis=1))
    near_part = finish(1, near_part, near_halo)

    def finish_fix(i, part, halo):
        body = functools.partial(finish_fix_body, i)
        args = (keep, part, halo, pair, gain, gain_kt)
        scratch = [tiles(rows, cols)] * 2
        return call(body, "finish_fix", [full], args, [SMEM] + [VMEM] * 5, scratch=scratch, work=8)[0]

    near = finish_fix(1, near_part, near_sums)
    far = finish_fix(0, far_part, far_sums)
    for sweep_index in range(SWEEPS - 2):
        far_halo, near_halo = swap_far(far), swap_near(near)
        far_part, near_part = part_of(far, near)
        far, near = finish(0, far_part, far_halo), finish(1, near_part, near_halo)

    far_halo, near_halo = swap_far(far), swap_near(near)
    far_part, near_part = part_of(far, near)
    outs = [(2, 2, rows, cols), full]
    scratch = [pltpu.VMEM(full, F32), pltpu.VMEM((rows, cols), F32), pltpu.SemaphoreType.DMA((4,))]
    args = (gain, gain_kt, phase_lin, phase_state)
    adjoint, design = call(
        last_near_body,
        "last_near",
        outs,
        (where, keep, near_part, near_halo, *args),
        [SMEM, SMEM] + [VMEM] * 6,
        [ANY, ANY],
        scratch,
        work=10,
    )
    adjoint, design = call(
        last_far_body,
        "last_far",
        outs,
        (where, keep, far_part, far_halo, *args, adjoint, design),
        [SMEM, SMEM] + [VMEM] * 6 + [ANY, ANY],
        [ANY, ANY],
        scratch,
        {8: 0, 9: 1},
        work=10,
    )
    return (adjoint, design)


def solution(mesh):
    in_specs = (
        P(("grp", "gx"), None, None),
        P(("grp", "gx"), None, None),
        P(None, ("grp", "gx"), None, None),
        P(None, ("grp", "gx"), None, None),
    )
    out_specs = (P(None, ("grp", "gx"), None, None), P(("grp", "gx"), None, None))
    return jax.shard_map(
        on_device, mesh=mesh, in_specs=in_specs, out_specs=out_specs, check_vma=False
    )
```

time: 244 us -> 82.3 us (0.34)
  the two profiles are of different devices: /device:TPU:1 before, /device:TPU:25 now
where the time goes in v2:
time: 82.3 us; the launch traced here: 82 us
  waiting for transfers between devices  55.7 us (68%)
  Pallas kernels  11.8 us (14%)
  starting transfers between devices  10.7 us (13%)
  local copies, waits for them, and re-layouts  2.5 us (3%)
  between operations  1.01 us (1%)
    ppermute x12, waiting for transfers between devices, swap_far(): return lax.ppermute(x, ('grp', 'gx'), across)  55.7 us
    pallas_call x26, Pallas kernels, call(): pl.pallas_call(body, out_shape=shapes, in_specs=in_specs or [VMEM] * len(...  11.8 us
    ppermute x12, starting transfers between devices, swap_far(): return lax.ppermute(x, ('grp', 'gx'), across)  7.31 us
    ppermute x9, starting transfers between devices, swap_near(): return lax.ppermute(x, 'gx', on_chip)  3.37 us
    unnamed x10, local copies, waits for them, and re-layouts  2.47 us
  transfers between devices with their start and end apart: 21, of which 12 were waited for; matrix products, arithmetic and copies ran while one was open for 0% of the time, Pallas kernels for 13%

profile of v2, /device:TPU:25, one launch (start us, length us, event | category | flops | bytes accessed | tf_op | source)
XLA Modules:
  0.0 82.0 jit_solution(3061781610910482124)
XLA Ops:
  0.7 1.2 %copy-done.4 = f32[2,2,128,512]{3,2,1,0:T(8,128)S(1)} copy-done((f32[2,2,128,512]{3,2,1,0:T(8,128)S(1)}, f32[2,2,128,512]{3,2,1,0:T(8,128)}, u32[]{:S(2)}) %copy-start.4) | copy-done | bytes 1048600
  1.9 0.1 split.1
  2.0 0.7 collective-permute-start.1
  2.7 1.2 %collective-permute-start = (f32[2,128,512]{2,1,0:T(8,128)S(1)}, f32[2,128,512]{2,1,0:T(8,128)S(1)}, u32[]{:S(2)}, u32[]{:S(2)}) collective-permute-start(f32[2,128,512]{2,1,0:T(8,128)S(1)} %get-tuple-element.37.far), channel_id=1, source_target_pairs={{1,2},{3,4},{5,6},{7,8},{9,10},{11,12},{13,14},{17,18},{19,20},{21... | collective-permute-start | bytes 1572872 | tf_op jit(solution)/shard_map/ppermute | solution.py:353
  3.9 1.2 %copy-done.1 = f32[2,2,128,512]{3,2,1,0:T(8,128)S(1)} copy-done((f32[2,2,128,512]{3,2,1,0:T(8,128)S(1)}, f32[2,2,128,512]{3,2,1,0:T(8,128)}, u32[]{:S(2)}) %copy-start.1) | copy-done | bytes 1048600
  5.1 0.3 setup.1
  5.4 0.9 %part.4 = (f32[2,128,512]{2,1,0:T(8,128)S(1)}, f32[2,128,512]{2,1,0:T(8,128)S(1)}) custom-call(f32[2,128,512]{2,1,0:T(8,128)S(1)} %get-tuple-element.37.far, f32[2,128,512]{2,1,0:T(8,128)S(1)} %get-tuple-element.38.near, f32[2,128,512]{2,1,0:T(8,128)S(1)} %get-tuple-element.39.gain, f32[2,128,512]{2,1,0:T(8,128)S(1)} %get-tuple-element.40.gain_kt, ...), custom_call_target="tpu_custom_call" | custom-call | flops 7864320 | bytes 4194304 | tf_op jit(solution)/shard_map/part/pallas_call | solution.py:48
  6.4 0.0 collective-permute-done.1.halo
  6.4 0.1 finish.5.near
  6.5 0.4 collective-permute-start.3
  6.8 15.7 %collective-permute-done.halo = f32[2,128,512]{2,1,0:T(8,128)S(1)} collective-permute-done((f32[2,128,512]{2,1,0:T(8,128)S(1)}, f32[2,128,512]{2,1,0:T(8,128)S(1)}, u32[]{:S(2)}, u32[]{:S(2)}) %collective-permute-start) | collective-permute-done | bytes 524320 | tf_op jit(solution)/shard_map/ppermute | solution.py:353
  22.6 0.1 finish.4.far
  22.7 0.1 collective-permute-start.2
  22.8 0.3 fusion.pair
  23.0 0.3 coarse_setup.1
  23.4 0.9 %part.5 = (f32[2,128,512]{2,1,0:T(8,128)S(1)}, f32[2,128,512]{2,1,0:T(8,128)S(1)}) custom-call(f32[2,128,512]{2,1,0:T(8,128)S(1)} %finish.4.far, f32[2,128,512]{2,1,0:T(8,128)S(1)} %finish.5.near, f32[2,128,512]{2,1,0:T(8,128)S(1)} %get-tuple-element.39.gain, f32[2,128,512]{2,1,0:T(8,128)S(1)} %get-tuple-element.40.gain_kt, ...), custom_call_target="tpu_custom_call" | custom-call | flops 7864320 | bytes 4194304 | tf_op jit(solution)/shard_map/part/pallas_call | solution.py:48
  24.3 0.5 finish_pool.3
  24.8 0.1 collective-permute-start.5
  24.9 9.3 %collective-permute-done.2.halo = f32[2,128,512]{2,1,0:T(8,128)S(1)} collective-permute-done((f32[2,128,512]{2,1,0:T(8,128)S(1)}, f32[2,128,512]{2,1,0:T(8,128)S(1)}, u32[]{:S(2)}, u32[]{:S(2)}) %collective-permute-start.2) | collective-permute-done | bytes 524320 | tf_op jit(solution)/shard_map/ppermute | solution.py:353
  34.1 0.5 finish_pool.2
  34.7 0.0 copy-start.2
  34.7 0.1 collective-permute-start.4
  34.8 1.8 %collective-permute-start.6 = (f32[2,32,512]{2,1,0:T(8,128)S(1)}, f32[2,32,512]{2,1,0:T(8,128)S(1)}, u32[]{:S(2)}, u32[]{:S(2)}) collective-permute-start(f32[2,32,512]{2,1,0:T(8,128)S(1)} %get-tuple-element.74), channel_id=1, source_target_pairs={{1,2},{3,4},{5,6},{7,8},{9,10},{11,12},{13,14},{17,18},{19,20},{21... | collective-permute-start | bytes 393224 | tf_op jit(solution)/shard_map/ppermute | solution.py:353
  36.6 1.4 %defect.1.local = f32[2,64,256]{2,1,0:T(8,128)S(1)} custom-call(s32[1]{0:T(128)} %bitcast.where, f32[2,128,512]{2,1,0:T(8,128)S(1)} %get-tuple-element.45.far, f32[2,128,512]{2,1,0:T(8,128)S(1)} %get-tuple-element.47.near, f32[2,128,512]{2,1,0:T(8,128)S(1)} %copy-done, f32[2,2,128,512]{3,2,1,0:T(8,128)S(1)} %copy-done.2, bf16[512,256]{1,0:T(8,128)(2,1)S(1)} %fusion.pair), custom_call_target="tpu_custom_call" | custom-call | flops 983040 | bytes 3276804 | tf_op jit(solution)/shard_map/defect/pallas_call | solution.py:48
  38.0 1.2 %collective-permute-done.4.far = f32[2,64,256]{2,1,0:T(8,128)S(1)} collective-permute-done((f32[2,64,256]{2,1,0:T(8,128)S(1)}, f32[2,64,256]{2,1,0:T(8,128)S(1)}, u32[]{:S(2)}, u32[]{:S(2)}) %collective-permute-start.4) | collective-permute-done | bytes 131104 | tf_op jit(solution)/shard_map/ppermute | solution.py:353
  39.2 0.1 collective-permute-start.7
  39.2 0.1 collective-permute-start.8
  39.3 0.5 collective-permute-start.17
  39.8 0.2 coarse_part.3.part
  40.0 0.5 collective-permute-done.6
  40.5 1.2 %collective-permute-start.9 = (f32[2,32,512]{2,1,0:T(8,128)S(1)}, f32[2,32,512]{2,1,0:T(8,128)S(1)}, u32[]{:S(2)}, u32[]{:S(2)}) collective-permute-start(f32[2,32,512]{2,1,0:T(8,128)S(1)} %get-tuple-element.55), channel_id=1, source_target_pairs={{1,2},{3,4},{5,6},{7,8},{9,10},{11,12},{13,14},{17,18},{19,20},{21... | collective-permute-start | bytes 393224 | tf_op jit(solution)/shard_map/ppermute | solution.py:353
  41.7 4.9 %collective-permute-done.7.far = f32[2,64,256]{2,1,0:T(8,128)S(1)} collective-permute-done((f32[2,64,256]{2,1,0:T(8,128)S(1)}, f32[2,64,256]{2,1,0:T(8,128)S(1)}, u32[]{:S(2)}, u32[]{:S(2)}) %collective-permute-start.7) | collective-permute-done | bytes 131104 | tf_op jit(solution)/shard_map/ppermute | solution.py:353
  46.6 0.0 collective-permute-done.8.near
  46.7 0.1 collective-permute-start.10
  46.8 0.1 collective-permute-start.11
  46.8 0.2 coarse_part.4.part
  47.0 0.8 %collective-permute-done.9 = f32[2,32,512]{2,1,0:T(8,128)S(1)} collective-permute-done((f32[2,32,512]{2,1,0:T(8,128)S(1)}, f32[2,32,512]{2,1,0:T(8,128)S(1)}, u32[]{:S(2)}, u32[]{:S(2)}) %collective-permute-start.9) | collective-permute-done | bytes 131104 | tf_op jit(solution)/shard_map/ppermute | solution.py:353
  47.8 0.9 %collective-permute-start.12 = (f32[2,32,512]{2,1,0:T(8,128)S(1)}, f32[2,32,512]{2,1,0:T(8,128)S(1)}, u32[]{:S(2)}, u32[]{:S(2)}) collective-permute-start(f32[2,32,512]{2,1,0:T(8,128)S(1)} %get-tuple-element.58), channel_id=1, source_target_pairs={{1,2},{3,4},{5,6},{7,8},{9,10},{11,12},{13,14},{17,18},{19,20},{21... | collective-permute-start | bytes 393224 | tf_op jit(solution)/shard_map/ppermute | solution.py:353
  48.7 5.2 %collective-permute-done.10.far = f32[2,64,256]{2,1,0:T(8,128)S(1)} collective-permute-done((f32[2,64,256]{2,1,0:T(8,128)S(1)}, f32[2,64,256]{2,1,0:T(8,128)S(1)}, u32[]{:S(2)}, u32[]{:S(2)}) %collective-permute-start.10) | collective-permute-done | bytes 131104 | tf_op jit(solution)/shard_map/ppermute | solution.py:353
  54.0 0.1 collective-permute-start.13
  54.1 0.1 collective-permute-start.14
  54.1 0.2 coarse_part.5.part
  54.3 1.0 %collective-permute-done.12 = f32[2,32,512]{2,1,0:T(8,128)S(1)} collective-permute-done((f32[2,32,512]{2,1,0:T(8,128)S(1)}, f32[2,32,512]{2,1,0:T(8,128)S(1)}, u32[]{:S(2)}, u32[]{:S(2)}) %collective-permute-start.12) | collective-permute-done | bytes 131104 | tf_op jit(solution)/shard_map/ppermute | solution.py:353
  55.3 3.1 %collective-permute-done.13.far = f32[2,64,256]{2,1,0:T(8,128)S(1)} collective-permute-done((f32[2,64,256]{2,1,0:T(8,128)S(1)}, f32[2,64,256]{2,1,0:T(8,128)S(1)}, u32[]{:S(2)}, u32[]{:S(2)}) %collective-permute-start.13) | collective-permute-done | bytes 131104 | tf_op jit(solution)/shard_map/ppermute | solution.py:353
  58.4 0.0 collective-permute-done.14.near
  58.5 0.1 collective-permute-start.18
  58.6 0.1 collective-permute-start.15
  58.7 1.7 %collective-permute-start.16 = (f32[2,64,256]{2,1,0:T(8,128)S(1)}, f32[2,64,256]{2,1,0:T(8,128)S(1)}, u32[]{:S(2)}, u32[]{:S(2)}) collective-permute-start(f32[2,64,256]{2,1,0:T(8,128)S(1)} %coarse_finish.5.fix), channel_id=1, source_target_pairs={{1,2},{3,4},{5,6},{7,8},{9,10},{11,12},{13,14},{17,18},{19,20},{21... | collective-permute-start | bytes 393224 | tf_op jit(solution)/shard_map/ppermute | solution.py:353
  60.4 0.7 correct.1
  61.1 1.0 %part.6 = (f32[2,128,512]{2,1,0:T(8,128)S(1)}, f32[2,128,512]{2,1,0:T(8,128)S(1)}) custom-call(f32[2,128,512]{2,1,0:T(8,128)S(1)} %get-tuple-element.60.far, f32[2,128,512]{2,1,0:T(8,128)S(1)} %get-tuple-element.61.near, f32[2,128,512]{2,1,0:T(8,128)S(1)} %get-tuple-element.39.gain, f32[2,128,512]{2,1,0:T(8,128)S(1)} %get-tuple-element.40.gain_kt, ...), custom_call_target="tpu_custom_call" | custom-call | flops 7864320 | bytes 4194304 | tf_op jit(solution)/shard_map/part/pallas_call | solution.py:48
  62.1 0.1 finish.7.part
  62.2 0.7 finish_fix.3.near
  62.9 1.4 %collective-permute-start.20 = (f32[2,128,512]{2,1,0:T(8,128)S(1)}, f32[2,128,512]{2,1,0:T(8,128)S(1)}, u32[]{:S(2)}, u32[]{:S(2)}) collective-permute-start(f32[2,128,512]{2,1,0:T(8,128)S(1)} %finish_fix.3.near), channel_id=1, source_target_pairs={{0,1},{1,0},{2,3},{3,2},{4,5},{5,4},{6,7},{7,6},{8,9},{9,8},{10,11... | collective-permute-start | bytes 1572872 | tf_op jit(solution)/shard_map/ppermute | solution.py:356
  64.3 1.6 %collective-permute-done.15 = f32[2,32,512]{2,1,0:T(8,128)S(1)} collective-permute-done((f32[2,32,512]{2,1,0:T(8,128)S(1)}, f32[2,32,512]{2,1,0:T(8,128)S(1)}, u32[]{:S(2)}, u32[]{:S(2)}) %collective-permute-start.15) | collective-permute-done | bytes 131104 | tf_op jit(solution)/shard_map/ppermute | solution.py:353
  65.9 0.1 finish.6.part
  66.0 1.3 %collective-permute-done.16.halo = f32[2,64,256]{2,1,0:T(8,128)S(1)} collective-permute-done((f32[2,64,256]{2,1,0:T(8,128)S(1)}, f32[2,64,256]{2,1,0:T(8,128)S(1)}, u32[]{:S(2)}, u32[]{:S(2)}) %collective-permute-start.16) | collective-permute-done | bytes 131104 | tf_op jit(solution)/shard_map/ppermute | solution.py:353
  67.2 0.7 finish_fix.2.far
  67.9 0.0 copy-start.3
  67.9 0.1 collective-permute-start.19
  68.0 0.9 %part.7 = (f32[2,128,512]{2,1,0:T(8,128)S(1)}, f32[2,128,512]{2,1,0:T(8,128)S(1)}) custom-call(f32[2,128,512]{2,1,0:T(8,128)S(1)} %finish_fix.2.far, f32[2,128,512]{2,1,0:T(8,128)S(1)} %finish_fix.3.near, f32[2,128,512]{2,1,0:T(8,128)S(1)} %get-tuple-element.39.gain, f32[2,128,512]{2,1,0:T(8,128)S(1)} %get-tuple-element.40.gain_kt, ...), custom_call_target="tpu_custom_call" | custom-call | flops 7864320 | bytes 4194304 | tf_op jit(solution)/shard_map/part/pallas_call | solution.py:48
  69.0 0.0 copy-done.3
  69.0 1.0 %last_near.1 = (f32[2,2,128,512]{3,2,1,0:T(8,128)}, f32[2,128,512]{2,1,0:T(8,128)}) custom-call(s32[1]{0:T(128)} %bitcast.where, f32[1]{0:T(128)} %bitcast.1.keep, f32[2,128,512]{2,1,0:T(8,128)S(1)} %get-tuple-element.69.part, f32[2,128,512]{2,1,0:T(8,128)S(1)} %collective-permute-done.20.halo, f32[2,128,512]{2,1,0:T(8,128)S(1)} %get-tuple-element.39.gain, ...), custom_call_target="tpu_custom_call" | custom-call | flops 3932160 | bytes 4718600 | tf_op jit(solution)/shard_map/last_near/pallas_call | solution.py:48
  70.0 11.1 %collective-permute-done.19.halo = f32[2,128,512]{2,1,0:T(8,128)S(1)} collective-permute-done((f32[2,128,512]{2,1,0:T(8,128)S(1)}, f32[2,128,512]{2,1,0:T(8,128)S(1)}, u32[]{:S(2)}, u32[]{:S(2)}) %collective-permute-start.19) | collective-permute-done | bytes 524320 | tf_op jit(solution)/shard_map/ppermute | solution.py:353
  81.1 1.0 %last_far.1 = (f32[2,2,128,512]{3,2,1,0:T(8,128)}, f32[2,128,512]{2,1,0:T(8,128)}) custom-call(s32[1]{0:T(128)} %bitcast.where, f32[1]{0:T(128)} %bitcast.1.keep, f32[2,128,512]{2,1,0:T(8,128)S(1)} %get-tuple-element.68.part, f32[2,128,512]{2,1,0:T(8,128)S(1)} %collective-permute-done.19.halo, ...), custom_call_target="tpu_custom_call", output_to_operand_aliasing={{0}: (8, {}), {1}: (9, {})} | custom-call | flops 3932160 | bytes 6291464 | tf_op jit(solution)/shard_map/last_far/pallas_call | solution.py:48
  (19 shorter events, 0.3 us)
Async XLA Ops:
  0.6 1.2 %copy-start.4 = (f32[2,2,128,512]{3,2,1,0:T(8,128)S(1)}, f32[2,2,128,512]{3,2,1,0:T(8,128)}, u32[]{:S(2)}) copy-start(f32[2,2,128,512]{3,2,1,0:T(8,128)} %warm.1) | copy-start | bytes 3145732
  1.9 2.0 %copy-start = (f32[2,128,512]{2,1,0:T(8,128)S(1)}, f32[2,128,512]{2,1,0:T(8,128)}, u32[]{:S(2)}) copy-start(f32[2,128,512]{2,1,0:T(8,128)} %phi.9) | copy-start | bytes 1572868
  2.0 4.4 %collective-permute-start.1 = (f32[2,128,512]{2,1,0:T(8,128)S(1)}, f32[2,128,512]{2,1,0:T(8,128)S(1)}, u32[]{:S(2)}, u32[]{:S(2)}) collective-permute-start(f32[2,128,512]{2,1,0:T(8,128)S(1)} %get-tuple-element.38.near), channel_id=1, source_target_pairs={{0,1},{1,0},{2,3},{3,2},{4,5},{5,4},{6,7},{7,6},{8,9},{9,8},{10,11... | collective-permute-start | bytes 1572872 | tf_op jit(solution)/shard_map/ppermute | solution.py:356
  2.7 19.8 %collective-permute-start = (f32[2,128,512]{2,1,0:T(8,128)S(1)}, f32[2,128,512]{2,1,0:T(8,128)S(1)}, u32[]{:S(2)}, u32[]{:S(2)}) collective-permute-start(f32[2,128,512]{2,1,0:T(8,128)S(1)} %get-tuple-element.37.far), channel_id=1, source_target_pairs={{1,2},{3,4},{5,6},{7,8},{9,10},{11,12},{13,14},{17,18},{19,20},{21... | collective-permute-start | bytes 1572872 | tf_op jit(solution)/shard_map/ppermute | solution.py:353
  3.9 1.2 %copy-start.1 = (f32[2,2,128,512]{3,2,1,0:T(8,128)S(1)}, f32[2,2,128,512]{3,2,1,0:T(8,128)}, u32[]{:S(2)}) copy-start(f32[2,2,128,512]{3,2,1,0:T(8,128)} %cot.3) | copy-start | bytes 3145732
  6.5 17.8 %collective-permute-start.3 = (f32[2,128,512]{2,1,0:T(8,128)S(1)}, f32[2,128,512]{2,1,0:T(8,128)S(1)}, u32[]{:S(2)}, u32[]{:S(2)}) collective-permute-start(f32[2,128,512]{2,1,0:T(8,128)S(1)} %finish.5.near), channel_id=1, source_target_pairs={{0,1},{1,0},{2,3},{3,2},{4,5},{5,4},{6,7},{7,6},{8,9},{9,8},{10,11... | collective-permute-start | bytes 1572872 | tf_op jit(solution)/shard_map/ppermute | solution.py:356
  22.7 11.5 %collective-permute-start.2 = (f32[2,128,512]{2,1,0:T(8,128)S(1)}, f32[2,128,512]{2,1,0:T(8,128)S(1)}, u32[]{:S(2)}, u32[]{:S(2)}) collective-permute-start(f32[2,128,512]{2,1,0:T(8,128)S(1)} %finish.4.far), channel_id=1, source_target_pairs={{1,2},{3,4},{5,6},{7,8},{9,10},{11,12},{13,14},{17,18},{19,20},{21... | collective-permute-start | bytes 1572872 | tf_op jit(solution)/shard_map/ppermute | solution.py:353
  24.8 13.2 %collective-permute-start.5 = (f32[2,64,256]{2,1,0:T(8,128)S(1)}, f32[2,64,256]{2,1,0:T(8,128)S(1)}, u32[]{:S(2)}, u32[]{:S(2)}) collective-permute-start(f32[2,64,256]{2,1,0:T(8,128)S(1)} %get-tuple-element.49), channel_id=1, source_target_pairs={{0,1},{1,0},{2,3},{3,2},{4,5},{5,4},{6,7},{7,6},{8,9},{9,8},{10,11... | collective-permute-start | bytes 393224 | tf_op jit(solution)/shard_map/ppermute | solution.py:356
  34.7 1.9 %copy-start.2 = (f32[2,2,128,512]{3,2,1,0:T(8,128)S(1)}, f32[2,2,128,512]{3,2,1,0:T(8,128)}, u32[]{:S(2)}) copy-start(f32[2,2,128,512]{3,2,1,0:T(8,128)} %cot.3) | copy-start | bytes 3145732
  34.7 4.5 %collective-permute-start.4 = (f32[2,64,256]{2,1,0:T(8,128)S(1)}, f32[2,64,256]{2,1,0:T(8,128)S(1)}, u32[]{:S(2)}, u32[]{:S(2)}) collective-permute-start(f32[2,64,256]{2,1,0:T(8,128)S(1)} %get-tuple-element.48), channel_id=1, source_target_pairs={{1,2},{3,4},{5,6},{7,8},{9,10},{11,12},{13,14},{17,18},{19,20},{21... | collective-permute-start | bytes 393224 | tf_op jit(solution)/shard_map/ppermute | solution.py:353
  34.8 5.7 %collective-permute-start.6 = (f32[2,32,512]{2,1,0:T(8,128)S(1)}, f32[2,32,512]{2,1,0:T(8,128)S(1)}, u32[]{:S(2)}, u32[]{:S(2)}) collective-permute-start(f32[2,32,512]{2,1,0:T(8,128)S(1)} %get-tuple-element.74), channel_id=1, source_target_pairs={{1,2},{3,4},{5,6},{7,8},{9,10},{11,12},{13,14},{17,18},{19,20},{21... | collective-permute-start | bytes 393224 | tf_op jit(solution)/shard_map/ppermute | solution.py:353
  39.2 7.5 %collective-permute-start.7 = (f32[2,64,256]{2,1,0:T(8,128)S(1)}, f32[2,64,256]{2,1,0:T(8,128)S(1)}, u32[]{:S(2)}, u32[]{:S(2)}) collective-permute-start(f32[2,64,256]{2,1,0:T(8,128)S(1)} %coarse_first.1.fix.own), channel_id=1, source_target_pairs={{1,2},{3,4},{5,6},{7,8},{9,10},{11,12},{13,14},{17,18},{19,20},{21... | collective-permute-start | bytes 393224 | tf_op jit(solution)/shard_map/ppermute | solution.py:353
  39.2 7.4 %collective-permute-start.8 = (f32[2,64,256]{2,1,0:T(8,128)S(1)}, f32[2,64,256]{2,1,0:T(8,128)S(1)}, u32[]{:S(2)}, u32[]{:S(2)}) collective-permute-start(f32[2,64,256]{2,1,0:T(8,128)S(1)} %coarse_first.1.fix.own), channel_id=1, source_target_pairs={{0,1},{1,0},{2,3},{3,2},{4,5},{5,4},{6,7},{7,6},{8,9},{9,8},{10,11... | collective-permute-start | bytes 393224 | tf_op jit(solution)/shard_map/ppermute | solution.py:356
  39.3 22.8 %collective-permute-start.17 = (f32[2,128,512]{2,1,0:T(8,128)S(1)}, f32[2,128,512]{2,1,0:T(8,128)S(1)}, u32[]{:S(2)}, u32[]{:S(2)}) collective-permute-start(f32[2,128,512]{2,1,0:T(8,128)S(1)} %get-tuple-element.47.near), channel_id=1, source_target_pairs={{0,1},{1,0},{2,3},{3,2},{4,5},{5,4},{6,7},{7,6},{8,9},{9,8},{10,11... | collective-permute-start | bytes 1572872 | tf_op jit(solution)/shard_map/ppermute | solution.py:356
  40.5 7.3 %collective-permute-start.9 = (f32[2,32,512]{2,1,0:T(8,128)S(1)}, f32[2,32,512]{2,1,0:T(8,128)S(1)}, u32[]{:S(2)}, u32[]{:S(2)}) collective-permute-start(f32[2,32,512]{2,1,0:T(8,128)S(1)} %get-tuple-element.55), channel_id=1, source_target_pairs={{1,2},{3,4},{5,6},{7,8},{9,10},{11,12},{13,14},{17,18},{19,20},{21... | collective-permute-start | bytes 393224 | tf_op jit(solution)/shard_map/ppermute | solution.py:353
  46.7 7.3 %collective-permute-start.10 = (f32[2,64,256]{2,1,0:T(8,128)S(1)}, f32[2,64,256]{2,1,0:T(8,128)S(1)}, u32[]{:S(2)}, u32[]{:S(2)}) collective-permute-start(f32[2,64,256]{2,1,0:T(8,128)S(1)} %coarse_finish.3.fix), channel_id=1, source_target_pairs={{1,2},{3,4},{5,6},{7,8},{9,10},{11,12},{13,14},{17,18},{19,20},{21... | collective-permute-start | bytes 393224 | tf_op jit(solution)/shard_map/ppermute | solution.py:353
  46.8 7.2 %collective-permute-start.11 = (f32[2,64,256]{2,1,0:T(8,128)S(1)}, f32[2,64,256]{2,1,0:T(8,128)S(1)}, u32[]{:S(2)}, u32[]{:S(2)}) collective-permute-start(f32[2,64,256]{2,1,0:T(8,128)S(1)} %coarse_finish.3.fix), channel_id=1, source_target_pairs={{0,1},{1,0},{2,3},{3,2},{4,5},{5,4},{6,7},{7,6},{8,9},{9,8},{10,11... | collective-permute-start | bytes 393224 | tf_op jit(solution)/shard_map/ppermute | solution.py:356
  47.8 7.5 %collective-permute-start.12 = (f32[2,32,512]{2,1,0:T(8,128)S(1)}, f32[2,32,512]{2,1,0:T(8,128)S(1)}, u32[]{:S(2)}, u32[]{:S(2)}) collective-permute-start(f32[2,32,512]{2,1,0:T(8,128)S(1)} %get-tuple-element.58), channel_id=1, source_target_pairs={{1,2},{3,4},{5,6},{7,8},{9,10},{11,12},{13,14},{17,18},{19,20},{21... | collective-permute-start | bytes 393224 | tf_op jit(solution)/shard_map/ppermute | solution.py:353
  54.0 4.5 %collective-permute-start.13 = (f32[2,64,256]{2,1,0:T(8,128)S(1)}, f32[2,64,256]{2,1,0:T(8,128)S(1)}, u32[]{:S(2)}, u32[]{:S(2)}) collective-permute-start(f32[2,64,256]{2,1,0:T(8,128)S(1)} %coarse_finish.4.fix), channel_id=1, source_target_pairs={{1,2},{3,4},{5,6},{7,8},{9,10},{11,12},{13,14},{17,18},{19,20},{21... | collective-permute-start | bytes 393224 | tf_op jit(solution)/shard_map/ppermute | solution.py:353
  54.1 4.4 %collective-permute-start.14 = (f32[2,64,256]{2,1,0:T(8,128)S(1)}, f32[2,64,256]{2,1,0:T(8,128)S(1)}, u32[]{:S(2)}, u32[]{:S(2)}) collective-permute-start(f32[2,64,256]{2,1,0:T(8,128)S(1)} %coarse_finish.4.fix), channel_id=1, source_target_pairs={{0,1},{1,0},{2,3},{3,2},{4,5},{5,4},{6,7},{7,6},{8,9},{9,8},{10,11... | collective-permute-start | bytes 393224 | tf_op jit(solution)/shard_map/ppermute | solution.py:356
  58.5 3.7 %collective-permute-start.18 = (f32[2,64,256]{2,1,0:T(8,128)S(1)}, f32[2,64,256]{2,1,0:T(8,128)S(1)}, u32[]{:S(2)}, u32[]{:S(2)}) collective-permute-start(f32[2,64,256]{2,1,0:T(8,128)S(1)} %coarse_finish.5.fix), channel_id=1, source_target_pairs={{0,1},{1,0},{2,3},{3,2},{4,5},{5,4},{6,7},{7,6},{8,9},{9,8},{10,11... | collective-permute-start | bytes 393224 | tf_op jit(solution)/shard_map/ppermute | solution.py:356
  58.6 7.3 %collective-permute-start.15 = (f32[2,32,512]{2,1,0:T(8,128)S(1)}, f32[2,32,512]{2,1,0:T(8,128)S(1)}, u32[]{:S(2)}, u32[]{:S(2)}) collective-permute-start(f32[2,32,512]{2,1,0:T(8,128)S(1)} %get-tuple-element.66), channel_id=1, source_target_pairs={{1,2},{3,4},{5,6},{7,8},{9,10},{11,12},{13,14},{17,18},{19,20},{21... | collective-permute-start | bytes 393224 | tf_op jit(solution)/shard_map/ppermute | solution.py:353
  58.7 8.6 %collective-permute-start.16 = (f32[2,64,256]{2,1,0:T(8,128)S(1)}, f32[2,64,256]{2,1,0:T(8,128)S(1)}, u32[]{:S(2)}, u32[]{:S(2)}) collective-permute-start(f32[2,64,256]{2,1,0:T(8,128)S(1)} %coarse_finish.5.fix), channel_id=1, source_target_pairs={{1,2},{3,4},{5,6},{7,8},{9,10},{11,12},{13,14},{17,18},{19,20},{21... | collective-permute-start | bytes 393224 | tf_op jit(solution)/shard_map/ppermute | solution.py:353
  62.9 6.1 %collective-permute-start.20 = (f32[2,128,512]{2,1,0:T(8,128)S(1)}, f32[2,128,512]{2,1,0:T(8,128)S(1)}, u32[]{:S(2)}, u32[]{:S(2)}) collective-permute-start(f32[2,128,512]{2,1,0:T(8,128)S(1)} %finish_fix.3.near), channel_id=1, source_target_pairs={{0,1},{1,0},{2,3},{3,2},{4,5},{5,4},{6,7},{7,6},{8,9},{9,8},{10,11... | collective-permute-start | bytes 1572872 | tf_op jit(solution)/shard_map/ppermute | solution.py:356
  67.9 1.0 %copy-start.3 = (f32[2,128,512]{2,1,0:T(8,128)S(1)}, f32[2,128,512]{2,1,0:T(8,128)}, u32[]{:S(2)}) copy-start(f32[2,128,512]{2,1,0:T(8,128)} %psi.3) | copy-start | bytes 1572868
  67.9 13.1 %collective-permute-start.19 = (f32[2,128,512]{2,1,0:T(8,128)S(1)}, f32[2,128,512]{2,1,0:T(8,128)S(1)}, u32[]{:S(2)}, u32[]{:S(2)}) collective-permute-start(f32[2,128,512]{2,1,0:T(8,128)S(1)} %finish_fix.2.far), channel_id=1, source_target_pairs={{1,2},{3,4},{5,6},{7,8},{9,10},{11,12},{13,14},{17,18},{19,20},{21... | collective-permute-start | bytes 1572872 | tf_op jit(solution)/shard_map/ppermute | solution.py:353

commit v3 on v2

v3 whole, which is shorter than its diff:
```python
import functools

import jax
import jax.numpy as jnp
from jax import lax
from jax.experimental import pallas as pl
from jax.experimental.pallas import tpu as pltpu
from jax.sharding import PartitionSpec as P

SWEEPS = 2
COARSE_SWEEPS = 4

GRADIENT_ENERGY = 1.0
TIME_STEP = 0.02
DAMPING = 0.8
KEEP = 1.0 - DAMPING
COARSE_ENERGY = GRADIENT_ENERGY / 4.0
COARSE_STEP = TIME_STEP / 4.0


VMEM = pl.BlockSpec(memory_space=pltpu.VMEM)
SMEM = pl.BlockSpec(memory_space=pltpu.SMEM)
ANY = pl.BlockSpec(memory_space=pl.ANY)
HBM = pl.BlockSpec(memory_space=pltpu.HBM)
BLOCK = 16
F32 = jnp.float32


def chip_pairs(count):
    return [(i, i ^ 1) for i in range(count)]


def cross_pairs(groups, count):
    pairs = []
    for g in range(groups):
        pairs += [(g * count + i, g * count + i + 1) for i in range(1, count - 1, 2)]
    for g in range(0, groups - 1, 2):
        pairs += [(g * count + i, (g + 1) * count + i) for i in (0, count - 1)]
    swaps = pairs + [(b, a) for a, b in pairs]
    if groups % 2 == 1:
        swaps += [((groups - 1) * count + i,) * 2 for i in (0, count - 1)]
    return swaps


def chunk_sizes(rows):
    return [rows // 2, rows // 2]


def call(body, name, outs, args, in_specs=None, out_specs=None, scratch=(), aliases=None, work=30):
    shapes = [jax.ShapeDtypeStruct(s, F32) for s in outs]
    return pl.pallas_call(
        body,
        out_shape=shapes,
        in_specs=in_specs or [VMEM] * len(args),
        out_specs=out_specs or [VMEM] * len(outs),
        scratch_shapes=list(scratch),
        input_output_aliases=aliases or {},
        name=name,
        cost_estimate=pl.CostEstimate(flops=work, bytes_accessed=work, transcendentals=0),
        compiler_params=pltpu.CompilerParams(vmem_limit_bytes=24 * 1024 * 1024),
    )(*args)


def blocks(rows):
    return range(0, rows, BLOCK)


def around(read, r, rows):
    x = read(r, r + BLOCK)
    cols = x.shape[-1]
    row = lax.broadcasted_iota(jnp.int32, x.shape, 0)
    col = lax.broadcasted_iota(jnp.int32, x.shape, 1)
    up = read(r - 1, r - 1 + BLOCK) if r > 0 else jnp.where(row == 0, 0.0, pltpu.roll(x, 1, 0))
    if r + BLOCK < rows:
        down = read(r + 1, r + 1 + BLOCK)
    else:
        down = jnp.where(row == BLOCK - 1, 0.0, pltpu.roll(x, BLOCK - 1, 0))
    left = jnp.where(col == 0, 0.0, pltpu.roll(x, 1, 1))
    right = jnp.where(col == cols - 1, 0.0, pltpu.roll(x, cols - 1, 1))
    return x, (up + down) + (left + right)


def reader(ref, *lead):
    return lambda lo, hi: ref[(*lead, slice(lo, hi))]


def add_terms(base_p, base_m, gain, gain_kt, nb_p, nb_m, energy, step):
    new_p = base_p - gain * (energy * nb_m) + gain_kt * nb_p
    new_m = base_m + gain * (step * nb_p + (6.0 * step * energy) * nb_m)
    return new_p, new_m


def parts3(x):
    high = x.astype(jnp.bfloat16)
    rest = x - high.astype(F32)
    middle = rest.astype(jnp.bfloat16)
    low = (rest - middle.astype(F32)).astype(jnp.bfloat16)
    return high, middle, low


def pair_cols(x, pair):
    return sum(jnp.dot(v, pair, preferred_element_type=F32) for v in parts3(x))


def copy_cols(x, pair):
    dims = (((1,), (1,)), ((), ()))
    return sum(lax.dot_general(v, pair, dims, preferred_element_type=F32) for v in parts3(x))


LANES = 128


def tiles(rows, cols):
    return pltpu.VMEM((cols // LANES, rows, LANES), F32)


def put_rows(ref, rows, x):
    for j in range(ref.shape[0]):
        ref[j, rows] = x[:, j * LANES : (j + 1) * LANES]


def get_rows(ref, rows):
    return jnp.concatenate([ref[j, rows] for j in range(ref.shape[0])], axis=1)


def even_odd(ref):
    half = ref.shape[1] // 2
    return pl.ds(0, half, stride=2), pl.ds(1, half, stride=2)


def pair_rows(ref):
    even, odd = even_odd(ref)
    return get_rows(ref, even) + get_rows(ref, odd)


def take_body(what, where, warm, *refs):
    outs, sems = refs[:-1], refs[-1]
    c = where[0]
    copies = []
    for n, ((is_near, lo), out) in enumerate(zip(what, outs)):
        plane = 1 - c if is_near else c
        rows = pl.ds(lo, out.shape[1])
        copies.append(pltpu.make_async_copy(warm.at[:, plane, rows], out, sems.at[n]))
        copies[-1].start()
    for copy in copies:
        copy.wait()


def setup_body(where, phi, cot, gain, gain_kt, own):
    c = where[0]
    for i in range(2):
        plane = c if i == 0 else 1 - c
        for r in blocks(phi.shape[1]):
            rows = slice(r, r + BLOCK)
            v = phi[plane, rows]
            k = 3.0 * v * v - 1.0 + 6.0 * GRADIENT_ENERGY
            g = DAMPING / (1.0 + 6.0 * TIME_STEP * k)
            s0, s1 = cot[0, plane, rows], cot[1, plane, rows]
            gain[i, rows] = g
            gain_kt[i, rows] = g * k * TIME_STEP
            own[i, 0, rows] = g * (s0 + k * s1)
            own[i, 1, rows] = g * (s1 - 6.0 * TIME_STEP * s0)


def coarse_setup_body(phi, pair, gain, gain_kt, both):
    for r in blocks(phi.shape[1]):
        rows = slice(r, r + BLOCK)
        a, b = phi[0, rows], phi[1, rows]
        put_rows(both, rows, (3.0 * a * a - 1.0) + (3.0 * b * b - 1.0))
    k = pair_cols(pair_rows(both), pair[...]) / 8.0 + 6.0 * COARSE_ENERGY
    g = DAMPING / (1.0 + 6.0 * COARSE_STEP * k)
    gain[...] = g
    gain_kt[...] = g * k * COARSE_STEP


def gather_rows(chunks, whole):
    lo = 0
    for chunk in chunks:
        n = chunk.shape[1]
        for r in blocks(n):
            for f in range(2):
                whole[f, slice(lo + r, lo + r + BLOCK)] = chunk[f, slice(r, r + BLOCK)]
        lo += n


def part_body(count, *refs):
    chunks, (near, gain, gain_kt, own, far_out, near_out, far) = refs[:count], refs[count:]
    gather_rows(chunks, far)
    rows_all = far.shape[1]
    for i, (mine, other, out) in enumerate(((far, near, far_out), (near, far, near_out))):
        for r in blocks(rows_all):
            rows = slice(r, r + BLOCK)
            p, nb_p = around(reader(mine, 0), r, rows_all)
            m, nb_m = around(reader(mine, 1), r, rows_all)
            out[0, rows], out[1, rows] = add_terms(
                KEEP * p + own[i, 0, rows],
                KEEP * m + own[i, 1, rows],
                gain[i, rows],
                gain_kt[i, rows],
                nb_p + other[0, rows],
                nb_m + other[1, rows],
                GRADIENT_ENERGY,
                TIME_STEP,
            )


def finish_body(i, lo, keep, part, halo, gain, gain_kt, out):
    for r in blocks(halo.shape[1]):
        rows, whole = slice(r, r + BLOCK), slice(lo + r, lo + r + BLOCK)
        hp, hm = halo[0, rows], halo[1, rows]
        if i == 0:
            hp, hm = hp * keep[0], hm * keep[0]
        out[0, rows], out[1, rows] = add_terms(
            part[0, whole], part[1, whole], gain[i, whole], gain_kt[i, whole], hp, hm, GRADIENT_ENERGY, TIME_STEP
        )


def finish_pool_body(i, lo, keep, part, halo, gain, gain_kt, pair, *refs):
    before, (pool, out, tile) = refs[:-3], refs[-3:]
    finish_body(i, lo, keep, part, halo, gain, gain_kt, out)
    for f in range(2):
        for r in blocks(out.shape[1]):
            rows = slice(r, r + BLOCK)
            put_rows(tile, rows, out[f, rows])
        for ref in before:
            pool[f, : lo // 2] = ref[f]
        pool[f, lo // 2 if before else 0 :] = pair_cols(pair_rows(tile), pair[...])


def three_body(count, *refs):
    chunks, (even_col, odd_col, first, second, third, tile) = refs[:count], refs[count:]
    for f in range(2):
        lo = 0
        for chunk in chunks:
            for r in blocks(chunk.shape[1]):
                put_rows(tile, slice(lo + r, lo + r + BLOCK), chunk[f, slice(r, r + BLOCK)])
            lo += chunk.shape[1]
        even, odd = even_odd(tile)
        top, bottom = get_rows(tile, even), get_rows(tile, odd)
        first[f] = pair_cols(top, even_col[...])
        second[f] = pair_cols(top, odd_col[...])
        third[f] = pair_cols(bottom, even_col[...])


def defect_body(count, where, *refs):
    chunks, (near, phi, cot, pair, out, far, total, tile) = refs[:count], refs[count:]
    gather_rows(chunks, far)
    c = where[0]
    rows_all = far.shape[1]
    for i, (mine, other) in enumerate(((far, near), (near, far))):
        plane = c if i == 0 else 1 - c
        for r in blocks(rows_all):
            rows = slice(r, r + BLOCK)
            p, nb_p = around(reader(mine, 0), r, rows_all)
            m, nb_m = around(reader(mine, 1), r, rows_all)
            v = phi[plane, rows]
            lap_p = nb_p + other[0, rows] - 6.0 * p
            lap_m = nb_m + other[1, rows] - 6.0 * m
            r0 = cot[0, plane, rows] - (p - (3.0 * v * v - 1.0) * m + GRADIENT_ENERGY * lap_m)
            r1 = cot[1, plane, rows] - (m - TIME_STEP * lap_p)
            total[0, rows] = r0 if i == 0 else total[0, rows] + r0
            total[1, rows] = r1 if i == 0 else total[1, rows] + r1
    for f in range(2):
        for r in blocks(rows_all):
            rows = slice(r, r + BLOCK)
            put_rows(tile, rows, total[f, rows])
        out[f] = pair_cols(pair_rows(tile), pair[...]) / 8.0


def coarse_first_body(keep, local, far, near, gain, gain_kt, out):
    for r in blocks(local.shape[1]):
        rows = slice(r, r + BLOCK)
        s0 = local[0, rows] - (GRADIENT_ENERGY / 8.0) * (far[1, rows] * keep[0] + near[1, rows])
        s1 = local[1, rows] + (TIME_STEP / 8.0) * (far[0, rows] * keep[0] + near[0, rows])
        g = gain[rows]
        out[0, rows] = g * s0 + (gain_kt[rows] / COARSE_STEP) * s1
        out[1, rows] = g * (s1 - 6.0 * COARSE_STEP * s0)


def coarse_part_body(fix, own, gain, gain_kt, out):
    rows_all = fix.shape[1]
    for r in blocks(rows_all):
        rows = slice(r, r + BLOCK)
        p, nb_p = around(reader(fix, 0), r, rows_all)
        m, nb_m = around(reader(fix, 1), r, rows_all)
        out[0, rows], out[1, rows] = add_terms(
            KEEP * p + own[0, rows],
            KEEP * m + own[1, rows],
            gain[rows],
            gain_kt[rows],
            nb_p,
            nb_m,
            COARSE_ENERGY,
            COARSE_STEP,
        )


def coarse_finish_body(keep, part, far, near, gain, gain_kt, out):
    for r in blocks(part.shape[1]):
        rows = slice(r, r + BLOCK)
        out[0, rows], out[1, rows] = add_terms(
            part[0, rows],
            part[1, rows],
            gain[rows],
            gain_kt[rows],
            far[0, rows] * keep[0] + near[0, rows],
            far[1, rows] * keep[0] + near[1, rows],
            COARSE_ENERGY,
            COARSE_STEP,
        )


def spread_into(tile, fix, pair):
    wide = copy_cols(fix, pair)
    for rows in even_odd(tile):
        put_rows(tile, rows, wide)


def third_body(count, keep, *refs):
    chunks, refs = refs[:count], refs[count:]
    near, fix, near_halo, sums, first, second, third, pair, even_col, odd_col, gain, gain_kt, own = refs[:13]
    far_out, near_out, far_fixed, near_fixed, tile, phase, chem = refs[13:]
    rows_all = near.shape[1]
    gather_rows(chunks, far_fixed)
    for f, halo in enumerate((phase, chem)):
        spread_into(tile, fix[f], pair[...])
        for r in blocks(rows_all):
            rows = slice(r, r + BLOCK)
            wide = get_rows(tile, rows)
            far_fixed[f, rows] = far_fixed[f, rows] + wide
            near_fixed[f, rows] = near[f, rows] + wide
        even, odd = even_odd(halo)
        a, b, c = first[f], second[f], third[f]
        d = sums[f] - ((a + b) + c)
        put_rows(halo, even, copy_cols(a, even_col[...]) + copy_cols(b, odd_col[...]))
        put_rows(halo, odd, copy_cols(c, even_col[...]) + copy_cols(d, odd_col[...]))
    for i, (mine, other, out) in enumerate(((far_fixed, near_fixed, far_out), (near_fixed, far_fixed, near_out))):
        for r in blocks(rows_all):
            rows = slice(r, r + BLOCK)
            p, nb_p = around(reader(mine, 0), r, rows_all)
            m, nb_m = around(reader(mine, 1), r, rows_all)
            if i == 0:
                hp, hm = get_rows(phase, rows) * keep[0], get_rows(chem, rows) * keep[0]
            else:
                hp, hm = near_halo[0, rows], near_halo[1, rows]
            out[0, rows], out[1, rows] = add_terms(
                KEEP * p + own[i, 0, rows],
                KEEP * m + own[i, 1, rows],
                gain[i, rows],
                gain_kt[i, rows],
                nb_p + other[0, rows] + hp,
                nb_m + other[1, rows] + hm,
                GRADIENT_ENERGY,
                TIME_STEP,
            )


def finish_fix_body(i, lo, keep, part, halo, pair, gain, gain_kt, out, phase, chem):
    n = out.shape[1]
    coarse = slice(lo // 2, (lo + n) // 2)
    spread_into(phase, halo[0, coarse], pair[...])
    spread_into(chem, halo[1, coarse], pair[...])
    for r in blocks(n):
        rows, whole = slice(r, r + BLOCK), slice(lo + r, lo + r + BLOCK)
        hp, hm = get_rows(phase, rows), get_rows(chem, rows)
        if i == 0:
            hp, hm = hp * keep[0], hm * keep[0]
        out[0, rows], out[1, rows] = add_terms(
            part[0, whole], part[1, whole], gain[i, whole], gain_kt[i, whole], hp, hm, GRADIENT_ENERGY, TIME_STEP
        )


def final_body(i, lo, where, keep, part, halo, gain, gain_kt, phi, psi, *refs):
    adjoint, design, plane_out, grad_out, sems = refs[-5:]
    c = where[0]
    plane = c if i == 0 else 1 - c
    rows_all = halo.shape[1]
    step = rows_all // 2
    copies = []
    for n, start in enumerate(range(0, rows_all, step)):
        for r in range(start, start + step, BLOCK):
            rows, whole = slice(r, r + BLOCK), slice(lo + r, lo + r + BLOCK)
            hp, hm = halo[0, rows], halo[1, rows]
            if i == 0:
                hp, hm = hp * keep[0], hm * keep[0]
            p, m = add_terms(
                part[0, whole], part[1, whole], gain[i, whole], gain_kt[i, whole], hp, hm, GRADIENT_ENERGY, TIME_STEP
            )
            plane_out[0, rows] = p
            plane_out[1, rows] = m
            grad_out[rows] = 6.0 * phi[plane, whole] * psi[plane, whole] * m
        here, there = pl.ds(start, step), pl.ds(lo + start, step)
        copies.append(pltpu.make_async_copy(plane_out.at[:, here], adjoint.at[:, plane, there], sems.at[2 * n]))
        copies.append(pltpu.make_async_copy(grad_out.at[here], design.at[plane, there], sems.at[2 * n + 1]))
        copies[-2].start()
        copies[-1].start()
    for copy in copies:
        copy.wait()


def on_device(phase_lin, phase_state, cotangent, warm_start):
    groups, count = lax.axis_size("grp"), lax.axis_size("gx")
    me = lax.axis_index("gx")
    where = jnp.reshape(me % 2, (1,)).astype(jnp.int32)
    keep = jnp.reshape(((me > 0) & (me < count - 1)).astype(F32), (1,))
    across, on_chip = cross_pairs(groups, count), chip_pairs(count)
    rows, cols = phase_lin.shape[1:]
    full, half = (2, rows, cols), (2, rows // 2, cols // 2)
    sizes = chunk_sizes(rows)
    starts = [sum(sizes[:n]) for n in range(len(sizes))]
    chunked = [(2, n, cols) for n in sizes]

    cell = lax.broadcasted_iota(jnp.int32, (cols, cols // 2), 0)
    pairs = 2 * lax.broadcasted_iota(jnp.int32, (cols, cols // 2), 1)
    even_col, odd_col = (cell == pairs).astype(jnp.bfloat16), (cell == pairs + 1).astype(jnp.bfloat16)
    pair = ((cell == pairs) | (cell == pairs + 1)).astype(jnp.bfloat16)

    def swap_far(x):
        return lax.ppermute(x, ("grp", "gx"), across)

    def swap_near(x):
        return lax.ppermute(x, "gx", on_chip)

    def run(body, name, outs, args, statics=(), smem=0, **kw):
        specs = [SMEM] * smem + [VMEM] * (len(args) - smem)
        return call(functools.partial(body, *statics), name, outs, args, specs, **kw)

    def take(what, name):
        outs = [(2, n, cols) for _, _, n in what]
        body = functools.partial(take_body, [(is_near, lo) for is_near, lo, _ in what])
        scratch = [pltpu.SemaphoreType.DMA((len(what),))]
        return call(body, name, outs, (where, warm_start), [SMEM, HBM], scratch=scratch, work=0)

    far = take([(False, starts[0], sizes[0])], "take_first")
    *rest, near = take([(False, lo, n) for lo, n in zip(starts[1:], sizes[1:])] + [(True, 0, rows)], "take_rest")
    far = list(far) + rest
    far_halo, near_halo = [swap_far(v) for v in far], swap_near(near)
    gain, gain_kt, own = run(setup_body, "setup", [full, full, (2, 2, rows, cols)], (where, phase_lin, cotangent), smem=1)
    coefs = (gain, gain_kt)

    def part_of(far, near):
        args = (*far, near, gain, gain_kt, own)
        return run(part_body, "part", [full, full], args, (len(far),), scratch=[pltpu.VMEM(full, F32)])

    def finish(i, lo, part, halo):
        shape = (2, halo.shape[1], cols)
        return run(finish_body, "finish", [shape], (keep, part, halo, *coefs), (i, lo), smem=1, work=8)[0]

    far_part, near_part = part_of(far, near)
    near = finish(1, 0, near_part, near_halo)
    far = [finish(0, lo, far_part, halo) for lo, halo in zip(starts, far_halo)]

    far_halo, near_halo = [swap_far(v) for v in far], swap_near(near)
    far_part, near_part = part_of(far, near)
    coarse = run(coarse_setup_body, "coarse_setup", [half[1:], half[1:]], (phase_lin, pair), scratch=[tiles(rows, cols)])

    def finish_pool(i, lo, part, halo, before=()):
        n = halo.shape[1]
        pool = (2, (n + (lo if before else 0)) // 2, cols // 2)
        args = (keep, part, halo, *coefs, pair, *before)
        outs, scratch = [pool, (2, n, cols)], [tiles(n, cols)]
        return run(finish_pool_body, "finish_pool", outs, args, (i, lo), smem=1, scratch=scratch, work=8)

    near_pool, near = finish_pool(1, 0, near_part, near_halo)
    far, before = [], ()
    for lo, halo in zip(starts, far_halo):
        far_pool, chunk = finish_pool(0, lo, far_part, halo, before)
        far.append(chunk)
        before = (far_pool,)

    far_sums, near_sums = swap_far(far_pool), swap_near(near_pool)
    plane_sums = far_sums
    near_halo = swap_near(near)
    args = (*far, even_col, odd_col)
    pieces = run(three_body, "three", [half] * 3, args, (len(far),), scratch=[tiles(rows, cols)])
    arrived = [swap_far(pieces[0])]
    args = (where, *far, near, phase_lin, cotangent, pair)
    scratch = [pltpu.VMEM(full, F32), pltpu.VMEM(full, F32), tiles(rows, cols)]
    local = run(defect_body, "defect", [half], args, (len(far),), smem=1, scratch=scratch)[0]
    fix = run(coarse_first_body, "coarse_first", [half], (keep, local, far_sums, near_sums, *coarse), smem=1, work=8)[0]
    first = fix
    for sweep_index in range(COARSE_SWEEPS - 1):
        far_sums, near_sums = swap_far(fix), swap_near(fix)
        if len(arrived) < len(pieces):
            fix, held = lax.optimization_barrier((fix, pieces[len(arrived)]))
            arrived.append(swap_far(held))
        part = run(coarse_part_body, "coarse_part", [half], (fix, first, *coarse))[0]
        part, arrived[sweep_index] = lax.optimization_barrier((part, arrived[sweep_index]))
        args = (keep, part, far_sums, near_sums, *coarse)
        fix = run(coarse_finish_body, "coarse_finish", [half], args, smem=1, work=8)[0]

    far_sums, near_sums = swap_far(fix), swap_near(fix)
    args = (keep, *far, near, fix, near_halo, plane_sums, *arrived, pair, even_col, odd_col, *coefs, own)
    scratch = [pltpu.VMEM(full, F32)] * 2 + [tiles(rows, cols)] * 3
    far_part, near_part = run(third_body, "third", [full, full], args, (len(far),), smem=1, scratch=scratch)

    def finish_fix(i, lo, n, part, halo):
        args, scratch = (keep, part, halo, pair, *coefs), [tiles(n, cols)] * 2
        return run(finish_fix_body, "finish_fix", [(2, n, cols)], args, (i, lo), smem=1, scratch=scratch, work=8)[0]

    far = [finish_fix(0, lo, n, far_part, far_sums) for lo, n in zip(starts, sizes)]
    near_sums, far[-1] = lax.optimization_barrier((near_sums, far[-1]))
    near = finish_fix(1, 0, rows, near_part, near_sums)

    far_halo, near_halo = [swap_far(v) for v in far], swap_near(near)
    far_part, near_part = part_of(far, near)
    outs = [(2, 2, rows, cols), full]

    def final(i, lo, part, halo, done):
        n = halo.shape[1]
        args = (where, keep, part, halo, *coefs, phase_lin, phase_state, *done)
        in_specs = [SMEM, SMEM] + [VMEM] * 6 + [ANY] * len(done)
        scratch = [pltpu.VMEM((2, n, cols), F32), pltpu.VMEM((n, cols), F32), pltpu.SemaphoreType.DMA((4,))]
        body = functools.partial(final_body, i, lo)
        aliases = {8: 0, 9: 1} if done else None
        return call(body, "final", outs, args, in_specs, [ANY, ANY], scratch, aliases, work=10)

    done = final(1, 0, near_part, near_halo, ())
    for lo, halo in zip(starts, far_halo):
        done = final(0, lo, far_part, halo, done)
    return tuple(done)


def solution(mesh):
    in_specs = (
        P(("grp", "gx"), None, None),
        P(("grp", "gx"), None, None),
        P(None, ("grp", "gx"), None, None),
        P(None, ("grp", "gx"), None, None),
    )
    out_specs = (P(None, ("grp", "gx"), None, None), P(("grp", "gx"), None, None))
    return jax.shard_map(
        on_device, mesh=mesh, in_specs=in_specs, out_specs=out_specs, check_vma=False
    )
```

time: 82.3 us -> 79.4 us (0.965)
  the two profiles are of different devices: /device:TPU:25 before, /device:TPU:1 now
where the time goes in v3:
time: 79.4 us; the launch traced here: 78.8 us
  starting transfers between devices  28.1 us (35%)
  waiting for transfers between devices  26 us (33%)
  Pallas kernels  20.5 us (26%)
  local copies, waits for them, and re-layouts  3.07 us (4%)
  between operations  0.95 us (1%)
    ppermute x14, waiting for transfers between devices, swap_far(): return lax.ppermute(x, ('grp', 'gx'), across)  26 us
    ppermute x14, starting transfers between devices, swap_far(): return lax.ppermute(x, ('grp', 'gx'), across)  24.9 us
    pallas_call x29, Pallas kernels, call(): pl.pallas_call(body, out_shape=shapes, in_specs=in_specs or [VMEM] * len(...  20.5 us
    ppermute x9, starting transfers between devices, swap_near(): return lax.ppermute(x, 'gx', on_chip)  3.23 us
    unnamed x14, local copies, waits for them, and re-layouts  3.07 us
  transfers between devices with their start and end apart: 23, of which 8 were waited for; matrix products, arithmetic and copies ran while one was open for 0% of the time, Pallas kernels for 23%

profile of v3, /device:TPU:1, one launch (start us, length us, event | category | flops | bytes accessed | tf_op | source)
XLA Modules:
  0.0 78.8 jit_solution(12337799914241956864)
XLA Ops:
  0.7 1.2 %copy-done.4 = f32[2,2,128,512]{3,2,1,0:T(8,128)S(1)} copy-done((f32[2,2,128,512]{3,2,1,0:T(8,128)S(1)}, f32[2,2,128,512]{3,2,1,0:T(8,128)}, u32[]{:S(2)}) %copy-start.4) | copy-done | bytes 1048600
  1.9 1.0 %take_rest.1 = (f32[2,64,512]{2,1,0:T(8,128)}, f32[2,128,512]{2,1,0:T(8,128)}) custom-call(s32[1]{0:T(128)} %bitcast.where, f32[2,2,128,512]{3,2,1,0:T(8,128)S(1)} %copy-done.4), custom_call_target="tpu_custom_call" | custom-call | tf_op jit(solution)/shard_map/take_rest/pallas_call | solution.py:51
  2.8 0.0 copy-start
  2.8 0.1 collective-permute-start.2
  3.0 2.7 %collective-permute-start = (f32[2,64,512]{2,1,0:T(8,128)S(1)}, f32[2,64,512]{2,1,0:T(8,128)}, u32[]{:S(2)}, u32[]{:S(2)}) collective-permute-start(f32[2,64,512]{2,1,0:T(8,128)S(1)} %take_first.1.refs_0_), channel_id=1, source_target_pairs={{1,2},{3,4},{5,6},{7,8},{9,10},{11,12},{13,14},{17,18},{19,20},{21... | collective-permute-start | bytes 786440 | tf_op jit(solution)/shard_map/ppermute | solution.py:419
  5.7 0.1 collective-permute-start.1
  5.7 0.3 setup.1
  6.0 2.0 %part.3 = (f32[2,128,512]{2,1,0:T(8,128)S(1)}, f32[2,128,512]{2,1,0:T(8,128)S(1)}) custom-call(f32[2,64,512]{2,1,0:T(8,128)S(1)} %take_first.1.refs_0_, f32[2,64,512]{2,1,0:T(8,128)} %get-tuple-element.42.refs_1_, f32[2,128,512]{2,1,0:T(8,128)} %get-tuple-element.43.refs_2_, f32[2,128,512]{2,1,0:T(8,128)S(1)} %get-tuple-element.44.refs_3_.gain.refs_12_, ...), custom_call_target="tpu_custom_call" | custom-call | flops 30 | bytes 30 | tf_op jit(solution)/shard_map/part/pallas_call | solution.py:51
  8.1 0.0 copy-start.5
  8.1 0.8 copy-done.5
  8.9 0.0 collective-permute-done.2.halo
  8.9 1.0 %copy-done.6 = f32[2,128,512]{2,1,0:T(8,128)S(1)} copy-done((f32[2,128,512]{2,1,0:T(8,128)S(1)}, f32[2,128,512]{2,1,0:T(8,128)}, u32[]{:S(2)}) %copy-start.6) | copy-done | bytes 524312
  9.9 1.1 %finish.5.refs_2_ = f32[2,128,512]{2,1,0:T(8,128)S(1)} custom-call(f32[1]{0:T(128)} %bitcast.1.keep, f32[2,128,512]{2,1,0:T(8,128)S(1)} %copy-done.6, f32[2,128,512]{2,1,0:T(8,128)} %collective-permute-done.2.halo, f32[2,128,512]{2,1,0:T(8,128)S(1)} %get-tuple-element.44.refs_3_.gain.refs_12_, f32[2,128,512]{2,1,0:T(8,128)S(1)} %get-tuple-element.45.refs_4_.gain_kt.refs_13_), custom_call_target="tpu_custom_call" | custom-call | flops 8 | bytes 8 | tf_op jit(solution)/shard_map/finish/pallas_call | solution.py:51
  11.1 0.4 collective-permute-start.5
  11.5 3.1 %collective-permute-done.halo = f32[2,64,512]{2,1,0:T(8,128)} collective-permute-done((f32[2,64,512]{2,1,0:T(8,128)S(1)}, f32[2,64,512]{2,1,0:T(8,128)}, u32[]{:S(2)}, u32[]{:S(2)}) %collective-permute-start) | collective-permute-done | bytes 262176 | tf_op jit(solution)/shard_map/ppermute | solution.py:419
  14.6 1.0 %finish.3.refs_0_ = f32[2,64,512]{2,1,0:T(8,128)S(1)} custom-call(f32[1]{0:T(128)} %bitcast.1.keep, f32[2,128,512]{2,1,0:T(8,128)S(1)} %get-tuple-element.47.part, f32[2,64,512]{2,1,0:T(8,128)} %collective-permute-done.halo, f32[2,128,512]{2,1,0:T(8,128)S(1)} %get-tuple-element.44.refs_3_.gain.refs_12_, ...), custom_call_target="tpu_custom_call" | custom-call | flops 8 | bytes 8 | tf_op jit(solution)/shard_map/finish/pallas_call | solution.py:51
  15.6 2.7 %collective-permute-start.3 = (f32[2,64,512]{2,1,0:T(8,128)S(1)}, f32[2,64,512]{2,1,0:T(8,128)S(1)}, u32[]{:S(2)}, u32[]{:S(2)}) collective-permute-start(f32[2,64,512]{2,1,0:T(8,128)S(1)} %finish.3.refs_0_), channel_id=1, source_target_pairs={{1,2},{3,4},{5,6},{7,8},{9,10},{11,12},{13,14},{17,18},{19,20},{21... | collective-permute-start | bytes 786440 | tf_op jit(solution)/shard_map/ppermute | solution.py:419
  18.2 4.9 %collective-permute-done.1.halo = f32[2,64,512]{2,1,0:T(8,128)} collective-permute-done((f32[2,64,512]{2,1,0:T(8,128)}, f32[2,64,512]{2,1,0:T(8,128)}, u32[]{:S(2)}, u32[]{:S(2)}) %collective-permute-start.1) | collective-permute-done | bytes 262176 | tf_op jit(solution)/shard_map/ppermute | solution.py:419
  23.2 1.0 %finish.4.refs_1_ = f32[2,64,512]{2,1,0:T(8,128)S(1)} custom-call(f32[1]{0:T(128)} %bitcast.1.keep, f32[2,128,512]{2,1,0:T(8,128)S(1)} %get-tuple-element.47.part, f32[2,64,512]{2,1,0:T(8,128)} %collective-permute-done.1.halo, f32[2,128,512]{2,1,0:T(8,128)S(1)} %get-tuple-element.44.refs_3_.gain.refs_12_, ...), custom_call_target="tpu_custom_call" | custom-call | flops 8 | bytes 8 | tf_op jit(solution)/shard_map/finish/pallas_call | solution.py:51
  24.2 2.5 %collective-permute-start.4 = (f32[2,64,512]{2,1,0:T(8,128)S(1)}, f32[2,64,512]{2,1,0:T(8,128)S(1)}, u32[]{:S(2)}, u32[]{:S(2)}) collective-permute-start(f32[2,64,512]{2,1,0:T(8,128)S(1)} %finish.4.refs_1_), channel_id=1, source_target_pairs={{1,2},{3,4},{5,6},{7,8},{9,10},{11,12},{13,14},{17,18},{19,20},{21... | collective-permute-start | bytes 786440 | tf_op jit(solution)/shard_map/ppermute | solution.py:419
  26.7 0.2 fusion.2
  26.9 0.9 %part.4 = (f32[2,128,512]{2,1,0:T(8,128)S(1)}, f32[2,128,512]{2,1,0:T(8,128)S(1)}) custom-call(f32[2,64,512]{2,1,0:T(8,128)S(1)} %finish.3.refs_0_, f32[2,64,512]{2,1,0:T(8,128)S(1)} %finish.4.refs_1_, f32[2,128,512]{2,1,0:T(8,128)S(1)} %finish.5.refs_2_, f32[2,128,512]{2,1,0:T(8,128)S(1)} %get-tuple-element.44.refs_3_.gain.refs_12_, ...), custom_call_target="tpu_custom_call" | custom-call | flops 30 | bytes 30 | tf_op jit(solution)/shard_map/part/pallas_call | solution.py:51
  27.8 0.0 collective-permute-done.3.halo
  27.9 0.4 finish_pool.3
  28.2 2.8 %collective-permute-done.4.halo = f32[2,64,512]{2,1,0:T(8,128)S(1)} collective-permute-done((f32[2,64,512]{2,1,0:T(8,128)S(1)}, f32[2,64,512]{2,1,0:T(8,128)S(1)}, u32[]{:S(2)}, u32[]{:S(2)}) %collective-permute-start.4) | collective-permute-done | bytes 262176 | tf_op jit(solution)/shard_map/ppermute | solution.py:419
  31.1 0.4 finish_pool.4
  31.5 2.5 %collective-permute-start.6 = (f32[2,64,256]{2,1,0:T(8,128)S(1)}, f32[2,64,256]{2,1,0:T(8,128)S(1)}, u32[]{:S(2)}, u32[]{:S(2)}) collective-permute-start(f32[2,64,256]{2,1,0:T(8,128)S(1)} %get-tuple-element.55), channel_id=1, source_target_pairs={{1,2},{3,4},{5,6},{7,8},{9,10},{11,12},{13,14},{17,18},{19,20},{21... | collective-permute-start | bytes 393224 | tf_op jit(solution)/shard_map/ppermute | solution.py:419
  34.0 0.0 collective-permute-done.5.halo
  34.0 0.5 finish_pool.5
  34.5 0.0 copy-start.3
  34.5 0.1 collective-permute-start.7
  34.6 0.3 coarse_setup.1
  34.9 1.0 %three.1 = (f32[2,64,256]{2,1,0:T(8,128)S(1)}, f32[2,64,256]{2,1,0:T(8,128)S(1)}, f32[2,64,256]{2,1,0:T(8,128)S(1)}) custom-call(f32[2,64,512]{2,1,0:T(8,128)S(1)} %get-tuple-element.50.refs_0_, f32[2,64,512]{2,1,0:T(8,128)S(1)} %get-tuple-element.52.refs_1_, bf16[512,256]{1,0:T(8,128)(2,1)S(1)} %get-tuple-element.84.refs_2_.refs_10_, ...), custom_call_target="tpu_custom_call" | custom-call | flops 30 | bytes 30 | tf_op jit(solution)/shard_map/three/pallas_call | solution.py:51
  35.9 0.1 collective-permute-start.8
  36.0 1.4 %defect.1.local = f32[2,64,256]{2,1,0:T(8,128)S(1)} custom-call(s32[1]{0:T(128)} %bitcast.where, f32[2,64,512]{2,1,0:T(8,128)S(1)} %get-tuple-element.50.refs_0_, f32[2,64,512]{2,1,0:T(8,128)S(1)} %get-tuple-element.52.refs_1_, f32[2,128,512]{2,1,0:T(8,128)S(1)} %get-tuple-element.54.refs_2_, f32[2,128,512]{2,1,0:T(8,128)S(1)} %copy-done, ...), custom_call_target="tpu_custom_call" | custom-call | flops 30 | bytes 30 | tf_op jit(solution)/shard_map/defect/pallas_call | solution.py:51
  37.4 0.0 collective-permute-done.6.far.refs_5_
  37.4 2.0 %collective-permute-start.10 = (f32[2,64,256]{2,1,0:T(8,128)S(1)}, f32[2,64,256]{2,1,0:T(8,128)S(1)}, u32[]{:S(2)}, u32[]{:S(2)}) collective-permute-start(f32[2,64,256]{2,1,0:T(8,128)S(1)} %coarse_first.1.fix.own), channel_id=1, source_target_pairs={{0,1},{1,0},{2,3},{3,2},{4,5},{5,4},{6,7},{7,6},{8,9},{9,8},{10,11... | collective-permute-start | bytes 393224 | tf_op jit(solution)/shard_map/ppermute | solution.py:422
  39.5 1.3 %collective-permute-start.9 = (f32[2,64,256]{2,1,0:T(8,128)S(1)}, f32[2,64,256]{2,1,0:T(8,128)S(1)}, u32[]{:S(2)}, u32[]{:S(2)}) collective-permute-start(f32[2,64,256]{2,1,0:T(8,128)S(1)} %coarse_first.1.fix.own), channel_id=1, source_target_pairs={{1,2},{3,4},{5,6},{7,8},{9,10},{11,12},{13,14},{17,18},{19,20},{21... | collective-permute-start | bytes 393224 | tf_op jit(solution)/shard_map/ppermute | solution.py:419
  40.7 0.0 collective-permute-start.17
  40.7 0.2 coarse_part.3.part
  40.9 0.5 collective-permute-start.11
  41.4 2.7 %collective-permute-done.9.far = f32[2,64,256]{2,1,0:T(8,128)S(1)} collective-permute-done((f32[2,64,256]{2,1,0:T(8,128)S(1)}, f32[2,64,256]{2,1,0:T(8,128)S(1)}, u32[]{:S(2)}, u32[]{:S(2)}) %collective-permute-start.9) | collective-permute-done | bytes 131104 | tf_op jit(solution)/shard_map/ppermute | solution.py:419
  44.1 3.9 %collective-permute-start.12 = (f32[2,64,256]{2,1,0:T(8,128)S(1)}, f32[2,64,256]{2,1,0:T(8,128)S(1)}, u32[]{:S(2)}, u32[]{:S(2)}) collective-permute-start(f32[2,64,256]{2,1,0:T(8,128)S(1)} %coarse_finish.3.fix), channel_id=1, source_target_pairs={{1,2},{3,4},{5,6},{7,8},{9,10},{11,12},{13,14},{17,18},{19,20},{21... | collective-permute-start | bytes 393224 | tf_op jit(solution)/shard_map/ppermute | solution.py:419
  48.0 0.2 coarse_part.4.part
  48.2 1.1 %collective-permute-start.14 = (f32[2,64,256]{2,1,0:T(8,128)S(1)}, f32[2,64,256]{2,1,0:T(8,128)S(1)}, u32[]{:S(2)}, u32[]{:S(2)}) collective-permute-start(f32[2,64,256]{2,1,0:T(8,128)S(1)} %get-tuple-element.67), channel_id=1, source_target_pairs={{1,2},{3,4},{5,6},{7,8},{9,10},{11,12},{13,14},{17,18},{19,20},{21... | collective-permute-start | bytes 393224 | tf_op jit(solution)/shard_map/ppermute | solution.py:419
  49.3 1.4 %collective-permute-done.12.far = f32[2,64,256]{2,1,0:T(8,128)S(1)} collective-permute-done((f32[2,64,256]{2,1,0:T(8,128)S(1)}, f32[2,64,256]{2,1,0:T(8,128)S(1)}, u32[]{:S(2)}, u32[]{:S(2)}) %collective-permute-start.12) | collective-permute-done | bytes 131104 | tf_op jit(solution)/shard_map/ppermute | solution.py:419
  50.7 4.0 %collective-permute-start.15 = (f32[2,64,256]{2,1,0:T(8,128)S(1)}, f32[2,64,256]{2,1,0:T(8,128)S(1)}, u32[]{:S(2)}, u32[]{:S(2)}) collective-permute-start(f32[2,64,256]{2,1,0:T(8,128)S(1)} %coarse_finish.4.fix), channel_id=1, source_target_pairs={{1,2},{3,4},{5,6},{7,8},{9,10},{11,12},{13,14},{17,18},{19,20},{21... | collective-permute-start | bytes 393224 | tf_op jit(solution)/shard_map/ppermute | solution.py:419
  54.7 0.2 coarse_part.5.part
  54.9 2.5 %collective-permute-done.15.far = f32[2,64,256]{2,1,0:T(8,128)S(1)} collective-permute-done((f32[2,64,256]{2,1,0:T(8,128)S(1)}, f32[2,64,256]{2,1,0:T(8,128)S(1)}, u32[]{:S(2)}, u32[]{:S(2)}) %collective-permute-start.15) | collective-permute-done | bytes 131104 | tf_op jit(solution)/shard_map/ppermute | solution.py:419
  57.4 1.8 %collective-permute-start.18 = (f32[2,64,256]{2,1,0:T(8,128)S(1)}, f32[2,64,256]{2,1,0:T(8,128)S(1)}, u32[]{:S(2)}, u32[]{:S(2)}) collective-permute-start(f32[2,64,256]{2,1,0:T(8,128)S(1)} %coarse_finish.5.refs_3_), channel_id=1, source_target_pairs={{1,2},{3,4},{5,6},{7,8},{9,10},{11,12},{13,14},{17,18},{19,20},{21... | collective-permute-start | bytes 393224 | tf_op jit(solution)/shard_map/ppermute | solution.py:419
  59.2 3.0 %third.1 = (f32[2,128,512]{2,1,0:T(8,128)S(1)}, f32[2,128,512]{2,1,0:T(8,128)S(1)}) custom-call(f32[1]{0:T(128)} %bitcast.1.keep, f32[2,64,512]{2,1,0:T(8,128)S(1)} %get-tuple-element.50.refs_0_, f32[2,64,512]{2,1,0:T(8,128)S(1)} %get-tuple-element.52.refs_1_, f32[2,128,512]{2,1,0:T(8,128)S(1)} %get-tuple-element.54.refs_2_, ...), custom_call_target="tpu_custom_call" | custom-call | flops 30 | bytes 30 | tf_op jit(solution)/shard_map/third/pallas_call | solution.py:51
  62.2 0.6 finish_fix.4.refs_1_
  62.9 0.7 finish_fix.5.refs_2_
  63.6 0.6 collective-permute-start.22
  64.1 0.6 finish_fix.3.refs_0_
  64.8 0.0 copy-start.1
  64.8 1.5 %collective-permute-start.21 = (f32[2,64,512]{2,1,0:T(8,128)S(1)}, f32[2,64,512]{2,1,0:T(8,128)S(1)}, u32[]{:S(2)}, u32[]{:S(2)}) collective-permute-start(f32[2,64,512]{2,1,0:T(8,128)S(1)} %finish_fix.3.refs_0_), channel_id=1, source_target_pairs={{1,2},{3,4},{5,6},{7,8},{9,10},{11,12},{13,14},{17,18},{19,20},{21... | collective-permute-start | bytes 786440 | tf_op jit(solution)/shard_map/ppermute | solution.py:419
  66.3 0.3 collective-permute-start.20
  66.6 1.0 %part.5 = (f32[2,128,512]{2,1,0:T(8,128)S(1)}, f32[2,128,512]{2,1,0:T(8,128)S(1)}) custom-call(f32[2,64,512]{2,1,0:T(8,128)S(1)} %finish_fix.3.refs_0_, f32[2,64,512]{2,1,0:T(8,128)S(1)} %finish_fix.4.refs_1_, f32[2,128,512]{2,1,0:T(8,128)S(1)} %finish_fix.5.refs_2_, f32[2,128,512]{2,1,0:T(8,128)S(1)} %get-tuple-element.44.refs_3_.gain.refs_12_, ...), custom_call_target="tpu_custom_call" | custom-call | flops 30 | bytes 30 | tf_op jit(solution)/shard_map/part/pallas_call | solution.py:51
  67.6 1.0 %final.3 = (f32[2,2,128,512]{3,2,1,0:T(8,128)}, f32[2,128,512]{2,1,0:T(8,128)}) custom-call(s32[1]{0:T(128)} %bitcast.where, f32[1]{0:T(128)} %bitcast.1.keep, f32[2,128,512]{2,1,0:T(8,128)S(1)} %get-tuple-element.77.part, f32[2,128,512]{2,1,0:T(8,128)S(1)} %collective-permute-done.22.halo, f32[2,128,512]{2,1,0:T(8,128)S(1)} %get-tuple-element.44.refs_3_.gain.refs_12_, ...), custom_call_target="tpu_custom_call" | custom-call | flops 10 | bytes 10 | tf_op jit(solution)/shard_map/final/pallas_call | solution.py:51
  68.6 6.6 %collective-permute-done.21.halo = f32[2,64,512]{2,1,0:T(8,128)S(1)} collective-permute-done((f32[2,64,512]{2,1,0:T(8,128)S(1)}, f32[2,64,512]{2,1,0:T(8,128)S(1)}, u32[]{:S(2)}, u32[]{:S(2)}) %collective-permute-start.21) | collective-permute-done | bytes 262176 | tf_op jit(solution)/shard_map/ppermute | solution.py:419
  75.2 0.8 %final.4 = (f32[2,2,128,512]{3,2,1,0:T(8,128)}, f32[2,128,512]{2,1,0:T(8,128)}) custom-call(s32[1]{0:T(128)} %bitcast.where, f32[1]{0:T(128)} %bitcast.1.keep, f32[2,128,512]{2,1,0:T(8,128)S(1)} %get-tuple-element.76.part, f32[2,64,512]{2,1,0:T(8,128)S(1)} %collective-permute-done.21.halo, ...), custom_call_target="tpu_custom_call", output_to_operand_aliasing={{0}: (8, {}), {1}: (9, {})} | custom-call | flops 10 | bytes 10 | tf_op jit(solution)/shard_map/final/pallas_call | solution.py:51
  76.0 2.0 %collective-permute-done.20.halo = f32[2,64,512]{2,1,0:T(8,128)S(1)} collective-permute-done((f32[2,64,512]{2,1,0:T(8,128)S(1)}, f32[2,64,512]{2,1,0:T(8,128)S(1)}, u32[]{:S(2)}, u32[]{:S(2)}) %collective-permute-start.20) | collective-permute-done | bytes 262176 | tf_op jit(solution)/shard_map/ppermute | solution.py:419
  78.0 0.8 %final.5 = (f32[2,2,128,512]{3,2,1,0:T(8,128)}, f32[2,128,512]{2,1,0:T(8,128)}) custom-call(s32[1]{0:T(128)} %bitcast.where, f32[1]{0:T(128)} %bitcast.1.keep, f32[2,128,512]{2,1,0:T(8,128)S(1)} %get-tuple-element.76.part, f32[2,64,512]{2,1,0:T(8,128)S(1)} %collective-permute-done.20.halo, ...), custom_call_target="tpu_custom_call", output_to_operand_aliasing={{0}: (8, {}), {1}: (9, {})} | custom-call | flops 10 | bytes 10 | tf_op jit(solution)/shard_map/final/pallas_call | solution.py:51
  (27 shorter events, 0.2 us)
Async XLA Ops:
  0.6 1.2 %copy-start.4 = (f32[2,2,128,512]{3,2,1,0:T(8,128)S(1)}, f32[2,2,128,512]{3,2,1,0:T(8,128)}, u32[]{:S(2)}) copy-start(f32[2,2,128,512]{3,2,1,0:T(8,128)} %warm.3) | copy-start | bytes 3145732
  1.9 3.9 %copy-start.2 = (f32[2,2,128,512]{3,2,1,0:T(8,128)S(1)}, f32[2,2,128,512]{3,2,1,0:T(8,128)}, u32[]{:S(2)}) copy-start(f32[2,2,128,512]{3,2,1,0:T(8,128)} %refs_4_.1) | copy-start | bytes 3145732
  2.8 2.9 %copy-start = (f32[2,128,512]{2,1,0:T(8,128)S(1)}, f32[2,128,512]{2,1,0:T(8,128)}, u32[]{:S(2)}) copy-start(f32[2,128,512]{2,1,0:T(8,128)} %phi.9) | copy-start | bytes 1572868
  2.8 6.0 %collective-permute-start.2 = (f32[2,128,512]{2,1,0:T(8,128)}, f32[2,128,512]{2,1,0:T(8,128)}, u32[]{:S(2)}, u32[]{:S(2)}) collective-permute-start(f32[2,128,512]{2,1,0:T(8,128)} %get-tuple-element.43.refs_2_), channel_id=1, source_target_pairs={{0,1},{1,0},{2,3},{3,2},{4,5},{5,4},{6,7},{7,6},{8,9},{9,8},{10,11... | collective-permute-start | bytes 1572872 | tf_op jit(solution)/shard_map/ppermute | solution.py:422
  3.0 11.6 %collective-permute-start = (f32[2,64,512]{2,1,0:T(8,128)S(1)}, f32[2,64,512]{2,1,0:T(8,128)}, u32[]{:S(2)}, u32[]{:S(2)}) collective-permute-start(f32[2,64,512]{2,1,0:T(8,128)S(1)} %take_first.1.refs_0_), channel_id=1, source_target_pairs={{1,2},{3,4},{5,6},{7,8},{9,10},{11,12},{13,14},{17,18},{19,20},{21... | collective-permute-start | bytes 786440 | tf_op jit(solution)/shard_map/ppermute | solution.py:419
  5.7 17.5 %collective-permute-start.1 = (f32[2,64,512]{2,1,0:T(8,128)}, f32[2,64,512]{2,1,0:T(8,128)}, u32[]{:S(2)}, u32[]{:S(2)}) collective-permute-start(f32[2,64,512]{2,1,0:T(8,128)} %get-tuple-element.42.refs_1_), channel_id=1, source_target_pairs={{1,2},{3,4},{5,6},{7,8},{9,10},{11,12},{13,14},{17,18},{19,20},{21... | collective-permute-start | bytes 786440 | tf_op jit(solution)/shard_map/ppermute | solution.py:419
  8.1 0.8 %copy-start.5 = (f32[2,128,512]{2,1,0:T(8,128)}, f32[2,128,512]{2,1,0:T(8,128)S(1)}, u32[]{:S(2)}) copy-start(f32[2,128,512]{2,1,0:T(8,128)S(1)} %get-tuple-element.48.part) | copy-start | bytes 1572868
  8.9 1.0 %copy-start.6 = (f32[2,128,512]{2,1,0:T(8,128)S(1)}, f32[2,128,512]{2,1,0:T(8,128)}, u32[]{:S(2)}) copy-start(f32[2,128,512]{2,1,0:T(8,128)} %copy-done.5) | copy-start | bytes 1572868
  11.1 22.9 %collective-permute-start.5 = (f32[2,128,512]{2,1,0:T(8,128)S(1)}, f32[2,128,512]{2,1,0:T(8,128)S(1)}, u32[]{:S(2)}, u32[]{:S(2)}) collective-permute-start(f32[2,128,512]{2,1,0:T(8,128)S(1)} %finish.5.refs_2_), channel_id=1, source_target_pairs={{0,1},{1,0},{2,3},{3,2},{4,5},{5,4},{6,7},{7,6},{8,9},{9,8},{10,11... | collective-permute-start | bytes 1572872 | tf_op jit(solution)/shard_map/ppermute | solution.py:422
  15.6 12.3 %collective-permute-start.3 = (f32[2,64,512]{2,1,0:T(8,128)S(1)}, f32[2,64,512]{2,1,0:T(8,128)S(1)}, u32[]{:S(2)}, u32[]{:S(2)}) collective-permute-start(f32[2,64,512]{2,1,0:T(8,128)S(1)} %finish.3.refs_0_), channel_id=1, source_target_pairs={{1,2},{3,4},{5,6},{7,8},{9,10},{11,12},{13,14},{17,18},{19,20},{21... | collective-permute-start | bytes 786440 | tf_op jit(solution)/shard_map/ppermute | solution.py:419
  24.2 6.9 %collective-permute-start.4 = (f32[2,64,512]{2,1,0:T(8,128)S(1)}, f32[2,64,512]{2,1,0:T(8,128)S(1)}, u32[]{:S(2)}, u32[]{:S(2)}) collective-permute-start(f32[2,64,512]{2,1,0:T(8,128)S(1)} %finish.4.refs_1_), channel_id=1, source_target_pairs={{1,2},{3,4},{5,6},{7,8},{9,10},{11,12},{13,14},{17,18},{19,20},{21... | collective-permute-start | bytes 786440 | tf_op jit(solution)/shard_map/ppermute | solution.py:419
  31.5 5.9 %collective-permute-start.6 = (f32[2,64,256]{2,1,0:T(8,128)S(1)}, f32[2,64,256]{2,1,0:T(8,128)S(1)}, u32[]{:S(2)}, u32[]{:S(2)}) collective-permute-start(f32[2,64,256]{2,1,0:T(8,128)S(1)} %get-tuple-element.55), channel_id=1, source_target_pairs={{1,2},{3,4},{5,6},{7,8},{9,10},{11,12},{13,14},{17,18},{19,20},{21... | collective-permute-start | bytes 393224 | tf_op jit(solution)/shard_map/ppermute | solution.py:419
  34.5 1.5 %copy-start.3 = (f32[2,2,128,512]{3,2,1,0:T(8,128)S(1)}, f32[2,2,128,512]{3,2,1,0:T(8,128)}, u32[]{:S(2)}) copy-start(f32[2,2,128,512]{3,2,1,0:T(8,128)} %refs_4_.1) | copy-start | bytes 3145732
  34.5 2.9 %collective-permute-start.7 = (f32[2,64,256]{2,1,0:T(8,128)S(1)}, f32[2,64,256]{2,1,0:T(8,128)S(1)}, u32[]{:S(2)}, u32[]{:S(2)}) collective-permute-start(f32[2,64,256]{2,1,0:T(8,128)S(1)} %get-tuple-element.56), channel_id=1, source_target_pairs={{0,1},{1,0},{2,3},{3,2},{4,5},{5,4},{6,7},{7,6},{8,9},{9,8},{10,11... | collective-permute-start | bytes 393224 | tf_op jit(solution)/shard_map/ppermute | solution.py:422
  35.9 5.0 %collective-permute-start.8 = (f32[2,64,256]{2,1,0:T(8,128)S(1)}, f32[2,64,256]{2,1,0:T(8,128)S(1)}, u32[]{:S(2)}, u32[]{:S(2)}) collective-permute-start(f32[2,64,256]{2,1,0:T(8,128)S(1)} %get-tuple-element.61), channel_id=1, source_target_pairs={{1,2},{3,4},{5,6},{7,8},{9,10},{11,12},{13,14},{17,18},{19,20},{21... | collective-permute-start | bytes 393224 | tf_op jit(solution)/shard_map/ppermute | solution.py:419
  37.4 4.0 %collective-permute-start.10 = (f32[2,64,256]{2,1,0:T(8,128)S(1)}, f32[2,64,256]{2,1,0:T(8,128)S(1)}, u32[]{:S(2)}, u32[]{:S(2)}) collective-permute-start(f32[2,64,256]{2,1,0:T(8,128)S(1)} %coarse_first.1.fix.own), channel_id=1, source_target_pairs={{0,1},{1,0},{2,3},{3,2},{4,5},{5,4},{6,7},{7,6},{8,9},{9,8},{10,11... | collective-permute-start | bytes 393224 | tf_op jit(solution)/shard_map/ppermute | solution.py:422
  39.5 4.7 %collective-permute-start.9 = (f32[2,64,256]{2,1,0:T(8,128)S(1)}, f32[2,64,256]{2,1,0:T(8,128)S(1)}, u32[]{:S(2)}, u32[]{:S(2)}) collective-permute-start(f32[2,64,256]{2,1,0:T(8,128)S(1)} %coarse_first.1.fix.own), channel_id=1, source_target_pairs={{1,2},{3,4},{5,6},{7,8},{9,10},{11,12},{13,14},{17,18},{19,20},{21... | collective-permute-start | bytes 393224 | tf_op jit(solution)/shard_map/ppermute | solution.py:419
  40.7 18.5 %collective-permute-start.17 = (f32[2,128,512]{2,1,0:T(8,128)S(1)}, f32[2,128,512]{2,1,0:T(8,128)S(1)}, u32[]{:S(2)}, u32[]{:S(2)}) collective-permute-start(f32[2,128,512]{2,1,0:T(8,128)S(1)} %get-tuple-element.54.refs_2_), channel_id=1, source_target_pairs={{0,1},{1,0},{2,3},{3,2},{4,5},{5,4},{6,7},{7,6},{8,9},{9,8},{10,11... | collective-permute-start | bytes 1572872 | tf_op jit(solution)/shard_map/ppermute | solution.py:422
  40.9 7.3 %collective-permute-start.11 = (f32[2,64,256]{2,1,0:T(8,128)S(1)}, f32[2,64,256]{2,1,0:T(8,128)S(1)}, u32[]{:S(2)}, u32[]{:S(2)}) collective-permute-start(f32[2,64,256]{2,1,0:T(8,128)S(1)} %get-tuple-element.65), channel_id=1, source_target_pairs={{1,2},{3,4},{5,6},{7,8},{9,10},{11,12},{13,14},{17,18},{19,20},{21... | collective-permute-start | bytes 393224 | tf_op jit(solution)/shard_map/ppermute | solution.py:419
  44.1 6.6 %collective-permute-start.12 = (f32[2,64,256]{2,1,0:T(8,128)S(1)}, f32[2,64,256]{2,1,0:T(8,128)S(1)}, u32[]{:S(2)}, u32[]{:S(2)}) collective-permute-start(f32[2,64,256]{2,1,0:T(8,128)S(1)} %coarse_finish.3.fix), channel_id=1, source_target_pairs={{1,2},{3,4},{5,6},{7,8},{9,10},{11,12},{13,14},{17,18},{19,20},{21... | collective-permute-start | bytes 393224 | tf_op jit(solution)/shard_map/ppermute | solution.py:419
  48.0 2.7 %collective-permute-start.13 = (f32[2,64,256]{2,1,0:T(8,128)S(1)}, f32[2,64,256]{2,1,0:T(8,128)S(1)}, u32[]{:S(2)}, u32[]{:S(2)}) collective-permute-start(f32[2,64,256]{2,1,0:T(8,128)S(1)} %coarse_finish.3.fix), channel_id=1, source_target_pairs={{0,1},{1,0},{2,3},{3,2},{4,5},{5,4},{6,7},{7,6},{8,9},{9,8},{10,11... | collective-permute-start | bytes 393224 | tf_op jit(solution)/shard_map/ppermute | solution.py:422
  48.2 6.7 %collective-permute-start.14 = (f32[2,64,256]{2,1,0:T(8,128)S(1)}, f32[2,64,256]{2,1,0:T(8,128)S(1)}, u32[]{:S(2)}, u32[]{:S(2)}) collective-permute-start(f32[2,64,256]{2,1,0:T(8,128)S(1)} %get-tuple-element.67), channel_id=1, source_target_pairs={{1,2},{3,4},{5,6},{7,8},{9,10},{11,12},{13,14},{17,18},{19,20},{21... | collective-permute-start | bytes 393224 | tf_op jit(solution)/shard_map/ppermute | solution.py:419
  50.7 6.6 %collective-permute-start.15 = (f32[2,64,256]{2,1,0:T(8,128)S(1)}, f32[2,64,256]{2,1,0:T(8,128)S(1)}, u32[]{:S(2)}, u32[]{:S(2)}) collective-permute-start(f32[2,64,256]{2,1,0:T(8,128)S(1)} %coarse_finish.4.fix), channel_id=1, source_target_pairs={{1,2},{3,4},{5,6},{7,8},{9,10},{11,12},{13,14},{17,18},{19,20},{21... | collective-permute-start | bytes 393224 | tf_op jit(solution)/shard_map/ppermute | solution.py:419
  54.7 2.7 %collective-permute-start.16 = (f32[2,64,256]{2,1,0:T(8,128)S(1)}, f32[2,64,256]{2,1,0:T(8,128)S(1)}, u32[]{:S(2)}, u32[]{:S(2)}) collective-permute-start(f32[2,64,256]{2,1,0:T(8,128)S(1)} %coarse_finish.4.fix), channel_id=1, source_target_pairs={{0,1},{1,0},{2,3},{3,2},{4,5},{5,4},{6,7},{7,6},{8,9},{9,8},{10,11... | collective-permute-start | bytes 393224 | tf_op jit(solution)/shard_map/ppermute | solution.py:422
  57.4 4.8 %collective-permute-start.18 = (f32[2,64,256]{2,1,0:T(8,128)S(1)}, f32[2,64,256]{2,1,0:T(8,128)S(1)}, u32[]{:S(2)}, u32[]{:S(2)}) collective-permute-start(f32[2,64,256]{2,1,0:T(8,128)S(1)} %coarse_finish.5.refs_3_), channel_id=1, source_target_pairs={{1,2},{3,4},{5,6},{7,8},{9,10},{11,12},{13,14},{17,18},{19,20},{21... | collective-permute-start | bytes 393224 | tf_op jit(solution)/shard_map/ppermute | solution.py:419
  59.2 3.7 %collective-permute-start.19 = (f32[2,64,256]{2,1,0:T(8,128)S(1)}, f32[2,64,256]{2,1,0:T(8,128)S(1)}, u32[]{:S(2)}, u32[]{:S(2)}) collective-permute-start(f32[2,64,256]{2,1,0:T(8,128)S(1)} %coarse_finish.5.refs_3_), channel_id=1, source_target_pairs={{0,1},{1,0},{2,3},{3,2},{4,5},{5,4},{6,7},{7,6},{8,9},{9,8},{10,11... | collective-permute-start | bytes 393224 | tf_op jit(solution)/shard_map/ppermute | solution.py:422
  63.6 4.0 %collective-permute-start.22 = (f32[2,128,512]{2,1,0:T(8,128)S(1)}, f32[2,128,512]{2,1,0:T(8,128)S(1)}, u32[]{:S(2)}, u32[]{:S(2)}) collective-permute-start(f32[2,128,512]{2,1,0:T(8,128)S(1)} %finish_fix.5.refs_2_), channel_id=1, source_target_pairs={{0,1},{1,0},{2,3},{3,2},{4,5},{5,4},{6,7},{7,6},{8,9},{9,8},{10,11... | collective-permute-start | bytes 1572872 | tf_op jit(solution)/shard_map/ppermute | solution.py:422
  64.8 2.9 %copy-start.1 = (f32[2,128,512]{2,1,0:T(8,128)S(1)}, f32[2,128,512]{2,1,0:T(8,128)}, u32[]{:S(2)}) copy-start(f32[2,128,512]{2,1,0:T(8,128)} %psi.5) | copy-start | bytes 1572868
  64.8 10.4 %collective-permute-start.21 = (f32[2,64,512]{2,1,0:T(8,128)S(1)}, f32[2,64,512]{2,1,0:T(8,128)S(1)}, u32[]{:S(2)}, u32[]{:S(2)}) collective-permute-start(f32[2,64,512]{2,1,0:T(8,128)S(1)} %finish_fix.3.refs_0_), channel_id=1, source_target_pairs={{1,2},{3,4},{5,6},{7,8},{9,10},{11,12},{13,14},{17,18},{19,20},{21... | collective-permute-start | bytes 786440 | tf_op jit(solution)/shard_map/ppermute | solution.py:419
  66.3 11.7 %collective-permute-start.20 = (f32[2,64,512]{2,1,0:T(8,128)S(1)}, f32[2,64,512]{2,1,0:T(8,128)S(1)}, u32[]{:S(2)}, u32[]{:S(2)}) collective-permute-start(f32[2,64,512]{2,1,0:T(8,128)S(1)} %finish_fix.4.refs_1_), channel_id=1, source_target_pairs={{1,2},{3,4},{5,6},{7,8},{9,10},{11,12},{13,14},{17,18},{19,20},{21... | collective-permute-start | bytes 786440 | tf_op jit(solution)/shard_map/ppermute | solution.py:419

commit v4 on v3

v4 whole, which is shorter than its diff:
```python
import functools

import jax
import jax.numpy as jnp
from jax import lax
from jax.experimental import pallas as pl
from jax.experimental.pallas import tpu as pltpu
from jax.sharding import PartitionSpec as P

SWEEPS = 2
COARSE_SWEEPS = 4

GRADIENT_ENERGY = 1.0
TIME_STEP = 0.02
DAMPING = 0.8
KEEP = 1.0 - DAMPING
COARSE_ENERGY = GRADIENT_ENERGY / 4.0
COARSE_STEP = TIME_STEP / 4.0


VMEM = pl.BlockSpec(memory_space=pltpu.VMEM)
SMEM = pl.BlockSpec(memory_space=pltpu.SMEM)
ANY = pl.BlockSpec(memory_space=pl.ANY)
HBM = pl.BlockSpec(memory_space=pltpu.HBM)
BLOCK = 16
F32 = jnp.float32


def chip_pairs(count):
    return [(i, i ^ 1) for i in range(count)]


def cross_pairs(groups, count):
    pairs = []
    for g in range(groups):
        pairs += [(g * count + i, g * count + i + 1) for i in range(1, count - 1, 2)]
    for g in range(0, groups - 1, 2):
        pairs += [(g * count + i, (g + 1) * count + i) for i in (0, count - 1)]
    swaps = pairs + [(b, a) for a, b in pairs]
    if groups % 2 == 1:
        swaps += [((groups - 1) * count + i,) * 2 for i in (0, count - 1)]
    return swaps


def early_chunks(rows):
    return [rows // 2, rows // 2]


def late_chunks(rows):
    return [rows]


def call(body, name, outs, args, in_specs=None, out_specs=None, scratch=(), aliases=None, work=30, dtype=F32):
    shapes = [jax.ShapeDtypeStruct(s, dtype) for s in outs]
    size = sum(int(a.size) for a in args)
    made = sum(s.size for s in shapes)
    return pl.pallas_call(
        body,
        out_shape=shapes,
        in_specs=in_specs or [VMEM] * len(args),
        out_specs=out_specs or [VMEM] * len(outs),
        scratch_shapes=list(scratch),
        input_output_aliases=aliases or {},
        name=name,
        cost_estimate=pl.CostEstimate(flops=0, bytes_accessed=4 * (size + made), transcendentals=0),
        compiler_params=pltpu.CompilerParams(vmem_limit_bytes=12 * 1024 * 1024),
    )(*args)


def blocks(rows):
    return range(0, rows, BLOCK)


def around(read, r, rows):
    x = read(r, r + BLOCK)
    cols = x.shape[-1]
    row = lax.broadcasted_iota(jnp.int32, x.shape, 0)
    col = lax.broadcasted_iota(jnp.int32, x.shape, 1)
    up = read(r - 1, r - 1 + BLOCK) if r > 0 else jnp.where(row == 0, 0.0, pltpu.roll(x, 1, 0))
    if r + BLOCK < rows:
        down = read(r + 1, r + 1 + BLOCK)
    else:
        down = jnp.where(row == BLOCK - 1, 0.0, pltpu.roll(x, BLOCK - 1, 0))
    left = jnp.where(col == 0, 0.0, pltpu.roll(x, 1, 1))
    right = jnp.where(col == cols - 1, 0.0, pltpu.roll(x, cols - 1, 1))
    return x, (up + down) + (left + right)


def reader(ref, *lead):
    return lambda lo, hi: ref[(*lead, slice(lo, hi))]


def add_terms(base_p, base_m, gain, nb_p, nb_m, energy, step):
    gain_kt = (DAMPING - gain) * (1.0 / 6.0)
    new_p = base_p - gain * (energy * nb_m) + gain_kt * nb_p
    new_m = base_m + gain * (step * nb_p + (6.0 * step * energy) * nb_m)
    return new_p, new_m


def parts3(x):
    high = x.astype(jnp.bfloat16)
    rest = x - high.astype(F32)
    middle = rest.astype(jnp.bfloat16)
    low = (rest - middle.astype(F32)).astype(jnp.bfloat16)
    return high, middle, low


def times(xs, matrix):
    n, width = xs[0].shape[0], matrix.shape[0]
    pieces = [x[:, j : j + width] for x in xs for j in range(0, x.shape[1], width)]
    stacked = jnp.concatenate([v for piece in pieces for v in parts3(piece)], axis=0)
    out = jnp.dot(stacked, matrix, preferred_element_type=F32)
    sums = [out[j : j + n] + out[j + n : j + 2 * n] + out[j + 2 * n : j + 3 * n] for j in range(0, out.shape[0], 3 * n)]
    each = len(sums) // len(xs)
    return [jnp.concatenate(sums[j : j + each], axis=1) for j in range(0, len(sums), each)]


LANES = 128


def tiles(rows, cols):
    return pltpu.VMEM((cols // LANES, rows, LANES), F32)


def put_rows(ref, rows, x):
    for j in range(ref.shape[0]):
        ref[j, rows] = x[:, j * LANES : (j + 1) * LANES]


def get_rows(ref, rows):
    return jnp.concatenate([ref[j, rows] for j in range(ref.shape[0])], axis=1)


def even_odd(ref):
    half = ref.shape[1] // 2
    return pl.ds(0, half, stride=2), pl.ds(1, half, stride=2)


def pair_rows(ref):
    even, odd = even_odd(ref)
    return get_rows(ref, even) + get_rows(ref, odd)


def take_body(what, where, warm, *refs):
    outs, sems = refs[:-1], refs[-1]
    c = where[0]
    copies = []
    for n, ((is_near, lo), out) in enumerate(zip(what, outs)):
        plane = 1 - c if is_near else c
        rows = pl.ds(lo, out.shape[1])
        copies.append(pltpu.make_async_copy(warm.at[:, plane, rows], out, sems.at[n]))
        copies[-1].start()
    for copy in copies:
        copy.wait()


def matrices_body(where, pair, even_col, odd_col, pair_t, even_t, odd_t):
    for dim, (both, even, odd) in enumerate(((pair, even_col, odd_col), (pair_t, even_t, odd_t))):
        cell = lax.broadcasted_iota(jnp.int32, both.shape, dim)
        coarse = 2 * lax.broadcasted_iota(jnp.int32, both.shape, 1 - dim)
        is_even = jnp.where(cell == coarse, 1.0, 0.0)
        is_odd = jnp.where(cell == coarse + 1, 1.0, 0.0)
        even[...] = is_even.astype(jnp.bfloat16)
        odd[...] = is_odd.astype(jnp.bfloat16)
        both[...] = (is_even + is_odd).astype(jnp.bfloat16)


def setup_body(where, phi, cot, gain, own):
    c = where[0]
    for i in range(2):
        plane = c if i == 0 else 1 - c
        for r in blocks(phi.shape[1]):
            rows = slice(r, r + BLOCK)
            v = phi[plane, rows]
            k = 3.0 * v * v - 1.0 + 6.0 * GRADIENT_ENERGY
            g = DAMPING / (1.0 + 6.0 * TIME_STEP * k)
            s0, s1 = cot[0, plane, rows], cot[1, plane, rows]
            gain[i, rows] = g
            own[i, 0, rows] = g * (s0 + k * s1)
            own[i, 1, rows] = g * (s1 - 6.0 * TIME_STEP * s0)


def coarse_setup_body(phi, pair, gain, both):
    for r in blocks(phi.shape[1]):
        rows = slice(r, r + BLOCK)
        a, b = phi[0, rows], phi[1, rows]
        put_rows(both, rows, (3.0 * a * a - 1.0) + (3.0 * b * b - 1.0))
    k = times([pair_rows(both)], pair[...])[0] / 8.0 + 6.0 * COARSE_ENERGY
    gain[...] = DAMPING / (1.0 + 6.0 * COARSE_STEP * k)


def gather_rows(chunks, whole):
    lo = 0
    for chunk in chunks:
        n = chunk.shape[1]
        for r in blocks(n):
            for f in range(2):
                whole[f, slice(lo + r, lo + r + BLOCK)] = chunk[f, slice(r, r + BLOCK)]
        lo += n


def part_body(count, *refs):
    chunks, (near, gain, own, far_out, near_out, far) = refs[:count], refs[count:]
    gather_rows(chunks, far)
    rows_all = far.shape[1]
    for i, (mine, other, out) in enumerate(((far, near, far_out), (near, far, near_out))):
        for r in blocks(rows_all):
            rows = slice(r, r + BLOCK)
            p, nb_p = around(reader(mine, 0), r, rows_all)
            m, nb_m = around(reader(mine, 1), r, rows_all)
            out[0, rows], out[1, rows] = add_terms(
                KEEP * p + own[i, 0, rows],
                KEEP * m + own[i, 1, rows],
                gain[i, rows],
                nb_p + other[0, rows],
                nb_m + other[1, rows],
                GRADIENT_ENERGY,
                TIME_STEP,
            )


def finish_body(i, lo, keep, part, halo, gain, out):
    for r in blocks(halo.shape[1]):
        rows, whole = slice(r, r + BLOCK), slice(lo + r, lo + r + BLOCK)
        hp, hm = halo[0, rows], halo[1, rows]
        if i == 0:
            hp, hm = hp * keep[0], hm * keep[0]
        out[0, rows], out[1, rows] = add_terms(
            part[0, whole], part[1, whole], gain[i, whole], hp, hm, GRADIENT_ENERGY, TIME_STEP
        )


def finish_pool_body(i, lo, keep, part, halo, gain, pair, *refs):
    before, (pool, out, phase, chem) = refs[:-4], refs[-4:]
    for r in blocks(halo.shape[1]):
        rows, whole = slice(r, r + BLOCK), slice(lo + r, lo + r + BLOCK)
        hp, hm = halo[0, rows], halo[1, rows]
        if i == 0:
            hp, hm = hp * keep[0], hm * keep[0]
        p, m = add_terms(
            part[0, whole], part[1, whole], gain[i, whole], hp, hm, GRADIENT_ENERGY, TIME_STEP
        )
        out[0, rows] = p
        out[1, rows] = m
        put_rows(phase, rows, p)
        put_rows(chem, rows, m)
    sums = times([pair_rows(phase), pair_rows(chem)], pair[...])
    for f in range(2):
        for ref in before:
            pool[f, : lo // 2] = ref[f]
        pool[f, lo // 2 if before else 0 :] = sums[f]


def three_body(count, *refs):
    chunks, (even_col, odd_col), outs, tile = refs[:count], refs[count : count + 2], refs[count + 2 : -1], refs[-1]
    for f in range(2):
        lo = 0
        for chunk in chunks:
            for r in blocks(chunk.shape[1]):
                put_rows(tile, slice(lo + r, lo + r + BLOCK), chunk[f, slice(r, r + BLOCK)])
            lo += chunk.shape[1]
        even, odd = even_odd(tile)
        top, bottom = get_rows(tile, even), get_rows(tile, odd)
        first, third = times([top, bottom], even_col[...])
        second = times([top], odd_col[...])[0]
        values = jnp.concatenate([first, second, third], axis=0)
        n = values.shape[0] // len(outs)
        for j, out in enumerate(outs):
            out[f] = values[j * n : (j + 1) * n]


def part_defect_body(count, *refs):
    chunks, (near, gain, own, pair, far_out, near_out, out, far, phase, chem) = refs[:count], refs[count:]
    part_body(count, *chunks, near, gain, own, far_out, near_out, far)
    for r in blocks(near.shape[1]):
        rows = slice(r, r + BLOCK)
        r0, r1 = 0.0, 0.0
        for i, (mine, new) in enumerate(((far, far_out), (near, near_out))):
            dp, dm = new[0, rows] - mine[0, rows], new[1, rows] - mine[1, rows]
            k = (DAMPING - gain[i, rows]) / (6.0 * TIME_STEP * gain[i, rows])
            r0 = r0 + (dp - k * dm)
            r1 = r1 + (dm + 6.0 * TIME_STEP * dp)
        put_rows(phase, rows, r0)
        put_rows(chem, rows, r1)
    sums = times([pair_rows(phase), pair_rows(chem)], pair[...])
    for f in range(2):
        out[f] = sums[f] * (1.0 / (8.0 * DAMPING))


def coarse_first_body(keep, local, far, near, gain, out):
    for r in blocks(local.shape[1]):
        rows = slice(r, r + BLOCK)
        s0 = local[0, rows] - (GRADIENT_ENERGY / 8.0) * (far[1, rows] * keep[0] + near[1, rows])
        s1 = local[1, rows] + (TIME_STEP / 8.0) * (far[0, rows] * keep[0] + near[0, rows])
        g = gain[rows]
        out[0, rows] = g * s0 + ((DAMPING - g) * (1.0 / (6.0 * COARSE_STEP))) * s1
        out[1, rows] = g * (s1 - 6.0 * COARSE_STEP * s0)


def coarse_part_body(fix, own, gain, out):
    rows_all = fix.shape[1]
    for r in blocks(rows_all):
        rows = slice(r, r + BLOCK)
        p, nb_p = around(reader(fix, 0), r, rows_all)
        m, nb_m = around(reader(fix, 1), r, rows_all)
        out[0, rows], out[1, rows] = add_terms(
            KEEP * p + own[0, rows],
            KEEP * m + own[1, rows],
            gain[rows],
            nb_p,
            nb_m,
            COARSE_ENERGY,
            COARSE_STEP,
        )


def coarse_finish_body(keep, part, far, near, gain, out):
    for r in blocks(part.shape[1]):
        rows = slice(r, r + BLOCK)
        out[0, rows], out[1, rows] = add_terms(
            part[0, rows],
            part[1, rows],
            gain[rows],
            far[0, rows] * keep[0] + near[0, rows],
            far[1, rows] * keep[0] + near[1, rows],
            COARSE_ENERGY,
            COARSE_STEP,
        )


def spread_into(tile_a, tile_b, fix_a, fix_b, pair_t):
    for tile, wide in zip((tile_a, tile_b), times([fix_a, fix_b], pair_t)):
        for rows in even_odd(tile):
            put_rows(tile, rows, wide)


def third_body(count, keep, *refs):
    far, near, fix, near_halo, sums = refs[:5]
    pieces, refs = refs[5 : 5 + count], refs[5 + count :]
    pair_t, even_t, odd_t, gain, far_out, near_out, fix_p, fix_m, halo_p, halo_m, wide_p, wide_m = refs
    rows_all = near.shape[1]
    half = rows_all // 2
    spread_into(fix_p, fix_m, fix[0], fix[1], pair_t[...])
    for f, tile in enumerate((halo_p, halo_m)):
        values = jnp.concatenate([piece[f] for piece in pieces], axis=0)
        a, b, c = values[:half], values[half : 2 * half], values[2 * half :]
        d = sums[f] - ((a + b) + c)
        even, odd = even_odd(tile)
        (a, c), (b, d) = times([a, c], even_t[...]), times([b, d], odd_t[...])
        put_rows(tile, even, a + b)
        put_rows(tile, odd, c + d)
    for r in blocks(rows_all):
        rows = slice(r, r + BLOCK)
        wide_p[rows], wide_m[rows] = get_rows(fix_p, rows), get_rows(fix_m, rows)
    for r in blocks(rows_all):
        rows = slice(r, r + BLOCK)
        p, nb_p = around(lambda lo, hi: wide_p[lo:hi], r, rows_all)
        m, nb_m = around(lambda lo, hi: wide_m[lo:hi], r, rows_all)
        nb_p, nb_m = nb_p + p, nb_m + m
        hp, hm = get_rows(halo_p, rows) * keep[0], get_rows(halo_m, rows) * keep[0]
        for i, (part, out, xp, xm) in enumerate(
            ((far, far_out, hp, hm), (near, near_out, near_halo[0, rows], near_halo[1, rows]))
        ):
            out[0, rows], out[1, rows] = add_terms(
                part[0, rows] + KEEP * p,
                part[1, rows] + KEEP * m,
                gain[i, rows],
                nb_p + xp,
                nb_m + xm,
                GRADIENT_ENERGY,
                TIME_STEP,
            )


def finish_fix_rows(i, lo, keep, part, halo, pair_t, gain, out, phase, chem):
    n = out.shape[1]
    coarse = slice(lo // 2, (lo + n) // 2)
    spread_into(phase, chem, halo[0, coarse], halo[1, coarse], pair_t[...])
    for r in blocks(n):
        rows, whole = slice(r, r + BLOCK), slice(lo + r, lo + r + BLOCK)
        hp, hm = get_rows(phase, rows), get_rows(chem, rows)
        if i == 0:
            hp, hm = hp * keep[0], hm * keep[0]
        out[0, rows], out[1, rows] = add_terms(
            part[0, whole], part[1, whole], gain[i, whole], hp, hm, GRADIENT_ENERGY, TIME_STEP
        )


def fix_body(starts, keep, far_part, near_part, far_halo, near_halo, pair_t, gain, *refs):
    count = len(starts)
    outs, scratch = refs[: count + 1], refs[count + 1 :]
    for n, (lo, out) in enumerate(zip(starts, outs)):
        finish_fix_rows(0, lo, keep, far_part, far_halo, pair_t, gain, out, *scratch[2 * n : 2 * n + 2])
    finish_fix_rows(1, 0, keep, near_part, near_halo, pair_t, gain, outs[-1], *scratch[-2:])


def final_rows(i, lo, where, keep, part, halo, gain, phi, psi, adjoint, design, plane_out, grad_out, sems):
    c = where[0]
    plane = c if i == 0 else 1 - c
    rows_all = halo.shape[1]
    step = rows_all // 2
    copies = []
    for n, start in enumerate(range(0, rows_all, step)):
        for r in range(start, start + step, BLOCK):
            rows, whole = slice(r, r + BLOCK), slice(lo + r, lo + r + BLOCK)
            hp, hm = halo[0, rows], halo[1, rows]
            if i == 0:
                hp, hm = hp * keep[0], hm * keep[0]
            p, m = add_terms(
                part[0, whole], part[1, whole], gain[i, whole], hp, hm, GRADIENT_ENERGY, TIME_STEP
            )
            plane_out[0, rows] = p
            plane_out[1, rows] = m
            grad_out[rows] = 6.0 * phi[plane, whole] * psi[plane, whole] * m
        here, there = pl.ds(start, step), pl.ds(lo + start, step)
        copies.append(pltpu.make_async_copy(plane_out.at[:, here], adjoint.at[:, plane, there], sems.at[2 * n]))
        copies.append(pltpu.make_async_copy(grad_out.at[here], design.at[plane, there], sems.at[2 * n + 1]))
        copies[-2].start()
        copies[-1].start()
    return copies


def final_body(which, where, keep, gain, phi, psi, *refs):
    count = len(which)
    halos, refs = refs[: 2 * count], refs[2 * count :]
    scratch = refs[-3 * count :]
    adjoint, design = refs[-3 * count - 2 : -3 * count]
    copies = []
    for n, (i, lo) in enumerate(which):
        part, halo = halos[2 * n : 2 * n + 2]
        copies += final_rows(
            i, lo, where, keep, part, halo, gain, phi, psi, adjoint, design, *scratch[3 * n : 3 * n + 3]
        )
    for copy in copies:
        copy.wait()


def on_device(phase_lin, phase_state, cotangent, warm_start):
    groups, count = lax.axis_size("grp"), lax.axis_size("gx")
    me = lax.axis_index("gx")
    where = jnp.reshape(me % 2, (1,)).astype(jnp.int32)
    keep = jnp.reshape(((me > 0) & (me < count - 1)).astype(F32), (1,))
    across, on_chip = cross_pairs(groups, count), chip_pairs(count)
    rows, cols = phase_lin.shape[1:]
    full, half = (2, rows, cols), (2, rows // 2, cols // 2)
    sizes = early_chunks(rows)
    starts = [sum(sizes[:n]) for n in range(len(sizes))]

    def swap_far(x):
        return lax.ppermute(x, ("grp", "gx"), across)

    def swap_near(x):
        return lax.ppermute(x, "gx", on_chip)

    def after(x, y):
        return lax.optimization_barrier((x, y))

    whole, tile = pltpu.VMEM(full, F32), tiles(rows, cols)

    def run(body, name, outs, args, statics=(), smem=0, **kw):
        specs = [SMEM] * smem + [VMEM] * (len(args) - smem)
        return call(functools.partial(body, *statics), name, outs, args, specs, **kw)

    def take(what, name):
        outs = [(2, n, cols) for _, _, n in what]
        body = functools.partial(take_body, [(is_near, lo) for is_near, lo, _ in what])
        scratch = [pltpu.SemaphoreType.DMA((len(what),))]
        source = pltpu.with_memory_space_constraint(warm_start, pltpu.HBM)
        return call(body, name, outs, (where, source), [SMEM, HBM], scratch=scratch, work=0)

    *far, near = take([(False, lo, n) for lo, n in zip(starts, sizes)] + [(True, 0, rows)], "take")
    far_halo = [swap_far(v) for v in far]
    near_halo = swap_near(near)
    gain, own = run(setup_body, "setup", [full, (2, 2, rows, cols)], (where, phase_lin, cotangent), smem=1)
    coefs = (gain,)
    far_part, near_part = run(part_body, "part", [full] * 2, (*far, near, *coefs, own), (len(far),), scratch=[whole])
    def finish(i, lo, part, halo):
        shape = (2, halo.shape[1], cols)
        return run(finish_body, "finish", [shape], (keep, part, halo, *coefs), (i, lo), smem=1, work=8)[0]

    far = [finish(0, lo, far_part, halo) for lo, halo in zip(starts, far_halo)]
    near_halo, far[-1] = after(near_halo, far[-1])
    near = finish(1, 0, near_part, near_halo)
    later, far[-1] = after(where, far[-1])
    shapes = [(2 * LANES, LANES)] * 3 + [(LANES, 2 * LANES)] * 3
    matrices = run(matrices_body, "matrices", shapes, (later,), smem=1, dtype=jnp.bfloat16)
    pair, even_col, odd_col, pair_t, even_t, odd_t = matrices
    coarse = run(coarse_setup_body, "coarse_setup", [half[1:]], (phase_lin, pair), scratch=[tile])

    far_halo = [swap_far(v) for v in far]
    near_halo = swap_near(near)
    far_part, near_part = run(part_body, "part", [full] * 2, (*far, near, *coefs, own), (len(far),), scratch=[whole])

    def finish_pool(i, lo, part, halo, before=()):
        n = halo.shape[1]
        pool = (2, (n + (lo if before else 0)) // 2, cols // 2)
        args = (keep, part, halo, *coefs, pair, *before)
        outs, scratch = [pool, (2, n, cols)], [tiles(n, cols)] * 2
        return run(finish_pool_body, "finish_pool", outs, args, (i, lo), smem=1, scratch=scratch, work=8)

    far, before = [], ()
    for lo, halo in zip(starts, far_halo):
        far_pool, chunk = finish_pool(0, lo, far_part, halo, before)
        far.append(chunk)
        before = (far_pool,)
    near_pool, near = finish_pool(1, 0, near_part, near_halo)
    near_pool, far_pool = after(near_pool, far_pool)

    far_sums, near_sums = swap_far(far_pool), swap_near(near_pool)
    plane_sums = far_sums
    many = COARSE_SWEEPS - 1
    pieces = [(2, 3 * rows // 2 // many, cols // 2)] * many
    pieces = run(three_body, "three", pieces, (*far, even_col, odd_col), (len(far),), scratch=[tile])
    arrived = [swap_far(pieces[0])]
    near_halo = swap_near(near)
    args, scratch = (*far, near, *coefs, own, pair), [whole, tile, tile]
    far_part, near_part, local = run(
        part_defect_body, "part_defect", [full, full, half], args, (len(far),), scratch=scratch
    )
    fix = run(coarse_first_body, "coarse_first", [half], (keep, local, far_sums, near_sums, *coarse), smem=1, work=8)[0]
    first = fix
    for sweep_index in range(COARSE_SWEEPS - 1):
        far_sums, near_sums = swap_far(fix), swap_near(fix)
        if len(arrived) < len(pieces):
            fix, held = lax.optimization_barrier((fix, pieces[len(arrived)]))
            arrived.append(swap_far(held))
        part = run(coarse_part_body, "coarse_part", [half], (fix, first, *coarse))[0]
        part, arrived[sweep_index] = after(part, arrived[sweep_index])
        args = (keep, part, far_sums, near_sums, *coarse)
        fix = run(coarse_finish_body, "coarse_finish", [half], args, smem=1, work=8)[0]

    far_sums, near_sums = swap_far(fix), swap_near(fix)
    args = (keep, far_part, near_part, fix, near_halo, plane_sums, *arrived, pair_t, even_t, odd_t, *coefs)
    scratch = [tile] * 4 + [pltpu.VMEM((rows, cols), F32)] * 2
    far_part, near_part = run(third_body, "third", [full, full], args, (len(arrived),), smem=1, scratch=scratch)
    sizes = late_chunks(rows)
    starts = [sum(sizes[:n]) for n in range(len(sizes))]
    args, shapes = (keep, far_part, near_part, far_sums, near_sums, pair_t, *coefs), [(2, n, cols) for n in sizes]
    scratch = [v for n in [*sizes, rows] for v in [tiles(n, cols)] * 2]
    *far, near = run(fix_body, "fix", [*shapes, full], args, (starts,), smem=1, scratch=scratch, work=8)

    far_halo, near_halo = [swap_far(v) for v in far], swap_near(near)
    far_part, near_part = run(part_body, "part", [full] * 2, (*far, near, *coefs, own), (len(far),), scratch=[whole])
    outs = [(2, 2, rows, cols), full]

    def final(which, fields, done):
        args = (where, keep, *coefs, phase_lin, phase_state, *fields, *done)
        in_specs = [SMEM, SMEM] + [VMEM] * (len(args) - len(done) - 2) + [ANY] * len(done)
        scratch = []
        for halo in fields[1::2]:
            n = halo.shape[1]
            scratch += [pltpu.VMEM((2, n, cols), F32), pltpu.VMEM((n, cols), F32), pltpu.SemaphoreType.DMA((4,))]
        body = functools.partial(final_body, which)
        aliases = {len(args) - 2: 0, len(args) - 1: 1} if done else None
        return call(body, "final", outs, args, in_specs, [ANY, ANY], scratch, aliases, work=10)

    done = ()
    for lo, halo in zip(starts[:-1], far_halo[:-1]):
        done = final([(0, lo)], (far_part, halo), done)
    done = final([(1, 0)], (near_part, near_halo), done)
    done = final([(0, starts[-1])], (far_part, far_halo[-1]), done)
    return tuple(done)


def solution(mesh):
    in_specs = (
        P(("grp", "gx"), None, None),
        P(("grp", "gx"), None, None),
        P(None, ("grp", "gx"), None, None),
        P(None, ("grp", "gx"), None, None),
    )
    out_specs = (P(None, ("grp", "gx"), None, None), P(("grp", "gx"), None, None))
    return jax.shard_map(
        on_device, mesh=mesh, in_specs=in_specs, out_specs=out_specs, check_vma=False
    )
```

time: 79.4 us -> 77.4 us (0.975)
  waiting for transfers between devices: 26 us -> 36.7 us
  Pallas kernels: 20.5 us -> 12.6 us
  starting transfers between devices: 28.1 us -> 25.8 us
  local copies, waits for them, and re-layouts: 3.07 us -> 1.24 us
    ppermute x14 -> x13, waiting for transfers between devices: 26 us -> 36.7 us  [swap_far(): return lax.ppermute(x, ('grp', 'gx'), across)]
    pallas_call x29 -> x26, Pallas kernels: 20.5 us -> 12.6 us  [call(): pl.pallas_call(body, out_shape=shapes, in_specs=in_specs or [VMEM] * len(...]
    unnamed x14 -> x6, local copies, waits for them, and re-layouts: 3.07 us -> 1.24 us
    ppermute x14 -> x13, starting transfers between devices: 24.9 us -> 23.6 us  [swap_far(): return lax.ppermute(x, ('grp', 'gx'), across)]
    ppermute x9, starting transfers between devices: 3.23 us -> 2.19 us  [swap_near(): return lax.ppermute(x, 'gx', on_chip)]
  transfers between devices with their start and end apart: 23 -> 22, of which waited for: 8 -> 10; matrix products, arithmetic and copies ran while one was open for 0% -> 0% of each run, Pallas kernels for 23% -> 12%
where the time goes in v4:
time: 77.4 us; the launch traced here: 77.2 us
  waiting for transfers between devices  36.7 us (47%)
  starting transfers between devices  25.8 us (33%)
  Pallas kernels  12.6 us (16%)
  local copies, waits for them, and re-layouts  1.24 us (2%)
  between operations  0.88 us (1%)
    ppermute x13, waiting for transfers between devices, swap_far(): return lax.ppermute(x, ('grp', 'gx'), across)  36.7 us
    ppermute x13, starting transfers between devices, swap_far(): return lax.ppermute(x, ('grp', 'gx'), across)  23.6 us
    pallas_call x26, Pallas kernels, call(): pl.pallas_call(body, out_shape=shapes, in_specs=in_specs or [VMEM] * len(...  12.6 us
    ppermute x9, starting transfers between devices, swap_near(): return lax.ppermute(x, 'gx', on_chip)  2.19 us
  transfers between devices with their start and end apart: 22, of which 10 were waited for; matrix products, arithmetic and copies ran while one was open for 0% of the time, Pallas kernels for 12%

profile of v4, /device:TPU:1, one launch (start us, length us, event | category | flops | bytes accessed | tf_op | source)
XLA Modules:
  0.0 77.2 jit_solution(15484552237877457407)
XLA Ops:
  0.7 1.3 %take.1 = (f32[2,64,512]{2,1,0:T(8,128)S(1)}, f32[2,64,512]{2,1,0:T(8,128)S(1)}, f32[2,128,512]{2,1,0:T(8,128)S(1)}) custom-call(s32[1]{0:T(128)} %bitcast.where, f32[2,2,128,512]{3,2,1,0:T(8,128)} %warm.1), custom_call_target="tpu_custom_call" | custom-call | bytes 2097156 | tf_op jit(solution)/shard_map/take/pallas_call | solution.py:57
  1.9 0.1 collective-permute-start.1
  2.1 2.6 %collective-permute-start.2 = (f32[2,64,512]{2,1,0:T(8,128)S(1)}, f32[2,64,512]{2,1,0:T(8,128)S(1)}, u32[]{:S(2)}, u32[]{:S(2)}) collective-permute-start(f32[2,64,512]{2,1,0:T(8,128)S(1)} %get-tuple-element.55.refs_1_), channel_id=1, source_target_pairs={{1,2},{3,4},{5,6},{7,8},{9,10},{11,12},{13,14},{17,18},{19,20},{21... | collective-permute-start | bytes 786440 | tf_op jit(solution)/shard_map/ppermute | solution.py:450
  4.7 0.1 collective-permute-start
  4.8 1.2 %copy-done.2 = f32[2,2,128,512]{3,2,1,0:T(8,128)S(1)} copy-done((f32[2,2,128,512]{3,2,1,0:T(8,128)S(1)}, f32[2,2,128,512]{3,2,1,0:T(8,128)}, u32[]{:S(2)}) %copy-start.2) | copy-done | bytes 1048600
  6.0 0.2 setup.1
  6.3 1.0 %part.3 = (f32[2,128,512]{2,1,0:T(8,128)S(1)}, f32[2,128,512]{2,1,0:T(8,128)S(1)}) custom-call(f32[2,64,512]{2,1,0:T(8,128)S(1)} %get-tuple-element.54.refs_0_, f32[2,64,512]{2,1,0:T(8,128)S(1)} %get-tuple-element.55.refs_1_, f32[2,128,512]{2,1,0:T(8,128)S(1)} %get-tuple-element.56.refs_2_, ...), custom_call_target="tpu_custom_call" | custom-call | bytes 3670016 | tf_op jit(solution)/shard_map/part/pallas_call | solution.py:57
  7.3 6.4 %collective-permute-done.2.halo = f32[2,64,512]{2,1,0:T(8,128)S(1)} collective-permute-done((f32[2,64,512]{2,1,0:T(8,128)S(1)}, f32[2,64,512]{2,1,0:T(8,128)S(1)}, u32[]{:S(2)}, u32[]{:S(2)}) %collective-permute-start.2) | collective-permute-done | bytes 262176 | tf_op jit(solution)/shard_map/ppermute | solution.py:450
  13.7 0.1 finish.4.refs_1_
  13.7 0.0 collective-permute-done.1.halo
  13.7 0.1 finish.5.refs_2_
  13.8 0.1 collective-permute-start.5
  13.9 2.5 %collective-permute-done.halo = f32[2,64,512]{2,1,0:T(8,128)S(1)} collective-permute-done((f32[2,64,512]{2,1,0:T(8,128)S(1)}, f32[2,64,512]{2,1,0:T(8,128)S(1)}, u32[]{:S(2)}, u32[]{:S(2)}) %collective-permute-start) | collective-permute-done | bytes 262176 | tf_op jit(solution)/shard_map/ppermute | solution.py:450
  16.5 0.1 finish.3.refs_0_
  16.5 2.5 %collective-permute-start.3 = (f32[2,64,512]{2,1,0:T(8,128)S(1)}, f32[2,64,512]{2,1,0:T(8,128)S(1)}, u32[]{:S(2)}, u32[]{:S(2)}) collective-permute-start(f32[2,64,512]{2,1,0:T(8,128)S(1)} %finish.3.refs_0_), channel_id=1, source_target_pairs={{1,2},{3,4},{5,6},{7,8},{9,10},{11,12},{13,14},{17,18},{19,20},{21... | collective-permute-start | bytes 786440 | tf_op jit(solution)/shard_map/ppermute | solution.py:450
  19.1 0.1 collective-permute-start.4
  19.2 1.0 %part.4 = (f32[2,128,512]{2,1,0:T(8,128)S(1)}, f32[2,128,512]{2,1,0:T(8,128)S(1)}) custom-call(f32[2,64,512]{2,1,0:T(8,128)S(1)} %finish.3.refs_0_, f32[2,64,512]{2,1,0:T(8,128)S(1)} %finish.4.refs_1_, f32[2,128,512]{2,1,0:T(8,128)S(1)} %finish.5.refs_2_, f32[2,128,512]{2,1,0:T(8,128)S(1)} %get-tuple-element.53.refs_3_.gain.refs_11_.refs_2_, ...), custom_call_target="tpu_custom_call" | custom-call | bytes 3670016 | tf_op jit(solution)/shard_map/part/pallas_call | solution.py:57
  20.2 0.1 matrices.1
  20.3 6.8 %collective-permute-done.3.halo = f32[2,64,512]{2,1,0:T(8,128)S(1)} collective-permute-done((f32[2,64,512]{2,1,0:T(8,128)S(1)}, f32[2,64,512]{2,1,0:T(8,128)S(1)}, u32[]{:S(2)}, u32[]{:S(2)}) %collective-permute-start.3) | collective-permute-done | bytes 262176 | tf_op jit(solution)/shard_map/ppermute | solution.py:450
  27.1 0.2 finish_pool.3
  27.3 4.0 %collective-permute-done.4.halo = f32[2,64,512]{2,1,0:T(8,128)S(1)} collective-permute-done((f32[2,64,512]{2,1,0:T(8,128)S(1)}, f32[2,64,512]{2,1,0:T(8,128)S(1)}, u32[]{:S(2)}, u32[]{:S(2)}) %collective-permute-start.4) | collective-permute-done | bytes 262176 | tf_op jit(solution)/shard_map/ppermute | solution.py:450
  31.3 0.2 finish_pool.4
  31.5 0.0 collective-permute-done.5.halo
  31.5 0.4 finish_pool.5
  31.9 2.5 %collective-permute-start.6 = (f32[2,64,256]{2,1,0:T(8,128)S(1)}, f32[2,64,256]{2,1,0:T(8,128)S(1)}, u32[]{:S(2)}, u32[]{:S(2)}) collective-permute-start(f32[2,64,256]{2,1,0:T(8,128)S(1)} %get-tuple-element.76), channel_id=1, source_target_pairs={{1,2},{3,4},{5,6},{7,8},{9,10},{11,12},{13,14},{17,18},{19,20},{21... | collective-permute-start | bytes 393224 | tf_op jit(solution)/shard_map/ppermute | solution.py:450
  34.5 0.0 collective-permute-start.7
  34.5 0.3 coarse_setup.1.gain
  34.7 0.5 three.1
  35.2 0.2 collective-permute-start.8
  35.4 1.6 %part_defect.1 = (f32[2,128,512]{2,1,0:T(8,128)S(1)}, f32[2,128,512]{2,1,0:T(8,128)S(1)}, f32[2,64,256]{2,1,0:T(8,128)S(1)}) custom-call(f32[2,64,512]{2,1,0:T(8,128)S(1)} %get-tuple-element.66.refs_0_, f32[2,64,512]{2,1,0:T(8,128)S(1)} %get-tuple-element.68.refs_1_, f32[2,128,512]{2,1,0:T(8,128)S(1)} %get-tuple-element.70.refs_2_, ...), custom_call_target="tpu_custom_call" | custom-call | bytes 3932160 | tf_op jit(solution)/shard_map/part_defect/pallas_call | solution.py:57
  37.0 0.1 collective-permute-done.6.far.refs_4_
  37.1 0.0 collective-permute-done.7.near
  37.2 1.9 %collective-permute-start.10 = (f32[2,64,256]{2,1,0:T(8,128)S(1)}, f32[2,64,256]{2,1,0:T(8,128)S(1)}, u32[]{:S(2)}, u32[]{:S(2)}) collective-permute-start(f32[2,64,256]{2,1,0:T(8,128)S(1)} %coarse_first.1.fix.own), channel_id=1, source_target_pairs={{0,1},{1,0},{2,3},{3,2},{4,5},{5,4},{6,7},{7,6},{8,9},{9,8},{10,11... | collective-permute-start | bytes 393224 | tf_op jit(solution)/shard_map/ppermute | solution.py:453
  39.1 1.3 %collective-permute-start.9 = (f32[2,64,256]{2,1,0:T(8,128)S(1)}, f32[2,64,256]{2,1,0:T(8,128)S(1)}, u32[]{:S(2)}, u32[]{:S(2)}) collective-permute-start(f32[2,64,256]{2,1,0:T(8,128)S(1)} %coarse_first.1.fix.own), channel_id=1, source_target_pairs={{1,2},{3,4},{5,6},{7,8},{9,10},{11,12},{13,14},{17,18},{19,20},{21... | collective-permute-start | bytes 393224 | tf_op jit(solution)/shard_map/ppermute | solution.py:450
  40.3 0.0 collective-permute-start.17
  40.3 0.2 coarse_part.3.part
  40.5 1.2 %collective-permute-start.11 = (f32[2,64,256]{2,1,0:T(8,128)S(1)}, f32[2,64,256]{2,1,0:T(8,128)S(1)}, u32[]{:S(2)}, u32[]{:S(2)}) collective-permute-start(f32[2,64,256]{2,1,0:T(8,128)S(1)} %get-tuple-element.86), channel_id=1, source_target_pairs={{1,2},{3,4},{5,6},{7,8},{9,10},{11,12},{13,14},{17,18},{19,20},{21... | collective-permute-start | bytes 393224 | tf_op jit(solution)/shard_map/ppermute | solution.py:450
  41.7 0.0 collective-permute-done.10.near
  41.7 2.1 %collective-permute-done.9.far = f32[2,64,256]{2,1,0:T(8,128)S(1)} collective-permute-done((f32[2,64,256]{2,1,0:T(8,128)S(1)}, f32[2,64,256]{2,1,0:T(8,128)S(1)}, u32[]{:S(2)}, u32[]{:S(2)}) %collective-permute-start.9) | collective-permute-done | bytes 131104 | tf_op jit(solution)/shard_map/ppermute | solution.py:450
  43.8 3.9 %collective-permute-start.12 = (f32[2,64,256]{2,1,0:T(8,128)S(1)}, f32[2,64,256]{2,1,0:T(8,128)S(1)}, u32[]{:S(2)}, u32[]{:S(2)}) collective-permute-start(f32[2,64,256]{2,1,0:T(8,128)S(1)} %coarse_finish.3.fix), channel_id=1, source_target_pairs={{1,2},{3,4},{5,6},{7,8},{9,10},{11,12},{13,14},{17,18},{19,20},{21... | collective-permute-start | bytes 393224 | tf_op jit(solution)/shard_map/ppermute | solution.py:450
  47.6 0.0 collective-permute-start.13
  47.6 0.2 coarse_part.4.part
  47.8 0.0 collective-permute-done.11.refs_6_
  47.8 1.1 %collective-permute-start.14 = (f32[2,64,256]{2,1,0:T(8,128)S(1)}, f32[2,64,256]{2,1,0:T(8,128)S(1)}, u32[]{:S(2)}, u32[]{:S(2)}) collective-permute-start(f32[2,64,256]{2,1,0:T(8,128)S(1)} %get-tuple-element.88), channel_id=1, source_target_pairs={{1,2},{3,4},{5,6},{7,8},{9,10},{11,12},{13,14},{17,18},{19,20},{21... | collective-permute-start | bytes 393224 | tf_op jit(solution)/shard_map/ppermute | solution.py:450
  48.9 1.4 %collective-permute-done.12.far = f32[2,64,256]{2,1,0:T(8,128)S(1)} collective-permute-done((f32[2,64,256]{2,1,0:T(8,128)S(1)}, f32[2,64,256]{2,1,0:T(8,128)S(1)}, u32[]{:S(2)}, u32[]{:S(2)}) %collective-permute-start.12) | collective-permute-done | bytes 131104 | tf_op jit(solution)/shard_map/ppermute | solution.py:450
  50.3 0.0 collective-permute-done.13.near
  50.4 4.0 %collective-permute-start.15 = (f32[2,64,256]{2,1,0:T(8,128)S(1)}, f32[2,64,256]{2,1,0:T(8,128)S(1)}, u32[]{:S(2)}, u32[]{:S(2)}) collective-permute-start(f32[2,64,256]{2,1,0:T(8,128)S(1)} %coarse_finish.4.fix), channel_id=1, source_target_pairs={{1,2},{3,4},{5,6},{7,8},{9,10},{11,12},{13,14},{17,18},{19,20},{21... | collective-permute-start | bytes 393224 | tf_op jit(solution)/shard_map/ppermute | solution.py:450
  54.3 0.0 collective-permute-start.16
  54.3 0.2 coarse_part.5.part
  54.5 2.5 %collective-permute-done.15.far = f32[2,64,256]{2,1,0:T(8,128)S(1)} collective-permute-done((f32[2,64,256]{2,1,0:T(8,128)S(1)}, f32[2,64,256]{2,1,0:T(8,128)S(1)}, u32[]{:S(2)}, u32[]{:S(2)}) %collective-permute-start.15) | collective-permute-done | bytes 131104 | tf_op jit(solution)/shard_map/ppermute | solution.py:450
  57.0 0.0 collective-permute-done.16.near
  57.0 1.8 %collective-permute-start.18 = (f32[2,64,256]{2,1,0:T(8,128)S(1)}, f32[2,64,256]{2,1,0:T(8,128)S(1)}, u32[]{:S(2)}, u32[]{:S(2)}) collective-permute-start(f32[2,64,256]{2,1,0:T(8,128)S(1)} %coarse_finish.5.refs_2_), channel_id=1, source_target_pairs={{1,2},{3,4},{5,6},{7,8},{9,10},{11,12},{13,14},{17,18},{19,20},{21... | collective-permute-start | bytes 393224 | tf_op jit(solution)/shard_map/ppermute | solution.py:450
  58.8 0.0 collective-permute-done.17.refs_3_
  58.8 1.3 %third.1 = (f32[2,128,512]{2,1,0:T(8,128)S(1)}, f32[2,128,512]{2,1,0:T(8,128)S(1)}) custom-call(f32[1]{0:T(128)} %bitcast.1.keep, f32[2,128,512]{2,1,0:T(8,128)S(1)} %get-tuple-element.71.refs_0_, f32[2,128,512]{2,1,0:T(8,128)S(1)} %get-tuple-element.72.refs_1_, f32[2,64,256]{2,1,0:T(8,128)S(1)} %coarse_finish.5.refs_2_, ...), custom_call_target="tpu_custom_call" | custom-call | bytes 4194308 | tf_op jit(solution)/shard_map/third/pallas_call | solution.py:57
  60.1 1.3 %collective-permute-done.18.far_halo = f32[2,64,256]{2,1,0:T(8,128)S(1)} collective-permute-done((f32[2,64,256]{2,1,0:T(8,128)S(1)}, f32[2,64,256]{2,1,0:T(8,128)S(1)}, u32[]{:S(2)}, u32[]{:S(2)}) %collective-permute-start.18) | collective-permute-done | bytes 131104 | tf_op jit(solution)/shard_map/ppermute | solution.py:450
  61.5 0.0 collective-permute-done.19.near_halo
  61.5 0.6 fix.1
  62.1 0.1 collective-permute-start.21
  62.1 0.0 copy-start.1
  62.2 2.4 %collective-permute-start.20 = (f32[2,128,512]{2,1,0:T(8,128)S(1)}, f32[2,128,512]{2,1,0:T(8,128)S(1)}, u32[]{:S(2)}, u32[]{:S(2)}) collective-permute-start(f32[2,128,512]{2,1,0:T(8,128)S(1)} %get-tuple-element.98.refs_0_), channel_id=1, source_target_pairs={{1,2},{3,4},{5,6},{7,8},{9,10},{11,12},{13,14},{17,18},{19,20},{21... | collective-permute-start | bytes 1572872 | tf_op jit(solution)/shard_map/ppermute | solution.py:450
  64.5 1.0 %part.5 = (f32[2,128,512]{2,1,0:T(8,128)S(1)}, f32[2,128,512]{2,1,0:T(8,128)S(1)}) custom-call(f32[2,128,512]{2,1,0:T(8,128)S(1)} %get-tuple-element.98.refs_0_, f32[2,128,512]{2,1,0:T(8,128)S(1)} %get-tuple-element.99.refs_1_, f32[2,128,512]{2,1,0:T(8,128)S(1)} %get-tuple-element.53.refs_3_.gain.refs_11_.refs_2_, ...), custom_call_target="tpu_custom_call" | custom-call | bytes 3670016 | tf_op jit(solution)/shard_map/part/pallas_call | solution.py:57
  65.6 1.0 %final.2 = (f32[2,2,128,512]{3,2,1,0:T(8,128)}, f32[2,128,512]{2,1,0:T(8,128)}) custom-call(s32[1]{0:T(128)} %bitcast.where, f32[1]{0:T(128)} %bitcast.1.keep, f32[2,128,512]{2,1,0:T(8,128)S(1)} %get-tuple-element.53.refs_3_.gain.refs_11_.refs_2_, f32[2,128,512]{2,1,0:T(8,128)S(1)} %copy-done, f32[2,128,512]{2,1,0:T(8,128)S(1)} %copy-done.1, ...), custom_call_target="tpu_custom_call" | custom-call | bytes 4194312 | tf_op jit(solution)/shard_map/final/pallas_call | solution.py:57
  66.5 9.7 %collective-permute-done.20.refs_1_ = f32[2,128,512]{2,1,0:T(8,128)S(1)} collective-permute-done((f32[2,128,512]{2,1,0:T(8,128)S(1)}, f32[2,128,512]{2,1,0:T(8,128)S(1)}, u32[]{:S(2)}, u32[]{:S(2)}) %collective-permute-start.20) | collective-permute-done | bytes 524320 | tf_op jit(solution)/shard_map/ppermute | solution.py:450
  76.3 1.0 %final.3 = (f32[2,2,128,512]{3,2,1,0:T(8,128)}, f32[2,128,512]{2,1,0:T(8,128)}) custom-call(s32[1]{0:T(128)} %bitcast.where, f32[1]{0:T(128)} %bitcast.1.keep, f32[2,128,512]{2,1,0:T(8,128)S(1)} %get-tuple-element.53.refs_3_.gain.refs_11_.refs_2_, f32[2,128,512]{2,1,0:T(8,128)S(1)} %copy-done, ...), custom_call_target="tpu_custom_call", output_to_operand_aliasing={{0}: (7, {}), {1}: (8, {})} | custom-call | bytes 5767176 | tf_op jit(solution)/shard_map/final/pallas_call | solution.py:57
  (12 shorter events, 0.2 us)
Async XLA Ops:
  0.6 4.2 %copy-start = (f32[2,128,512]{2,1,0:T(8,128)S(1)}, f32[2,128,512]{2,1,0:T(8,128)}, u32[]{:S(2)}) copy-start(f32[2,128,512]{2,1,0:T(8,128)} %phi.7) | copy-start | bytes 1572868
  1.9 11.8 %collective-permute-start.1 = (f32[2,128,512]{2,1,0:T(8,128)S(1)}, f32[2,128,512]{2,1,0:T(8,128)S(1)}, u32[]{:S(2)}, u32[]{:S(2)}) collective-permute-start(f32[2,128,512]{2,1,0:T(8,128)S(1)} %get-tuple-element.56.refs_2_), channel_id=1, source_target_pairs={{0,1},{1,0},{2,3},{3,2},{4,5},{5,4},{6,7},{7,6},{8,9},{9,8},{10,11... | collective-permute-start | bytes 1572872 | tf_op jit(solution)/shard_map/ppermute | solution.py:453
  2.1 11.6 %collective-permute-start.2 = (f32[2,64,512]{2,1,0:T(8,128)S(1)}, f32[2,64,512]{2,1,0:T(8,128)S(1)}, u32[]{:S(2)}, u32[]{:S(2)}) collective-permute-start(f32[2,64,512]{2,1,0:T(8,128)S(1)} %get-tuple-element.55.refs_1_), channel_id=1, source_target_pairs={{1,2},{3,4},{5,6},{7,8},{9,10},{11,12},{13,14},{17,18},{19,20},{21... | collective-permute-start | bytes 786440 | tf_op jit(solution)/shard_map/ppermute | solution.py:450
  4.7 11.7 %collective-permute-start = (f32[2,64,512]{2,1,0:T(8,128)S(1)}, f32[2,64,512]{2,1,0:T(8,128)S(1)}, u32[]{:S(2)}, u32[]{:S(2)}) collective-permute-start(f32[2,64,512]{2,1,0:T(8,128)S(1)} %get-tuple-element.54.refs_0_), channel_id=1, source_target_pairs={{1,2},{3,4},{5,6},{7,8},{9,10},{11,12},{13,14},{17,18},{19,20},{21... | collective-permute-start | bytes 786440 | tf_op jit(solution)/shard_map/ppermute | solution.py:450
  4.8 1.2 %copy-start.2 = (f32[2,2,128,512]{3,2,1,0:T(8,128)S(1)}, f32[2,2,128,512]{3,2,1,0:T(8,128)}, u32[]{:S(2)}) copy-start(f32[2,2,128,512]{3,2,1,0:T(8,128)} %cot.1) | copy-start | bytes 3145732
  13.8 17.7 %collective-permute-start.5 = (f32[2,128,512]{2,1,0:T(8,128)S(1)}, f32[2,128,512]{2,1,0:T(8,128)S(1)}, u32[]{:S(2)}, u32[]{:S(2)}) collective-permute-start(f32[2,128,512]{2,1,0:T(8,128)S(1)} %finish.5.refs_2_), channel_id=1, source_target_pairs={{0,1},{1,0},{2,3},{3,2},{4,5},{5,4},{6,7},{7,6},{8,9},{9,8},{10,11... | collective-permute-start | bytes 1572872 | tf_op jit(solution)/shard_map/ppermute | solution.py:453
  16.5 10.5 %collective-permute-start.3 = (f32[2,64,512]{2,1,0:T(8,128)S(1)}, f32[2,64,512]{2,1,0:T(8,128)S(1)}, u32[]{:S(2)}, u32[]{:S(2)}) collective-permute-start(f32[2,64,512]{2,1,0:T(8,128)S(1)} %finish.3.refs_0_), channel_id=1, source_target_pairs={{1,2},{3,4},{5,6},{7,8},{9,10},{11,12},{13,14},{17,18},{19,20},{21... | collective-permute-start | bytes 786440 | tf_op jit(solution)/shard_map/ppermute | solution.py:450
  19.1 12.2 %collective-permute-start.4 = (f32[2,64,512]{2,1,0:T(8,128)S(1)}, f32[2,64,512]{2,1,0:T(8,128)S(1)}, u32[]{:S(2)}, u32[]{:S(2)}) collective-permute-start(f32[2,64,512]{2,1,0:T(8,128)S(1)} %finish.4.refs_1_), channel_id=1, source_target_pairs={{1,2},{3,4},{5,6},{7,8},{9,10},{11,12},{13,14},{17,18},{19,20},{21... | collective-permute-start | bytes 786440 | tf_op jit(solution)/shard_map/ppermute | solution.py:450
  31.9 5.2 %collective-permute-start.6 = (f32[2,64,256]{2,1,0:T(8,128)S(1)}, f32[2,64,256]{2,1,0:T(8,128)S(1)}, u32[]{:S(2)}, u32[]{:S(2)}) collective-permute-start(f32[2,64,256]{2,1,0:T(8,128)S(1)} %get-tuple-element.76), channel_id=1, source_target_pairs={{1,2},{3,4},{5,6},{7,8},{9,10},{11,12},{13,14},{17,18},{19,20},{21... | collective-permute-start | bytes 393224 | tf_op jit(solution)/shard_map/ppermute | solution.py:450
  34.5 2.7 %collective-permute-start.7 = (f32[2,64,256]{2,1,0:T(8,128)S(1)}, f32[2,64,256]{2,1,0:T(8,128)S(1)}, u32[]{:S(2)}, u32[]{:S(2)}) collective-permute-start(f32[2,64,256]{2,1,0:T(8,128)S(1)} %get-tuple-element.77), channel_id=1, source_target_pairs={{0,1},{1,0},{2,3},{3,2},{4,5},{5,4},{6,7},{7,6},{8,9},{9,8},{10,11... | collective-permute-start | bytes 393224 | tf_op jit(solution)/shard_map/ppermute | solution.py:453
  35.2 5.3 %collective-permute-start.8 = (f32[2,64,256]{2,1,0:T(8,128)S(1)}, f32[2,64,256]{2,1,0:T(8,128)S(1)}, u32[]{:S(2)}, u32[]{:S(2)}) collective-permute-start(f32[2,64,256]{2,1,0:T(8,128)S(1)} %get-tuple-element.82), channel_id=1, source_target_pairs={{1,2},{3,4},{5,6},{7,8},{9,10},{11,12},{13,14},{17,18},{19,20},{21... | collective-permute-start | bytes 393224 | tf_op jit(solution)/shard_map/ppermute | solution.py:450
  37.2 4.5 %collective-permute-start.10 = (f32[2,64,256]{2,1,0:T(8,128)S(1)}, f32[2,64,256]{2,1,0:T(8,128)S(1)}, u32[]{:S(2)}, u32[]{:S(2)}) collective-permute-start(f32[2,64,256]{2,1,0:T(8,128)S(1)} %coarse_first.1.fix.own), channel_id=1, source_target_pairs={{0,1},{1,0},{2,3},{3,2},{4,5},{5,4},{6,7},{7,6},{8,9},{9,8},{10,11... | collective-permute-start | bytes 393224 | tf_op jit(solution)/shard_map/ppermute | solution.py:453
  39.1 4.7 %collective-permute-start.9 = (f32[2,64,256]{2,1,0:T(8,128)S(1)}, f32[2,64,256]{2,1,0:T(8,128)S(1)}, u32[]{:S(2)}, u32[]{:S(2)}) collective-permute-start(f32[2,64,256]{2,1,0:T(8,128)S(1)} %coarse_first.1.fix.own), channel_id=1, source_target_pairs={{1,2},{3,4},{5,6},{7,8},{9,10},{11,12},{13,14},{17,18},{19,20},{21... | collective-permute-start | bytes 393224 | tf_op jit(solution)/shard_map/ppermute | solution.py:450
  40.3 18.5 %collective-permute-start.17 = (f32[2,128,512]{2,1,0:T(8,128)S(1)}, f32[2,128,512]{2,1,0:T(8,128)S(1)}, u32[]{:S(2)}, u32[]{:S(2)}) collective-permute-start(f32[2,128,512]{2,1,0:T(8,128)S(1)} %get-tuple-element.70.refs_2_), channel_id=1, source_target_pairs={{0,1},{1,0},{2,3},{3,2},{4,5},{5,4},{6,7},{7,6},{8,9},{9,8},{10,11... | collective-permute-start | bytes 1572872 | tf_op jit(solution)/shard_map/ppermute | solution.py:453
  40.5 7.3 %collective-permute-start.11 = (f32[2,64,256]{2,1,0:T(8,128)S(1)}, f32[2,64,256]{2,1,0:T(8,128)S(1)}, u32[]{:S(2)}, u32[]{:S(2)}) collective-permute-start(f32[2,64,256]{2,1,0:T(8,128)S(1)} %get-tuple-element.86), channel_id=1, source_target_pairs={{1,2},{3,4},{5,6},{7,8},{9,10},{11,12},{13,14},{17,18},{19,20},{21... | collective-permute-start | bytes 393224 | tf_op jit(solution)/shard_map/ppermute | solution.py:450
  43.8 6.5 %collective-permute-start.12 = (f32[2,64,256]{2,1,0:T(8,128)S(1)}, f32[2,64,256]{2,1,0:T(8,128)S(1)}, u32[]{:S(2)}, u32[]{:S(2)}) collective-permute-start(f32[2,64,256]{2,1,0:T(8,128)S(1)} %coarse_finish.3.fix), channel_id=1, source_target_pairs={{1,2},{3,4},{5,6},{7,8},{9,10},{11,12},{13,14},{17,18},{19,20},{21... | collective-permute-start | bytes 393224 | tf_op jit(solution)/shard_map/ppermute | solution.py:450
  47.6 2.7 %collective-permute-start.13 = (f32[2,64,256]{2,1,0:T(8,128)S(1)}, f32[2,64,256]{2,1,0:T(8,128)S(1)}, u32[]{:S(2)}, u32[]{:S(2)}) collective-permute-start(f32[2,64,256]{2,1,0:T(8,128)S(1)} %coarse_finish.3.fix), channel_id=1, source_target_pairs={{0,1},{1,0},{2,3},{3,2},{4,5},{5,4},{6,7},{7,6},{8,9},{9,8},{10,11... | collective-permute-start | bytes 393224 | tf_op jit(solution)/shard_map/ppermute | solution.py:453
  47.8 6.7 %collective-permute-start.14 = (f32[2,64,256]{2,1,0:T(8,128)S(1)}, f32[2,64,256]{2,1,0:T(8,128)S(1)}, u32[]{:S(2)}, u32[]{:S(2)}) collective-permute-start(f32[2,64,256]{2,1,0:T(8,128)S(1)} %get-tuple-element.88), channel_id=1, source_target_pairs={{1,2},{3,4},{5,6},{7,8},{9,10},{11,12},{13,14},{17,18},{19,20},{21... | collective-permute-start | bytes 393224 | tf_op jit(solution)/shard_map/ppermute | solution.py:450
  50.4 6.6 %collective-permute-start.15 = (f32[2,64,256]{2,1,0:T(8,128)S(1)}, f32[2,64,256]{2,1,0:T(8,128)S(1)}, u32[]{:S(2)}, u32[]{:S(2)}) collective-permute-start(f32[2,64,256]{2,1,0:T(8,128)S(1)} %coarse_finish.4.fix), channel_id=1, source_target_pairs={{1,2},{3,4},{5,6},{7,8},{9,10},{11,12},{13,14},{17,18},{19,20},{21... | collective-permute-start | bytes 393224 | tf_op jit(solution)/shard_map/ppermute | solution.py:450
  54.3 2.7 %collective-permute-start.16 = (f32[2,64,256]{2,1,0:T(8,128)S(1)}, f32[2,64,256]{2,1,0:T(8,128)S(1)}, u32[]{:S(2)}, u32[]{:S(2)}) collective-permute-start(f32[2,64,256]{2,1,0:T(8,128)S(1)} %coarse_finish.4.fix), channel_id=1, source_target_pairs={{0,1},{1,0},{2,3},{3,2},{4,5},{5,4},{6,7},{7,6},{8,9},{9,8},{10,11... | collective-permute-start | bytes 393224 | tf_op jit(solution)/shard_map/ppermute | solution.py:453
  57.0 4.5 %collective-permute-start.18 = (f32[2,64,256]{2,1,0:T(8,128)S(1)}, f32[2,64,256]{2,1,0:T(8,128)S(1)}, u32[]{:S(2)}, u32[]{:S(2)}) collective-permute-start(f32[2,64,256]{2,1,0:T(8,128)S(1)} %coarse_finish.5.refs_2_), channel_id=1, source_target_pairs={{1,2},{3,4},{5,6},{7,8},{9,10},{11,12},{13,14},{17,18},{19,20},{21... | collective-permute-start | bytes 393224 | tf_op jit(solution)/shard_map/ppermute | solution.py:450
  58.8 2.7 %collective-permute-start.19 = (f32[2,64,256]{2,1,0:T(8,128)S(1)}, f32[2,64,256]{2,1,0:T(8,128)S(1)}, u32[]{:S(2)}, u32[]{:S(2)}) collective-permute-start(f32[2,64,256]{2,1,0:T(8,128)S(1)} %coarse_finish.5.refs_2_), channel_id=1, source_target_pairs={{0,1},{1,0},{2,3},{3,2},{4,5},{5,4},{6,7},{7,6},{8,9},{9,8},{10,11... | collective-permute-start | bytes 393224 | tf_op jit(solution)/shard_map/ppermute | solution.py:453
  62.1 3.5 %collective-permute-start.21 = (f32[2,128,512]{2,1,0:T(8,128)S(1)}, f32[2,128,512]{2,1,0:T(8,128)S(1)}, u32[]{:S(2)}, u32[]{:S(2)}) collective-permute-start(f32[2,128,512]{2,1,0:T(8,128)S(1)} %get-tuple-element.99.refs_1_), channel_id=1, source_target_pairs={{0,1},{1,0},{2,3},{3,2},{4,5},{5,4},{6,7},{7,6},{8,9},{9,8},{10,11... | collective-permute-start | bytes 1572872 | tf_op jit(solution)/shard_map/ppermute | solution.py:453
  62.1 3.4 %copy-start.1 = (f32[2,128,512]{2,1,0:T(8,128)S(1)}, f32[2,128,512]{2,1,0:T(8,128)}, u32[]{:S(2)}) copy-start(f32[2,128,512]{2,1,0:T(8,128)} %psi.3) | copy-start | bytes 1572868
  62.2 14.1 %collective-permute-start.20 = (f32[2,128,512]{2,1,0:T(8,128)S(1)}, f32[2,128,512]{2,1,0:T(8,128)S(1)}, u32[]{:S(2)}, u32[]{:S(2)}) collective-permute-start(f32[2,128,512]{2,1,0:T(8,128)S(1)} %get-tuple-element.98.refs_0_), channel_id=1, source_target_pairs={{1,2},{3,4},{5,6},{7,8},{9,10},{11,12},{13,14},{17,18},{19,20},{21... | collective-permute-start | bytes 1572872 | tf_op jit(solution)/shard_map/ppermute | solution.py:450

commit v5 on v4

--- a/solution.py
+++ b/solution.py
@@ -334,21 +334,9 @@
             put_rows(tile, rows, wide)
 
 
-def third_body(count, keep, *refs):
-    far, near, fix, near_halo, sums = refs[:5]
-    pieces, refs = refs[5 : 5 + count], refs[5 + count :]
-    pair_t, even_t, odd_t, gain, far_out, near_out, fix_p, fix_m, halo_p, halo_m, wide_p, wide_m = refs
+def third_body(far, near, fix, near_halo, pair_t, gain, far_out, near_out, fix_p, fix_m, wide_p, wide_m):
     rows_all = near.shape[1]
-    half = rows_all // 2
     spread_into(fix_p, fix_m, fix[0], fix[1], pair_t[...])
-    for f, tile in enumerate((halo_p, halo_m)):
-        values = jnp.concatenate([piece[f] for piece in pieces], axis=0)
-        a, b, c = values[:half], values[half : 2 * half], values[2 * half :]
-        d = sums[f] - ((a + b) + c)
-        even, odd = even_odd(tile)
-        (a, c), (b, d) = times([a, c], even_t[...]), times([b, d], odd_t[...])
-        put_rows(tile, even, a + b)
-        put_rows(tile, odd, c + d)
     for r in blocks(rows_all):
         rows = slice(r, r + BLOCK)
         wide_p[rows], wide_m[rows] = get_rows(fix_p, rows), get_rows(fix_m, rows)
@@ -357,10 +345,8 @@
         p, nb_p = around(lambda lo, hi: wide_p[lo:hi], r, rows_all)
         m, nb_m = around(lambda lo, hi: wide_m[lo:hi], r, rows_all)
         nb_p, nb_m = nb_p + p, nb_m + m
-        hp, hm = get_rows(halo_p, rows) * keep[0], get_rows(halo_m, rows) * keep[0]
-        for i, (part, out, xp, xm) in enumerate(
-            ((far, far_out, hp, hm), (near, near_out, near_halo[0, rows], near_halo[1, rows]))
-        ):
+        for i, (part, out) in enumerate(((far, far_out), (near, near_out))):
+            xp, xm = (near_halo[0, rows], near_halo[1, rows]) if i == 1 else (0.0, 0.0)
             out[0, rows], out[1, rows] = add_terms(
                 part[0, rows] + KEEP * p,
                 part[1, rows] + KEEP * m,
@@ -372,7 +358,23 @@
             )
 
 
-def finish_fix_rows(i, lo, keep, part, halo, pair_t, gain, out, phase, chem):
+def rebuild_body(sums, *refs):
+    pieces, (even_t, odd_t, out, halo_p, halo_m) = refs[:-5], refs[-5:]
+    half = sums.shape[1]
+    for f, tile in enumerate((halo_p, halo_m)):
+        values = jnp.concatenate([piece[f] for piece in pieces], axis=0)
+        a, b, c = values[:half], values[half : 2 * half], values[2 * half :]
+        d = sums[f] - ((a + b) + c)
+        even, odd = even_odd(tile)
+        (a, c), (b, d) = times([a, c], even_t[...]), times([b, d], odd_t[...])
+        put_rows(tile, even, a + b)
+        put_rows(tile, odd, c + d)
+        for r in blocks(2 * half):
+            rows = slice(r, r + BLOCK)
+            out[f, rows] = get_rows(tile, rows)
+
+
+def finish_fix_rows(i, lo, keep, part, halo, pair_t, gain, out, phase, chem, state_nb=None):
     n = out.shape[1]
     coarse = slice(lo // 2, (lo + n) // 2)
     spread_into(phase, chem, halo[0, coarse], halo[1, coarse], pair_t[...])
@@ -380,17 +382,17 @@
         rows, whole = slice(r, r + BLOCK), slice(lo + r, lo + r + BLOCK)
         hp, hm = get_rows(phase, rows), get_rows(chem, rows)
         if i == 0:
-            hp, hm = hp * keep[0], hm * keep[0]
+            hp, hm = (hp + state_nb[0, whole]) * keep[0], (hm + state_nb[1, whole]) * keep[0]
         out[0, rows], out[1, rows] = add_terms(
             part[0, whole], part[1, whole], gain[i, whole], hp, hm, GRADIENT_ENERGY, TIME_STEP
         )
 
 
-def fix_body(starts, keep, far_part, near_part, far_halo, near_halo, pair_t, gain, *refs):
+def fix_body(starts, keep, far_part, near_part, far_halo, near_halo, state_nb, pair_t, gain, *refs):
     count = len(starts)
     outs, scratch = refs[: count + 1], refs[count + 1 :]
     for n, (lo, out) in enumerate(zip(starts, outs)):
-        finish_fix_rows(0, lo, keep, far_part, far_halo, pair_t, gain, out, *scratch[2 * n : 2 * n + 2])
+        finish_fix_rows(0, lo, keep, far_part, far_halo, pair_t, gain, out, *scratch[2 * n : 2 * n + 2], state_nb)
     finish_fix_rows(1, 0, keep, near_part, near_halo, pair_t, gain, outs[-1], *scratch[-2:])
 
 
@@ -504,7 +506,6 @@
         far.append(chunk)
         before = (far_pool,)
     near_pool, near = finish_pool(1, 0, near_part, near_halo)
-    near_pool, far_pool = after(near_pool, far_pool)
 
     far_sums, near_sums = swap_far(far_pool), swap_near(near_pool)
     plane_sums = far_sums
@@ -525,17 +526,21 @@
             fix, held = lax.optimization_barrier((fix, pieces[len(arrived)]))
             arrived.append(swap_far(held))
         part = run(coarse_part_body, "coarse_part", [half], (fix, first, *coarse))[0]
-        part, arrived[sweep_index] = after(part, arrived[sweep_index])
+        if sweep_index:
+            part, arrived[sweep_index - 1] = after(part, arrived[sweep_index - 1])
         args = (keep, part, far_sums, near_sums, *coarse)
         fix = run(coarse_finish_body, "coarse_finish", [half], args, smem=1, work=8)[0]
 
     far_sums, near_sums = swap_far(fix), swap_near(fix)
-    args = (keep, far_part, near_part, fix, near_halo, plane_sums, *arrived, pair_t, even_t, odd_t, *coefs)
-    scratch = [tile] * 4 + [pltpu.VMEM((rows, cols), F32)] * 2
-    far_part, near_part = run(third_body, "third", [full, full], args, (len(arrived),), smem=1, scratch=scratch)
+    args = (far_part, near_part, fix, near_halo, pair_t, *coefs)
+    scratch = [tile] * 2 + [pltpu.VMEM((rows, cols), F32)] * 2
+    far_part, near_part = run(third_body, "third", [full, full], args, scratch=scratch)
+    plane_sums, far_part = after(plane_sums, far_part)
+    state_nb = run(rebuild_body, "rebuild", [full], (plane_sums, *arrived, even_t, odd_t), scratch=[tile] * 2)[0]
     sizes = late_chunks(rows)
     starts = [sum(sizes[:n]) for n in range(len(sizes))]
-    args, shapes = (keep, far_part, near_part, far_sums, near_sums, pair_t, *coefs), [(2, n, cols) for n in sizes]
+    args = (keep, far_part, near_part, far_sums, near_sums, state_nb, pair_t, *coefs)
+    shapes = [(2, n, cols) for n in sizes]
     scratch = [v for n in [*sizes, rows] for v in [tiles(n, cols)] * 2]
     *far, near = run(fix_body, "fix", [*shapes, full], args, (starts,), smem=1, scratch=scratch, work=8)
 

time: 77.4 us -> 75.3 us (0.973)
  starting transfers between devices: 25.8 us -> 23.8 us
    ppermute x9, starting transfers between devices: 2.19 us -> 0.91 us  [swap_near(): return lax.ppermute(x, 'gx', on_chip)]
    pallas_call x26 -> x27, Pallas kernels: 12.6 us -> 12.5 us  [call(): pl.pallas_call(body, out_shape=shapes, in_specs=in_specs or [VMEM] * len(...]
  transfers between devices with their start and end apart: 22 -> 22, of which waited for: 10 -> 9; matrix products, arithmetic and copies ran while one was open for 0% -> 0% of each run, Pallas kernels for 12% -> 13%
where the time goes in v5:
time: 75.3 us; the launch traced here: 74.9 us
  waiting for transfers between devices  36.4 us (48%)
  starting transfers between devices  23.8 us (32%)
  Pallas kernels  12.5 us (17%)
  local copies, waits for them, and re-layouts  1.24 us (2%)
  between operations  0.91 us (1%)
    ppermute x13, waiting for transfers between devices, swap_far(): return lax.ppermute(x, ('grp', 'gx'), across)  36.4 us
    ppermute x13, starting transfers between devices, swap_far(): return lax.ppermute(x, ('grp', 'gx'), across)  22.8 us
    pallas_call x27, Pallas kernels, call(): pl.pallas_call(body, out_shape=shapes, in_specs=in_specs or [VMEM] * len(...  12.5 us
  transfers between devices with their start and end apart: 22, of which 9 were waited for; matrix products, arithmetic and copies ran while one was open for 0% of the time, Pallas kernels for 13%

profile of v5, /device:TPU:1, one launch (start us, length us, event | category | flops | bytes accessed | tf_op | source)
XLA Modules:
  0.0 74.9 jit_solution(429004380169443092)
XLA Ops:
  0.7 1.3 %take.1 = (f32[2,64,512]{2,1,0:T(8,128)S(1)}, f32[2,64,512]{2,1,0:T(8,128)S(1)}, f32[2,128,512]{2,1,0:T(8,128)S(1)}) custom-call(s32[1]{0:T(128)} %bitcast.where, f32[2,2,128,512]{3,2,1,0:T(8,128)} %warm.1), custom_call_target="tpu_custom_call" | custom-call | bytes 2097156 | tf_op jit(solution)/shard_map/take/pallas_call | solution.py:57
  1.9 0.1 collective-permute-start.1
  2.1 2.6 %collective-permute-start.2 = (f32[2,64,512]{2,1,0:T(8,128)S(1)}, f32[2,64,512]{2,1,0:T(8,128)S(1)}, u32[]{:S(2)}, u32[]{:S(2)}) collective-permute-start(f32[2,64,512]{2,1,0:T(8,128)S(1)} %get-tuple-element.53.refs_1_), channel_id=1, source_target_pairs={{1,2},{3,4},{5,6},{7,8},{9,10},{11,12},{13,14},{17,18},{19,20},{21... | collective-permute-start | bytes 786440 | tf_op jit(solution)/shard_map/ppermute | solution.py:452
  4.7 0.1 collective-permute-start
  4.8 1.2 %copy-done.2 = f32[2,2,128,512]{3,2,1,0:T(8,128)S(1)} copy-done((f32[2,2,128,512]{3,2,1,0:T(8,128)S(1)}, f32[2,2,128,512]{3,2,1,0:T(8,128)}, u32[]{:S(2)}) %copy-start.2) | copy-done | bytes 1048600
  6.0 0.2 setup.1
  6.3 0.9 %part.3 = (f32[2,128,512]{2,1,0:T(8,128)S(1)}, f32[2,128,512]{2,1,0:T(8,128)S(1)}) custom-call(f32[2,64,512]{2,1,0:T(8,128)S(1)} %get-tuple-element.52.refs_0_, f32[2,64,512]{2,1,0:T(8,128)S(1)} %get-tuple-element.53.refs_1_, f32[2,128,512]{2,1,0:T(8,128)S(1)} %get-tuple-element.54.refs_2_, f32[2,128,512]{2,1,0:T(8,128)S(1)} %get-tuple-element.51.refs_3_.gain.refs_2_, ...), custom_call_target="tpu_custom_call" | custom-call | bytes 3670016 | tf_op jit(solution)/shard_map/part/pallas_call | solution.py:57
  7.2 6.4 %collective-permute-done.2.halo = f32[2,64,512]{2,1,0:T(8,128)S(1)} collective-permute-done((f32[2,64,512]{2,1,0:T(8,128)S(1)}, f32[2,64,512]{2,1,0:T(8,128)S(1)}, u32[]{:S(2)}, u32[]{:S(2)}) %collective-permute-start.2) | collective-permute-done | bytes 262176 | tf_op jit(solution)/shard_map/ppermute | solution.py:452
  13.7 0.1 finish.4.refs_1_
  13.7 0.0 collective-permute-done.1.halo
  13.7 0.1 finish.5.refs_2_
  13.8 0.1 collective-permute-start.6
  13.9 2.5 %collective-permute-done.halo = f32[2,64,512]{2,1,0:T(8,128)S(1)} collective-permute-done((f32[2,64,512]{2,1,0:T(8,128)S(1)}, f32[2,64,512]{2,1,0:T(8,128)S(1)}, u32[]{:S(2)}, u32[]{:S(2)}) %collective-permute-start) | collective-permute-done | bytes 262176 | tf_op jit(solution)/shard_map/ppermute | solution.py:452
  16.5 0.1 finish.3.refs_0_
  16.5 2.5 %collective-permute-start.4 = (f32[2,64,512]{2,1,0:T(8,128)S(1)}, f32[2,64,512]{2,1,0:T(8,128)S(1)}, u32[]{:S(2)}, u32[]{:S(2)}) collective-permute-start(f32[2,64,512]{2,1,0:T(8,128)S(1)} %finish.3.refs_0_), channel_id=1, source_target_pairs={{1,2},{3,4},{5,6},{7,8},{9,10},{11,12},{13,14},{17,18},{19,20},{21... | collective-permute-start | bytes 786440 | tf_op jit(solution)/shard_map/ppermute | solution.py:452
  19.1 0.1 collective-permute-start.3
  19.1 0.9 %part.4 = (f32[2,128,512]{2,1,0:T(8,128)S(1)}, f32[2,128,512]{2,1,0:T(8,128)S(1)}) custom-call(f32[2,64,512]{2,1,0:T(8,128)S(1)} %finish.3.refs_0_, f32[2,64,512]{2,1,0:T(8,128)S(1)} %finish.4.refs_1_, f32[2,128,512]{2,1,0:T(8,128)S(1)} %finish.5.refs_2_, f32[2,128,512]{2,1,0:T(8,128)S(1)} %get-tuple-element.51.refs_3_.gain.refs_2_, ...), custom_call_target="tpu_custom_call" | custom-call | bytes 3670016 | tf_op jit(solution)/shard_map/part/pallas_call | solution.py:57
  20.1 0.1 matrices.1
  20.2 6.9 %collective-permute-done.4.halo = f32[2,64,512]{2,1,0:T(8,128)S(1)} collective-permute-done((f32[2,64,512]{2,1,0:T(8,128)S(1)}, f32[2,64,512]{2,1,0:T(8,128)S(1)}, u32[]{:S(2)}, u32[]{:S(2)}) %collective-permute-start.4) | collective-permute-done | bytes 262176 | tf_op jit(solution)/shard_map/ppermute | solution.py:452
  27.0 0.2 finish_pool.3
  27.3 4.0 %collective-permute-done.3.halo = f32[2,64,512]{2,1,0:T(8,128)S(1)} collective-permute-done((f32[2,64,512]{2,1,0:T(8,128)S(1)}, f32[2,64,512]{2,1,0:T(8,128)S(1)}, u32[]{:S(2)}, u32[]{:S(2)}) %collective-permute-start.3) | collective-permute-done | bytes 262176 | tf_op jit(solution)/shard_map/ppermute | solution.py:452
  31.2 0.2 finish_pool.4
  31.5 2.5 %collective-permute-start.5 = (f32[2,64,256]{2,1,0:T(8,128)S(1)}, f32[2,64,256]{2,1,0:T(8,128)S(1)}, u32[]{:S(2)}, u32[]{:S(2)}) collective-permute-start(f32[2,64,256]{2,1,0:T(8,128)S(1)} %get-tuple-element.65), channel_id=1, source_target_pairs={{1,2},{3,4},{5,6},{7,8},{9,10},{11,12},{13,14},{17,18},{19,20},{21... | collective-permute-start | bytes 393224 | tf_op jit(solution)/shard_map/ppermute | solution.py:452
  34.0 0.4 finish_pool.5
  34.4 0.1 collective-permute-start.7
  34.5 0.3 coarse_setup.1.gain
  34.7 0.6 collective-permute-start.16
  35.3 1.5 %part_defect.1 = (f32[2,128,512]{2,1,0:T(8,128)S(1)}, f32[2,128,512]{2,1,0:T(8,128)S(1)}, f32[2,64,256]{2,1,0:T(8,128)S(1)}) custom-call(f32[2,64,512]{2,1,0:T(8,128)S(1)} %get-tuple-element.66.refs_0_, f32[2,64,512]{2,1,0:T(8,128)S(1)} %get-tuple-element.67.refs_1_, f32[2,128,512]{2,1,0:T(8,128)S(1)} %get-tuple-element.69.refs_2_, ...), custom_call_target="tpu_custom_call" | custom-call | bytes 3932160 | tf_op jit(solution)/shard_map/part_defect/pallas_call | solution.py:57
  36.8 0.0 collective-permute-done.5.far.sums
  36.8 0.0 collective-permute-done.7.near
  36.9 1.6 %collective-permute-start.8 = (f32[2,64,256]{2,1,0:T(8,128)S(1)}, f32[2,64,256]{2,1,0:T(8,128)S(1)}, u32[]{:S(2)}, u32[]{:S(2)}) collective-permute-start(f32[2,64,256]{2,1,0:T(8,128)S(1)} %coarse_first.1.fix.own), channel_id=1, source_target_pairs={{1,2},{3,4},{5,6},{7,8},{9,10},{11,12},{13,14},{17,18},{19,20},{21... | collective-permute-start | bytes 393224 | tf_op jit(solution)/shard_map/ppermute | solution.py:452
  38.5 0.0 collective-permute-start.9
  38.5 0.5 three.1
  39.0 1.3 %collective-permute-start.10 = (f32[2,64,256]{2,1,0:T(8,128)S(1)}, f32[2,64,256]{2,1,0:T(8,128)S(1)}, u32[]{:S(2)}, u32[]{:S(2)}) collective-permute-start(f32[2,64,256]{2,1,0:T(8,128)S(1)} %get-tuple-element.80), channel_id=1, source_target_pairs={{1,2},{3,4},{5,6},{7,8},{9,10},{11,12},{13,14},{17,18},{19,20},{21... | collective-permute-start | bytes 393224 | tf_op jit(solution)/shard_map/ppermute | solution.py:452
  40.3 0.1 coarse_part.3.part
  40.4 1.1 %collective-permute-done.8.far = f32[2,64,256]{2,1,0:T(8,128)S(1)} collective-permute-done((f32[2,64,256]{2,1,0:T(8,128)S(1)}, f32[2,64,256]{2,1,0:T(8,128)S(1)}, u32[]{:S(2)}, u32[]{:S(2)}) %collective-permute-start.8) | collective-permute-done | bytes 131104 | tf_op jit(solution)/shard_map/ppermute | solution.py:452
  41.5 0.0 collective-permute-done.9.near
  41.6 2.5 %collective-permute-start.11 = (f32[2,64,256]{2,1,0:T(8,128)S(1)}, f32[2,64,256]{2,1,0:T(8,128)S(1)}, u32[]{:S(2)}, u32[]{:S(2)}) collective-permute-start(f32[2,64,256]{2,1,0:T(8,128)S(1)} %coarse_finish.3.fix), channel_id=1, source_target_pairs={{1,2},{3,4},{5,6},{7,8},{9,10},{11,12},{13,14},{17,18},{19,20},{21... | collective-permute-start | bytes 393224 | tf_op jit(solution)/shard_map/ppermute | solution.py:452
  44.1 0.0 collective-permute-start.12
  44.1 1.2 %collective-permute-start.13 = (f32[2,64,256]{2,1,0:T(8,128)S(1)}, f32[2,64,256]{2,1,0:T(8,128)S(1)}, u32[]{:S(2)}, u32[]{:S(2)}) collective-permute-start(f32[2,64,256]{2,1,0:T(8,128)S(1)} %get-tuple-element.82), channel_id=1, source_target_pairs={{1,2},{3,4},{5,6},{7,8},{9,10},{11,12},{13,14},{17,18},{19,20},{21... | collective-permute-start | bytes 393224 | tf_op jit(solution)/shard_map/ppermute | solution.py:452
  45.3 0.2 coarse_part.4.part
  45.4 1.7 %collective-permute-done.11.far = f32[2,64,256]{2,1,0:T(8,128)S(1)} collective-permute-done((f32[2,64,256]{2,1,0:T(8,128)S(1)}, f32[2,64,256]{2,1,0:T(8,128)S(1)}, u32[]{:S(2)}, u32[]{:S(2)}) %collective-permute-start.11) | collective-permute-done | bytes 131104 | tf_op jit(solution)/shard_map/ppermute | solution.py:452
  47.1 0.0 collective-permute-done.12.near
  47.2 3.9 %collective-permute-start.14 = (f32[2,64,256]{2,1,0:T(8,128)S(1)}, f32[2,64,256]{2,1,0:T(8,128)S(1)}, u32[]{:S(2)}, u32[]{:S(2)}) collective-permute-start(f32[2,64,256]{2,1,0:T(8,128)S(1)} %coarse_finish.4.fix), channel_id=1, source_target_pairs={{1,2},{3,4},{5,6},{7,8},{9,10},{11,12},{13,14},{17,18},{19,20},{21... | collective-permute-start | bytes 393224 | tf_op jit(solution)/shard_map/ppermute | solution.py:452
  51.1 0.0 collective-permute-start.15
  51.1 0.2 collective-permute-start.19
  51.3 0.2 coarse_part.5.part
  51.4 0.0 collective-permute-done.13.refs_1_
  51.4 2.3 %collective-permute-done.14.far = f32[2,64,256]{2,1,0:T(8,128)S(1)} collective-permute-done((f32[2,64,256]{2,1,0:T(8,128)S(1)}, f32[2,64,256]{2,1,0:T(8,128)S(1)}, u32[]{:S(2)}, u32[]{:S(2)}) %collective-permute-start.14) | collective-permute-done | bytes 131104 | tf_op jit(solution)/shard_map/ppermute | solution.py:452
  53.8 0.0 collective-permute-done.15.near
  53.8 1.8 %collective-permute-start.17 = (f32[2,64,256]{2,1,0:T(8,128)S(1)}, f32[2,64,256]{2,1,0:T(8,128)S(1)}, u32[]{:S(2)}, u32[]{:S(2)}) collective-permute-start(f32[2,64,256]{2,1,0:T(8,128)S(1)} %coarse_finish.5.fix), channel_id=1, source_target_pairs={{1,2},{3,4},{5,6},{7,8},{9,10},{11,12},{13,14},{17,18},{19,20},{21... | collective-permute-start | bytes 393224 | tf_op jit(solution)/shard_map/ppermute | solution.py:452
  55.6 0.0 collective-permute-done.16.near_halo
  55.6 1.1 %third.1 = (f32[2,128,512]{2,1,0:T(8,128)S(1)}, f32[2,128,512]{2,1,0:T(8,128)S(1)}) custom-call(f32[2,128,512]{2,1,0:T(8,128)S(1)} %get-tuple-element.70.far, f32[2,128,512]{2,1,0:T(8,128)S(1)} %get-tuple-element.71.near, f32[2,64,256]{2,1,0:T(8,128)S(1)} %coarse_finish.5.fix, f32[2,128,512]{2,1,0:T(8,128)S(1)} %collective-permute-done.16.near_halo, ...), custom_call_target="tpu_custom_call" | custom-call | bytes 3407872 | tf_op jit(solution)/shard_map/third/pallas_call | solution.py:57
  56.7 0.6 rebuild.1.state_nb
  57.3 1.6 %collective-permute-done.17.far_halo = f32[2,64,256]{2,1,0:T(8,128)S(1)} collective-permute-done((f32[2,64,256]{2,1,0:T(8,128)S(1)}, f32[2,64,256]{2,1,0:T(8,128)S(1)}, u32[]{:S(2)}, u32[]{:S(2)}) %collective-permute-start.17) | collective-permute-done | bytes 131104 | tf_op jit(solution)/shard_map/ppermute | solution.py:452
  58.9 0.0 collective-permute-done.18.near_halo
  58.9 0.6 fix.1
  59.5 0.1 collective-permute-start.21
  59.6 0.0 copy-start.1
  59.6 2.5 %collective-permute-start.20 = (f32[2,128,512]{2,1,0:T(8,128)S(1)}, f32[2,128,512]{2,1,0:T(8,128)S(1)}, u32[]{:S(2)}, u32[]{:S(2)}) collective-permute-start(f32[2,128,512]{2,1,0:T(8,128)S(1)} %get-tuple-element.94.refs_0_), channel_id=1, source_target_pairs={{1,2},{3,4},{5,6},{7,8},{9,10},{11,12},{13,14},{17,18},{19,20},{21... | collective-permute-start | bytes 1572872 | tf_op jit(solution)/shard_map/ppermute | solution.py:452
  62.1 0.9 %part.5 = (f32[2,128,512]{2,1,0:T(8,128)S(1)}, f32[2,128,512]{2,1,0:T(8,128)S(1)}) custom-call(f32[2,128,512]{2,1,0:T(8,128)S(1)} %get-tuple-element.94.refs_0_, f32[2,128,512]{2,1,0:T(8,128)S(1)} %get-tuple-element.95.refs_1_, f32[2,128,512]{2,1,0:T(8,128)S(1)} %get-tuple-element.51.refs_3_.gain.refs_2_, ...), custom_call_target="tpu_custom_call" | custom-call | bytes 3670016 | tf_op jit(solution)/shard_map/part/pallas_call | solution.py:57
  63.1 1.0 %final.2 = (f32[2,2,128,512]{3,2,1,0:T(8,128)}, f32[2,128,512]{2,1,0:T(8,128)}) custom-call(s32[1]{0:T(128)} %bitcast.where, f32[1]{0:T(128)} %bitcast.1.keep, f32[2,128,512]{2,1,0:T(8,128)S(1)} %get-tuple-element.51.refs_3_.gain.refs_2_, f32[2,128,512]{2,1,0:T(8,128)S(1)} %copy-done, f32[2,128,512]{2,1,0:T(8,128)S(1)} %copy-done.1, ...), custom_call_target="tpu_custom_call" | custom-call | bytes 4194312 | tf_op jit(solution)/shard_map/final/pallas_call | solution.py:57
  64.1 9.8 %collective-permute-done.20.refs_1_ = f32[2,128,512]{2,1,0:T(8,128)S(1)} collective-permute-done((f32[2,128,512]{2,1,0:T(8,128)S(1)}, f32[2,128,512]{2,1,0:T(8,128)S(1)}, u32[]{:S(2)}, u32[]{:S(2)}) %collective-permute-start.20) | collective-permute-done | bytes 524320 | tf_op jit(solution)/shard_map/ppermute | solution.py:452
  73.9 1.0 %final.3 = (f32[2,2,128,512]{3,2,1,0:T(8,128)}, f32[2,128,512]{2,1,0:T(8,128)}) custom-call(s32[1]{0:T(128)} %bitcast.where, f32[1]{0:T(128)} %bitcast.1.keep, f32[2,128,512]{2,1,0:T(8,128)S(1)} %get-tuple-element.51.refs_3_.gain.refs_2_, f32[2,128,512]{2,1,0:T(8,128)S(1)} %copy-done, ...), custom_call_target="tpu_custom_call", output_to_operand_aliasing={{0}: (7, {}), {1}: (8, {})} | custom-call | bytes 5767176 | tf_op jit(solution)/shard_map/final/pallas_call | solution.py:57
  (13 shorter events, 0.2 us)
Async XLA Ops:
  0.6 4.2 %copy-start = (f32[2,128,512]{2,1,0:T(8,128)S(1)}, f32[2,128,512]{2,1,0:T(8,128)}, u32[]{:S(2)}) copy-start(f32[2,128,512]{2,1,0:T(8,128)} %phi.7) | copy-start | bytes 1572868
  1.9 11.8 %collective-permute-start.1 = (f32[2,128,512]{2,1,0:T(8,128)S(1)}, f32[2,128,512]{2,1,0:T(8,128)S(1)}, u32[]{:S(2)}, u32[]{:S(2)}) collective-permute-start(f32[2,128,512]{2,1,0:T(8,128)S(1)} %get-tuple-element.54.refs_2_), channel_id=1, source_target_pairs={{0,1},{1,0},{2,3},{3,2},{4,5},{5,4},{6,7},{7,6},{8,9},{9,8},{10,11... | collective-permute-start | bytes 1572872 | tf_op jit(solution)/shard_map/ppermute | solution.py:455
  2.1 11.6 %collective-permute-start.2 = (f32[2,64,512]{2,1,0:T(8,128)S(1)}, f32[2,64,512]{2,1,0:T(8,128)S(1)}, u32[]{:S(2)}, u32[]{:S(2)}) collective-permute-start(f32[2,64,512]{2,1,0:T(8,128)S(1)} %get-tuple-element.53.refs_1_), channel_id=1, source_target_pairs={{1,2},{3,4},{5,6},{7,8},{9,10},{11,12},{13,14},{17,18},{19,20},{21... | collective-permute-start | bytes 786440 | tf_op jit(solution)/shard_map/ppermute | solution.py:452
  4.7 11.7 %collective-permute-start = (f32[2,64,512]{2,1,0:T(8,128)S(1)}, f32[2,64,512]{2,1,0:T(8,128)S(1)}, u32[]{:S(2)}, u32[]{:S(2)}) collective-permute-start(f32[2,64,512]{2,1,0:T(8,128)S(1)} %get-tuple-element.52.refs_0_), channel_id=1, source_target_pairs={{1,2},{3,4},{5,6},{7,8},{9,10},{11,12},{13,14},{17,18},{19,20},{21... | collective-permute-start | bytes 786440 | tf_op jit(solution)/shard_map/ppermute | solution.py:452
  4.8 1.2 %copy-start.2 = (f32[2,2,128,512]{3,2,1,0:T(8,128)S(1)}, f32[2,2,128,512]{3,2,1,0:T(8,128)}, u32[]{:S(2)}) copy-start(f32[2,2,128,512]{3,2,1,0:T(8,128)} %cot.1) | copy-start | bytes 3145732
  13.8 20.2 %collective-permute-start.6 = (f32[2,128,512]{2,1,0:T(8,128)S(1)}, f32[2,128,512]{2,1,0:T(8,128)S(1)}, u32[]{:S(2)}, u32[]{:S(2)}) collective-permute-start(f32[2,128,512]{2,1,0:T(8,128)S(1)} %finish.5.refs_2_), channel_id=1, source_target_pairs={{0,1},{1,0},{2,3},{3,2},{4,5},{5,4},{6,7},{7,6},{8,9},{9,8},{10,11... | collective-permute-start | bytes 1572872 | tf_op jit(solution)/shard_map/ppermute | solution.py:455
  16.5 10.5 %collective-permute-start.4 = (f32[2,64,512]{2,1,0:T(8,128)S(1)}, f32[2,64,512]{2,1,0:T(8,128)S(1)}, u32[]{:S(2)}, u32[]{:S(2)}) collective-permute-start(f32[2,64,512]{2,1,0:T(8,128)S(1)} %finish.3.refs_0_), channel_id=1, source_target_pairs={{1,2},{3,4},{5,6},{7,8},{9,10},{11,12},{13,14},{17,18},{19,20},{21... | collective-permute-start | bytes 786440 | tf_op jit(solution)/shard_map/ppermute | solution.py:452
  19.1 12.2 %collective-permute-start.3 = (f32[2,64,512]{2,1,0:T(8,128)S(1)}, f32[2,64,512]{2,1,0:T(8,128)S(1)}, u32[]{:S(2)}, u32[]{:S(2)}) collective-permute-start(f32[2,64,512]{2,1,0:T(8,128)S(1)} %finish.4.refs_1_), channel_id=1, source_target_pairs={{1,2},{3,4},{5,6},{7,8},{9,10},{11,12},{13,14},{17,18},{19,20},{21... | collective-permute-start | bytes 786440 | tf_op jit(solution)/shard_map/ppermute | solution.py:452
  31.5 5.3 %collective-permute-start.5 = (f32[2,64,256]{2,1,0:T(8,128)S(1)}, f32[2,64,256]{2,1,0:T(8,128)S(1)}, u32[]{:S(2)}, u32[]{:S(2)}) collective-permute-start(f32[2,64,256]{2,1,0:T(8,128)S(1)} %get-tuple-element.65), channel_id=1, source_target_pairs={{1,2},{3,4},{5,6},{7,8},{9,10},{11,12},{13,14},{17,18},{19,20},{21... | collective-permute-start | bytes 393224 | tf_op jit(solution)/shard_map/ppermute | solution.py:452
  34.4 2.5 %collective-permute-start.7 = (f32[2,64,256]{2,1,0:T(8,128)S(1)}, f32[2,64,256]{2,1,0:T(8,128)S(1)}, u32[]{:S(2)}, u32[]{:S(2)}) collective-permute-start(f32[2,64,256]{2,1,0:T(8,128)S(1)} %get-tuple-element.73), channel_id=1, source_target_pairs={{0,1},{1,0},{2,3},{3,2},{4,5},{5,4},{6,7},{7,6},{8,9},{9,8},{10,11... | collective-permute-start | bytes 393224 | tf_op jit(solution)/shard_map/ppermute | solution.py:455
  34.7 20.9 %collective-permute-start.16 = (f32[2,128,512]{2,1,0:T(8,128)S(1)}, f32[2,128,512]{2,1,0:T(8,128)S(1)}, u32[]{:S(2)}, u32[]{:S(2)}) collective-permute-start(f32[2,128,512]{2,1,0:T(8,128)S(1)} %get-tuple-element.69.refs_2_), channel_id=1, source_target_pairs={{0,1},{1,0},{2,3},{3,2},{4,5},{5,4},{6,7},{7,6},{8,9},{9,8},{10,11... | collective-permute-start | bytes 1572872 | tf_op jit(solution)/shard_map/ppermute | solution.py:455
  36.9 4.7 %collective-permute-start.8 = (f32[2,64,256]{2,1,0:T(8,128)S(1)}, f32[2,64,256]{2,1,0:T(8,128)S(1)}, u32[]{:S(2)}, u32[]{:S(2)}) collective-permute-start(f32[2,64,256]{2,1,0:T(8,128)S(1)} %coarse_first.1.fix.own), channel_id=1, source_target_pairs={{1,2},{3,4},{5,6},{7,8},{9,10},{11,12},{13,14},{17,18},{19,20},{21... | collective-permute-start | bytes 393224 | tf_op jit(solution)/shard_map/ppermute | solution.py:452
  38.5 3.0 %collective-permute-start.9 = (f32[2,64,256]{2,1,0:T(8,128)S(1)}, f32[2,64,256]{2,1,0:T(8,128)S(1)}, u32[]{:S(2)}, u32[]{:S(2)}) collective-permute-start(f32[2,64,256]{2,1,0:T(8,128)S(1)} %coarse_first.1.fix.own), channel_id=1, source_target_pairs={{0,1},{1,0},{2,3},{3,2},{4,5},{5,4},{6,7},{7,6},{8,9},{9,8},{10,11... | collective-permute-start | bytes 393224 | tf_op jit(solution)/shard_map/ppermute | solution.py:455
  39.0 6.4 %collective-permute-start.10 = (f32[2,64,256]{2,1,0:T(8,128)S(1)}, f32[2,64,256]{2,1,0:T(8,128)S(1)}, u32[]{:S(2)}, u32[]{:S(2)}) collective-permute-start(f32[2,64,256]{2,1,0:T(8,128)S(1)} %get-tuple-element.80), channel_id=1, source_target_pairs={{1,2},{3,4},{5,6},{7,8},{9,10},{11,12},{13,14},{17,18},{19,20},{21... | collective-permute-start | bytes 393224 | tf_op jit(solution)/shard_map/ppermute | solution.py:452
  41.6 5.5 %collective-permute-start.11 = (f32[2,64,256]{2,1,0:T(8,128)S(1)}, f32[2,64,256]{2,1,0:T(8,128)S(1)}, u32[]{:S(2)}, u32[]{:S(2)}) collective-permute-start(f32[2,64,256]{2,1,0:T(8,128)S(1)} %coarse_finish.3.fix), channel_id=1, source_target_pairs={{1,2},{3,4},{5,6},{7,8},{9,10},{11,12},{13,14},{17,18},{19,20},{21... | collective-permute-start | bytes 393224 | tf_op jit(solution)/shard_map/ppermute | solution.py:452
  44.1 3.0 %collective-permute-start.12 = (f32[2,64,256]{2,1,0:T(8,128)S(1)}, f32[2,64,256]{2,1,0:T(8,128)S(1)}, u32[]{:S(2)}, u32[]{:S(2)}) collective-permute-start(f32[2,64,256]{2,1,0:T(8,128)S(1)} %coarse_finish.3.fix), channel_id=1, source_target_pairs={{0,1},{1,0},{2,3},{3,2},{4,5},{5,4},{6,7},{7,6},{8,9},{9,8},{10,11... | collective-permute-start | bytes 393224 | tf_op jit(solution)/shard_map/ppermute | solution.py:455
  44.1 7.3 %collective-permute-start.13 = (f32[2,64,256]{2,1,0:T(8,128)S(1)}, f32[2,64,256]{2,1,0:T(8,128)S(1)}, u32[]{:S(2)}, u32[]{:S(2)}) collective-permute-start(f32[2,64,256]{2,1,0:T(8,128)S(1)} %get-tuple-element.82), channel_id=1, source_target_pairs={{1,2},{3,4},{5,6},{7,8},{9,10},{11,12},{13,14},{17,18},{19,20},{21... | collective-permute-start | bytes 393224 | tf_op jit(solution)/shard_map/ppermute | solution.py:452
  47.2 6.6 %collective-permute-start.14 = (f32[2,64,256]{2,1,0:T(8,128)S(1)}, f32[2,64,256]{2,1,0:T(8,128)S(1)}, u32[]{:S(2)}, u32[]{:S(2)}) collective-permute-start(f32[2,64,256]{2,1,0:T(8,128)S(1)} %coarse_finish.4.fix), channel_id=1, source_target_pairs={{1,2},{3,4},{5,6},{7,8},{9,10},{11,12},{13,14},{17,18},{19,20},{21... | collective-permute-start | bytes 393224 | tf_op jit(solution)/shard_map/ppermute | solution.py:452
  51.1 2.7 %collective-permute-start.15 = (f32[2,64,256]{2,1,0:T(8,128)S(1)}, f32[2,64,256]{2,1,0:T(8,128)S(1)}, u32[]{:S(2)}, u32[]{:S(2)}) collective-permute-start(f32[2,64,256]{2,1,0:T(8,128)S(1)} %coarse_finish.4.fix), channel_id=1, source_target_pairs={{0,1},{1,0},{2,3},{3,2},{4,5},{5,4},{6,7},{7,6},{8,9},{9,8},{10,11... | collective-permute-start | bytes 393224 | tf_op jit(solution)/shard_map/ppermute | solution.py:455
  51.1 5.6 %collective-permute-start.19 = (f32[2,64,256]{2,1,0:T(8,128)S(1)}, f32[2,64,256]{2,1,0:T(8,128)S(1)}, u32[]{:S(2)}, u32[]{:S(2)}) collective-permute-start(f32[2,64,256]{2,1,0:T(8,128)S(1)} %get-tuple-element.91), channel_id=1, source_target_pairs={{1,2},{3,4},{5,6},{7,8},{9,10},{11,12},{13,14},{17,18},{19,20},{21... | collective-permute-start | bytes 393224 | tf_op jit(solution)/shard_map/ppermute | solution.py:452
  53.8 5.1 %collective-permute-start.17 = (f32[2,64,256]{2,1,0:T(8,128)S(1)}, f32[2,64,256]{2,1,0:T(8,128)S(1)}, u32[]{:S(2)}, u32[]{:S(2)}) collective-permute-start(f32[2,64,256]{2,1,0:T(8,128)S(1)} %coarse_finish.5.fix), channel_id=1, source_target_pairs={{1,2},{3,4},{5,6},{7,8},{9,10},{11,12},{13,14},{17,18},{19,20},{21... | collective-permute-start | bytes 393224 | tf_op jit(solution)/shard_map/ppermute | solution.py:452
  55.6 3.3 %collective-permute-start.18 = (f32[2,64,256]{2,1,0:T(8,128)S(1)}, f32[2,64,256]{2,1,0:T(8,128)S(1)}, u32[]{:S(2)}, u32[]{:S(2)}) collective-permute-start(f32[2,64,256]{2,1,0:T(8,128)S(1)} %coarse_finish.5.fix), channel_id=1, source_target_pairs={{0,1},{1,0},{2,3},{3,2},{4,5},{5,4},{6,7},{7,6},{8,9},{9,8},{10,11... | collective-permute-start | bytes 393224 | tf_op jit(solution)/shard_map/ppermute | solution.py:455
  59.5 3.6 %collective-permute-start.21 = (f32[2,128,512]{2,1,0:T(8,128)S(1)}, f32[2,128,512]{2,1,0:T(8,128)S(1)}, u32[]{:S(2)}, u32[]{:S(2)}) collective-permute-start(f32[2,128,512]{2,1,0:T(8,128)S(1)} %get-tuple-element.95.refs_1_), channel_id=1, source_target_pairs={{0,1},{1,0},{2,3},{3,2},{4,5},{5,4},{6,7},{7,6},{8,9},{9,8},{10,11... | collective-permute-start | bytes 1572872 | tf_op jit(solution)/shard_map/ppermute | solution.py:455
  59.6 3.5 %copy-start.1 = (f32[2,128,512]{2,1,0:T(8,128)S(1)}, f32[2,128,512]{2,1,0:T(8,128)}, u32[]{:S(2)}) copy-start(f32[2,128,512]{2,1,0:T(8,128)} %psi.3) | copy-start | bytes 1572868
  59.6 14.3 %collective-permute-start.20 = (f32[2,128,512]{2,1,0:T(8,128)S(1)}, f32[2,128,512]{2,1,0:T(8,128)S(1)}, u32[]{:S(2)}, u32[]{:S(2)}) collective-permute-start(f32[2,128,512]{2,1,0:T(8,128)S(1)} %get-tuple-element.94.refs_0_), channel_id=1, source_target_pairs={{1,2},{3,4},{5,6},{7,8},{9,10},{11,12},{13,14},{17,18},{19,20},{21... | collective-permute-start | bytes 1572872 | tf_op jit(solution)/shard_map/ppermute | solution.py:452

commit v6 on v5

--- a/solution.py
+++ b/solution.py
@@ -43,7 +43,7 @@
 
 
 def early_chunks(rows):
-    return [rows // 2, rows // 2]
+    return [5 * rows // 8, 3 * rows // 8]
 
 
 def late_chunks(rows):

time: 75.3 us -> 74.7 us (level)
    ppermute x13, waiting for transfers between devices: 36.4 us -> 35.6 us  [swap_far(): return lax.ppermute(x, ('grp', 'gx'), across)]
where the time goes in v6:
time: 74.7 us; the launch traced here: 74.2 us
  waiting for transfers between devices  35.7 us (48%)
  starting transfers between devices  23.8 us (32%)
  Pallas kernels  12.6 us (17%)
  local copies, waits for them, and re-layouts  1.24 us (2%)
  between operations  0.93 us (1%)
    ppermute x13, waiting for transfers between devices, swap_far(): return lax.ppermute(x, ('grp', 'gx'), across)  35.6 us
    ppermute x13, starting transfers between devices, swap_far(): return lax.ppermute(x, ('grp', 'gx'), across)  22.9 us
    pallas_call x27, Pallas kernels, call(): pl.pallas_call(body, out_shape=shapes, in_specs=in_specs or [VMEM] * len(...  12.6 us
  transfers between devices with their start and end apart: 22, of which 9 were waited for; matrix products, arithmetic and copies ran while one was open for 0% of the time, Pallas kernels for 13%

profile of v6, /device:TPU:1, one launch (start us, length us, event | category | flops | bytes accessed | tf_op | source)
XLA Modules:
  0.0 74.2 jit_solution(3812404247225251471)
XLA Ops:
  0.7 1.3 %take.1 = (f32[2,80,512]{2,1,0:T(8,128)S(1)}, f32[2,48,512]{2,1,0:T(8,128)S(1)}, f32[2,128,512]{2,1,0:T(8,128)S(1)}) custom-call(s32[1]{0:T(128)} %bitcast.where, f32[2,2,128,512]{3,2,1,0:T(8,128)} %warm.1), custom_call_target="tpu_custom_call" | custom-call | bytes 2097156 | tf_op jit(solution)/shard_map/take/pallas_call | solution.py:57
  2.0 0.1 collective-permute-start.1
  2.1 2.6 %collective-permute-start.2 = (f32[2,48,512]{2,1,0:T(8,128)S(1)}, f32[2,48,512]{2,1,0:T(8,128)S(1)}, u32[]{:S(2)}, u32[]{:S(2)}) collective-permute-start(f32[2,48,512]{2,1,0:T(8,128)S(1)} %get-tuple-element.53.refs_1_), channel_id=1, source_target_pairs={{1,2},{3,4},{5,6},{7,8},{9,10},{11,12},{13,14},{17,18},{19,20},{21... | collective-permute-start | bytes 589832 | tf_op jit(solution)/shard_map/ppermute | solution.py:452
  4.8 0.1 collective-permute-start
  4.8 1.2 %copy-done.2 = f32[2,2,128,512]{3,2,1,0:T(8,128)S(1)} copy-done((f32[2,2,128,512]{3,2,1,0:T(8,128)S(1)}, f32[2,2,128,512]{3,2,1,0:T(8,128)}, u32[]{:S(2)}) %copy-start.2) | copy-done | bytes 1048600
  6.1 0.2 setup.1
  6.3 0.9 %part.3 = (f32[2,128,512]{2,1,0:T(8,128)S(1)}, f32[2,128,512]{2,1,0:T(8,128)S(1)}) custom-call(f32[2,80,512]{2,1,0:T(8,128)S(1)} %get-tuple-element.52.refs_0_, f32[2,48,512]{2,1,0:T(8,128)S(1)} %get-tuple-element.53.refs_1_, f32[2,128,512]{2,1,0:T(8,128)S(1)} %get-tuple-element.54.refs_2_, f32[2,128,512]{2,1,0:T(8,128)S(1)} %get-tuple-element.51.refs_3_.gain.refs_2_, ...), custom_call_target="tpu_custom_call" | custom-call | bytes 3670016 | tf_op jit(solution)/shard_map/part/pallas_call | solution.py:57
  7.3 5.7 %collective-permute-done.2.halo = f32[2,48,512]{2,1,0:T(8,128)S(1)} collective-permute-done((f32[2,48,512]{2,1,0:T(8,128)S(1)}, f32[2,48,512]{2,1,0:T(8,128)S(1)}, u32[]{:S(2)}, u32[]{:S(2)}) %collective-permute-start.2) | collective-permute-done | bytes 196640 | tf_op jit(solution)/shard_map/ppermute | solution.py:452
  13.0 0.1 finish.5.refs_2_
  13.2 0.1 collective-permute-start.6
  13.2 3.3 %collective-permute-done.halo = f32[2,80,512]{2,1,0:T(8,128)S(1)} collective-permute-done((f32[2,80,512]{2,1,0:T(8,128)S(1)}, f32[2,80,512]{2,1,0:T(8,128)S(1)}, u32[]{:S(2)}, u32[]{:S(2)}) %collective-permute-start) | collective-permute-done | bytes 327712 | tf_op jit(solution)/shard_map/ppermute | solution.py:452
  16.5 0.1 finish.3.refs_0_
  16.6 2.5 %collective-permute-start.4 = (f32[2,80,512]{2,1,0:T(8,128)S(1)}, f32[2,80,512]{2,1,0:T(8,128)S(1)}, u32[]{:S(2)}, u32[]{:S(2)}) collective-permute-start(f32[2,80,512]{2,1,0:T(8,128)S(1)} %finish.3.refs_0_), channel_id=1, source_target_pairs={{1,2},{3,4},{5,6},{7,8},{9,10},{11,12},{13,14},{17,18},{19,20},{21... | collective-permute-start | bytes 983048 | tf_op jit(solution)/shard_map/ppermute | solution.py:452
  19.1 0.1 collective-permute-start.3
  19.2 0.9 %part.4 = (f32[2,128,512]{2,1,0:T(8,128)S(1)}, f32[2,128,512]{2,1,0:T(8,128)S(1)}) custom-call(f32[2,80,512]{2,1,0:T(8,128)S(1)} %finish.3.refs_0_, f32[2,48,512]{2,1,0:T(8,128)S(1)} %finish.4.refs_1_, f32[2,128,512]{2,1,0:T(8,128)S(1)} %finish.5.refs_2_, f32[2,128,512]{2,1,0:T(8,128)S(1)} %get-tuple-element.51.refs_3_.gain.refs_2_, ...), custom_call_target="tpu_custom_call" | custom-call | bytes 3670016 | tf_op jit(solution)/shard_map/part/pallas_call | solution.py:57
  20.1 0.1 matrices.1
  20.2 6.8 %collective-permute-done.4.halo = f32[2,80,512]{2,1,0:T(8,128)S(1)} collective-permute-done((f32[2,80,512]{2,1,0:T(8,128)S(1)}, f32[2,80,512]{2,1,0:T(8,128)S(1)}, u32[]{:S(2)}, u32[]{:S(2)}) %collective-permute-start.4) | collective-permute-done | bytes 327712 | tf_op jit(solution)/shard_map/ppermute | solution.py:452
  27.1 0.3 finish_pool.3
  27.4 3.2 %collective-permute-done.3.halo = f32[2,48,512]{2,1,0:T(8,128)S(1)} collective-permute-done((f32[2,48,512]{2,1,0:T(8,128)S(1)}, f32[2,48,512]{2,1,0:T(8,128)S(1)}, u32[]{:S(2)}, u32[]{:S(2)}) %collective-permute-start.3) | collective-permute-done | bytes 196640 | tf_op jit(solution)/shard_map/ppermute | solution.py:452
  30.6 0.2 finish_pool.4
  30.8 2.5 %collective-permute-start.5 = (f32[2,64,256]{2,1,0:T(8,128)S(1)}, f32[2,64,256]{2,1,0:T(8,128)S(1)}, u32[]{:S(2)}, u32[]{:S(2)}) collective-permute-start(f32[2,64,256]{2,1,0:T(8,128)S(1)} %get-tuple-element.65), channel_id=1, source_target_pairs={{1,2},{3,4},{5,6},{7,8},{9,10},{11,12},{13,14},{17,18},{19,20},{21... | collective-permute-start | bytes 393224 | tf_op jit(solution)/shard_map/ppermute | solution.py:452
  33.4 0.0 collective-permute-done.6.halo
  33.4 0.4 finish_pool.5
  33.7 0.1 collective-permute-start.7
  33.8 0.3 coarse_setup.1.gain
  34.1 0.6 collective-permute-start.16
  34.7 1.5 %part_defect.1 = (f32[2,128,512]{2,1,0:T(8,128)S(1)}, f32[2,128,512]{2,1,0:T(8,128)S(1)}, f32[2,64,256]{2,1,0:T(8,128)S(1)}) custom-call(f32[2,80,512]{2,1,0:T(8,128)S(1)} %get-tuple-element.66.refs_0_, f32[2,48,512]{2,1,0:T(8,128)S(1)} %get-tuple-element.67.refs_1_, f32[2,128,512]{2,1,0:T(8,128)S(1)} %get-tuple-element.69.refs_2_, ...), custom_call_target="tpu_custom_call" | custom-call | bytes 3932160 | tf_op jit(solution)/shard_map/part_defect/pallas_call | solution.py:57
  36.2 0.0 collective-permute-done.5.far.sums
  36.2 0.0 collective-permute-done.7.near
  36.2 1.6 %collective-permute-start.8 = (f32[2,64,256]{2,1,0:T(8,128)S(1)}, f32[2,64,256]{2,1,0:T(8,128)S(1)}, u32[]{:S(2)}, u32[]{:S(2)}) collective-permute-start(f32[2,64,256]{2,1,0:T(8,128)S(1)} %coarse_first.1.fix.own), channel_id=1, source_target_pairs={{1,2},{3,4},{5,6},{7,8},{9,10},{11,12},{13,14},{17,18},{19,20},{21... | collective-permute-start | bytes 393224 | tf_op jit(solution)/shard_map/ppermute | solution.py:452
  37.9 0.0 collective-permute-start.9
  37.9 0.5 three.1
  38.4 1.3 %collective-permute-start.10 = (f32[2,64,256]{2,1,0:T(8,128)S(1)}, f32[2,64,256]{2,1,0:T(8,128)S(1)}, u32[]{:S(2)}, u32[]{:S(2)}) collective-permute-start(f32[2,64,256]{2,1,0:T(8,128)S(1)} %get-tuple-element.80), channel_id=1, source_target_pairs={{1,2},{3,4},{5,6},{7,8},{9,10},{11,12},{13,14},{17,18},{19,20},{21... | collective-permute-start | bytes 393224 | tf_op jit(solution)/shard_map/ppermute | solution.py:452
  39.6 0.1 coarse_part.3.part
  39.8 1.1 %collective-permute-done.8.far = f32[2,64,256]{2,1,0:T(8,128)S(1)} collective-permute-done((f32[2,64,256]{2,1,0:T(8,128)S(1)}, f32[2,64,256]{2,1,0:T(8,128)S(1)}, u32[]{:S(2)}, u32[]{:S(2)}) %collective-permute-start.8) | collective-permute-done | bytes 131104 | tf_op jit(solution)/shard_map/ppermute | solution.py:452
  40.9 0.0 collective-permute-done.9.near
  41.0 2.5 %collective-permute-start.11 = (f32[2,64,256]{2,1,0:T(8,128)S(1)}, f32[2,64,256]{2,1,0:T(8,128)S(1)}, u32[]{:S(2)}, u32[]{:S(2)}) collective-permute-start(f32[2,64,256]{2,1,0:T(8,128)S(1)} %coarse_finish.3.fix), channel_id=1, source_target_pairs={{1,2},{3,4},{5,6},{7,8},{9,10},{11,12},{13,14},{17,18},{19,20},{21... | collective-permute-start | bytes 393224 | tf_op jit(solution)/shard_map/ppermute | solution.py:452
  43.4 0.0 collective-permute-start.12
  43.4 1.2 %collective-permute-start.13 = (f32[2,64,256]{2,1,0:T(8,128)S(1)}, f32[2,64,256]{2,1,0:T(8,128)S(1)}, u32[]{:S(2)}, u32[]{:S(2)}) collective-permute-start(f32[2,64,256]{2,1,0:T(8,128)S(1)} %get-tuple-element.82), channel_id=1, source_target_pairs={{1,2},{3,4},{5,6},{7,8},{9,10},{11,12},{13,14},{17,18},{19,20},{21... | collective-permute-start | bytes 393224 | tf_op jit(solution)/shard_map/ppermute | solution.py:452
  44.6 0.2 coarse_part.4.part
  44.8 1.7 %collective-permute-done.11.far = f32[2,64,256]{2,1,0:T(8,128)S(1)} collective-permute-done((f32[2,64,256]{2,1,0:T(8,128)S(1)}, f32[2,64,256]{2,1,0:T(8,128)S(1)}, u32[]{:S(2)}, u32[]{:S(2)}) %collective-permute-start.11) | collective-permute-done | bytes 131104 | tf_op jit(solution)/shard_map/ppermute | solution.py:452
  46.5 0.0 collective-permute-done.12.near
  46.5 3.9 %collective-permute-start.14 = (f32[2,64,256]{2,1,0:T(8,128)S(1)}, f32[2,64,256]{2,1,0:T(8,128)S(1)}, u32[]{:S(2)}, u32[]{:S(2)}) collective-permute-start(f32[2,64,256]{2,1,0:T(8,128)S(1)} %coarse_finish.4.fix), channel_id=1, source_target_pairs={{1,2},{3,4},{5,6},{7,8},{9,10},{11,12},{13,14},{17,18},{19,20},{21... | collective-permute-start | bytes 393224 | tf_op jit(solution)/shard_map/ppermute | solution.py:452
  50.5 0.2 collective-permute-start.19
  50.6 0.2 coarse_part.5.part
  50.8 0.0 collective-permute-done.13.refs_1_
  50.8 2.3 %collective-permute-done.14.far = f32[2,64,256]{2,1,0:T(8,128)S(1)} collective-permute-done((f32[2,64,256]{2,1,0:T(8,128)S(1)}, f32[2,64,256]{2,1,0:T(8,128)S(1)}, u32[]{:S(2)}, u32[]{:S(2)}) %collective-permute-start.14) | collective-permute-done | bytes 131104 | tf_op jit(solution)/shard_map/ppermute | solution.py:452
  53.1 0.0 collective-permute-done.15.near
  53.2 1.8 %collective-permute-start.17 = (f32[2,64,256]{2,1,0:T(8,128)S(1)}, f32[2,64,256]{2,1,0:T(8,128)S(1)}, u32[]{:S(2)}, u32[]{:S(2)}) collective-permute-start(f32[2,64,256]{2,1,0:T(8,128)S(1)} %coarse_finish.5.fix), channel_id=1, source_target_pairs={{1,2},{3,4},{5,6},{7,8},{9,10},{11,12},{13,14},{17,18},{19,20},{21... | collective-permute-start | bytes 393224 | tf_op jit(solution)/shard_map/ppermute | solution.py:452
  55.0 0.0 collective-permute-start.18
  55.0 0.0 collective-permute-done.16.near_halo
  55.0 1.0 %third.1 = (f32[2,128,512]{2,1,0:T(8,128)S(1)}, f32[2,128,512]{2,1,0:T(8,128)S(1)}) custom-call(f32[2,128,512]{2,1,0:T(8,128)S(1)} %get-tuple-element.70.far, f32[2,128,512]{2,1,0:T(8,128)S(1)} %get-tuple-element.71.near, f32[2,64,256]{2,1,0:T(8,128)S(1)} %coarse_finish.5.fix, f32[2,128,512]{2,1,0:T(8,128)S(1)} %collective-permute-done.16.near_halo, ...), custom_call_target="tpu_custom_call" | custom-call | bytes 3407872 | tf_op jit(solution)/shard_map/third/pallas_call | solution.py:57
  56.0 0.0 collective-permute-done.19.refs_2_
  56.0 0.6 rebuild.1.state_nb
  56.6 1.7 %collective-permute-done.17.far_halo = f32[2,64,256]{2,1,0:T(8,128)S(1)} collective-permute-done((f32[2,64,256]{2,1,0:T(8,128)S(1)}, f32[2,64,256]{2,1,0:T(8,128)S(1)}, u32[]{:S(2)}, u32[]{:S(2)}) %collective-permute-start.17) | collective-permute-done | bytes 131104 | tf_op jit(solution)/shard_map/ppermute | solution.py:452
  58.3 0.6 fix.1
  58.9 0.1 collective-permute-start.21
  58.9 0.0 copy-start.1
  59.0 2.5 %collective-permute-start.20 = (f32[2,128,512]{2,1,0:T(8,128)S(1)}, f32[2,128,512]{2,1,0:T(8,128)S(1)}, u32[]{:S(2)}, u32[]{:S(2)}) collective-permute-start(f32[2,128,512]{2,1,0:T(8,128)S(1)} %get-tuple-element.94.refs_0_), channel_id=1, source_target_pairs={{1,2},{3,4},{5,6},{7,8},{9,10},{11,12},{13,14},{17,18},{19,20},{21... | collective-permute-start | bytes 1572872 | tf_op jit(solution)/shard_map/ppermute | solution.py:452
  61.5 0.9 %part.5 = (f32[2,128,512]{2,1,0:T(8,128)S(1)}, f32[2,128,512]{2,1,0:T(8,128)S(1)}) custom-call(f32[2,128,512]{2,1,0:T(8,128)S(1)} %get-tuple-element.94.refs_0_, f32[2,128,512]{2,1,0:T(8,128)S(1)} %get-tuple-element.95.refs_1_, f32[2,128,512]{2,1,0:T(8,128)S(1)} %get-tuple-element.51.refs_3_.gain.refs_2_, ...), custom_call_target="tpu_custom_call" | custom-call | bytes 3670016 | tf_op jit(solution)/shard_map/part/pallas_call | solution.py:57
  62.4 0.0 collective-permute-done.21.refs_1_
  62.5 1.0 %final.2 = (f32[2,2,128,512]{3,2,1,0:T(8,128)}, f32[2,128,512]{2,1,0:T(8,128)}) custom-call(s32[1]{0:T(128)} %bitcast.where, f32[1]{0:T(128)} %bitcast.1.keep, f32[2,128,512]{2,1,0:T(8,128)S(1)} %get-tuple-element.51.refs_3_.gain.refs_2_, f32[2,128,512]{2,1,0:T(8,128)S(1)} %copy-done, f32[2,128,512]{2,1,0:T(8,128)S(1)} %copy-done.1, ...), custom_call_target="tpu_custom_call" | custom-call | bytes 4194312 | tf_op jit(solution)/shard_map/final/pallas_call | solution.py:57
  63.4 9.8 %collective-permute-done.20.refs_1_ = f32[2,128,512]{2,1,0:T(8,128)S(1)} collective-permute-done((f32[2,128,512]{2,1,0:T(8,128)S(1)}, f32[2,128,512]{2,1,0:T(8,128)S(1)}, u32[]{:S(2)}, u32[]{:S(2)}) %collective-permute-start.20) | collective-permute-done | bytes 524320 | tf_op jit(solution)/shard_map/ppermute | solution.py:452
  73.2 1.0 %final.3 = (f32[2,2,128,512]{3,2,1,0:T(8,128)}, f32[2,128,512]{2,1,0:T(8,128)}) custom-call(s32[1]{0:T(128)} %bitcast.where, f32[1]{0:T(128)} %bitcast.1.keep, f32[2,128,512]{2,1,0:T(8,128)S(1)} %get-tuple-element.51.refs_3_.gain.refs_2_, f32[2,128,512]{2,1,0:T(8,128)S(1)} %copy-done, ...), custom_call_target="tpu_custom_call", output_to_operand_aliasing={{0}: (7, {}), {1}: (8, {})} | custom-call | bytes 5767176 | tf_op jit(solution)/shard_map/final/pallas_call | solution.py:57
  (13 shorter events, 0.2 us)
Async XLA Ops:
  0.6 4.2 %copy-start = (f32[2,128,512]{2,1,0:T(8,128)S(1)}, f32[2,128,512]{2,1,0:T(8,128)}, u32[]{:S(2)}) copy-start(f32[2,128,512]{2,1,0:T(8,128)} %phi.7) | copy-start | bytes 1572868
  2.0 11.1 %collective-permute-start.1 = (f32[2,128,512]{2,1,0:T(8,128)S(1)}, f32[2,128,512]{2,1,0:T(8,128)S(1)}, u32[]{:S(2)}, u32[]{:S(2)}) collective-permute-start(f32[2,128,512]{2,1,0:T(8,128)S(1)} %get-tuple-element.54.refs_2_), channel_id=1, source_target_pairs={{0,1},{1,0},{2,3},{3,2},{4,5},{5,4},{6,7},{7,6},{8,9},{9,8},{10,11... | collective-permute-start | bytes 1572872 | tf_op jit(solution)/shard_map/ppermute | solution.py:455
  2.1 10.9 %collective-permute-start.2 = (f32[2,48,512]{2,1,0:T(8,128)S(1)}, f32[2,48,512]{2,1,0:T(8,128)S(1)}, u32[]{:S(2)}, u32[]{:S(2)}) collective-permute-start(f32[2,48,512]{2,1,0:T(8,128)S(1)} %get-tuple-element.53.refs_1_), channel_id=1, source_target_pairs={{1,2},{3,4},{5,6},{7,8},{9,10},{11,12},{13,14},{17,18},{19,20},{21... | collective-permute-start | bytes 589832 | tf_op jit(solution)/shard_map/ppermute | solution.py:452
  4.8 11.7 %collective-permute-start = (f32[2,80,512]{2,1,0:T(8,128)S(1)}, f32[2,80,512]{2,1,0:T(8,128)S(1)}, u32[]{:S(2)}, u32[]{:S(2)}) collective-permute-start(f32[2,80,512]{2,1,0:T(8,128)S(1)} %get-tuple-element.52.refs_0_), channel_id=1, source_target_pairs={{1,2},{3,4},{5,6},{7,8},{9,10},{11,12},{13,14},{17,18},{19,20},{21... | collective-permute-start | bytes 983048 | tf_op jit(solution)/shard_map/ppermute | solution.py:452
  4.8 1.2 %copy-start.2 = (f32[2,2,128,512]{3,2,1,0:T(8,128)S(1)}, f32[2,2,128,512]{3,2,1,0:T(8,128)}, u32[]{:S(2)}) copy-start(f32[2,2,128,512]{3,2,1,0:T(8,128)} %cot.1) | copy-start | bytes 3145732
  13.2 20.2 %collective-permute-start.6 = (f32[2,128,512]{2,1,0:T(8,128)S(1)}, f32[2,128,512]{2,1,0:T(8,128)S(1)}, u32[]{:S(2)}, u32[]{:S(2)}) collective-permute-start(f32[2,128,512]{2,1,0:T(8,128)S(1)} %finish.5.refs_2_), channel_id=1, source_target_pairs={{0,1},{1,0},{2,3},{3,2},{4,5},{5,4},{6,7},{7,6},{8,9},{9,8},{10,11... | collective-permute-start | bytes 1572872 | tf_op jit(solution)/shard_map/ppermute | solution.py:455
  16.6 10.5 %collective-permute-start.4 = (f32[2,80,512]{2,1,0:T(8,128)S(1)}, f32[2,80,512]{2,1,0:T(8,128)S(1)}, u32[]{:S(2)}, u32[]{:S(2)}) collective-permute-start(f32[2,80,512]{2,1,0:T(8,128)S(1)} %finish.3.refs_0_), channel_id=1, source_target_pairs={{1,2},{3,4},{5,6},{7,8},{9,10},{11,12},{13,14},{17,18},{19,20},{21... | collective-permute-start | bytes 983048 | tf_op jit(solution)/shard_map/ppermute | solution.py:452
  19.1 11.5 %collective-permute-start.3 = (f32[2,48,512]{2,1,0:T(8,128)S(1)}, f32[2,48,512]{2,1,0:T(8,128)S(1)}, u32[]{:S(2)}, u32[]{:S(2)}) collective-permute-start(f32[2,48,512]{2,1,0:T(8,128)S(1)} %finish.4.refs_1_), channel_id=1, source_target_pairs={{1,2},{3,4},{5,6},{7,8},{9,10},{11,12},{13,14},{17,18},{19,20},{21... | collective-permute-start | bytes 589832 | tf_op jit(solution)/shard_map/ppermute | solution.py:452
  30.8 5.4 %collective-permute-start.5 = (f32[2,64,256]{2,1,0:T(8,128)S(1)}, f32[2,64,256]{2,1,0:T(8,128)S(1)}, u32[]{:S(2)}, u32[]{:S(2)}) collective-permute-start(f32[2,64,256]{2,1,0:T(8,128)S(1)} %get-tuple-element.65), channel_id=1, source_target_pairs={{1,2},{3,4},{5,6},{7,8},{9,10},{11,12},{13,14},{17,18},{19,20},{21... | collective-permute-start | bytes 393224 | tf_op jit(solution)/shard_map/ppermute | solution.py:452
  33.7 2.5 %collective-permute-start.7 = (f32[2,64,256]{2,1,0:T(8,128)S(1)}, f32[2,64,256]{2,1,0:T(8,128)S(1)}, u32[]{:S(2)}, u32[]{:S(2)}) collective-permute-start(f32[2,64,256]{2,1,0:T(8,128)S(1)} %get-tuple-element.73), channel_id=1, source_target_pairs={{0,1},{1,0},{2,3},{3,2},{4,5},{5,4},{6,7},{7,6},{8,9},{9,8},{10,11... | collective-permute-start | bytes 393224 | tf_op jit(solution)/shard_map/ppermute | solution.py:455
  34.1 20.9 %collective-permute-start.16 = (f32[2,128,512]{2,1,0:T(8,128)S(1)}, f32[2,128,512]{2,1,0:T(8,128)S(1)}, u32[]{:S(2)}, u32[]{:S(2)}) collective-permute-start(f32[2,128,512]{2,1,0:T(8,128)S(1)} %get-tuple-element.69.refs_2_), channel_id=1, source_target_pairs={{0,1},{1,0},{2,3},{3,2},{4,5},{5,4},{6,7},{7,6},{8,9},{9,8},{10,11... | collective-permute-start | bytes 1572872 | tf_op jit(solution)/shard_map/ppermute | solution.py:455
  36.2 4.7 %collective-permute-start.8 = (f32[2,64,256]{2,1,0:T(8,128)S(1)}, f32[2,64,256]{2,1,0:T(8,128)S(1)}, u32[]{:S(2)}, u32[]{:S(2)}) collective-permute-start(f32[2,64,256]{2,1,0:T(8,128)S(1)} %coarse_first.1.fix.own), channel_id=1, source_target_pairs={{1,2},{3,4},{5,6},{7,8},{9,10},{11,12},{13,14},{17,18},{19,20},{21... | collective-permute-start | bytes 393224 | tf_op jit(solution)/shard_map/ppermute | solution.py:452
  37.9 3.0 %collective-permute-start.9 = (f32[2,64,256]{2,1,0:T(8,128)S(1)}, f32[2,64,256]{2,1,0:T(8,128)S(1)}, u32[]{:S(2)}, u32[]{:S(2)}) collective-permute-start(f32[2,64,256]{2,1,0:T(8,128)S(1)} %coarse_first.1.fix.own), channel_id=1, source_target_pairs={{0,1},{1,0},{2,3},{3,2},{4,5},{5,4},{6,7},{7,6},{8,9},{9,8},{10,11... | collective-permute-start | bytes 393224 | tf_op jit(solution)/shard_map/ppermute | solution.py:455
  38.4 6.4 %collective-permute-start.10 = (f32[2,64,256]{2,1,0:T(8,128)S(1)}, f32[2,64,256]{2,1,0:T(8,128)S(1)}, u32[]{:S(2)}, u32[]{:S(2)}) collective-permute-start(f32[2,64,256]{2,1,0:T(8,128)S(1)} %get-tuple-element.80), channel_id=1, source_target_pairs={{1,2},{3,4},{5,6},{7,8},{9,10},{11,12},{13,14},{17,18},{19,20},{21... | collective-permute-start | bytes 393224 | tf_op jit(solution)/shard_map/ppermute | solution.py:452
  41.0 5.5 %collective-permute-start.11 = (f32[2,64,256]{2,1,0:T(8,128)S(1)}, f32[2,64,256]{2,1,0:T(8,128)S(1)}, u32[]{:S(2)}, u32[]{:S(2)}) collective-permute-start(f32[2,64,256]{2,1,0:T(8,128)S(1)} %coarse_finish.3.fix), channel_id=1, source_target_pairs={{1,2},{3,4},{5,6},{7,8},{9,10},{11,12},{13,14},{17,18},{19,20},{21... | collective-permute-start | bytes 393224 | tf_op jit(solution)/shard_map/ppermute | solution.py:452
  43.4 3.0 %collective-permute-start.12 = (f32[2,64,256]{2,1,0:T(8,128)S(1)}, f32[2,64,256]{2,1,0:T(8,128)S(1)}, u32[]{:S(2)}, u32[]{:S(2)}) collective-permute-start(f32[2,64,256]{2,1,0:T(8,128)S(1)} %coarse_finish.3.fix), channel_id=1, source_target_pairs={{0,1},{1,0},{2,3},{3,2},{4,5},{5,4},{6,7},{7,6},{8,9},{9,8},{10,11... | collective-permute-start | bytes 393224 | tf_op jit(solution)/shard_map/ppermute | solution.py:455
  43.4 7.3 %collective-permute-start.13 = (f32[2,64,256]{2,1,0:T(8,128)S(1)}, f32[2,64,256]{2,1,0:T(8,128)S(1)}, u32[]{:S(2)}, u32[]{:S(2)}) collective-permute-start(f32[2,64,256]{2,1,0:T(8,128)S(1)} %get-tuple-element.82), channel_id=1, source_target_pairs={{1,2},{3,4},{5,6},{7,8},{9,10},{11,12},{13,14},{17,18},{19,20},{21... | collective-permute-start | bytes 393224 | tf_op jit(solution)/shard_map/ppermute | solution.py:452
  46.5 6.6 %collective-permute-start.14 = (f32[2,64,256]{2,1,0:T(8,128)S(1)}, f32[2,64,256]{2,1,0:T(8,128)S(1)}, u32[]{:S(2)}, u32[]{:S(2)}) collective-permute-start(f32[2,64,256]{2,1,0:T(8,128)S(1)} %coarse_finish.4.fix), channel_id=1, source_target_pairs={{1,2},{3,4},{5,6},{7,8},{9,10},{11,12},{13,14},{17,18},{19,20},{21... | collective-permute-start | bytes 393224 | tf_op jit(solution)/shard_map/ppermute | solution.py:452
  50.5 2.7 %collective-permute-start.15 = (f32[2,64,256]{2,1,0:T(8,128)S(1)}, f32[2,64,256]{2,1,0:T(8,128)S(1)}, u32[]{:S(2)}, u32[]{:S(2)}) collective-permute-start(f32[2,64,256]{2,1,0:T(8,128)S(1)} %coarse_finish.4.fix), channel_id=1, source_target_pairs={{0,1},{1,0},{2,3},{3,2},{4,5},{5,4},{6,7},{7,6},{8,9},{9,8},{10,11... | collective-permute-start | bytes 393224 | tf_op jit(solution)/shard_map/ppermute | solution.py:455
  50.5 5.6 %collective-permute-start.19 = (f32[2,64,256]{2,1,0:T(8,128)S(1)}, f32[2,64,256]{2,1,0:T(8,128)S(1)}, u32[]{:S(2)}, u32[]{:S(2)}) collective-permute-start(f32[2,64,256]{2,1,0:T(8,128)S(1)} %get-tuple-element.91), channel_id=1, source_target_pairs={{1,2},{3,4},{5,6},{7,8},{9,10},{11,12},{13,14},{17,18},{19,20},{21... | collective-permute-start | bytes 393224 | tf_op jit(solution)/shard_map/ppermute | solution.py:452
  53.2 5.1 %collective-permute-start.17 = (f32[2,64,256]{2,1,0:T(8,128)S(1)}, f32[2,64,256]{2,1,0:T(8,128)S(1)}, u32[]{:S(2)}, u32[]{:S(2)}) collective-permute-start(f32[2,64,256]{2,1,0:T(8,128)S(1)} %coarse_finish.5.fix), channel_id=1, source_target_pairs={{1,2},{3,4},{5,6},{7,8},{9,10},{11,12},{13,14},{17,18},{19,20},{21... | collective-permute-start | bytes 393224 | tf_op jit(solution)/shard_map/ppermute | solution.py:452
  55.0 3.3 %collective-permute-start.18 = (f32[2,64,256]{2,1,0:T(8,128)S(1)}, f32[2,64,256]{2,1,0:T(8,128)S(1)}, u32[]{:S(2)}, u32[]{:S(2)}) collective-permute-start(f32[2,64,256]{2,1,0:T(8,128)S(1)} %coarse_finish.5.fix), channel_id=1, source_target_pairs={{0,1},{1,0},{2,3},{3,2},{4,5},{5,4},{6,7},{7,6},{8,9},{9,8},{10,11... | collective-permute-start | bytes 393224 | tf_op jit(solution)/shard_map/ppermute | solution.py:455
  58.9 3.6 %collective-permute-start.21 = (f32[2,128,512]{2,1,0:T(8,128)S(1)}, f32[2,128,512]{2,1,0:T(8,128)S(1)}, u32[]{:S(2)}, u32[]{:S(2)}) collective-permute-start(f32[2,128,512]{2,1,0:T(8,128)S(1)} %get-tuple-element.95.refs_1_), channel_id=1, source_target_pairs={{0,1},{1,0},{2,3},{3,2},{4,5},{5,4},{6,7},{7,6},{8,9},{9,8},{10,11... | collective-permute-start | bytes 1572872 | tf_op jit(solution)/shard_map/ppermute | solution.py:455
  58.9 3.5 %copy-start.1 = (f32[2,128,512]{2,1,0:T(8,128)S(1)}, f32[2,128,512]{2,1,0:T(8,128)}, u32[]{:S(2)}) copy-start(f32[2,128,512]{2,1,0:T(8,128)} %psi.3) | copy-start | bytes 1572868
  59.0 14.3 %collective-permute-start.20 = (f32[2,128,512]{2,1,0:T(8,128)S(1)}, f32[2,128,512]{2,1,0:T(8,128)S(1)}, u32[]{:S(2)}, u32[]{:S(2)}) collective-permute-start(f32[2,128,512]{2,1,0:T(8,128)S(1)} %get-tuple-element.94.refs_0_), channel_id=1, source_target_pairs={{1,2},{3,4},{5,6},{7,8},{9,10},{11,12},{13,14},{17,18},{19,20},{21... | collective-permute-start | bytes 1572872 | tf_op jit(solution)/shard_map/ppermute | solution.py:452

commit v7 on v6

--- a/solution.py
+++ b/solution.py
@@ -44,10 +44,6 @@
 
 def early_chunks(rows):
     return [5 * rows // 8, 3 * rows // 8]
-
-
-def late_chunks(rows):
-    return [rows]
 
 
 def call(body, name, outs, args, in_specs=None, out_specs=None, scratch=(), aliases=None, work=30, dtype=F32):
@@ -388,12 +384,18 @@
         )
 
 
-def fix_body(starts, keep, far_part, near_part, far_halo, near_halo, state_nb, pair_t, gain, *refs):
-    count = len(starts)
-    outs, scratch = refs[: count + 1], refs[count + 1 :]
-    for n, (lo, out) in enumerate(zip(starts, outs)):
-        finish_fix_rows(0, lo, keep, far_part, far_halo, pair_t, gain, out, *scratch[2 * n : 2 * n + 2], state_nb)
-    finish_fix_rows(1, 0, keep, near_part, near_halo, pair_t, gain, outs[-1], *scratch[-2:])
+def fix_far_body(keep, part, halo, state_nb, pair_t, gain, out, phase, chem):
+    finish_fix_rows(0, 0, keep, part, halo, pair_t, gain, out, phase, chem, state_nb)
+
+
+def fix_near_body(part, halo, pair_t, gain, out, top, bottom, phase, chem):
+    finish_fix_rows(1, 0, None, part, halo, pair_t, gain, out, phase, chem)
+    n = top.shape[1]
+    for f in range(2):
+        for r in blocks(n):
+            rows = slice(r, r + BLOCK)
+            top[f, rows] = out[f, rows]
+            bottom[f, rows] = out[f, slice(n + r, n + r + BLOCK)]
 
 
 def final_rows(i, lo, where, keep, part, halo, gain, phi, psi, adjoint, design, plane_out, grad_out, sems):
@@ -537,14 +539,14 @@
     far_part, near_part = run(third_body, "third", [full, full], args, scratch=scratch)
     plane_sums, far_part = after(plane_sums, far_part)
     state_nb = run(rebuild_body, "rebuild", [full], (plane_sums, *arrived, even_t, odd_t), scratch=[tile] * 2)[0]
-    sizes = late_chunks(rows)
-    starts = [sum(sizes[:n]) for n in range(len(sizes))]
-    args = (keep, far_part, near_part, far_sums, near_sums, state_nb, pair_t, *coefs)
-    shapes = [(2, n, cols) for n in sizes]
-    scratch = [v for n in [*sizes, rows] for v in [tiles(n, cols)] * 2]
-    *far, near = run(fix_body, "fix", [*shapes, full], args, (starts,), smem=1, scratch=scratch, work=8)
-
-    far_halo, near_halo = [swap_far(v) for v in far], swap_near(near)
+    args = (keep, far_part, far_sums, state_nb, pair_t, *coefs)
+    far = run(fix_far_body, "fix_far", [full], args, smem=1, scratch=[tile] * 2, work=8)
+    starts = [0]
+    top = (2, rows // 2, cols)
+    args = (near_part, near_sums, pair_t, *coefs)
+    near, *near_chunks = run(fix_near_body, "fix_near", [full, top, top], args, scratch=[tile] * 2, work=8)
+
+    far_halo, near_halos = [swap_far(v) for v in far], [swap_near(v) for v in near_chunks]
     far_part, near_part = run(part_body, "part", [full] * 2, (*far, near, *coefs, own), (len(far),), scratch=[whole])
     outs = [(2, 2, rows, cols), full]
 
@@ -562,7 +564,8 @@
     done = ()
     for lo, halo in zip(starts[:-1], far_halo[:-1]):
         done = final([(0, lo)], (far_part, halo), done)
-    done = final([(1, 0)], (near_part, near_halo), done)
+    fields = (near_part, near_halos[0], near_part, near_halos[1])
+    done = final([(1, 0), (1, rows // 2)], fields, done)
     done = final([(0, starts[-1])], (far_part, far_halo[-1]), done)
     return tuple(done)
 

time: 74.7 us -> 73.8 us (0.988)
  waiting for transfers between devices: 35.7 us -> 34.5 us
    ppermute x13, waiting for transfers between devices: 35.6 us -> 32.7 us  [swap_far(): return lax.ppermute(x, ('grp', 'gx'), across)]
    ppermute x9 -> x10, waiting for transfers between devices: 0.02 us -> 1.81 us  [swap_near(): return lax.ppermute(x, 'gx', on_chip)]
    pallas_call x27 -> x28, Pallas kernels: 12.6 us -> 12.7 us  [call(): pl.pallas_call(body, out_shape=shapes, in_specs=in_specs or [VMEM] * len(...]
  transfers between devices with their start and end apart: 22 -> 23, of which waited for: 9 -> 12; matrix products, arithmetic and copies ran while one was open for 0% -> 0% of each run, Pallas kernels for 13% -> 14%
where the time goes in v7:
time: 73.8 us; the launch traced here: 73.6 us
  waiting for transfers between devices  34.5 us (47%)
  starting transfers between devices  24.3 us (33%)
  Pallas kernels  12.7 us (17%)
  local copies, waits for them, and re-layouts  1.23 us (2%)
  between operations  0.9 us (1%)
    ppermute x13, waiting for transfers between devices, swap_far(): return lax.ppermute(x, ('grp', 'gx'), across)  32.7 us
    ppermute x13, starting transfers between devices, swap_far(): return lax.ppermute(x, ('grp', 'gx'), across)  22.9 us
    pallas_call x28, Pallas kernels, call(): pl.pallas_call(body, out_shape=shapes, in_specs=in_specs or [VMEM] * len(...  12.7 us
    ppermute x10, waiting for transfers between devices, swap_near(): return lax.ppermute(x, 'gx', on_chip)  1.81 us
  transfers between devices with their start and end apart: 23, of which 12 were waited for; matrix products, arithmetic and copies ran while one was open for 0% of the time, Pallas kernels for 14%

profile of v7, /device:TPU:1, one launch (start us, length us, event | category | flops | bytes accessed | tf_op | source)
XLA Modules:
  0.0 73.6 jit_solution(12868505360693707776)
XLA Ops:
  0.7 1.3 %take.1 = (f32[2,80,512]{2,1,0:T(8,128)S(1)}, f32[2,48,512]{2,1,0:T(8,128)S(1)}, f32[2,128,512]{2,1,0:T(8,128)S(1)}) custom-call(s32[1]{0:T(128)} %bitcast.where, f32[2,2,128,512]{3,2,1,0:T(8,128)} %warm.1), custom_call_target="tpu_custom_call" | custom-call | bytes 2097156 | tf_op jit(solution)/shard_map/take/pallas_call | solution.py:53
  2.0 0.1 collective-permute-start.1
  2.1 2.6 %collective-permute-start.2 = (f32[2,48,512]{2,1,0:T(8,128)S(1)}, f32[2,48,512]{2,1,0:T(8,128)S(1)}, u32[]{:S(2)}, u32[]{:S(2)}) collective-permute-start(f32[2,48,512]{2,1,0:T(8,128)S(1)} %get-tuple-element.54.refs_1_), channel_id=1, source_target_pairs={{1,2},{3,4},{5,6},{7,8},{9,10},{11,12},{13,14},{17,18},{19,20},{21... | collective-permute-start | bytes 589832 | tf_op jit(solution)/shard_map/ppermute | solution.py:454
  4.8 0.1 collective-permute-start
  4.8 1.2 %copy-done.2 = f32[2,2,128,512]{3,2,1,0:T(8,128)S(1)} copy-done((f32[2,2,128,512]{3,2,1,0:T(8,128)S(1)}, f32[2,2,128,512]{3,2,1,0:T(8,128)}, u32[]{:S(2)}) %copy-start.2) | copy-done | bytes 1048600
  6.1 0.2 setup.1
  6.3 0.9 %part.3 = (f32[2,128,512]{2,1,0:T(8,128)S(1)}, f32[2,128,512]{2,1,0:T(8,128)S(1)}) custom-call(f32[2,80,512]{2,1,0:T(8,128)S(1)} %get-tuple-element.53.refs_0_, f32[2,48,512]{2,1,0:T(8,128)S(1)} %get-tuple-element.54.refs_1_, f32[2,128,512]{2,1,0:T(8,128)S(1)} %get-tuple-element.55.refs_2_, f32[2,128,512]{2,1,0:T(8,128)S(1)} %get-tuple-element.52.refs_3_.gain.refs_2_, ...), custom_call_target="tpu_custom_call" | custom-call | bytes 3670016 | tf_op jit(solution)/shard_map/part/pallas_call | solution.py:53
  7.3 5.7 %collective-permute-done.2.halo = f32[2,48,512]{2,1,0:T(8,128)S(1)} collective-permute-done((f32[2,48,512]{2,1,0:T(8,128)S(1)}, f32[2,48,512]{2,1,0:T(8,128)S(1)}, u32[]{:S(2)}, u32[]{:S(2)}) %collective-permute-start.2) | collective-permute-done | bytes 196640 | tf_op jit(solution)/shard_map/ppermute | solution.py:454
  13.0 0.1 finish.5.refs_2_
  13.2 0.1 collective-permute-start.6
  13.2 3.3 %collective-permute-done.halo = f32[2,80,512]{2,1,0:T(8,128)S(1)} collective-permute-done((f32[2,80,512]{2,1,0:T(8,128)S(1)}, f32[2,80,512]{2,1,0:T(8,128)S(1)}, u32[]{:S(2)}, u32[]{:S(2)}) %collective-permute-start) | collective-permute-done | bytes 327712 | tf_op jit(solution)/shard_map/ppermute | solution.py:454
  16.5 0.1 finish.3.refs_0_
  16.6 2.5 %collective-permute-start.4 = (f32[2,80,512]{2,1,0:T(8,128)S(1)}, f32[2,80,512]{2,1,0:T(8,128)S(1)}, u32[]{:S(2)}, u32[]{:S(2)}) collective-permute-start(f32[2,80,512]{2,1,0:T(8,128)S(1)} %finish.3.refs_0_), channel_id=1, source_target_pairs={{1,2},{3,4},{5,6},{7,8},{9,10},{11,12},{13,14},{17,18},{19,20},{21... | collective-permute-start | bytes 983048 | tf_op jit(solution)/shard_map/ppermute | solution.py:454
  19.1 0.1 collective-permute-start.3
  19.2 0.9 %part.4 = (f32[2,128,512]{2,1,0:T(8,128)S(1)}, f32[2,128,512]{2,1,0:T(8,128)S(1)}) custom-call(f32[2,80,512]{2,1,0:T(8,128)S(1)} %finish.3.refs_0_, f32[2,48,512]{2,1,0:T(8,128)S(1)} %finish.4.refs_1_, f32[2,128,512]{2,1,0:T(8,128)S(1)} %finish.5.refs_2_, f32[2,128,512]{2,1,0:T(8,128)S(1)} %get-tuple-element.52.refs_3_.gain.refs_2_, ...), custom_call_target="tpu_custom_call" | custom-call | bytes 3670016 | tf_op jit(solution)/shard_map/part/pallas_call | solution.py:53
  20.1 0.1 matrices.1
  20.2 6.8 %collective-permute-done.4.halo = f32[2,80,512]{2,1,0:T(8,128)S(1)} collective-permute-done((f32[2,80,512]{2,1,0:T(8,128)S(1)}, f32[2,80,512]{2,1,0:T(8,128)S(1)}, u32[]{:S(2)}, u32[]{:S(2)}) %collective-permute-start.4) | collective-permute-done | bytes 327712 | tf_op jit(solution)/shard_map/ppermute | solution.py:454
  27.1 0.3 finish_pool.3
  27.4 3.2 %collective-permute-done.3.halo = f32[2,48,512]{2,1,0:T(8,128)S(1)} collective-permute-done((f32[2,48,512]{2,1,0:T(8,128)S(1)}, f32[2,48,512]{2,1,0:T(8,128)S(1)}, u32[]{:S(2)}, u32[]{:S(2)}) %collective-permute-start.3) | collective-permute-done | bytes 196640 | tf_op jit(solution)/shard_map/ppermute | solution.py:454
  30.6 0.2 finish_pool.4
  30.8 2.5 %collective-permute-start.5 = (f32[2,64,256]{2,1,0:T(8,128)S(1)}, f32[2,64,256]{2,1,0:T(8,128)S(1)}, u32[]{:S(2)}, u32[]{:S(2)}) collective-permute-start(f32[2,64,256]{2,1,0:T(8,128)S(1)} %get-tuple-element.66), channel_id=1, source_target_pairs={{1,2},{3,4},{5,6},{7,8},{9,10},{11,12},{13,14},{17,18},{19,20},{21... | collective-permute-start | bytes 393224 | tf_op jit(solution)/shard_map/ppermute | solution.py:454
  33.4 0.0 collective-permute-done.6.halo
  33.4 0.4 finish_pool.5
  33.7 0.1 collective-permute-start.7
  33.8 0.3 coarse_setup.1.gain
  34.1 0.6 collective-permute-start.16
  34.7 1.5 %part_defect.1 = (f32[2,128,512]{2,1,0:T(8,128)S(1)}, f32[2,128,512]{2,1,0:T(8,128)S(1)}, f32[2,64,256]{2,1,0:T(8,128)S(1)}) custom-call(f32[2,80,512]{2,1,0:T(8,128)S(1)} %get-tuple-element.67.refs_0_, f32[2,48,512]{2,1,0:T(8,128)S(1)} %get-tuple-element.68.refs_1_, f32[2,128,512]{2,1,0:T(8,128)S(1)} %get-tuple-element.70.refs_2_, ...), custom_call_target="tpu_custom_call" | custom-call | bytes 3932160 | tf_op jit(solution)/shard_map/part_defect/pallas_call | solution.py:53
  36.2 0.0 collective-permute-done.7.near
  36.2 1.6 %collective-permute-start.8 = (f32[2,64,256]{2,1,0:T(8,128)S(1)}, f32[2,64,256]{2,1,0:T(8,128)S(1)}, u32[]{:S(2)}, u32[]{:S(2)}) collective-permute-start(f32[2,64,256]{2,1,0:T(8,128)S(1)} %coarse_first.1.fix.own), channel_id=1, source_target_pairs={{1,2},{3,4},{5,6},{7,8},{9,10},{11,12},{13,14},{17,18},{19,20},{21... | collective-permute-start | bytes 393224 | tf_op jit(solution)/shard_map/ppermute | solution.py:454
  37.9 0.0 collective-permute-start.9
  37.9 0.5 three.1
  38.4 1.3 %collective-permute-start.10 = (f32[2,64,256]{2,1,0:T(8,128)S(1)}, f32[2,64,256]{2,1,0:T(8,128)S(1)}, u32[]{:S(2)}, u32[]{:S(2)}) collective-permute-start(f32[2,64,256]{2,1,0:T(8,128)S(1)} %get-tuple-element.81), channel_id=1, source_target_pairs={{1,2},{3,4},{5,6},{7,8},{9,10},{11,12},{13,14},{17,18},{19,20},{21... | collective-permute-start | bytes 393224 | tf_op jit(solution)/shard_map/ppermute | solution.py:454
  39.6 0.1 coarse_part.3.part
  39.8 1.1 %collective-permute-done.8.far = f32[2,64,256]{2,1,0:T(8,128)S(1)} collective-permute-done((f32[2,64,256]{2,1,0:T(8,128)S(1)}, f32[2,64,256]{2,1,0:T(8,128)S(1)}, u32[]{:S(2)}, u32[]{:S(2)}) %collective-permute-start.8) | collective-permute-done | bytes 131104 | tf_op jit(solution)/shard_map/ppermute | solution.py:454
  40.9 0.0 collective-permute-done.9.near
  41.0 2.5 %collective-permute-start.11 = (f32[2,64,256]{2,1,0:T(8,128)S(1)}, f32[2,64,256]{2,1,0:T(8,128)S(1)}, u32[]{:S(2)}, u32[]{:S(2)}) collective-permute-start(f32[2,64,256]{2,1,0:T(8,128)S(1)} %coarse_finish.3.fix), channel_id=1, source_target_pairs={{1,2},{3,4},{5,6},{7,8},{9,10},{11,12},{13,14},{17,18},{19,20},{21... | collective-permute-start | bytes 393224 | tf_op jit(solution)/shard_map/ppermute | solution.py:454
  43.4 0.0 collective-permute-start.12
  43.4 1.2 %collective-permute-start.13 = (f32[2,64,256]{2,1,0:T(8,128)S(1)}, f32[2,64,256]{2,1,0:T(8,128)S(1)}, u32[]{:S(2)}, u32[]{:S(2)}) collective-permute-start(f32[2,64,256]{2,1,0:T(8,128)S(1)} %get-tuple-element.83), channel_id=1, source_target_pairs={{1,2},{3,4},{5,6},{7,8},{9,10},{11,12},{13,14},{17,18},{19,20},{21... | collective-permute-start | bytes 393224 | tf_op jit(solution)/shard_map/ppermute | solution.py:454
  44.6 0.2 coarse_part.4.part
  44.8 1.7 %collective-permute-done.11.far = f32[2,64,256]{2,1,0:T(8,128)S(1)} collective-permute-done((f32[2,64,256]{2,1,0:T(8,128)S(1)}, f32[2,64,256]{2,1,0:T(8,128)S(1)}, u32[]{:S(2)}, u32[]{:S(2)}) %collective-permute-start.11) | collective-permute-done | bytes 131104 | tf_op jit(solution)/shard_map/ppermute | solution.py:454
  46.5 3.9 %collective-permute-start.14 = (f32[2,64,256]{2,1,0:T(8,128)S(1)}, f32[2,64,256]{2,1,0:T(8,128)S(1)}, u32[]{:S(2)}, u32[]{:S(2)}) collective-permute-start(f32[2,64,256]{2,1,0:T(8,128)S(1)} %coarse_finish.4.fix), channel_id=1, source_target_pairs={{1,2},{3,4},{5,6},{7,8},{9,10},{11,12},{13,14},{17,18},{19,20},{21... | collective-permute-start | bytes 393224 | tf_op jit(solution)/shard_map/ppermute | solution.py:454
  50.5 0.0 collective-permute-start.15
  50.5 0.2 collective-permute-start.18
  50.6 0.2 coarse_part.5.part
  50.8 2.3 %collective-permute-done.14.far = f32[2,64,256]{2,1,0:T(8,128)S(1)} collective-permute-done((f32[2,64,256]{2,1,0:T(8,128)S(1)}, f32[2,64,256]{2,1,0:T(8,128)S(1)}, u32[]{:S(2)}, u32[]{:S(2)}) %collective-permute-start.14) | collective-permute-done | bytes 131104 | tf_op jit(solution)/shard_map/ppermute | solution.py:454
  53.1 0.0 collective-permute-done.15.near
  53.2 1.8 %collective-permute-start.17 = (f32[2,64,256]{2,1,0:T(8,128)S(1)}, f32[2,64,256]{2,1,0:T(8,128)S(1)}, u32[]{:S(2)}, u32[]{:S(2)}) collective-permute-start(f32[2,64,256]{2,1,0:T(8,128)S(1)} %coarse_finish.5.fix), channel_id=1, source_target_pairs={{1,2},{3,4},{5,6},{7,8},{9,10},{11,12},{13,14},{17,18},{19,20},{21... | collective-permute-start | bytes 393224 | tf_op jit(solution)/shard_map/ppermute | solution.py:454
  55.0 1.0 %third.1 = (f32[2,128,512]{2,1,0:T(8,128)S(1)}, f32[2,128,512]{2,1,0:T(8,128)S(1)}) custom-call(f32[2,128,512]{2,1,0:T(8,128)S(1)} %get-tuple-element.71.far, f32[2,128,512]{2,1,0:T(8,128)S(1)} %get-tuple-element.72.near, f32[2,64,256]{2,1,0:T(8,128)S(1)} %coarse_finish.5.fix, f32[2,128,512]{2,1,0:T(8,128)S(1)} %collective-permute-done.16.near_halo, ...), custom_call_target="tpu_custom_call" | custom-call | bytes 3407872 | tf_op jit(solution)/shard_map/third/pallas_call | solution.py:53
  56.0 0.0 collective-permute-done.18.refs_2_
  56.0 0.6 rebuild.1.state_nb
  56.6 1.7 %collective-permute-done.17.halo = f32[2,64,256]{2,1,0:T(8,128)S(1)} collective-permute-done((f32[2,64,256]{2,1,0:T(8,128)S(1)}, f32[2,64,256]{2,1,0:T(8,128)S(1)}, u32[]{:S(2)}, u32[]{:S(2)}) %collective-permute-start.17) | collective-permute-done | bytes 131104 | tf_op jit(solution)/shard_map/ppermute | solution.py:454
  58.3 0.3 fix_far.1.refs_0_
  58.6 2.5 %collective-permute-start.20 = (f32[2,128,512]{2,1,0:T(8,128)S(1)}, f32[2,128,512]{2,1,0:T(8,128)S(1)}, u32[]{:S(2)}, u32[]{:S(2)}) collective-permute-start(f32[2,128,512]{2,1,0:T(8,128)S(1)} %fix_far.1.refs_0_), channel_id=1, source_target_pairs={{1,2},{3,4},{5,6},{7,8},{9,10},{11,12},{13,14},{17,18},{19,20},{21... | collective-permute-start | bytes 1572872 | tf_op jit(solution)/shard_map/ppermute | solution.py:454
  61.2 0.0 collective-permute-start.19
  61.2 1.3 %collective-permute-done.19.halo = f32[2,64,256]{2,1,0:T(8,128)S(1)} collective-permute-done((f32[2,64,256]{2,1,0:T(8,128)S(1)}, f32[2,64,256]{2,1,0:T(8,128)S(1)}, u32[]{:S(2)}, u32[]{:S(2)}) %collective-permute-start.19) | collective-permute-done | bytes 131104 | tf_op jit(solution)/shard_map/ppermute | solution.py:457
  62.5 0.3 fix_near.1
  62.9 0.2 collective-permute-start.21
  63.1 0.4 collective-permute-start.22
  63.4 0.9 %part.5 = (f32[2,128,512]{2,1,0:T(8,128)S(1)}, f32[2,128,512]{2,1,0:T(8,128)S(1)}) custom-call(f32[2,128,512]{2,1,0:T(8,128)S(1)} %fix_far.1.refs_0_, f32[2,128,512]{2,1,0:T(8,128)S(1)} %get-tuple-element.95.refs_1_, f32[2,128,512]{2,1,0:T(8,128)S(1)} %get-tuple-element.52.refs_3_.gain.refs_2_, f32[2,2,128,512]{3,2,1,0:T(8,128)S(1)} %get-tuple-element.56.refs_4_.refs_3_), custom_call_target="tpu_custom_call" | custom-call | bytes 3670016 | tf_op jit(solution)/shard_map/part/pallas_call | solution.py:53
  64.4 0.1 collective-permute-done.21.refs_1_
  64.5 0.4 collective-permute-done.22.refs_3_
  64.8 1.0 %final.2 = (f32[2,2,128,512]{3,2,1,0:T(8,128)}, f32[2,128,512]{2,1,0:T(8,128)}) custom-call(s32[1]{0:T(128)} %bitcast.where, f32[1]{0:T(128)} %bitcast.1.keep, f32[2,128,512]{2,1,0:T(8,128)S(1)} %get-tuple-element.52.refs_3_.gain.refs_2_, f32[2,128,512]{2,1,0:T(8,128)S(1)} %copy-done, f32[2,128,512]{2,1,0:T(8,128)S(1)} %copy-done.1, ...), custom_call_target="tpu_custom_call" | custom-call | bytes 4718600 | tf_op jit(solution)/shard_map/final/pallas_call | solution.py:53
  65.8 6.9 %collective-permute-done.20.refs_1_ = f32[2,128,512]{2,1,0:T(8,128)S(1)} collective-permute-done((f32[2,128,512]{2,1,0:T(8,128)S(1)}, f32[2,128,512]{2,1,0:T(8,128)S(1)}, u32[]{:S(2)}, u32[]{:S(2)}) %collective-permute-start.20) | collective-permute-done | bytes 524320 | tf_op jit(solution)/shard_map/ppermute | solution.py:454
  72.7 1.0 %final.3 = (f32[2,2,128,512]{3,2,1,0:T(8,128)}, f32[2,128,512]{2,1,0:T(8,128)}) custom-call(s32[1]{0:T(128)} %bitcast.where, f32[1]{0:T(128)} %bitcast.1.keep, f32[2,128,512]{2,1,0:T(8,128)S(1)} %get-tuple-element.52.refs_3_.gain.refs_2_, f32[2,128,512]{2,1,0:T(8,128)S(1)} %copy-done, ...), custom_call_target="tpu_custom_call", output_to_operand_aliasing={{0}: (7, {}), {1}: (8, {})} | custom-call | bytes 5767176 | tf_op jit(solution)/shard_map/final/pallas_call | solution.py:53
  (16 shorter events, 0.3 us)
Async XLA Ops:
  0.6 4.2 %copy-start = (f32[2,128,512]{2,1,0:T(8,128)S(1)}, f32[2,128,512]{2,1,0:T(8,128)}, u32[]{:S(2)}) copy-start(f32[2,128,512]{2,1,0:T(8,128)} %phi.7) | copy-start | bytes 1572868
  2.0 11.1 %collective-permute-start.1 = (f32[2,128,512]{2,1,0:T(8,128)S(1)}, f32[2,128,512]{2,1,0:T(8,128)S(1)}, u32[]{:S(2)}, u32[]{:S(2)}) collective-permute-start(f32[2,128,512]{2,1,0:T(8,128)S(1)} %get-tuple-element.55.refs_2_), channel_id=1, source_target_pairs={{0,1},{1,0},{2,3},{3,2},{4,5},{5,4},{6,7},{7,6},{8,9},{9,8},{10,11... | collective-permute-start | bytes 1572872 | tf_op jit(solution)/shard_map/ppermute | solution.py:457
  2.1 10.9 %collective-permute-start.2 = (f32[2,48,512]{2,1,0:T(8,128)S(1)}, f32[2,48,512]{2,1,0:T(8,128)S(1)}, u32[]{:S(2)}, u32[]{:S(2)}) collective-permute-start(f32[2,48,512]{2,1,0:T(8,128)S(1)} %get-tuple-element.54.refs_1_), channel_id=1, source_target_pairs={{1,2},{3,4},{5,6},{7,8},{9,10},{11,12},{13,14},{17,18},{19,20},{21... | collective-permute-start | bytes 589832 | tf_op jit(solution)/shard_map/ppermute | solution.py:454
  4.8 11.7 %collective-permute-start = (f32[2,80,512]{2,1,0:T(8,128)S(1)}, f32[2,80,512]{2,1,0:T(8,128)S(1)}, u32[]{:S(2)}, u32[]{:S(2)}) collective-permute-start(f32[2,80,512]{2,1,0:T(8,128)S(1)} %get-tuple-element.53.refs_0_), channel_id=1, source_target_pairs={{1,2},{3,4},{5,6},{7,8},{9,10},{11,12},{13,14},{17,18},{19,20},{21... | collective-permute-start | bytes 983048 | tf_op jit(solution)/shard_map/ppermute | solution.py:454
  4.8 1.2 %copy-start.2 = (f32[2,2,128,512]{3,2,1,0:T(8,128)S(1)}, f32[2,2,128,512]{3,2,1,0:T(8,128)}, u32[]{:S(2)}) copy-start(f32[2,2,128,512]{3,2,1,0:T(8,128)} %cot.1) | copy-start | bytes 3145732
  13.2 20.2 %collective-permute-start.6 = (f32[2,128,512]{2,1,0:T(8,128)S(1)}, f32[2,128,512]{2,1,0:T(8,128)S(1)}, u32[]{:S(2)}, u32[]{:S(2)}) collective-permute-start(f32[2,128,512]{2,1,0:T(8,128)S(1)} %finish.5.refs_2_), channel_id=1, source_target_pairs={{0,1},{1,0},{2,3},{3,2},{4,5},{5,4},{6,7},{7,6},{8,9},{9,8},{10,11... | collective-permute-start | bytes 1572872 | tf_op jit(solution)/shard_map/ppermute | solution.py:457
  16.6 10.5 %collective-permute-start.4 = (f32[2,80,512]{2,1,0:T(8,128)S(1)}, f32[2,80,512]{2,1,0:T(8,128)S(1)}, u32[]{:S(2)}, u32[]{:S(2)}) collective-permute-start(f32[2,80,512]{2,1,0:T(8,128)S(1)} %finish.3.refs_0_), channel_id=1, source_target_pairs={{1,2},{3,4},{5,6},{7,8},{9,10},{11,12},{13,14},{17,18},{19,20},{21... | collective-permute-start | bytes 983048 | tf_op jit(solution)/shard_map/ppermute | solution.py:454
  19.1 11.5 %collective-permute-start.3 = (f32[2,48,512]{2,1,0:T(8,128)S(1)}, f32[2,48,512]{2,1,0:T(8,128)S(1)}, u32[]{:S(2)}, u32[]{:S(2)}) collective-permute-start(f32[2,48,512]{2,1,0:T(8,128)S(1)} %finish.4.refs_1_), channel_id=1, source_target_pairs={{1,2},{3,4},{5,6},{7,8},{9,10},{11,12},{13,14},{17,18},{19,20},{21... | collective-permute-start | bytes 589832 | tf_op jit(solution)/shard_map/ppermute | solution.py:454
  30.8 5.4 %collective-permute-start.5 = (f32[2,64,256]{2,1,0:T(8,128)S(1)}, f32[2,64,256]{2,1,0:T(8,128)S(1)}, u32[]{:S(2)}, u32[]{:S(2)}) collective-permute-start(f32[2,64,256]{2,1,0:T(8,128)S(1)} %get-tuple-element.66), channel_id=1, source_target_pairs={{1,2},{3,4},{5,6},{7,8},{9,10},{11,12},{13,14},{17,18},{19,20},{21... | collective-permute-start | bytes 393224 | tf_op jit(solution)/shard_map/ppermute | solution.py:454
  33.7 2.5 %collective-permute-start.7 = (f32[2,64,256]{2,1,0:T(8,128)S(1)}, f32[2,64,256]{2,1,0:T(8,128)S(1)}, u32[]{:S(2)}, u32[]{:S(2)}) collective-permute-start(f32[2,64,256]{2,1,0:T(8,128)S(1)} %get-tuple-element.74), channel_id=1, source_target_pairs={{0,1},{1,0},{2,3},{3,2},{4,5},{5,4},{6,7},{7,6},{8,9},{9,8},{10,11... | collective-permute-start | bytes 393224 | tf_op jit(solution)/shard_map/ppermute | solution.py:457
  34.1 20.9 %collective-permute-start.16 = (f32[2,128,512]{2,1,0:T(8,128)S(1)}, f32[2,128,512]{2,1,0:T(8,128)S(1)}, u32[]{:S(2)}, u32[]{:S(2)}) collective-permute-start(f32[2,128,512]{2,1,0:T(8,128)S(1)} %get-tuple-element.70.refs_2_), channel_id=1, source_target_pairs={{0,1},{1,0},{2,3},{3,2},{4,5},{5,4},{6,7},{7,6},{8,9},{9,8},{10,11... | collective-permute-start | bytes 1572872 | tf_op jit(solution)/shard_map/ppermute | solution.py:457
  36.2 4.7 %collective-permute-start.8 = (f32[2,64,256]{2,1,0:T(8,128)S(1)}, f32[2,64,256]{2,1,0:T(8,128)S(1)}, u32[]{:S(2)}, u32[]{:S(2)}) collective-permute-start(f32[2,64,256]{2,1,0:T(8,128)S(1)} %coarse_first.1.fix.own), channel_id=1, source_target_pairs={{1,2},{3,4},{5,6},{7,8},{9,10},{11,12},{13,14},{17,18},{19,20},{21... | collective-permute-start | bytes 393224 | tf_op jit(solution)/shard_map/ppermute | solution.py:454
  37.9 3.0 %collective-permute-start.9 = (f32[2,64,256]{2,1,0:T(8,128)S(1)}, f32[2,64,256]{2,1,0:T(8,128)S(1)}, u32[]{:S(2)}, u32[]{:S(2)}) collective-permute-start(f32[2,64,256]{2,1,0:T(8,128)S(1)} %coarse_first.1.fix.own), channel_id=1, source_target_pairs={{0,1},{1,0},{2,3},{3,2},{4,5},{5,4},{6,7},{7,6},{8,9},{9,8},{10,11... | collective-permute-start | bytes 393224 | tf_op jit(solution)/shard_map/ppermute | solution.py:457
  38.4 6.4 %collective-permute-start.10 = (f32[2,64,256]{2,1,0:T(8,128)S(1)}, f32[2,64,256]{2,1,0:T(8,128)S(1)}, u32[]{:S(2)}, u32[]{:S(2)}) collective-permute-start(f32[2,64,256]{2,1,0:T(8,128)S(1)} %get-tuple-element.81), channel_id=1, source_target_pairs={{1,2},{3,4},{5,6},{7,8},{9,10},{11,12},{13,14},{17,18},{19,20},{21... | collective-permute-start | bytes 393224 | tf_op jit(solution)/shard_map/ppermute | solution.py:454
  41.0 5.5 %collective-permute-start.11 = (f32[2,64,256]{2,1,0:T(8,128)S(1)}, f32[2,64,256]{2,1,0:T(8,128)S(1)}, u32[]{:S(2)}, u32[]{:S(2)}) collective-permute-start(f32[2,64,256]{2,1,0:T(8,128)S(1)} %coarse_finish.3.fix), channel_id=1, source_target_pairs={{1,2},{3,4},{5,6},{7,8},{9,10},{11,12},{13,14},{17,18},{19,20},{21... | collective-permute-start | bytes 393224 | tf_op jit(solution)/shard_map/ppermute | solution.py:454
  43.4 3.0 %collective-permute-start.12 = (f32[2,64,256]{2,1,0:T(8,128)S(1)}, f32[2,64,256]{2,1,0:T(8,128)S(1)}, u32[]{:S(2)}, u32[]{:S(2)}) collective-permute-start(f32[2,64,256]{2,1,0:T(8,128)S(1)} %coarse_finish.3.fix), channel_id=1, source_target_pairs={{0,1},{1,0},{2,3},{3,2},{4,5},{5,4},{6,7},{7,6},{8,9},{9,8},{10,11... | collective-permute-start | bytes 393224 | tf_op jit(solution)/shard_map/ppermute | solution.py:457
  43.4 7.3 %collective-permute-start.13 = (f32[2,64,256]{2,1,0:T(8,128)S(1)}, f32[2,64,256]{2,1,0:T(8,128)S(1)}, u32[]{:S(2)}, u32[]{:S(2)}) collective-permute-start(f32[2,64,256]{2,1,0:T(8,128)S(1)} %get-tuple-element.83), channel_id=1, source_target_pairs={{1,2},{3,4},{5,6},{7,8},{9,10},{11,12},{13,14},{17,18},{19,20},{21... | collective-permute-start | bytes 393224 | tf_op jit(solution)/shard_map/ppermute | solution.py:454
  46.5 6.6 %collective-permute-start.14 = (f32[2,64,256]{2,1,0:T(8,128)S(1)}, f32[2,64,256]{2,1,0:T(8,128)S(1)}, u32[]{:S(2)}, u32[]{:S(2)}) collective-permute-start(f32[2,64,256]{2,1,0:T(8,128)S(1)} %coarse_finish.4.fix), channel_id=1, source_target_pairs={{1,2},{3,4},{5,6},{7,8},{9,10},{11,12},{13,14},{17,18},{19,20},{21... | collective-permute-start | bytes 393224 | tf_op jit(solution)/shard_map/ppermute | solution.py:454
  50.5 2.7 %collective-permute-start.15 = (f32[2,64,256]{2,1,0:T(8,128)S(1)}, f32[2,64,256]{2,1,0:T(8,128)S(1)}, u32[]{:S(2)}, u32[]{:S(2)}) collective-permute-start(f32[2,64,256]{2,1,0:T(8,128)S(1)} %coarse_finish.4.fix), channel_id=1, source_target_pairs={{0,1},{1,0},{2,3},{3,2},{4,5},{5,4},{6,7},{7,6},{8,9},{9,8},{10,11... | collective-permute-start | bytes 393224 | tf_op jit(solution)/shard_map/ppermute | solution.py:457
  50.5 5.6 %collective-permute-start.18 = (f32[2,64,256]{2,1,0:T(8,128)S(1)}, f32[2,64,256]{2,1,0:T(8,128)S(1)}, u32[]{:S(2)}, u32[]{:S(2)}) collective-permute-start(f32[2,64,256]{2,1,0:T(8,128)S(1)} %get-tuple-element.91), channel_id=1, source_target_pairs={{1,2},{3,4},{5,6},{7,8},{9,10},{11,12},{13,14},{17,18},{19,20},{21... | collective-permute-start | bytes 393224 | tf_op jit(solution)/shard_map/ppermute | solution.py:454
  53.2 5.1 %collective-permute-start.17 = (f32[2,64,256]{2,1,0:T(8,128)S(1)}, f32[2,64,256]{2,1,0:T(8,128)S(1)}, u32[]{:S(2)}, u32[]{:S(2)}) collective-permute-start(f32[2,64,256]{2,1,0:T(8,128)S(1)} %coarse_finish.5.fix), channel_id=1, source_target_pairs={{1,2},{3,4},{5,6},{7,8},{9,10},{11,12},{13,14},{17,18},{19,20},{21... | collective-permute-start | bytes 393224 | tf_op jit(solution)/shard_map/ppermute | solution.py:454
  58.6 14.0 %collective-permute-start.20 = (f32[2,128,512]{2,1,0:T(8,128)S(1)}, f32[2,128,512]{2,1,0:T(8,128)S(1)}, u32[]{:S(2)}, u32[]{:S(2)}) collective-permute-start(f32[2,128,512]{2,1,0:T(8,128)S(1)} %fix_far.1.refs_0_), channel_id=1, source_target_pairs={{1,2},{3,4},{5,6},{7,8},{9,10},{11,12},{13,14},{17,18},{19,20},{21... | collective-permute-start | bytes 1572872 | tf_op jit(solution)/shard_map/ppermute | solution.py:454
  61.2 1.3 %collective-permute-start.19 = (f32[2,64,256]{2,1,0:T(8,128)S(1)}, f32[2,64,256]{2,1,0:T(8,128)S(1)}, u32[]{:S(2)}, u32[]{:S(2)}) collective-permute-start(f32[2,64,256]{2,1,0:T(8,128)S(1)} %coarse_finish.5.fix), channel_id=1, source_target_pairs={{0,1},{1,0},{2,3},{3,2},{4,5},{5,4},{6,7},{7,6},{8,9},{9,8},{10,11... | collective-permute-start | bytes 393224 | tf_op jit(solution)/shard_map/ppermute | solution.py:457
  62.9 1.6 %collective-permute-start.21 = (f32[2,64,512]{2,1,0:T(8,128)S(1)}, f32[2,64,512]{2,1,0:T(8,128)S(1)}, u32[]{:S(2)}, u32[]{:S(2)}) collective-permute-start(f32[2,64,512]{2,1,0:T(8,128)S(1)} %get-tuple-element.98), channel_id=1, source_target_pairs={{0,1},{1,0},{2,3},{3,2},{4,5},{5,4},{6,7},{7,6},{8,9},{9,8},{10,11... | collective-permute-start | bytes 786440 | tf_op jit(solution)/shard_map/ppermute | solution.py:457
  63.1 1.8 %collective-permute-start.22 = (f32[2,64,512]{2,1,0:T(8,128)S(1)}, f32[2,64,512]{2,1,0:T(8,128)S(1)}, u32[]{:S(2)}, u32[]{:S(2)}) collective-permute-start(f32[2,64,512]{2,1,0:T(8,128)S(1)} %get-tuple-element.99), channel_id=1, source_target_pairs={{0,1},{1,0},{2,3},{3,2},{4,5},{5,4},{6,7},{7,6},{8,9},{9,8},{10,11... | collective-permute-start | bytes 786440 | tf_op jit(solution)/shard_map/ppermute | solution.py:457
  63.4 1.4 %copy-start.1 = (f32[2,128,512]{2,1,0:T(8,128)S(1)}, f32[2,128,512]{2,1,0:T(8,128)}, u32[]{:S(2)}) copy-start(f32[2,128,512]{2,1,0:T(8,128)} %psi.3) | copy-start | bytes 1572868

commit v8 on v7

--- a/solution.py
+++ b/solution.py
@@ -524,10 +524,10 @@
     first = fix
     for sweep_index in range(COARSE_SWEEPS - 1):
         far_sums, near_sums = swap_far(fix), swap_near(fix)
+        part = run(coarse_part_body, "coarse_part", [half], (fix, first, *coarse))[0]
         if len(arrived) < len(pieces):
-            fix, held = lax.optimization_barrier((fix, pieces[len(arrived)]))
+            held, part = after(pieces[len(arrived)], part)
             arrived.append(swap_far(held))
-        part = run(coarse_part_body, "coarse_part", [half], (fix, first, *coarse))[0]
         if sweep_index:
             part, arrived[sweep_index - 1] = after(part, arrived[sweep_index - 1])
         args = (keep, part, far_sums, near_sums, *coarse)

time: 73.8 us -> 73.8 us (level)
  no operation moved by 1% of the time
where the time goes in v8:
time: 73.8 us; the launch traced here: 73.6 us
  waiting for transfers between devices  34.5 us (47%)
  starting transfers between devices  24.3 us (33%)
  Pallas kernels  12.7 us (17%)
  local copies, waits for them, and re-layouts  1.23 us (2%)
  between operations  0.9 us (1%)
    ppermute x13, waiting for transfers between devices, swap_far(): return lax.ppermute(x, ('grp', 'gx'), across)  32.7 us
    ppermute x13, starting transfers between devices, swap_far(): return lax.ppermute(x, ('grp', 'gx'), across)  22.9 us
    pallas_call x28, Pallas kernels, call(): pl.pallas_call(body, out_shape=shapes, in_specs=in_specs or [VMEM] * len(...  12.7 us
    ppermute x10, waiting for transfers between devices, swap_near(): return lax.ppermute(x, 'gx', on_chip)  1.81 us
  transfers between devices with their start and end apart: 23, of which 12 were waited for; matrix products, arithmetic and copies ran while one was open for 0% of the time, Pallas kernels for 14%

profile of v8, /device:TPU:1, one launch (start us, length us, event | category | flops | bytes accessed | tf_op | source)
XLA Modules:
  0.0 73.6 jit_solution(16952502999632522496)
XLA Ops:
  0.7 1.3 %take.1 = (f32[2,80,512]{2,1,0:T(8,128)S(1)}, f32[2,48,512]{2,1,0:T(8,128)S(1)}, f32[2,128,512]{2,1,0:T(8,128)S(1)}) custom-call(s32[1]{0:T(128)} %bitcast.where, f32[2,2,128,512]{3,2,1,0:T(8,128)} %warm.1), custom_call_target="tpu_custom_call" | custom-call | bytes 2097156 | tf_op jit(solution)/shard_map/take/pallas_call | solution.py:53
  2.0 0.1 collective-permute-start.1
  2.1 2.6 %collective-permute-start.2 = (f32[2,48,512]{2,1,0:T(8,128)S(1)}, f32[2,48,512]{2,1,0:T(8,128)S(1)}, u32[]{:S(2)}, u32[]{:S(2)}) collective-permute-start(f32[2,48,512]{2,1,0:T(8,128)S(1)} %get-tuple-element.54.refs_1_), channel_id=1, source_target_pairs={{1,2},{3,4},{5,6},{7,8},{9,10},{11,12},{13,14},{17,18},{19,20},{21... | collective-permute-start | bytes 589832 | tf_op jit(solution)/shard_map/ppermute | solution.py:454
  4.8 0.1 collective-permute-start
  4.8 1.2 %copy-done.2 = f32[2,2,128,512]{3,2,1,0:T(8,128)S(1)} copy-done((f32[2,2,128,512]{3,2,1,0:T(8,128)S(1)}, f32[2,2,128,512]{3,2,1,0:T(8,128)}, u32[]{:S(2)}) %copy-start.2) | copy-done | bytes 1048600
  6.1 0.2 setup.1
  6.3 0.9 %part.3 = (f32[2,128,512]{2,1,0:T(8,128)S(1)}, f32[2,128,512]{2,1,0:T(8,128)S(1)}) custom-call(f32[2,80,512]{2,1,0:T(8,128)S(1)} %get-tuple-element.53.refs_0_, f32[2,48,512]{2,1,0:T(8,128)S(1)} %get-tuple-element.54.refs_1_, f32[2,128,512]{2,1,0:T(8,128)S(1)} %get-tuple-element.55.refs_2_, f32[2,128,512]{2,1,0:T(8,128)S(1)} %get-tuple-element.52.refs_3_.gain.refs_2_, ...), custom_call_target="tpu_custom_call" | custom-call | bytes 3670016 | tf_op jit(solution)/shard_map/part/pallas_call | solution.py:53
  7.3 5.7 %collective-permute-done.2.halo = f32[2,48,512]{2,1,0:T(8,128)S(1)} collective-permute-done((f32[2,48,512]{2,1,0:T(8,128)S(1)}, f32[2,48,512]{2,1,0:T(8,128)S(1)}, u32[]{:S(2)}, u32[]{:S(2)}) %collective-permute-start.2) | collective-permute-done | bytes 196640 | tf_op jit(solution)/shard_map/ppermute | solution.py:454
  13.0 0.1 finish.5.refs_2_
  13.2 0.1 collective-permute-start.6
  13.2 3.3 %collective-permute-done.halo = f32[2,80,512]{2,1,0:T(8,128)S(1)} collective-permute-done((f32[2,80,512]{2,1,0:T(8,128)S(1)}, f32[2,80,512]{2,1,0:T(8,128)S(1)}, u32[]{:S(2)}, u32[]{:S(2)}) %collective-permute-start) | collective-permute-done | bytes 327712 | tf_op jit(solution)/shard_map/ppermute | solution.py:454
  16.5 0.1 finish.3.refs_0_
  16.6 2.5 %collective-permute-start.4 = (f32[2,80,512]{2,1,0:T(8,128)S(1)}, f32[2,80,512]{2,1,0:T(8,128)S(1)}, u32[]{:S(2)}, u32[]{:S(2)}) collective-permute-start(f32[2,80,512]{2,1,0:T(8,128)S(1)} %finish.3.refs_0_), channel_id=1, source_target_pairs={{1,2},{3,4},{5,6},{7,8},{9,10},{11,12},{13,14},{17,18},{19,20},{21... | collective-permute-start | bytes 983048 | tf_op jit(solution)/shard_map/ppermute | solution.py:454
  19.1 0.1 collective-permute-start.3
  19.2 0.9 %part.4 = (f32[2,128,512]{2,1,0:T(8,128)S(1)}, f32[2,128,512]{2,1,0:T(8,128)S(1)}) custom-call(f32[2,80,512]{2,1,0:T(8,128)S(1)} %finish.3.refs_0_, f32[2,48,512]{2,1,0:T(8,128)S(1)} %finish.4.refs_1_, f32[2,128,512]{2,1,0:T(8,128)S(1)} %finish.5.refs_2_, f32[2,128,512]{2,1,0:T(8,128)S(1)} %get-tuple-element.52.refs_3_.gain.refs_2_, ...), custom_call_target="tpu_custom_call" | custom-call | bytes 3670016 | tf_op jit(solution)/shard_map/part/pallas_call | solution.py:53
  20.1 0.1 matrices.1
  20.2 6.8 %collective-permute-done.4.halo = f32[2,80,512]{2,1,0:T(8,128)S(1)} collective-permute-done((f32[2,80,512]{2,1,0:T(8,128)S(1)}, f32[2,80,512]{2,1,0:T(8,128)S(1)}, u32[]{:S(2)}, u32[]{:S(2)}) %collective-permute-start.4) | collective-permute-done | bytes 327712 | tf_op jit(solution)/shard_map/ppermute | solution.py:454
  27.1 0.3 finish_pool.3
  27.4 3.2 %collective-permute-done.3.halo = f32[2,48,512]{2,1,0:T(8,128)S(1)} collective-permute-done((f32[2,48,512]{2,1,0:T(8,128)S(1)}, f32[2,48,512]{2,1,0:T(8,128)S(1)}, u32[]{:S(2)}, u32[]{:S(2)}) %collective-permute-start.3) | collective-permute-done | bytes 196640 | tf_op jit(solution)/shard_map/ppermute | solution.py:454
  30.6 0.2 finish_pool.4
  30.8 2.5 %collective-permute-start.5 = (f32[2,64,256]{2,1,0:T(8,128)S(1)}, f32[2,64,256]{2,1,0:T(8,128)S(1)}, u32[]{:S(2)}, u32[]{:S(2)}) collective-permute-start(f32[2,64,256]{2,1,0:T(8,128)S(1)} %get-tuple-element.66), channel_id=1, source_target_pairs={{1,2},{3,4},{5,6},{7,8},{9,10},{11,12},{13,14},{17,18},{19,20},{21... | collective-permute-start | bytes 393224 | tf_op jit(solution)/shard_map/ppermute | solution.py:454
  33.4 0.0 collective-permute-done.6.halo
  33.4 0.4 finish_pool.5
  33.7 0.1 collective-permute-start.7
  33.8 0.3 coarse_setup.1.gain
  34.1 0.6 collective-permute-start.16
  34.7 1.5 %part_defect.1 = (f32[2,128,512]{2,1,0:T(8,128)S(1)}, f32[2,128,512]{2,1,0:T(8,128)S(1)}, f32[2,64,256]{2,1,0:T(8,128)S(1)}) custom-call(f32[2,80,512]{2,1,0:T(8,128)S(1)} %get-tuple-element.67.refs_0_, f32[2,48,512]{2,1,0:T(8,128)S(1)} %get-tuple-element.68.refs_1_, f32[2,128,512]{2,1,0:T(8,128)S(1)} %get-tuple-element.70.refs_2_, ...), custom_call_target="tpu_custom_call" | custom-call | bytes 3932160 | tf_op jit(solution)/shard_map/part_defect/pallas_call | solution.py:53
  36.2 0.0 collective-permute-done.7.near
  36.2 1.6 %collective-permute-start.8 = (f32[2,64,256]{2,1,0:T(8,128)S(1)}, f32[2,64,256]{2,1,0:T(8,128)S(1)}, u32[]{:S(2)}, u32[]{:S(2)}) collective-permute-start(f32[2,64,256]{2,1,0:T(8,128)S(1)} %coarse_first.1.fix.own), channel_id=1, source_target_pairs={{1,2},{3,4},{5,6},{7,8},{9,10},{11,12},{13,14},{17,18},{19,20},{21... | collective-permute-start | bytes 393224 | tf_op jit(solution)/shard_map/ppermute | solution.py:454
  37.9 0.0 collective-permute-start.9
  37.9 0.5 three.1
  38.4 1.3 %collective-permute-start.10 = (f32[2,64,256]{2,1,0:T(8,128)S(1)}, f32[2,64,256]{2,1,0:T(8,128)S(1)}, u32[]{:S(2)}, u32[]{:S(2)}) collective-permute-start(f32[2,64,256]{2,1,0:T(8,128)S(1)} %get-tuple-element.81), channel_id=1, source_target_pairs={{1,2},{3,4},{5,6},{7,8},{9,10},{11,12},{13,14},{17,18},{19,20},{21... | collective-permute-start | bytes 393224 | tf_op jit(solution)/shard_map/ppermute | solution.py:454
  39.6 0.1 coarse_part.3.part
  39.8 1.1 %collective-permute-done.8.far = f32[2,64,256]{2,1,0:T(8,128)S(1)} collective-permute-done((f32[2,64,256]{2,1,0:T(8,128)S(1)}, f32[2,64,256]{2,1,0:T(8,128)S(1)}, u32[]{:S(2)}, u32[]{:S(2)}) %collective-permute-start.8) | collective-permute-done | bytes 131104 | tf_op jit(solution)/shard_map/ppermute | solution.py:454
  40.9 0.0 collective-permute-done.9.near
  41.0 2.5 %collective-permute-start.11 = (f32[2,64,256]{2,1,0:T(8,128)S(1)}, f32[2,64,256]{2,1,0:T(8,128)S(1)}, u32[]{:S(2)}, u32[]{:S(2)}) collective-permute-start(f32[2,64,256]{2,1,0:T(8,128)S(1)} %coarse_finish.3.fix), channel_id=1, source_target_pairs={{1,2},{3,4},{5,6},{7,8},{9,10},{11,12},{13,14},{17,18},{19,20},{21... | collective-permute-start | bytes 393224 | tf_op jit(solution)/shard_map/ppermute | solution.py:454
  43.4 0.0 collective-permute-start.12
  43.4 1.2 %collective-permute-start.13 = (f32[2,64,256]{2,1,0:T(8,128)S(1)}, f32[2,64,256]{2,1,0:T(8,128)S(1)}, u32[]{:S(2)}, u32[]{:S(2)}) collective-permute-start(f32[2,64,256]{2,1,0:T(8,128)S(1)} %get-tuple-element.83), channel_id=1, source_target_pairs={{1,2},{3,4},{5,6},{7,8},{9,10},{11,12},{13,14},{17,18},{19,20},{21... | collective-permute-start | bytes 393224 | tf_op jit(solution)/shard_map/ppermute | solution.py:454
  44.6 0.2 coarse_part.4.part
  44.8 1.7 %collective-permute-done.11.far = f32[2,64,256]{2,1,0:T(8,128)S(1)} collective-permute-done((f32[2,64,256]{2,1,0:T(8,128)S(1)}, f32[2,64,256]{2,1,0:T(8,128)S(1)}, u32[]{:S(2)}, u32[]{:S(2)}) %collective-permute-start.11) | collective-permute-done | bytes 131104 | tf_op jit(solution)/shard_map/ppermute | solution.py:454
  46.5 3.9 %collective-permute-start.14 = (f32[2,64,256]{2,1,0:T(8,128)S(1)}, f32[2,64,256]{2,1,0:T(8,128)S(1)}, u32[]{:S(2)}, u32[]{:S(2)}) collective-permute-start(f32[2,64,256]{2,1,0:T(8,128)S(1)} %coarse_finish.4.fix), channel_id=1, source_target_pairs={{1,2},{3,4},{5,6},{7,8},{9,10},{11,12},{13,14},{17,18},{19,20},{21... | collective-permute-start | bytes 393224 | tf_op jit(solution)/shard_map/ppermute | solution.py:454
  50.5 0.0 collective-permute-start.15
  50.5 0.2 collective-permute-start.18
  50.6 0.2 coarse_part.5.part
  50.8 2.3 %collective-permute-done.14.far = f32[2,64,256]{2,1,0:T(8,128)S(1)} collective-permute-done((f32[2,64,256]{2,1,0:T(8,128)S(1)}, f32[2,64,256]{2,1,0:T(8,128)S(1)}, u32[]{:S(2)}, u32[]{:S(2)}) %collective-permute-start.14) | collective-permute-done | bytes 131104 | tf_op jit(solution)/shard_map/ppermute | solution.py:454
  53.1 0.0 collective-permute-done.15.near
  53.2 1.8 %collective-permute-start.17 = (f32[2,64,256]{2,1,0:T(8,128)S(1)}, f32[2,64,256]{2,1,0:T(8,128)S(1)}, u32[]{:S(2)}, u32[]{:S(2)}) collective-permute-start(f32[2,64,256]{2,1,0:T(8,128)S(1)} %coarse_finish.5.fix), channel_id=1, source_target_pairs={{1,2},{3,4},{5,6},{7,8},{9,10},{11,12},{13,14},{17,18},{19,20},{21... | collective-permute-start | bytes 393224 | tf_op jit(solution)/shard_map/ppermute | solution.py:454
  55.0 1.0 %third.1 = (f32[2,128,512]{2,1,0:T(8,128)S(1)}, f32[2,128,512]{2,1,0:T(8,128)S(1)}) custom-call(f32[2,128,512]{2,1,0:T(8,128)S(1)} %get-tuple-element.71.far, f32[2,128,512]{2,1,0:T(8,128)S(1)} %get-tuple-element.72.near, f32[2,64,256]{2,1,0:T(8,128)S(1)} %coarse_finish.5.fix, f32[2,128,512]{2,1,0:T(8,128)S(1)} %collective-permute-done.16.near_halo, ...), custom_call_target="tpu_custom_call" | custom-call | bytes 3407872 | tf_op jit(solution)/shard_map/third/pallas_call | solution.py:53
  56.0 0.0 collective-permute-done.18.refs_2_
  56.0 0.6 rebuild.1.state_nb
  56.6 1.7 %collective-permute-done.17.halo = f32[2,64,256]{2,1,0:T(8,128)S(1)} collective-permute-done((f32[2,64,256]{2,1,0:T(8,128)S(1)}, f32[2,64,256]{2,1,0:T(8,128)S(1)}, u32[]{:S(2)}, u32[]{:S(2)}) %collective-permute-start.17) | collective-permute-done | bytes 131104 | tf_op jit(solution)/shard_map/ppermute | solution.py:454
  58.3 0.3 fix_far.1.refs_0_
  58.6 2.5 %collective-permute-start.20 = (f32[2,128,512]{2,1,0:T(8,128)S(1)}, f32[2,128,512]{2,1,0:T(8,128)S(1)}, u32[]{:S(2)}, u32[]{:S(2)}) collective-permute-start(f32[2,128,512]{2,1,0:T(8,128)S(1)} %fix_far.1.refs_0_), channel_id=1, source_target_pairs={{1,2},{3,4},{5,6},{7,8},{9,10},{11,12},{13,14},{17,18},{19,20},{21... | collective-permute-start | bytes 1572872 | tf_op jit(solution)/shard_map/ppermute | solution.py:454
  61.2 0.0 collective-permute-start.19
  61.2 1.3 %collective-permute-done.19.halo = f32[2,64,256]{2,1,0:T(8,128)S(1)} collective-permute-done((f32[2,64,256]{2,1,0:T(8,128)S(1)}, f32[2,64,256]{2,1,0:T(8,128)S(1)}, u32[]{:S(2)}, u32[]{:S(2)}) %collective-permute-start.19) | collective-permute-done | bytes 131104 | tf_op jit(solution)/shard_map/ppermute | solution.py:457
  62.5 0.3 fix_near.1
  62.9 0.2 collective-permute-start.21
  63.1 0.4 collective-permute-start.22
  63.4 0.9 %part.5 = (f32[2,128,512]{2,1,0:T(8,128)S(1)}, f32[2,128,512]{2,1,0:T(8,128)S(1)}) custom-call(f32[2,128,512]{2,1,0:T(8,128)S(1)} %fix_far.1.refs_0_, f32[2,128,512]{2,1,0:T(8,128)S(1)} %get-tuple-element.95.refs_1_, f32[2,128,512]{2,1,0:T(8,128)S(1)} %get-tuple-element.52.refs_3_.gain.refs_2_, f32[2,2,128,512]{3,2,1,0:T(8,128)S(1)} %get-tuple-element.56.refs_4_.refs_3_), custom_call_target="tpu_custom_call" | custom-call | bytes 3670016 | tf_op jit(solution)/shard_map/part/pallas_call | solution.py:53
  64.4 0.1 collective-permute-done.21.refs_1_
  64.5 0.4 collective-permute-done.22.refs_3_
  64.8 1.0 %final.2 = (f32[2,2,128,512]{3,2,1,0:T(8,128)}, f32[2,128,512]{2,1,0:T(8,128)}) custom-call(s32[1]{0:T(128)} %bitcast.where, f32[1]{0:T(128)} %bitcast.1.keep, f32[2,128,512]{2,1,0:T(8,128)S(1)} %get-tuple-element.52.refs_3_.gain.refs_2_, f32[2,128,512]{2,1,0:T(8,128)S(1)} %copy-done, f32[2,128,512]{2,1,0:T(8,128)S(1)} %copy-done.1, ...), custom_call_target="tpu_custom_call" | custom-call | bytes 4718600 | tf_op jit(solution)/shard_map/final/pallas_call | solution.py:53
  65.8 6.9 %collective-permute-done.20.refs_1_ = f32[2,128,512]{2,1,0:T(8,128)S(1)} collective-permute-done((f32[2,128,512]{2,1,0:T(8,128)S(1)}, f32[2,128,512]{2,1,0:T(8,128)S(1)}, u32[]{:S(2)}, u32[]{:S(2)}) %collective-permute-start.20) | collective-permute-done | bytes 524320 | tf_op jit(solution)/shard_map/ppermute | solution.py:454
  72.7 1.0 %final.3 = (f32[2,2,128,512]{3,2,1,0:T(8,128)}, f32[2,128,512]{2,1,0:T(8,128)}) custom-call(s32[1]{0:T(128)} %bitcast.where, f32[1]{0:T(128)} %bitcast.1.keep, f32[2,128,512]{2,1,0:T(8,128)S(1)} %get-tuple-element.52.refs_3_.gain.refs_2_, f32[2,128,512]{2,1,0:T(8,128)S(1)} %copy-done, ...), custom_call_target="tpu_custom_call", output_to_operand_aliasing={{0}: (7, {}), {1}: (8, {})} | custom-call | bytes 5767176 | tf_op jit(solution)/shard_map/final/pallas_call | solution.py:53
  (16 shorter events, 0.3 us)
Async XLA Ops:
  0.6 4.2 %copy-start = (f32[2,128,512]{2,1,0:T(8,128)S(1)}, f32[2,128,512]{2,1,0:T(8,128)}, u32[]{:S(2)}) copy-start(f32[2,128,512]{2,1,0:T(8,128)} %phi.7) | copy-start | bytes 1572868
  2.0 11.1 %collective-permute-start.1 = (f32[2,128,512]{2,1,0:T(8,128)S(1)}, f32[2,128,512]{2,1,0:T(8,128)S(1)}, u32[]{:S(2)}, u32[]{:S(2)}) collective-permute-start(f32[2,128,512]{2,1,0:T(8,128)S(1)} %get-tuple-element.55.refs_2_), channel_id=1, source_target_pairs={{0,1},{1,0},{2,3},{3,2},{4,5},{5,4},{6,7},{7,6},{8,9},{9,8},{10,11... | collective-permute-start | bytes 1572872 | tf_op jit(solution)/shard_map/ppermute | solution.py:457
  2.1 10.9 %collective-permute-start.2 = (f32[2,48,512]{2,1,0:T(8,128)S(1)}, f32[2,48,512]{2,1,0:T(8,128)S(1)}, u32[]{:S(2)}, u32[]{:S(2)}) collective-permute-start(f32[2,48,512]{2,1,0:T(8,128)S(1)} %get-tuple-element.54.refs_1_), channel_id=1, source_target_pairs={{1,2},{3,4},{5,6},{7,8},{9,10},{11,12},{13,14},{17,18},{19,20},{21... | collective-permute-start | bytes 589832 | tf_op jit(solution)/shard_map/ppermute | solution.py:454
  4.8 11.7 %collective-permute-start = (f32[2,80,512]{2,1,0:T(8,128)S(1)}, f32[2,80,512]{2,1,0:T(8,128)S(1)}, u32[]{:S(2)}, u32[]{:S(2)}) collective-permute-start(f32[2,80,512]{2,1,0:T(8,128)S(1)} %get-tuple-element.53.refs_0_), channel_id=1, source_target_pairs={{1,2},{3,4},{5,6},{7,8},{9,10},{11,12},{13,14},{17,18},{19,20},{21... | collective-permute-start | bytes 983048 | tf_op jit(solution)/shard_map/ppermute | solution.py:454
  4.8 1.2 %copy-start.2 = (f32[2,2,128,512]{3,2,1,0:T(8,128)S(1)}, f32[2,2,128,512]{3,2,1,0:T(8,128)}, u32[]{:S(2)}) copy-start(f32[2,2,128,512]{3,2,1,0:T(8,128)} %cot.1) | copy-start | bytes 3145732
  13.2 20.2 %collective-permute-start.6 = (f32[2,128,512]{2,1,0:T(8,128)S(1)}, f32[2,128,512]{2,1,0:T(8,128)S(1)}, u32[]{:S(2)}, u32[]{:S(2)}) collective-permute-start(f32[2,128,512]{2,1,0:T(8,128)S(1)} %finish.5.refs_2_), channel_id=1, source_target_pairs={{0,1},{1,0},{2,3},{3,2},{4,5},{5,4},{6,7},{7,6},{8,9},{9,8},{10,11... | collective-permute-start | bytes 1572872 | tf_op jit(solution)/shard_map/ppermute | solution.py:457
  16.6 10.5 %collective-permute-start.4 = (f32[2,80,512]{2,1,0:T(8,128)S(1)}, f32[2,80,512]{2,1,0:T(8,128)S(1)}, u32[]{:S(2)}, u32[]{:S(2)}) collective-permute-start(f32[2,80,512]{2,1,0:T(8,128)S(1)} %finish.3.refs_0_), channel_id=1, source_target_pairs={{1,2},{3,4},{5,6},{7,8},{9,10},{11,12},{13,14},{17,18},{19,20},{21... | collective-permute-start | bytes 983048 | tf_op jit(solution)/shard_map/ppermute | solution.py:454
  19.1 11.5 %collective-permute-start.3 = (f32[2,48,512]{2,1,0:T(8,128)S(1)}, f32[2,48,512]{2,1,0:T(8,128)S(1)}, u32[]{:S(2)}, u32[]{:S(2)}) collective-permute-start(f32[2,48,512]{2,1,0:T(8,128)S(1)} %finish.4.refs_1_), channel_id=1, source_target_pairs={{1,2},{3,4},{5,6},{7,8},{9,10},{11,12},{13,14},{17,18},{19,20},{21... | collective-permute-start | bytes 589832 | tf_op jit(solution)/shard_map/ppermute | solution.py:454
  30.8 5.4 %collective-permute-start.5 = (f32[2,64,256]{2,1,0:T(8,128)S(1)}, f32[2,64,256]{2,1,0:T(8,128)S(1)}, u32[]{:S(2)}, u32[]{:S(2)}) collective-permute-start(f32[2,64,256]{2,1,0:T(8,128)S(1)} %get-tuple-element.66), channel_id=1, source_target_pairs={{1,2},{3,4},{5,6},{7,8},{9,10},{11,12},{13,14},{17,18},{19,20},{21... | collective-permute-start | bytes 393224 | tf_op jit(solution)/shard_map/ppermute | solution.py:454
  33.7 2.5 %collective-permute-start.7 = (f32[2,64,256]{2,1,0:T(8,128)S(1)}, f32[2,64,256]{2,1,0:T(8,128)S(1)}, u32[]{:S(2)}, u32[]{:S(2)}) collective-permute-start(f32[2,64,256]{2,1,0:T(8,128)S(1)} %get-tuple-element.78), channel_id=1, source_target_pairs={{0,1},{1,0},{2,3},{3,2},{4,5},{5,4},{6,7},{7,6},{8,9},{9,8},{10,11... | collective-permute-start | bytes 393224 | tf_op jit(solution)/shard_map/ppermute | solution.py:457
  34.1 20.9 %collective-permute-start.16 = (f32[2,128,512]{2,1,0:T(8,128)S(1)}, f32[2,128,512]{2,1,0:T(8,128)S(1)}, u32[]{:S(2)}, u32[]{:S(2)}) collective-permute-start(f32[2,128,512]{2,1,0:T(8,128)S(1)} %get-tuple-element.70.refs_2_), channel_id=1, source_target_pairs={{0,1},{1,0},{2,3},{3,2},{4,5},{5,4},{6,7},{7,6},{8,9},{9,8},{10,11... | collective-permute-start | bytes 1572872 | tf_op jit(solution)/shard_map/ppermute | solution.py:457
  36.2 4.7 %collective-permute-start.8 = (f32[2,64,256]{2,1,0:T(8,128)S(1)}, f32[2,64,256]{2,1,0:T(8,128)S(1)}, u32[]{:S(2)}, u32[]{:S(2)}) collective-permute-start(f32[2,64,256]{2,1,0:T(8,128)S(1)} %coarse_first.1.fix.own), channel_id=1, source_target_pairs={{1,2},{3,4},{5,6},{7,8},{9,10},{11,12},{13,14},{17,18},{19,20},{21... | collective-permute-start | bytes 393224 | tf_op jit(solution)/shard_map/ppermute | solution.py:454
  37.9 3.0 %collective-permute-start.9 = (f32[2,64,256]{2,1,0:T(8,128)S(1)}, f32[2,64,256]{2,1,0:T(8,128)S(1)}, u32[]{:S(2)}, u32[]{:S(2)}) collective-permute-start(f32[2,64,256]{2,1,0:T(8,128)S(1)} %coarse_first.1.fix.own), channel_id=1, source_target_pairs={{0,1},{1,0},{2,3},{3,2},{4,5},{5,4},{6,7},{7,6},{8,9},{9,8},{10,11... | collective-permute-start | bytes 393224 | tf_op jit(solution)/shard_map/ppermute | solution.py:457
  38.4 6.4 %collective-permute-start.10 = (f32[2,64,256]{2,1,0:T(8,128)S(1)}, f32[2,64,256]{2,1,0:T(8,128)S(1)}, u32[]{:S(2)}, u32[]{:S(2)}) collective-permute-start(f32[2,64,256]{2,1,0:T(8,128)S(1)} %get-tuple-element.81), channel_id=1, source_target_pairs={{1,2},{3,4},{5,6},{7,8},{9,10},{11,12},{13,14},{17,18},{19,20},{21... | collective-permute-start | bytes 393224 | tf_op jit(solution)/shard_map/ppermute | solution.py:454
  41.0 5.5 %collective-permute-start.11 = (f32[2,64,256]{2,1,0:T(8,128)S(1)}, f32[2,64,256]{2,1,0:T(8,128)S(1)}, u32[]{:S(2)}, u32[]{:S(2)}) collective-permute-start(f32[2,64,256]{2,1,0:T(8,128)S(1)} %coarse_finish.3.fix), channel_id=1, source_target_pairs={{1,2},{3,4},{5,6},{7,8},{9,10},{11,12},{13,14},{17,18},{19,20},{21... | collective-permute-start | bytes 393224 | tf_op jit(solution)/shard_map/ppermute | solution.py:454
  43.4 3.0 %collective-permute-start.12 = (f32[2,64,256]{2,1,0:T(8,128)S(1)}, f32[2,64,256]{2,1,0:T(8,128)S(1)}, u32[]{:S(2)}, u32[]{:S(2)}) collective-permute-start(f32[2,64,256]{2,1,0:T(8,128)S(1)} %coarse_finish.3.fix), channel_id=1, source_target_pairs={{0,1},{1,0},{2,3},{3,2},{4,5},{5,4},{6,7},{7,6},{8,9},{9,8},{10,11... | collective-permute-start | bytes 393224 | tf_op jit(solution)/shard_map/ppermute | solution.py:457
  43.4 7.3 %collective-permute-start.13 = (f32[2,64,256]{2,1,0:T(8,128)S(1)}, f32[2,64,256]{2,1,0:T(8,128)S(1)}, u32[]{:S(2)}, u32[]{:S(2)}) collective-permute-start(f32[2,64,256]{2,1,0:T(8,128)S(1)} %get-tuple-element.83), channel_id=1, source_target_pairs={{1,2},{3,4},{5,6},{7,8},{9,10},{11,12},{13,14},{17,18},{19,20},{21... | collective-permute-start | bytes 393224 | tf_op jit(solution)/shard_map/ppermute | solution.py:454
  46.5 6.6 %collective-permute-start.14 = (f32[2,64,256]{2,1,0:T(8,128)S(1)}, f32[2,64,256]{2,1,0:T(8,128)S(1)}, u32[]{:S(2)}, u32[]{:S(2)}) collective-permute-start(f32[2,64,256]{2,1,0:T(8,128)S(1)} %coarse_finish.4.fix), channel_id=1, source_target_pairs={{1,2},{3,4},{5,6},{7,8},{9,10},{11,12},{13,14},{17,18},{19,20},{21... | collective-permute-start | bytes 393224 | tf_op jit(solution)/shard_map/ppermute | solution.py:454
  50.5 2.7 %collective-permute-start.15 = (f32[2,64,256]{2,1,0:T(8,128)S(1)}, f32[2,64,256]{2,1,0:T(8,128)S(1)}, u32[]{:S(2)}, u32[]{:S(2)}) collective-permute-start(f32[2,64,256]{2,1,0:T(8,128)S(1)} %coarse_finish.4.fix), channel_id=1, source_target_pairs={{0,1},{1,0},{2,3},{3,2},{4,5},{5,4},{6,7},{7,6},{8,9},{9,8},{10,11... | collective-permute-start | bytes 393224 | tf_op jit(solution)/shard_map/ppermute | solution.py:457
  50.5 5.6 %collective-permute-start.18 = (f32[2,64,256]{2,1,0:T(8,128)S(1)}, f32[2,64,256]{2,1,0:T(8,128)S(1)}, u32[]{:S(2)}, u32[]{:S(2)}) collective-permute-start(f32[2,64,256]{2,1,0:T(8,128)S(1)} %get-tuple-element.91), channel_id=1, source_target_pairs={{1,2},{3,4},{5,6},{7,8},{9,10},{11,12},{13,14},{17,18},{19,20},{21... | collective-permute-start | bytes 393224 | tf_op jit(solution)/shard_map/ppermute | solution.py:454
  53.2 5.1 %collective-permute-start.17 = (f32[2,64,256]{2,1,0:T(8,128)S(1)}, f32[2,64,256]{2,1,0:T(8,128)S(1)}, u32[]{:S(2)}, u32[]{:S(2)}) collective-permute-start(f32[2,64,256]{2,1,0:T(8,128)S(1)} %coarse_finish.5.fix), channel_id=1, source_target_pairs={{1,2},{3,4},{5,6},{7,8},{9,10},{11,12},{13,14},{17,18},{19,20},{21... | collective-permute-start | bytes 393224 | tf_op jit(solution)/shard_map/ppermute | solution.py:454
  58.6 14.0 %collective-permute-start.20 = (f32[2,128,512]{2,1,0:T(8,128)S(1)}, f32[2,128,512]{2,1,0:T(8,128)S(1)}, u32[]{:S(2)}, u32[]{:S(2)}) collective-permute-start(f32[2,128,512]{2,1,0:T(8,128)S(1)} %fix_far.1.refs_0_), channel_id=1, source_target_pairs={{1,2},{3,4},{5,6},{7,8},{9,10},{11,12},{13,14},{17,18},{19,20},{21... | collective-permute-start | bytes 1572872 | tf_op jit(solution)/shard_map/ppermute | solution.py:454
  61.2 1.3 %collective-permute-start.19 = (f32[2,64,256]{2,1,0:T(8,128)S(1)}, f32[2,64,256]{2,1,0:T(8,128)S(1)}, u32[]{:S(2)}, u32[]{:S(2)}) collective-permute-start(f32[2,64,256]{2,1,0:T(8,128)S(1)} %coarse_finish.5.fix), channel_id=1, source_target_pairs={{0,1},{1,0},{2,3},{3,2},{4,5},{5,4},{6,7},{7,6},{8,9},{9,8},{10,11... | collective-permute-start | bytes 393224 | tf_op jit(solution)/shard_map/ppermute | solution.py:457
  62.9 1.6 %collective-permute-start.21 = (f32[2,64,512]{2,1,0:T(8,128)S(1)}, f32[2,64,512]{2,1,0:T(8,128)S(1)}, u32[]{:S(2)}, u32[]{:S(2)}) collective-permute-start(f32[2,64,512]{2,1,0:T(8,128)S(1)} %get-tuple-element.98), channel_id=1, source_target_pairs={{0,1},{1,0},{2,3},{3,2},{4,5},{5,4},{6,7},{7,6},{8,9},{9,8},{10,11... | collective-permute-start | bytes 786440 | tf_op jit(solution)/shard_map/ppermute | solution.py:457
  63.1 1.8 %collective-permute-start.22 = (f32[2,64,512]{2,1,0:T(8,128)S(1)}, f32[2,64,512]{2,1,0:T(8,128)S(1)}, u32[]{:S(2)}, u32[]{:S(2)}) collective-permute-start(f32[2,64,512]{2,1,0:T(8,128)S(1)} %get-tuple-element.99), channel_id=1, source_target_pairs={{0,1},{1,0},{2,3},{3,2},{4,5},{5,4},{6,7},{7,6},{8,9},{9,8},{10,11... | collective-permute-start | bytes 786440 | tf_op jit(solution)/shard_map/ppermute | solution.py:457
  63.4 1.4 %copy-start.1 = (f32[2,128,512]{2,1,0:T(8,128)S(1)}, f32[2,128,512]{2,1,0:T(8,128)}, u32[]{:S(2)}) copy-start(f32[2,128,512]{2,1,0:T(8,128)} %psi.3) | copy-start | bytes 1572868

commit v9 on v7

--- a/solution.py
+++ b/solution.py
@@ -494,6 +494,8 @@
     far_halo = [swap_far(v) for v in far]
     near_halo = swap_near(near)
     far_part, near_part = run(part_body, "part", [full] * 2, (*far, near, *coefs, own), (len(far),), scratch=[whole])
+    coarse = list(coarse)
+    far_part, coarse[0] = after(far_part, coarse[0])
 
     def finish_pool(i, lo, part, halo, before=()):
         n = halo.shape[1]

time: 73.8 us -> 73.7 us (level)
  starting transfers between devices: 24.3 us -> 22.7 us
  waiting for transfers between devices: 34.5 us -> 36 us
    ppermute x13, starting transfers between devices: 22.9 us -> 21.4 us  [swap_far(): return lax.ppermute(x, ('grp', 'gx'), across)]
    ppermute x13, waiting for transfers between devices: 32.7 us -> 34.2 us  [swap_far(): return lax.ppermute(x, ('grp', 'gx'), across)]
  transfers between devices with their start and end apart: 23 -> 23, of which waited for: 12 -> 13; matrix products, arithmetic and copies ran while one was open for 0% -> 0% of each run, Pallas kernels for 14% -> 14%
where the time goes in v9:
time: 73.7 us; the launch traced here: 73.6 us
  waiting for transfers between devices  36 us (49%)
  starting transfers between devices  22.7 us (31%)
  Pallas kernels  12.7 us (17%)
  local copies, waits for them, and re-layouts  1.23 us (2%)
  between operations  0.89 us (1%)
    ppermute x13, waiting for transfers between devices, swap_far(): return lax.ppermute(x, ('grp', 'gx'), across)  34.2 us
    ppermute x13, starting transfers between devices, swap_far(): return lax.ppermute(x, ('grp', 'gx'), across)  21.4 us
    pallas_call x28, Pallas kernels, call(): pl.pallas_call(body, out_shape=shapes, in_specs=in_specs or [VMEM] * len(...  12.7 us
    ppermute x10, waiting for transfers between devices, swap_near(): return lax.ppermute(x, 'gx', on_chip)  1.81 us
  transfers between devices with their start and end apart: 23, of which 13 were waited for; matrix products, arithmetic and copies ran while one was open for 0% of the time, Pallas kernels for 14%

profile of v9, /device:TPU:1, one launch (start us, length us, event | category | flops | bytes accessed | tf_op | source)
XLA Modules:
  0.0 73.6 jit_solution(11480442158619001574)
XLA Ops:
  0.7 1.3 %take.1 = (f32[2,80,512]{2,1,0:T(8,128)S(1)}, f32[2,48,512]{2,1,0:T(8,128)S(1)}, f32[2,128,512]{2,1,0:T(8,128)S(1)}) custom-call(s32[1]{0:T(128)} %bitcast.where, f32[2,2,128,512]{3,2,1,0:T(8,128)} %warm.1), custom_call_target="tpu_custom_call" | custom-call | bytes 2097156 | tf_op jit(solution)/shard_map/take/pallas_call | solution.py:53
  2.0 0.1 collective-permute-start.1
  2.1 2.6 %collective-permute-start.2 = (f32[2,48,512]{2,1,0:T(8,128)S(1)}, f32[2,48,512]{2,1,0:T(8,128)S(1)}, u32[]{:S(2)}, u32[]{:S(2)}) collective-permute-start(f32[2,48,512]{2,1,0:T(8,128)S(1)} %get-tuple-element.56.refs_1_), channel_id=1, source_target_pairs={{1,2},{3,4},{5,6},{7,8},{9,10},{11,12},{13,14},{17,18},{19,20},{21... | collective-permute-start | bytes 589832 | tf_op jit(solution)/shard_map/ppermute | solution.py:454
  4.8 0.1 collective-permute-start
  4.8 1.2 %copy-done.2 = f32[2,2,128,512]{3,2,1,0:T(8,128)S(1)} copy-done((f32[2,2,128,512]{3,2,1,0:T(8,128)S(1)}, f32[2,2,128,512]{3,2,1,0:T(8,128)}, u32[]{:S(2)}) %copy-start.2) | copy-done | bytes 1048600
  6.1 0.2 setup.1
  6.3 0.9 %part.3 = (f32[2,128,512]{2,1,0:T(8,128)S(1)}, f32[2,128,512]{2,1,0:T(8,128)S(1)}) custom-call(f32[2,80,512]{2,1,0:T(8,128)S(1)} %get-tuple-element.55.refs_0_, f32[2,48,512]{2,1,0:T(8,128)S(1)} %get-tuple-element.56.refs_1_, f32[2,128,512]{2,1,0:T(8,128)S(1)} %get-tuple-element.57.refs_2_, f32[2,128,512]{2,1,0:T(8,128)S(1)} %get-tuple-element.54.refs_3_.gain.refs_2_, ...), custom_call_target="tpu_custom_call" | custom-call | bytes 3670016 | tf_op jit(solution)/shard_map/part/pallas_call | solution.py:53
  7.3 5.7 %collective-permute-done.2.halo = f32[2,48,512]{2,1,0:T(8,128)S(1)} collective-permute-done((f32[2,48,512]{2,1,0:T(8,128)S(1)}, f32[2,48,512]{2,1,0:T(8,128)S(1)}, u32[]{:S(2)}, u32[]{:S(2)}) %collective-permute-start.2) | collective-permute-done | bytes 196640 | tf_op jit(solution)/shard_map/ppermute | solution.py:454
  13.0 0.0 collective-permute-done.1.halo
  13.0 0.1 finish.5.refs_2_
  13.2 0.1 collective-permute-start.6
  13.2 3.3 %collective-permute-done.halo = f32[2,80,512]{2,1,0:T(8,128)S(1)} collective-permute-done((f32[2,80,512]{2,1,0:T(8,128)S(1)}, f32[2,80,512]{2,1,0:T(8,128)S(1)}, u32[]{:S(2)}, u32[]{:S(2)}) %collective-permute-start) | collective-permute-done | bytes 327712 | tf_op jit(solution)/shard_map/ppermute | solution.py:454
  16.5 0.1 finish.3.refs_0_
  16.6 2.5 %collective-permute-start.4 = (f32[2,80,512]{2,1,0:T(8,128)S(1)}, f32[2,80,512]{2,1,0:T(8,128)S(1)}, u32[]{:S(2)}, u32[]{:S(2)}) collective-permute-start(f32[2,80,512]{2,1,0:T(8,128)S(1)} %finish.3.refs_0_), channel_id=1, source_target_pairs={{1,2},{3,4},{5,6},{7,8},{9,10},{11,12},{13,14},{17,18},{19,20},{21... | collective-permute-start | bytes 983048 | tf_op jit(solution)/shard_map/ppermute | solution.py:454
  19.1 0.1 collective-permute-start.3
  19.2 0.9 %part.4 = (f32[2,128,512]{2,1,0:T(8,128)S(1)}, f32[2,128,512]{2,1,0:T(8,128)S(1)}) custom-call(f32[2,80,512]{2,1,0:T(8,128)S(1)} %finish.3.refs_0_, f32[2,48,512]{2,1,0:T(8,128)S(1)} %finish.4.refs_1_, f32[2,128,512]{2,1,0:T(8,128)S(1)} %finish.5.refs_2_, f32[2,128,512]{2,1,0:T(8,128)S(1)} %get-tuple-element.54.refs_3_.gain.refs_2_, ...), custom_call_target="tpu_custom_call" | custom-call | bytes 3670016 | tf_op jit(solution)/shard_map/part/pallas_call | solution.py:53
  20.1 0.1 matrices.1
  20.2 0.3 coarse_setup.1.gain
  20.5 6.6 %collective-permute-done.4.halo = f32[2,80,512]{2,1,0:T(8,128)S(1)} collective-permute-done((f32[2,80,512]{2,1,0:T(8,128)S(1)}, f32[2,80,512]{2,1,0:T(8,128)S(1)}, u32[]{:S(2)}, u32[]{:S(2)}) %collective-permute-start.4) | collective-permute-done | bytes 327712 | tf_op jit(solution)/shard_map/ppermute | solution.py:454
  27.1 0.3 finish_pool.3
  27.4 3.2 %collective-permute-done.3.halo = f32[2,48,512]{2,1,0:T(8,128)S(1)} collective-permute-done((f32[2,48,512]{2,1,0:T(8,128)S(1)}, f32[2,48,512]{2,1,0:T(8,128)S(1)}, u32[]{:S(2)}, u32[]{:S(2)}) %collective-permute-start.3) | collective-permute-done | bytes 196640 | tf_op jit(solution)/shard_map/ppermute | solution.py:454
  30.6 0.2 finish_pool.4
  30.8 2.5 %collective-permute-start.5 = (f32[2,64,256]{2,1,0:T(8,128)S(1)}, f32[2,64,256]{2,1,0:T(8,128)S(1)}, u32[]{:S(2)}, u32[]{:S(2)}) collective-permute-start(f32[2,64,256]{2,1,0:T(8,128)S(1)} %get-tuple-element.69), channel_id=1, source_target_pairs={{1,2},{3,4},{5,6},{7,8},{9,10},{11,12},{13,14},{17,18},{19,20},{21... | collective-permute-start | bytes 393224 | tf_op jit(solution)/shard_map/ppermute | solution.py:454
  33.4 0.0 collective-permute-done.6.halo
  33.4 0.4 finish_pool.5
  33.7 0.1 collective-permute-start.7
  33.8 0.5 collective-permute-start.16
  34.3 1.5 %part_defect.1 = (f32[2,128,512]{2,1,0:T(8,128)S(1)}, f32[2,128,512]{2,1,0:T(8,128)S(1)}, f32[2,64,256]{2,1,0:T(8,128)S(1)}) custom-call(f32[2,80,512]{2,1,0:T(8,128)S(1)} %get-tuple-element.70.refs_0_, f32[2,48,512]{2,1,0:T(8,128)S(1)} %get-tuple-element.71.refs_1_, f32[2,128,512]{2,1,0:T(8,128)S(1)} %get-tuple-element.73.refs_2_, ...), custom_call_target="tpu_custom_call" | custom-call | bytes 3932160 | tf_op jit(solution)/shard_map/part_defect/pallas_call | solution.py:53
  35.8 0.2 collective-permute-done.5.far.sums
  36.0 0.0 collective-permute-done.7.near
  36.1 1.8 %collective-permute-start.8 = (f32[2,64,256]{2,1,0:T(8,128)S(1)}, f32[2,64,256]{2,1,0:T(8,128)S(1)}, u32[]{:S(2)}, u32[]{:S(2)}) collective-permute-start(f32[2,64,256]{2,1,0:T(8,128)S(1)} %coarse_first.1.fix.own), channel_id=1, source_target_pairs={{1,2},{3,4},{5,6},{7,8},{9,10},{11,12},{13,14},{17,18},{19,20},{21... | collective-permute-start | bytes 393224 | tf_op jit(solution)/shard_map/ppermute | solution.py:454
  37.9 0.5 three.1
  38.4 1.0 %collective-permute-start.10 = (f32[2,64,256]{2,1,0:T(8,128)S(1)}, f32[2,64,256]{2,1,0:T(8,128)S(1)}, u32[]{:S(2)}, u32[]{:S(2)}) collective-permute-start(f32[2,64,256]{2,1,0:T(8,128)S(1)} %get-tuple-element.85), channel_id=1, source_target_pairs={{1,2},{3,4},{5,6},{7,8},{9,10},{11,12},{13,14},{17,18},{19,20},{21... | collective-permute-start | bytes 393224 | tf_op jit(solution)/shard_map/ppermute | solution.py:454
  39.3 0.1 coarse_part.3.part
  39.5 1.1 %collective-permute-done.8.far = f32[2,64,256]{2,1,0:T(8,128)S(1)} collective-permute-done((f32[2,64,256]{2,1,0:T(8,128)S(1)}, f32[2,64,256]{2,1,0:T(8,128)S(1)}, u32[]{:S(2)}, u32[]{:S(2)}) %collective-permute-start.8) | collective-permute-done | bytes 131104 | tf_op jit(solution)/shard_map/ppermute | solution.py:454
  40.7 2.5 %collective-permute-start.11 = (f32[2,64,256]{2,1,0:T(8,128)S(1)}, f32[2,64,256]{2,1,0:T(8,128)S(1)}, u32[]{:S(2)}, u32[]{:S(2)}) collective-permute-start(f32[2,64,256]{2,1,0:T(8,128)S(1)} %coarse_finish.3.fix), channel_id=1, source_target_pairs={{1,2},{3,4},{5,6},{7,8},{9,10},{11,12},{13,14},{17,18},{19,20},{21... | collective-permute-start | bytes 393224 | tf_op jit(solution)/shard_map/ppermute | solution.py:454
  43.2 0.0 collective-permute-start.12
  43.2 1.2 %collective-permute-start.13 = (f32[2,64,256]{2,1,0:T(8,128)S(1)}, f32[2,64,256]{2,1,0:T(8,128)S(1)}, u32[]{:S(2)}, u32[]{:S(2)}) collective-permute-start(f32[2,64,256]{2,1,0:T(8,128)S(1)} %get-tuple-element.87), channel_id=1, source_target_pairs={{1,2},{3,4},{5,6},{7,8},{9,10},{11,12},{13,14},{17,18},{19,20},{21... | collective-permute-start | bytes 393224 | tf_op jit(solution)/shard_map/ppermute | solution.py:454
  44.3 0.2 coarse_part.4.part
  44.5 3.3 %collective-permute-done.11.far = f32[2,64,256]{2,1,0:T(8,128)S(1)} collective-permute-done((f32[2,64,256]{2,1,0:T(8,128)S(1)}, f32[2,64,256]{2,1,0:T(8,128)S(1)}, u32[]{:S(2)}, u32[]{:S(2)}) %collective-permute-start.11) | collective-permute-done | bytes 131104 | tf_op jit(solution)/shard_map/ppermute | solution.py:454
  47.8 2.5 %collective-permute-start.14 = (f32[2,64,256]{2,1,0:T(8,128)S(1)}, f32[2,64,256]{2,1,0:T(8,128)S(1)}, u32[]{:S(2)}, u32[]{:S(2)}) collective-permute-start(f32[2,64,256]{2,1,0:T(8,128)S(1)} %coarse_finish.4.fix), channel_id=1, source_target_pairs={{1,2},{3,4},{5,6},{7,8},{9,10},{11,12},{13,14},{17,18},{19,20},{21... | collective-permute-start | bytes 393224 | tf_op jit(solution)/shard_map/ppermute | solution.py:454
  50.4 0.0 collective-permute-start.15
  50.4 0.2 collective-permute-start.18
  50.5 0.2 coarse_part.5.part
  50.7 0.0 collective-permute-done.13.refs_1_
  50.7 2.3 %collective-permute-done.14.far = f32[2,64,256]{2,1,0:T(8,128)S(1)} collective-permute-done((f32[2,64,256]{2,1,0:T(8,128)S(1)}, f32[2,64,256]{2,1,0:T(8,128)S(1)}, u32[]{:S(2)}, u32[]{:S(2)}) %collective-permute-start.14) | collective-permute-done | bytes 131104 | tf_op jit(solution)/shard_map/ppermute | solution.py:454
  53.0 0.0 collective-permute-done.15.near
  53.1 1.8 %collective-permute-start.17 = (f32[2,64,256]{2,1,0:T(8,128)S(1)}, f32[2,64,256]{2,1,0:T(8,128)S(1)}, u32[]{:S(2)}, u32[]{:S(2)}) collective-permute-start(f32[2,64,256]{2,1,0:T(8,128)S(1)} %coarse_finish.5.fix), channel_id=1, source_target_pairs={{1,2},{3,4},{5,6},{7,8},{9,10},{11,12},{13,14},{17,18},{19,20},{21... | collective-permute-start | bytes 393224 | tf_op jit(solution)/shard_map/ppermute | solution.py:454
  54.9 1.1 %third.1 = (f32[2,128,512]{2,1,0:T(8,128)S(1)}, f32[2,128,512]{2,1,0:T(8,128)S(1)}) custom-call(f32[2,128,512]{2,1,0:T(8,128)S(1)} %get-tuple-element.74.far, f32[2,128,512]{2,1,0:T(8,128)S(1)} %get-tuple-element.75.near, f32[2,64,256]{2,1,0:T(8,128)S(1)} %coarse_finish.5.fix, f32[2,128,512]{2,1,0:T(8,128)S(1)} %collective-permute-done.16.near_halo, ...), custom_call_target="tpu_custom_call" | custom-call | bytes 3407872 | tf_op jit(solution)/shard_map/third/pallas_call | solution.py:53
  56.0 0.0 collective-permute-done.18.refs_2_
  56.0 0.6 rebuild.1.state_nb
  56.6 1.7 %collective-permute-done.17.halo = f32[2,64,256]{2,1,0:T(8,128)S(1)} collective-permute-done((f32[2,64,256]{2,1,0:T(8,128)S(1)}, f32[2,64,256]{2,1,0:T(8,128)S(1)}, u32[]{:S(2)}, u32[]{:S(2)}) %collective-permute-start.17) | collective-permute-done | bytes 131104 | tf_op jit(solution)/shard_map/ppermute | solution.py:454
  58.2 0.3 fix_far.1.refs_0_
  58.6 2.5 %collective-permute-start.20 = (f32[2,128,512]{2,1,0:T(8,128)S(1)}, f32[2,128,512]{2,1,0:T(8,128)S(1)}, u32[]{:S(2)}, u32[]{:S(2)}) collective-permute-start(f32[2,128,512]{2,1,0:T(8,128)S(1)} %fix_far.1.refs_0_), channel_id=1, source_target_pairs={{1,2},{3,4},{5,6},{7,8},{9,10},{11,12},{13,14},{17,18},{19,20},{21... | collective-permute-start | bytes 1572872 | tf_op jit(solution)/shard_map/ppermute | solution.py:454
  61.1 1.3 %collective-permute-done.19.halo = f32[2,64,256]{2,1,0:T(8,128)S(1)} collective-permute-done((f32[2,64,256]{2,1,0:T(8,128)S(1)}, f32[2,64,256]{2,1,0:T(8,128)S(1)}, u32[]{:S(2)}, u32[]{:S(2)}) %collective-permute-start.19) | collective-permute-done | bytes 131104 | tf_op jit(solution)/shard_map/ppermute | solution.py:457
  62.4 0.3 fix_near.1
  62.8 0.2 collective-permute-start.21
  63.0 0.4 collective-permute-start.22
  63.4 0.9 %part.5 = (f32[2,128,512]{2,1,0:T(8,128)S(1)}, f32[2,128,512]{2,1,0:T(8,128)S(1)}) custom-call(f32[2,128,512]{2,1,0:T(8,128)S(1)} %fix_far.1.refs_0_, f32[2,128,512]{2,1,0:T(8,128)S(1)} %get-tuple-element.99.refs_1_, f32[2,128,512]{2,1,0:T(8,128)S(1)} %get-tuple-element.54.refs_3_.gain.refs_2_, f32[2,2,128,512]{3,2,1,0:T(8,128)S(1)} %get-tuple-element.58.refs_4_.refs_3_), custom_call_target="tpu_custom_call" | custom-call | bytes 3670016 | tf_op jit(solution)/shard_map/part/pallas_call | solution.py:53
  64.3 0.1 collective-permute-done.21.refs_1_
  64.4 0.4 collective-permute-done.22.refs_3_
  64.8 1.0 %final.2 = (f32[2,2,128,512]{3,2,1,0:T(8,128)}, f32[2,128,512]{2,1,0:T(8,128)}) custom-call(s32[1]{0:T(128)} %bitcast.where, f32[1]{0:T(128)} %bitcast.1.keep, f32[2,128,512]{2,1,0:T(8,128)S(1)} %get-tuple-element.54.refs_3_.gain.refs_2_, f32[2,128,512]{2,1,0:T(8,128)S(1)} %copy-done, f32[2,128,512]{2,1,0:T(8,128)S(1)} %copy-done.1, ...), custom_call_target="tpu_custom_call" | custom-call | bytes 4718600 | tf_op jit(solution)/shard_map/final/pallas_call | solution.py:53
  65.7 6.9 %collective-permute-done.20.refs_1_ = f32[2,128,512]{2,1,0:T(8,128)S(1)} collective-permute-done((f32[2,128,512]{2,1,0:T(8,128)S(1)}, f32[2,128,512]{2,1,0:T(8,128)S(1)}, u32[]{:S(2)}, u32[]{:S(2)}) %collective-permute-start.20) | collective-permute-done | bytes 524320 | tf_op jit(solution)/shard_map/ppermute | solution.py:454
  72.6 1.0 %final.3 = (f32[2,2,128,512]{3,2,1,0:T(8,128)}, f32[2,128,512]{2,1,0:T(8,128)}) custom-call(s32[1]{0:T(128)} %bitcast.where, f32[1]{0:T(128)} %bitcast.1.keep, f32[2,128,512]{2,1,0:T(8,128)S(1)} %get-tuple-element.54.refs_3_.gain.refs_2_, f32[2,128,512]{2,1,0:T(8,128)S(1)} %copy-done, ...), custom_call_target="tpu_custom_call", output_to_operand_aliasing={{0}: (7, {}), {1}: (8, {})} | custom-call | bytes 5767176 | tf_op jit(solution)/shard_map/final/pallas_call | solution.py:53
  (16 shorter events, 0.3 us)
Async XLA Ops:
  0.6 4.2 %copy-start = (f32[2,128,512]{2,1,0:T(8,128)S(1)}, f32[2,128,512]{2,1,0:T(8,128)}, u32[]{:S(2)}) copy-start(f32[2,128,512]{2,1,0:T(8,128)} %phi.7) | copy-start | bytes 1572868
  2.0 11.1 %collective-permute-start.1 = (f32[2,128,512]{2,1,0:T(8,128)S(1)}, f32[2,128,512]{2,1,0:T(8,128)S(1)}, u32[]{:S(2)}, u32[]{:S(2)}) collective-permute-start(f32[2,128,512]{2,1,0:T(8,128)S(1)} %get-tuple-element.57.refs_2_), channel_id=1, source_target_pairs={{0,1},{1,0},{2,3},{3,2},{4,5},{5,4},{6,7},{7,6},{8,9},{9,8},{10,11... | collective-permute-start | bytes 1572872 | tf_op jit(solution)/shard_map/ppermute | solution.py:457
  2.1 10.9 %collective-permute-start.2 = (f32[2,48,512]{2,1,0:T(8,128)S(1)}, f32[2,48,512]{2,1,0:T(8,128)S(1)}, u32[]{:S(2)}, u32[]{:S(2)}) collective-permute-start(f32[2,48,512]{2,1,0:T(8,128)S(1)} %get-tuple-element.56.refs_1_), channel_id=1, source_target_pairs={{1,2},{3,4},{5,6},{7,8},{9,10},{11,12},{13,14},{17,18},{19,20},{21... | collective-permute-start | bytes 589832 | tf_op jit(solution)/shard_map/ppermute | solution.py:454
  4.8 11.7 %collective-permute-start = (f32[2,80,512]{2,1,0:T(8,128)S(1)}, f32[2,80,512]{2,1,0:T(8,128)S(1)}, u32[]{:S(2)}, u32[]{:S(2)}) collective-permute-start(f32[2,80,512]{2,1,0:T(8,128)S(1)} %get-tuple-element.55.refs_0_), channel_id=1, source_target_pairs={{1,2},{3,4},{5,6},{7,8},{9,10},{11,12},{13,14},{17,18},{19,20},{21... | collective-permute-start | bytes 983048 | tf_op jit(solution)/shard_map/ppermute | solution.py:454
  4.8 1.2 %copy-start.2 = (f32[2,2,128,512]{3,2,1,0:T(8,128)S(1)}, f32[2,2,128,512]{3,2,1,0:T(8,128)}, u32[]{:S(2)}) copy-start(f32[2,2,128,512]{3,2,1,0:T(8,128)} %cot.1) | copy-start | bytes 3145732
  13.2 20.2 %collective-permute-start.6 = (f32[2,128,512]{2,1,0:T(8,128)S(1)}, f32[2,128,512]{2,1,0:T(8,128)S(1)}, u32[]{:S(2)}, u32[]{:S(2)}) collective-permute-start(f32[2,128,512]{2,1,0:T(8,128)S(1)} %finish.5.refs_2_), channel_id=1, source_target_pairs={{0,1},{1,0},{2,3},{3,2},{4,5},{5,4},{6,7},{7,6},{8,9},{9,8},{10,11... | collective-permute-start | bytes 1572872 | tf_op jit(solution)/shard_map/ppermute | solution.py:457
  16.6 10.5 %collective-permute-start.4 = (f32[2,80,512]{2,1,0:T(8,128)S(1)}, f32[2,80,512]{2,1,0:T(8,128)S(1)}, u32[]{:S(2)}, u32[]{:S(2)}) collective-permute-start(f32[2,80,512]{2,1,0:T(8,128)S(1)} %finish.3.refs_0_), channel_id=1, source_target_pairs={{1,2},{3,4},{5,6},{7,8},{9,10},{11,12},{13,14},{17,18},{19,20},{21... | collective-permute-start | bytes 983048 | tf_op jit(solution)/shard_map/ppermute | solution.py:454
  19.1 11.5 %collective-permute-start.3 = (f32[2,48,512]{2,1,0:T(8,128)S(1)}, f32[2,48,512]{2,1,0:T(8,128)S(1)}, u32[]{:S(2)}, u32[]{:S(2)}) collective-permute-start(f32[2,48,512]{2,1,0:T(8,128)S(1)} %finish.4.refs_1_), channel_id=1, source_target_pairs={{1,2},{3,4},{5,6},{7,8},{9,10},{11,12},{13,14},{17,18},{19,20},{21... | collective-permute-start | bytes 589832 | tf_op jit(solution)/shard_map/ppermute | solution.py:454
  30.8 5.2 %collective-permute-start.5 = (f32[2,64,256]{2,1,0:T(8,128)S(1)}, f32[2,64,256]{2,1,0:T(8,128)S(1)}, u32[]{:S(2)}, u32[]{:S(2)}) collective-permute-start(f32[2,64,256]{2,1,0:T(8,128)S(1)} %get-tuple-element.69), channel_id=1, source_target_pairs={{1,2},{3,4},{5,6},{7,8},{9,10},{11,12},{13,14},{17,18},{19,20},{21... | collective-permute-start | bytes 393224 | tf_op jit(solution)/shard_map/ppermute | solution.py:454
  33.7 2.3 %collective-permute-start.7 = (f32[2,64,256]{2,1,0:T(8,128)S(1)}, f32[2,64,256]{2,1,0:T(8,128)S(1)}, u32[]{:S(2)}, u32[]{:S(2)}) collective-permute-start(f32[2,64,256]{2,1,0:T(8,128)S(1)} %get-tuple-element.77), channel_id=1, source_target_pairs={{0,1},{1,0},{2,3},{3,2},{4,5},{5,4},{6,7},{7,6},{8,9},{9,8},{10,11... | collective-permute-start | bytes 393224 | tf_op jit(solution)/shard_map/ppermute | solution.py:457
  33.8 21.1 %collective-permute-start.16 = (f32[2,128,512]{2,1,0:T(8,128)S(1)}, f32[2,128,512]{2,1,0:T(8,128)S(1)}, u32[]{:S(2)}, u32[]{:S(2)}) collective-permute-start(f32[2,128,512]{2,1,0:T(8,128)S(1)} %get-tuple-element.73.refs_2_), channel_id=1, source_target_pairs={{0,1},{1,0},{2,3},{3,2},{4,5},{5,4},{6,7},{7,6},{8,9},{9,8},{10,11... | collective-permute-start | bytes 1572872 | tf_op jit(solution)/shard_map/ppermute | solution.py:457
  36.1 4.5 %collective-permute-start.8 = (f32[2,64,256]{2,1,0:T(8,128)S(1)}, f32[2,64,256]{2,1,0:T(8,128)S(1)}, u32[]{:S(2)}, u32[]{:S(2)}) collective-permute-start(f32[2,64,256]{2,1,0:T(8,128)S(1)} %coarse_first.1.fix.own), channel_id=1, source_target_pairs={{1,2},{3,4},{5,6},{7,8},{9,10},{11,12},{13,14},{17,18},{19,20},{21... | collective-permute-start | bytes 393224 | tf_op jit(solution)/shard_map/ppermute | solution.py:454
  37.9 2.7 %collective-permute-start.9 = (f32[2,64,256]{2,1,0:T(8,128)S(1)}, f32[2,64,256]{2,1,0:T(8,128)S(1)}, u32[]{:S(2)}, u32[]{:S(2)}) collective-permute-start(f32[2,64,256]{2,1,0:T(8,128)S(1)} %coarse_first.1.fix.own), channel_id=1, source_target_pairs={{0,1},{1,0},{2,3},{3,2},{4,5},{5,4},{6,7},{7,6},{8,9},{9,8},{10,11... | collective-permute-start | bytes 393224 | tf_op jit(solution)/shard_map/ppermute | solution.py:457
  38.4 6.1 %collective-permute-start.10 = (f32[2,64,256]{2,1,0:T(8,128)S(1)}, f32[2,64,256]{2,1,0:T(8,128)S(1)}, u32[]{:S(2)}, u32[]{:S(2)}) collective-permute-start(f32[2,64,256]{2,1,0:T(8,128)S(1)} %get-tuple-element.85), channel_id=1, source_target_pairs={{1,2},{3,4},{5,6},{7,8},{9,10},{11,12},{13,14},{17,18},{19,20},{21... | collective-permute-start | bytes 393224 | tf_op jit(solution)/shard_map/ppermute | solution.py:454
  40.7 7.1 %collective-permute-start.11 = (f32[2,64,256]{2,1,0:T(8,128)S(1)}, f32[2,64,256]{2,1,0:T(8,128)S(1)}, u32[]{:S(2)}, u32[]{:S(2)}) collective-permute-start(f32[2,64,256]{2,1,0:T(8,128)S(1)} %coarse_finish.3.fix), channel_id=1, source_target_pairs={{1,2},{3,4},{5,6},{7,8},{9,10},{11,12},{13,14},{17,18},{19,20},{21... | collective-permute-start | bytes 393224 | tf_op jit(solution)/shard_map/ppermute | solution.py:454
  43.2 4.6 %collective-permute-start.12 = (f32[2,64,256]{2,1,0:T(8,128)S(1)}, f32[2,64,256]{2,1,0:T(8,128)S(1)}, u32[]{:S(2)}, u32[]{:S(2)}) collective-permute-start(f32[2,64,256]{2,1,0:T(8,128)S(1)} %coarse_finish.3.fix), channel_id=1, source_target_pairs={{0,1},{1,0},{2,3},{3,2},{4,5},{5,4},{6,7},{7,6},{8,9},{9,8},{10,11... | collective-permute-start | bytes 393224 | tf_op jit(solution)/shard_map/ppermute | solution.py:457
  43.2 7.5 %collective-permute-start.13 = (f32[2,64,256]{2,1,0:T(8,128)S(1)}, f32[2,64,256]{2,1,0:T(8,128)S(1)}, u32[]{:S(2)}, u32[]{:S(2)}) collective-permute-start(f32[2,64,256]{2,1,0:T(8,128)S(1)} %get-tuple-element.87), channel_id=1, source_target_pairs={{1,2},{3,4},{5,6},{7,8},{9,10},{11,12},{13,14},{17,18},{19,20},{21... | collective-permute-start | bytes 393224 | tf_op jit(solution)/shard_map/ppermute | solution.py:454
  47.8 5.2 %collective-permute-start.14 = (f32[2,64,256]{2,1,0:T(8,128)S(1)}, f32[2,64,256]{2,1,0:T(8,128)S(1)}, u32[]{:S(2)}, u32[]{:S(2)}) collective-permute-start(f32[2,64,256]{2,1,0:T(8,128)S(1)} %coarse_finish.4.fix), channel_id=1, source_target_pairs={{1,2},{3,4},{5,6},{7,8},{9,10},{11,12},{13,14},{17,18},{19,20},{21... | collective-permute-start | bytes 393224 | tf_op jit(solution)/shard_map/ppermute | solution.py:454
  50.4 2.7 %collective-permute-start.15 = (f32[2,64,256]{2,1,0:T(8,128)S(1)}, f32[2,64,256]{2,1,0:T(8,128)S(1)}, u32[]{:S(2)}, u32[]{:S(2)}) collective-permute-start(f32[2,64,256]{2,1,0:T(8,128)S(1)} %coarse_finish.4.fix), channel_id=1, source_target_pairs={{0,1},{1,0},{2,3},{3,2},{4,5},{5,4},{6,7},{7,6},{8,9},{9,8},{10,11... | collective-permute-start | bytes 393224 | tf_op jit(solution)/shard_map/ppermute | solution.py:457
  50.4 5.6 %collective-permute-start.18 = (f32[2,64,256]{2,1,0:T(8,128)S(1)}, f32[2,64,256]{2,1,0:T(8,128)S(1)}, u32[]{:S(2)}, u32[]{:S(2)}) collective-permute-start(f32[2,64,256]{2,1,0:T(8,128)S(1)} %get-tuple-element.95), channel_id=1, source_target_pairs={{1,2},{3,4},{5,6},{7,8},{9,10},{11,12},{13,14},{17,18},{19,20},{21... | collective-permute-start | bytes 393224 | tf_op jit(solution)/shard_map/ppermute | solution.py:454
  53.1 5.1 %collective-permute-start.17 = (f32[2,64,256]{2,1,0:T(8,128)S(1)}, f32[2,64,256]{2,1,0:T(8,128)S(1)}, u32[]{:S(2)}, u32[]{:S(2)}) collective-permute-start(f32[2,64,256]{2,1,0:T(8,128)S(1)} %coarse_finish.5.fix), channel_id=1, source_target_pairs={{1,2},{3,4},{5,6},{7,8},{9,10},{11,12},{13,14},{17,18},{19,20},{21... | collective-permute-start | bytes 393224 | tf_op jit(solution)/shard_map/ppermute | solution.py:454
  58.6 14.0 %collective-permute-start.20 = (f32[2,128,512]{2,1,0:T(8,128)S(1)}, f32[2,128,512]{2,1,0:T(8,128)S(1)}, u32[]{:S(2)}, u32[]{:S(2)}) collective-permute-start(f32[2,128,512]{2,1,0:T(8,128)S(1)} %fix_far.1.refs_0_), channel_id=1, source_target_pairs={{1,2},{3,4},{5,6},{7,8},{9,10},{11,12},{13,14},{17,18},{19,20},{21... | collective-permute-start | bytes 1572872 | tf_op jit(solution)/shard_map/ppermute | solution.py:454
  61.1 1.3 %collective-permute-start.19 = (f32[2,64,256]{2,1,0:T(8,128)S(1)}, f32[2,64,256]{2,1,0:T(8,128)S(1)}, u32[]{:S(2)}, u32[]{:S(2)}) collective-permute-start(f32[2,64,256]{2,1,0:T(8,128)S(1)} %coarse_finish.5.fix), channel_id=1, source_target_pairs={{0,1},{1,0},{2,3},{3,2},{4,5},{5,4},{6,7},{7,6},{8,9},{9,8},{10,11... | collective-permute-start | bytes 393224 | tf_op jit(solution)/shard_map/ppermute | solution.py:457
  62.8 1.6 %collective-permute-start.21 = (f32[2,64,512]{2,1,0:T(8,128)S(1)}, f32[2,64,512]{2,1,0:T(8,128)S(1)}, u32[]{:S(2)}, u32[]{:S(2)}) collective-permute-start(f32[2,64,512]{2,1,0:T(8,128)S(1)} %get-tuple-element.102), channel_id=1, source_target_pairs={{0,1},{1,0},{2,3},{3,2},{4,5},{5,4},{6,7},{7,6},{8,9},{9,8},{10,11... | collective-permute-start | bytes 786440 | tf_op jit(solution)/shard_map/ppermute | solution.py:457
  63.0 1.8 %collective-permute-start.22 = (f32[2,64,512]{2,1,0:T(8,128)S(1)}, f32[2,64,512]{2,1,0:T(8,128)S(1)}, u32[]{:S(2)}, u32[]{:S(2)}) collective-permute-start(f32[2,64,512]{2,1,0:T(8,128)S(1)} %get-tuple-element.103), channel_id=1, source_target_pairs={{0,1},{1,0},{2,3},{3,2},{4,5},{5,4},{6,7},{7,6},{8,9},{9,8},{10,11... | collective-permute-start | bytes 786440 | tf_op jit(solution)/shard_map/ppermute | solution.py:457
  63.4 1.4 %copy-start.1 = (f32[2,128,512]{2,1,0:T(8,128)S(1)}, f32[2,128,512]{2,1,0:T(8,128)}, u32[]{:S(2)}) copy-start(f32[2,128,512]{2,1,0:T(8,128)} %psi.3) | copy-start | bytes 1572868

commit v10 on v7

--- a/solution.py
+++ b/solution.py
@@ -402,7 +402,7 @@
     c = where[0]
     plane = c if i == 0 else 1 - c
     rows_all = halo.shape[1]
-    step = rows_all // 2
+    step = rows_all // 4
     copies = []
     for n, start in enumerate(range(0, rows_all, step)):
         for r in range(start, start + step, BLOCK):
@@ -556,7 +556,7 @@
         scratch = []
         for halo in fields[1::2]:
             n = halo.shape[1]
-            scratch += [pltpu.VMEM((2, n, cols), F32), pltpu.VMEM((n, cols), F32), pltpu.SemaphoreType.DMA((4,))]
+            scratch += [pltpu.VMEM((2, n, cols), F32), pltpu.VMEM((n, cols), F32), pltpu.SemaphoreType.DMA((8,))]
         body = functools.partial(final_body, which)
         aliases = {len(args) - 2: 0, len(args) - 1: 1} if done else None
         return call(body, "final", outs, args, in_specs, [ANY, ANY], scratch, aliases, work=10)

time: 73.8 us -> 73.8 us (level)
  no operation moved by 1% of the time
where the time goes in v10:
time: 73.8 us; the launch traced here: 73.6 us
  waiting for transfers between devices  34.5 us (47%)
  starting transfers between devices  24.3 us (33%)
  Pallas kernels  12.7 us (17%)
  local copies, waits for them, and re-layouts  1.23 us (2%)
  between operations  0.9 us (1%)
    ppermute x13, waiting for transfers between devices, swap_far(): return lax.ppermute(x, ('grp', 'gx'), across)  32.6 us
    ppermute x13, starting transfers between devices, swap_far(): return lax.ppermute(x, ('grp', 'gx'), across)  22.9 us
    pallas_call x28, Pallas kernels, call(): pl.pallas_call(body, out_shape=shapes, in_specs=in_specs or [VMEM] * len(...  12.7 us
    ppermute x10, waiting for transfers between devices, swap_near(): return lax.ppermute(x, 'gx', on_chip)  1.81 us
  transfers between devices with their start and end apart: 23, of which 12 were waited for; matrix products, arithmetic and copies ran while one was open for 0% of the time, Pallas kernels for 14%

profile of v10, /device:TPU:1, one launch (start us, length us, event | category | flops | bytes accessed | tf_op | source)
XLA Modules:
  0.0 73.6 jit_solution(17578791451866588218)
XLA Ops:
  0.7 1.3 %take.1 = (f32[2,80,512]{2,1,0:T(8,128)S(1)}, f32[2,48,512]{2,1,0:T(8,128)S(1)}, f32[2,128,512]{2,1,0:T(8,128)S(1)}) custom-call(s32[1]{0:T(128)} %bitcast.where, f32[2,2,128,512]{3,2,1,0:T(8,128)} %warm.1), custom_call_target="tpu_custom_call" | custom-call | bytes 2097156 | tf_op jit(solution)/shard_map/take/pallas_call | solution.py:53
  2.0 0.1 collective-permute-start.1
  2.1 2.6 %collective-permute-start.2 = (f32[2,48,512]{2,1,0:T(8,128)S(1)}, f32[2,48,512]{2,1,0:T(8,128)S(1)}, u32[]{:S(2)}, u32[]{:S(2)}) collective-permute-start(f32[2,48,512]{2,1,0:T(8,128)S(1)} %get-tuple-element.54.refs_1_), channel_id=1, source_target_pairs={{1,2},{3,4},{5,6},{7,8},{9,10},{11,12},{13,14},{17,18},{19,20},{21... | collective-permute-start | bytes 589832 | tf_op jit(solution)/shard_map/ppermute | solution.py:454
  4.8 0.1 collective-permute-start
  4.8 1.2 %copy-done.2 = f32[2,2,128,512]{3,2,1,0:T(8,128)S(1)} copy-done((f32[2,2,128,512]{3,2,1,0:T(8,128)S(1)}, f32[2,2,128,512]{3,2,1,0:T(8,128)}, u32[]{:S(2)}) %copy-start.2) | copy-done | bytes 1048600
  6.1 0.2 setup.1
  6.3 0.9 %part.3 = (f32[2,128,512]{2,1,0:T(8,128)S(1)}, f32[2,128,512]{2,1,0:T(8,128)S(1)}) custom-call(f32[2,80,512]{2,1,0:T(8,128)S(1)} %get-tuple-element.53.refs_0_, f32[2,48,512]{2,1,0:T(8,128)S(1)} %get-tuple-element.54.refs_1_, f32[2,128,512]{2,1,0:T(8,128)S(1)} %get-tuple-element.55.refs_2_, f32[2,128,512]{2,1,0:T(8,128)S(1)} %get-tuple-element.52.refs_3_.gain.refs_2_, ...), custom_call_target="tpu_custom_call" | custom-call | bytes 3670016 | tf_op jit(solution)/shard_map/part/pallas_call | solution.py:53
  7.3 5.7 %collective-permute-done.2.halo = f32[2,48,512]{2,1,0:T(8,128)S(1)} collective-permute-done((f32[2,48,512]{2,1,0:T(8,128)S(1)}, f32[2,48,512]{2,1,0:T(8,128)S(1)}, u32[]{:S(2)}, u32[]{:S(2)}) %collective-permute-start.2) | collective-permute-done | bytes 196640 | tf_op jit(solution)/shard_map/ppermute | solution.py:454
  13.0 0.1 finish.5.refs_2_
  13.2 0.1 collective-permute-start.6
  13.2 3.3 %collective-permute-done.halo = f32[2,80,512]{2,1,0:T(8,128)S(1)} collective-permute-done((f32[2,80,512]{2,1,0:T(8,128)S(1)}, f32[2,80,512]{2,1,0:T(8,128)S(1)}, u32[]{:S(2)}, u32[]{:S(2)}) %collective-permute-start) | collective-permute-done | bytes 327712 | tf_op jit(solution)/shard_map/ppermute | solution.py:454
  16.5 0.1 finish.3.refs_0_
  16.6 2.5 %collective-permute-start.4 = (f32[2,80,512]{2,1,0:T(8,128)S(1)}, f32[2,80,512]{2,1,0:T(8,128)S(1)}, u32[]{:S(2)}, u32[]{:S(2)}) collective-permute-start(f32[2,80,512]{2,1,0:T(8,128)S(1)} %finish.3.refs_0_), channel_id=1, source_target_pairs={{1,2},{3,4},{5,6},{7,8},{9,10},{11,12},{13,14},{17,18},{19,20},{21... | collective-permute-start | bytes 983048 | tf_op jit(solution)/shard_map/ppermute | solution.py:454
  19.1 0.1 collective-permute-start.3
  19.2 0.9 %part.4 = (f32[2,128,512]{2,1,0:T(8,128)S(1)}, f32[2,128,512]{2,1,0:T(8,128)S(1)}) custom-call(f32[2,80,512]{2,1,0:T(8,128)S(1)} %finish.3.refs_0_, f32[2,48,512]{2,1,0:T(8,128)S(1)} %finish.4.refs_1_, f32[2,128,512]{2,1,0:T(8,128)S(1)} %finish.5.refs_2_, f32[2,128,512]{2,1,0:T(8,128)S(1)} %get-tuple-element.52.refs_3_.gain.refs_2_, ...), custom_call_target="tpu_custom_call" | custom-call | bytes 3670016 | tf_op jit(solution)/shard_map/part/pallas_call | solution.py:53
  20.1 0.1 matrices.1
  20.2 6.8 %collective-permute-done.4.halo = f32[2,80,512]{2,1,0:T(8,128)S(1)} collective-permute-done((f32[2,80,512]{2,1,0:T(8,128)S(1)}, f32[2,80,512]{2,1,0:T(8,128)S(1)}, u32[]{:S(2)}, u32[]{:S(2)}) %collective-permute-start.4) | collective-permute-done | bytes 327712 | tf_op jit(solution)/shard_map/ppermute | solution.py:454
  27.1 0.3 finish_pool.3
  27.4 3.2 %collective-permute-done.3.halo = f32[2,48,512]{2,1,0:T(8,128)S(1)} collective-permute-done((f32[2,48,512]{2,1,0:T(8,128)S(1)}, f32[2,48,512]{2,1,0:T(8,128)S(1)}, u32[]{:S(2)}, u32[]{:S(2)}) %collective-permute-start.3) | collective-permute-done | bytes 196640 | tf_op jit(solution)/shard_map/ppermute | solution.py:454
  30.6 0.2 finish_pool.4
  30.8 2.5 %collective-permute-start.5 = (f32[2,64,256]{2,1,0:T(8,128)S(1)}, f32[2,64,256]{2,1,0:T(8,128)S(1)}, u32[]{:S(2)}, u32[]{:S(2)}) collective-permute-start(f32[2,64,256]{2,1,0:T(8,128)S(1)} %get-tuple-element.66), channel_id=1, source_target_pairs={{1,2},{3,4},{5,6},{7,8},{9,10},{11,12},{13,14},{17,18},{19,20},{21... | collective-permute-start | bytes 393224 | tf_op jit(solution)/shard_map/ppermute | solution.py:454
  33.4 0.0 collective-permute-done.6.halo
  33.4 0.4 finish_pool.5
  33.7 0.1 collective-permute-start.7
  33.8 0.3 coarse_setup.1.gain
  34.1 0.6 collective-permute-start.16
  34.7 1.5 %part_defect.1 = (f32[2,128,512]{2,1,0:T(8,128)S(1)}, f32[2,128,512]{2,1,0:T(8,128)S(1)}, f32[2,64,256]{2,1,0:T(8,128)S(1)}) custom-call(f32[2,80,512]{2,1,0:T(8,128)S(1)} %get-tuple-element.67.refs_0_, f32[2,48,512]{2,1,0:T(8,128)S(1)} %get-tuple-element.68.refs_1_, f32[2,128,512]{2,1,0:T(8,128)S(1)} %get-tuple-element.70.refs_2_, ...), custom_call_target="tpu_custom_call" | custom-call | bytes 3932160 | tf_op jit(solution)/shard_map/part_defect/pallas_call | solution.py:53
  36.2 0.0 collective-permute-done.7.near
  36.2 1.6 %collective-permute-start.8 = (f32[2,64,256]{2,1,0:T(8,128)S(1)}, f32[2,64,256]{2,1,0:T(8,128)S(1)}, u32[]{:S(2)}, u32[]{:S(2)}) collective-permute-start(f32[2,64,256]{2,1,0:T(8,128)S(1)} %coarse_first.1.fix.own), channel_id=1, source_target_pairs={{1,2},{3,4},{5,6},{7,8},{9,10},{11,12},{13,14},{17,18},{19,20},{21... | collective-permute-start | bytes 393224 | tf_op jit(solution)/shard_map/ppermute | solution.py:454
  37.9 0.0 collective-permute-start.9
  37.9 0.5 three.1
  38.4 1.3 %collective-permute-start.10 = (f32[2,64,256]{2,1,0:T(8,128)S(1)}, f32[2,64,256]{2,1,0:T(8,128)S(1)}, u32[]{:S(2)}, u32[]{:S(2)}) collective-permute-start(f32[2,64,256]{2,1,0:T(8,128)S(1)} %get-tuple-element.81), channel_id=1, source_target_pairs={{1,2},{3,4},{5,6},{7,8},{9,10},{11,12},{13,14},{17,18},{19,20},{21... | collective-permute-start | bytes 393224 | tf_op jit(solution)/shard_map/ppermute | solution.py:454
  39.6 0.1 coarse_part.3.part
  39.8 1.1 %collective-permute-done.8.far = f32[2,64,256]{2,1,0:T(8,128)S(1)} collective-permute-done((f32[2,64,256]{2,1,0:T(8,128)S(1)}, f32[2,64,256]{2,1,0:T(8,128)S(1)}, u32[]{:S(2)}, u32[]{:S(2)}) %collective-permute-start.8) | collective-permute-done | bytes 131104 | tf_op jit(solution)/shard_map/ppermute | solution.py:454
  40.9 0.0 collective-permute-done.9.near
  41.0 2.5 %collective-permute-start.11 = (f32[2,64,256]{2,1,0:T(8,128)S(1)}, f32[2,64,256]{2,1,0:T(8,128)S(1)}, u32[]{:S(2)}, u32[]{:S(2)}) collective-permute-start(f32[2,64,256]{2,1,0:T(8,128)S(1)} %coarse_finish.3.fix), channel_id=1, source_target_pairs={{1,2},{3,4},{5,6},{7,8},{9,10},{11,12},{13,14},{17,18},{19,20},{21... | collective-permute-start | bytes 393224 | tf_op jit(solution)/shard_map/ppermute | solution.py:454
  43.4 0.0 collective-permute-start.12
  43.4 1.2 %collective-permute-start.13 = (f32[2,64,256]{2,1,0:T(8,128)S(1)}, f32[2,64,256]{2,1,0:T(8,128)S(1)}, u32[]{:S(2)}, u32[]{:S(2)}) collective-permute-start(f32[2,64,256]{2,1,0:T(8,128)S(1)} %get-tuple-element.83), channel_id=1, source_target_pairs={{1,2},{3,4},{5,6},{7,8},{9,10},{11,12},{13,14},{17,18},{19,20},{21... | collective-permute-start | bytes 393224 | tf_op jit(solution)/shard_map/ppermute | solution.py:454
  44.6 0.2 coarse_part.4.part
  44.8 1.7 %collective-permute-done.11.far = f32[2,64,256]{2,1,0:T(8,128)S(1)} collective-permute-done((f32[2,64,256]{2,1,0:T(8,128)S(1)}, f32[2,64,256]{2,1,0:T(8,128)S(1)}, u32[]{:S(2)}, u32[]{:S(2)}) %collective-permute-start.11) | collective-permute-done | bytes 131104 | tf_op jit(solution)/shard_map/ppermute | solution.py:454
  46.5 3.9 %collective-permute-start.14 = (f32[2,64,256]{2,1,0:T(8,128)S(1)}, f32[2,64,256]{2,1,0:T(8,128)S(1)}, u32[]{:S(2)}, u32[]{:S(2)}) collective-permute-start(f32[2,64,256]{2,1,0:T(8,128)S(1)} %coarse_finish.4.fix), channel_id=1, source_target_pairs={{1,2},{3,4},{5,6},{7,8},{9,10},{11,12},{13,14},{17,18},{19,20},{21... | collective-permute-start | bytes 393224 | tf_op jit(solution)/shard_map/ppermute | solution.py:454
  50.5 0.0 collective-permute-start.15
  50.5 0.2 collective-permute-start.18
  50.6 0.2 coarse_part.5.part
  50.8 2.3 %collective-permute-done.14.far = f32[2,64,256]{2,1,0:T(8,128)S(1)} collective-permute-done((f32[2,64,256]{2,1,0:T(8,128)S(1)}, f32[2,64,256]{2,1,0:T(8,128)S(1)}, u32[]{:S(2)}, u32[]{:S(2)}) %collective-permute-start.14) | collective-permute-done | bytes 131104 | tf_op jit(solution)/shard_map/ppermute | solution.py:454
  53.1 0.0 collective-permute-done.15.near
  53.2 1.8 %collective-permute-start.17 = (f32[2,64,256]{2,1,0:T(8,128)S(1)}, f32[2,64,256]{2,1,0:T(8,128)S(1)}, u32[]{:S(2)}, u32[]{:S(2)}) collective-permute-start(f32[2,64,256]{2,1,0:T(8,128)S(1)} %coarse_finish.5.fix), channel_id=1, source_target_pairs={{1,2},{3,4},{5,6},{7,8},{9,10},{11,12},{13,14},{17,18},{19,20},{21... | collective-permute-start | bytes 393224 | tf_op jit(solution)/shard_map/ppermute | solution.py:454
  55.0 1.0 %third.1 = (f32[2,128,512]{2,1,0:T(8,128)S(1)}, f32[2,128,512]{2,1,0:T(8,128)S(1)}) custom-call(f32[2,128,512]{2,1,0:T(8,128)S(1)} %get-tuple-element.71.far, f32[2,128,512]{2,1,0:T(8,128)S(1)} %get-tuple-element.72.near, f32[2,64,256]{2,1,0:T(8,128)S(1)} %coarse_finish.5.fix, f32[2,128,512]{2,1,0:T(8,128)S(1)} %collective-permute-done.16.near_halo, ...), custom_call_target="tpu_custom_call" | custom-call | bytes 3407872 | tf_op jit(solution)/shard_map/third/pallas_call | solution.py:53
  56.0 0.0 collective-permute-done.18.refs_2_
  56.0 0.6 rebuild.1.state_nb
  56.6 1.7 %collective-permute-done.17.halo = f32[2,64,256]{2,1,0:T(8,128)S(1)} collective-permute-done((f32[2,64,256]{2,1,0:T(8,128)S(1)}, f32[2,64,256]{2,1,0:T(8,128)S(1)}, u32[]{:S(2)}, u32[]{:S(2)}) %collective-permute-start.17) | collective-permute-done | bytes 131104 | tf_op jit(solution)/shard_map/ppermute | solution.py:454
  58.3 0.3 fix_far.1.refs_0_
  58.6 2.5 %collective-permute-start.20 = (f32[2,128,512]{2,1,0:T(8,128)S(1)}, f32[2,128,512]{2,1,0:T(8,128)S(1)}, u32[]{:S(2)}, u32[]{:S(2)}) collective-permute-start(f32[2,128,512]{2,1,0:T(8,128)S(1)} %fix_far.1.refs_0_), channel_id=1, source_target_pairs={{1,2},{3,4},{5,6},{7,8},{9,10},{11,12},{13,14},{17,18},{19,20},{21... | collective-permute-start | bytes 1572872 | tf_op jit(solution)/shard_map/ppermute | solution.py:454
  61.2 0.0 collective-permute-start.19
  61.2 1.3 %collective-permute-done.19.halo = f32[2,64,256]{2,1,0:T(8,128)S(1)} collective-permute-done((f32[2,64,256]{2,1,0:T(8,128)S(1)}, f32[2,64,256]{2,1,0:T(8,128)S(1)}, u32[]{:S(2)}, u32[]{:S(2)}) %collective-permute-start.19) | collective-permute-done | bytes 131104 | tf_op jit(solution)/shard_map/ppermute | solution.py:457
  62.5 0.3 fix_near.1
  62.9 0.2 collective-permute-start.21
  63.1 0.4 collective-permute-start.22
  63.4 0.9 %part.5 = (f32[2,128,512]{2,1,0:T(8,128)S(1)}, f32[2,128,512]{2,1,0:T(8,128)S(1)}) custom-call(f32[2,128,512]{2,1,0:T(8,128)S(1)} %fix_far.1.refs_0_, f32[2,128,512]{2,1,0:T(8,128)S(1)} %get-tuple-element.95.refs_1_, f32[2,128,512]{2,1,0:T(8,128)S(1)} %get-tuple-element.52.refs_3_.gain.refs_2_, f32[2,2,128,512]{3,2,1,0:T(8,128)S(1)} %get-tuple-element.56.refs_4_.refs_3_), custom_call_target="tpu_custom_call" | custom-call | bytes 3670016 | tf_op jit(solution)/shard_map/part/pallas_call | solution.py:53
  64.4 0.1 collective-permute-done.21.refs_1_
  64.5 0.4 collective-permute-done.22.refs_3_
  64.8 1.0 %final.2 = (f32[2,2,128,512]{3,2,1,0:T(8,128)}, f32[2,128,512]{2,1,0:T(8,128)}) custom-call(s32[1]{0:T(128)} %bitcast.where, f32[1]{0:T(128)} %bitcast.1.keep, f32[2,128,512]{2,1,0:T(8,128)S(1)} %get-tuple-element.52.refs_3_.gain.refs_2_, f32[2,128,512]{2,1,0:T(8,128)S(1)} %copy-done, f32[2,128,512]{2,1,0:T(8,128)S(1)} %copy-done.1, ...), custom_call_target="tpu_custom_call" | custom-call | bytes 4718600 | tf_op jit(solution)/shard_map/final/pallas_call | solution.py:53
  65.9 6.8 %collective-permute-done.20.refs_1_ = f32[2,128,512]{2,1,0:T(8,128)S(1)} collective-permute-done((f32[2,128,512]{2,1,0:T(8,128)S(1)}, f32[2,128,512]{2,1,0:T(8,128)S(1)}, u32[]{:S(2)}, u32[]{:S(2)}) %collective-permute-start.20) | collective-permute-done | bytes 524320 | tf_op jit(solution)/shard_map/ppermute | solution.py:454
  72.7 1.0 %final.3 = (f32[2,2,128,512]{3,2,1,0:T(8,128)}, f32[2,128,512]{2,1,0:T(8,128)}) custom-call(s32[1]{0:T(128)} %bitcast.where, f32[1]{0:T(128)} %bitcast.1.keep, f32[2,128,512]{2,1,0:T(8,128)S(1)} %get-tuple-element.52.refs_3_.gain.refs_2_, f32[2,128,512]{2,1,0:T(8,128)S(1)} %copy-done, ...), custom_call_target="tpu_custom_call", output_to_operand_aliasing={{0}: (7, {}), {1}: (8, {})} | custom-call | bytes 5767176 | tf_op jit(solution)/shard_map/final/pallas_call | solution.py:53
  (16 shorter events, 0.3 us)
Async XLA Ops:
  0.6 4.2 %copy-start = (f32[2,128,512]{2,1,0:T(8,128)S(1)}, f32[2,128,512]{2,1,0:T(8,128)}, u32[]{:S(2)}) copy-start(f32[2,128,512]{2,1,0:T(8,128)} %phi.7) | copy-start | bytes 1572868
  2.0 11.1 %collective-permute-start.1 = (f32[2,128,512]{2,1,0:T(8,128)S(1)}, f32[2,128,512]{2,1,0:T(8,128)S(1)}, u32[]{:S(2)}, u32[]{:S(2)}) collective-permute-start(f32[2,128,512]{2,1,0:T(8,128)S(1)} %get-tuple-element.55.refs_2_), channel_id=1, source_target_pairs={{0,1},{1,0},{2,3},{3,2},{4,5},{5,4},{6,7},{7,6},{8,9},{9,8},{10,11... | collective-permute-start | bytes 1572872 | tf_op jit(solution)/shard_map/ppermute | solution.py:457
  2.1 10.9 %collective-permute-start.2 = (f32[2,48,512]{2,1,0:T(8,128)S(1)}, f32[2,48,512]{2,1,0:T(8,128)S(1)}, u32[]{:S(2)}, u32[]{:S(2)}) collective-permute-start(f32[2,48,512]{2,1,0:T(8,128)S(1)} %get-tuple-element.54.refs_1_), channel_id=1, source_target_pairs={{1,2},{3,4},{5,6},{7,8},{9,10},{11,12},{13,14},{17,18},{19,20},{21... | collective-permute-start | bytes 589832 | tf_op jit(solution)/shard_map/ppermute | solution.py:454
  4.8 11.7 %collective-permute-start = (f32[2,80,512]{2,1,0:T(8,128)S(1)}, f32[2,80,512]{2,1,0:T(8,128)S(1)}, u32[]{:S(2)}, u32[]{:S(2)}) collective-permute-start(f32[2,80,512]{2,1,0:T(8,128)S(1)} %get-tuple-element.53.refs_0_), channel_id=1, source_target_pairs={{1,2},{3,4},{5,6},{7,8},{9,10},{11,12},{13,14},{17,18},{19,20},{21... | collective-permute-start | bytes 983048 | tf_op jit(solution)/shard_map/ppermute | solution.py:454
  4.8 1.2 %copy-start.2 = (f32[2,2,128,512]{3,2,1,0:T(8,128)S(1)}, f32[2,2,128,512]{3,2,1,0:T(8,128)}, u32[]{:S(2)}) copy-start(f32[2,2,128,512]{3,2,1,0:T(8,128)} %cot.1) | copy-start | bytes 3145732
  13.2 20.2 %collective-permute-start.6 = (f32[2,128,512]{2,1,0:T(8,128)S(1)}, f32[2,128,512]{2,1,0:T(8,128)S(1)}, u32[]{:S(2)}, u32[]{:S(2)}) collective-permute-start(f32[2,128,512]{2,1,0:T(8,128)S(1)} %finish.5.refs_2_), channel_id=1, source_target_pairs={{0,1},{1,0},{2,3},{3,2},{4,5},{5,4},{6,7},{7,6},{8,9},{9,8},{10,11... | collective-permute-start | bytes 1572872 | tf_op jit(solution)/shard_map/ppermute | solution.py:457
  16.6 10.5 %collective-permute-start.4 = (f32[2,80,512]{2,1,0:T(8,128)S(1)}, f32[2,80,512]{2,1,0:T(8,128)S(1)}, u32[]{:S(2)}, u32[]{:S(2)}) collective-permute-start(f32[2,80,512]{2,1,0:T(8,128)S(1)} %finish.3.refs_0_), channel_id=1, source_target_pairs={{1,2},{3,4},{5,6},{7,8},{9,10},{11,12},{13,14},{17,18},{19,20},{21... | collective-permute-start | bytes 983048 | tf_op jit(solution)/shard_map/ppermute | solution.py:454
  19.1 11.5 %collective-permute-start.3 = (f32[2,48,512]{2,1,0:T(8,128)S(1)}, f32[2,48,512]{2,1,0:T(8,128)S(1)}, u32[]{:S(2)}, u32[]{:S(2)}) collective-permute-start(f32[2,48,512]{2,1,0:T(8,128)S(1)} %finish.4.refs_1_), channel_id=1, source_target_pairs={{1,2},{3,4},{5,6},{7,8},{9,10},{11,12},{13,14},{17,18},{19,20},{21... | collective-permute-start | bytes 589832 | tf_op jit(solution)/shard_map/ppermute | solution.py:454
  30.8 5.4 %collective-permute-start.5 = (f32[2,64,256]{2,1,0:T(8,128)S(1)}, f32[2,64,256]{2,1,0:T(8,128)S(1)}, u32[]{:S(2)}, u32[]{:S(2)}) collective-permute-start(f32[2,64,256]{2,1,0:T(8,128)S(1)} %get-tuple-element.66), channel_id=1, source_target_pairs={{1,2},{3,4},{5,6},{7,8},{9,10},{11,12},{13,14},{17,18},{19,20},{21... | collective-permute-start | bytes 393224 | tf_op jit(solution)/shard_map/ppermute | solution.py:454
  33.7 2.5 %collective-permute-start.7 = (f32[2,64,256]{2,1,0:T(8,128)S(1)}, f32[2,64,256]{2,1,0:T(8,128)S(1)}, u32[]{:S(2)}, u32[]{:S(2)}) collective-permute-start(f32[2,64,256]{2,1,0:T(8,128)S(1)} %get-tuple-element.74), channel_id=1, source_target_pairs={{0,1},{1,0},{2,3},{3,2},{4,5},{5,4},{6,7},{7,6},{8,9},{9,8},{10,11... | collective-permute-start | bytes 393224 | tf_op jit(solution)/shard_map/ppermute | solution.py:457
  34.1 20.9 %collective-permute-start.16 = (f32[2,128,512]{2,1,0:T(8,128)S(1)}, f32[2,128,512]{2,1,0:T(8,128)S(1)}, u32[]{:S(2)}, u32[]{:S(2)}) collective-permute-start(f32[2,128,512]{2,1,0:T(8,128)S(1)} %get-tuple-element.70.refs_2_), channel_id=1, source_target_pairs={{0,1},{1,0},{2,3},{3,2},{4,5},{5,4},{6,7},{7,6},{8,9},{9,8},{10,11... | collective-permute-start | bytes 1572872 | tf_op jit(solution)/shard_map/ppermute | solution.py:457
  36.2 4.7 %collective-permute-start.8 = (f32[2,64,256]{2,1,0:T(8,128)S(1)}, f32[2,64,256]{2,1,0:T(8,128)S(1)}, u32[]{:S(2)}, u32[]{:S(2)}) collective-permute-start(f32[2,64,256]{2,1,0:T(8,128)S(1)} %coarse_first.1.fix.own), channel_id=1, source_target_pairs={{1,2},{3,4},{5,6},{7,8},{9,10},{11,12},{13,14},{17,18},{19,20},{21... | collective-permute-start | bytes 393224 | tf_op jit(solution)/shard_map/ppermute | solution.py:454
  37.9 3.0 %collective-permute-start.9 = (f32[2,64,256]{2,1,0:T(8,128)S(1)}, f32[2,64,256]{2,1,0:T(8,128)S(1)}, u32[]{:S(2)}, u32[]{:S(2)}) collective-permute-start(f32[2,64,256]{2,1,0:T(8,128)S(1)} %coarse_first.1.fix.own), channel_id=1, source_target_pairs={{0,1},{1,0},{2,3},{3,2},{4,5},{5,4},{6,7},{7,6},{8,9},{9,8},{10,11... | collective-permute-start | bytes 393224 | tf_op jit(solution)/shard_map/ppermute | solution.py:457
  38.4 6.4 %collective-permute-start.10 = (f32[2,64,256]{2,1,0:T(8,128)S(1)}, f32[2,64,256]{2,1,0:T(8,128)S(1)}, u32[]{:S(2)}, u32[]{:S(2)}) collective-permute-start(f32[2,64,256]{2,1,0:T(8,128)S(1)} %get-tuple-element.81), channel_id=1, source_target_pairs={{1,2},{3,4},{5,6},{7,8},{9,10},{11,12},{13,14},{17,18},{19,20},{21... | collective-permute-start | bytes 393224 | tf_op jit(solution)/shard_map/ppermute | solution.py:454
  41.0 5.5 %collective-permute-start.11 = (f32[2,64,256]{2,1,0:T(8,128)S(1)}, f32[2,64,256]{2,1,0:T(8,128)S(1)}, u32[]{:S(2)}, u32[]{:S(2)}) collective-permute-start(f32[2,64,256]{2,1,0:T(8,128)S(1)} %coarse_finish.3.fix), channel_id=1, source_target_pairs={{1,2},{3,4},{5,6},{7,8},{9,10},{11,12},{13,14},{17,18},{19,20},{21... | collective-permute-start | bytes 393224 | tf_op jit(solution)/shard_map/ppermute | solution.py:454
  43.4 3.0 %collective-permute-start.12 = (f32[2,64,256]{2,1,0:T(8,128)S(1)}, f32[2,64,256]{2,1,0:T(8,128)S(1)}, u32[]{:S(2)}, u32[]{:S(2)}) collective-permute-start(f32[2,64,256]{2,1,0:T(8,128)S(1)} %coarse_finish.3.fix), channel_id=1, source_target_pairs={{0,1},{1,0},{2,3},{3,2},{4,5},{5,4},{6,7},{7,6},{8,9},{9,8},{10,11... | collective-permute-start | bytes 393224 | tf_op jit(solution)/shard_map/ppermute | solution.py:457
  43.4 7.3 %collective-permute-start.13 = (f32[2,64,256]{2,1,0:T(8,128)S(1)}, f32[2,64,256]{2,1,0:T(8,128)S(1)}, u32[]{:S(2)}, u32[]{:S(2)}) collective-permute-start(f32[2,64,256]{2,1,0:T(8,128)S(1)} %get-tuple-element.83), channel_id=1, source_target_pairs={{1,2},{3,4},{5,6},{7,8},{9,10},{11,12},{13,14},{17,18},{19,20},{21... | collective-permute-start | bytes 393224 | tf_op jit(solution)/shard_map/ppermute | solution.py:454
  46.5 6.6 %collective-permute-start.14 = (f32[2,64,256]{2,1,0:T(8,128)S(1)}, f32[2,64,256]{2,1,0:T(8,128)S(1)}, u32[]{:S(2)}, u32[]{:S(2)}) collective-permute-start(f32[2,64,256]{2,1,0:T(8,128)S(1)} %coarse_finish.4.fix), channel_id=1, source_target_pairs={{1,2},{3,4},{5,6},{7,8},{9,10},{11,12},{13,14},{17,18},{19,20},{21... | collective-permute-start | bytes 393224 | tf_op jit(solution)/shard_map/ppermute | solution.py:454
  50.5 2.7 %collective-permute-start.15 = (f32[2,64,256]{2,1,0:T(8,128)S(1)}, f32[2,64,256]{2,1,0:T(8,128)S(1)}, u32[]{:S(2)}, u32[]{:S(2)}) collective-permute-start(f32[2,64,256]{2,1,0:T(8,128)S(1)} %coarse_finish.4.fix), channel_id=1, source_target_pairs={{0,1},{1,0},{2,3},{3,2},{4,5},{5,4},{6,7},{7,6},{8,9},{9,8},{10,11... | collective-permute-start | bytes 393224 | tf_op jit(solution)/shard_map/ppermute | solution.py:457
  50.5 5.6 %collective-permute-start.18 = (f32[2,64,256]{2,1,0:T(8,128)S(1)}, f32[2,64,256]{2,1,0:T(8,128)S(1)}, u32[]{:S(2)}, u32[]{:S(2)}) collective-permute-start(f32[2,64,256]{2,1,0:T(8,128)S(1)} %get-tuple-element.91), channel_id=1, source_target_pairs={{1,2},{3,4},{5,6},{7,8},{9,10},{11,12},{13,14},{17,18},{19,20},{21... | collective-permute-start | bytes 393224 | tf_op jit(solution)/shard_map/ppermute | solution.py:454
  53.2 5.1 %collective-permute-start.17 = (f32[2,64,256]{2,1,0:T(8,128)S(1)}, f32[2,64,256]{2,1,0:T(8,128)S(1)}, u32[]{:S(2)}, u32[]{:S(2)}) collective-permute-start(f32[2,64,256]{2,1,0:T(8,128)S(1)} %coarse_finish.5.fix), channel_id=1, source_target_pairs={{1,2},{3,4},{5,6},{7,8},{9,10},{11,12},{13,14},{17,18},{19,20},{21... | collective-permute-start | bytes 393224 | tf_op jit(solution)/shard_map/ppermute | solution.py:454
  58.6 14.0 %collective-permute-start.20 = (f32[2,128,512]{2,1,0:T(8,128)S(1)}, f32[2,128,512]{2,1,0:T(8,128)S(1)}, u32[]{:S(2)}, u32[]{:S(2)}) collective-permute-start(f32[2,128,512]{2,1,0:T(8,128)S(1)} %fix_far.1.refs_0_), channel_id=1, source_target_pairs={{1,2},{3,4},{5,6},{7,8},{9,10},{11,12},{13,14},{17,18},{19,20},{21... | collective-permute-start | bytes 1572872 | tf_op jit(solution)/shard_map/ppermute | solution.py:454
  61.2 1.3 %collective-permute-start.19 = (f32[2,64,256]{2,1,0:T(8,128)S(1)}, f32[2,64,256]{2,1,0:T(8,128)S(1)}, u32[]{:S(2)}, u32[]{:S(2)}) collective-permute-start(f32[2,64,256]{2,1,0:T(8,128)S(1)} %coarse_finish.5.fix), channel_id=1, source_target_pairs={{0,1},{1,0},{2,3},{3,2},{4,5},{5,4},{6,7},{7,6},{8,9},{9,8},{10,11... | collective-permute-start | bytes 393224 | tf_op jit(solution)/shard_map/ppermute | solution.py:457
  62.9 1.6 %collective-permute-start.21 = (f32[2,64,512]{2,1,0:T(8,128)S(1)}, f32[2,64,512]{2,1,0:T(8,128)S(1)}, u32[]{:S(2)}, u32[]{:S(2)}) collective-permute-start(f32[2,64,512]{2,1,0:T(8,128)S(1)} %get-tuple-element.98), channel_id=1, source_target_pairs={{0,1},{1,0},{2,3},{3,2},{4,5},{5,4},{6,7},{7,6},{8,9},{9,8},{10,11... | collective-permute-start | bytes 786440 | tf_op jit(solution)/shard_map/ppermute | solution.py:457
  63.1 1.8 %collective-permute-start.22 = (f32[2,64,512]{2,1,0:T(8,128)S(1)}, f32[2,64,512]{2,1,0:T(8,128)S(1)}, u32[]{:S(2)}, u32[]{:S(2)}) collective-permute-start(f32[2,64,512]{2,1,0:T(8,128)S(1)} %get-tuple-element.99), channel_id=1, source_target_pairs={{0,1},{1,0},{2,3},{3,2},{4,5},{5,4},{6,7},{7,6},{8,9},{9,8},{10,11... | collective-permute-start | bytes 786440 | tf_op jit(solution)/shard_map/ppermute | solution.py:457
  63.4 1.4 %copy-start.1 = (f32[2,128,512]{2,1,0:T(8,128)S(1)}, f32[2,128,512]{2,1,0:T(8,128)}, u32[]{:S(2)}) copy-start(f32[2,128,512]{2,1,0:T(8,128)} %psi.3) | copy-start | bytes 1572868

commit v11 on v10

--- a/solution.py
+++ b/solution.py
@@ -524,10 +524,10 @@
     first = fix
     for sweep_index in range(COARSE_SWEEPS - 1):
         far_sums, near_sums = swap_far(fix), swap_near(fix)
+        part = run(coarse_part_body, "coarse_part", [half], (fix, first, *coarse))[0]
         if len(arrived) < len(pieces):
-            fix, held = lax.optimization_barrier((fix, pieces[len(arrived)]))
+            held, part = after(pieces[len(arrived)], part)
             arrived.append(swap_far(held))
-        part = run(coarse_part_body, "coarse_part", [half], (fix, first, *coarse))[0]
         if sweep_index:
             part, arrived[sweep_index - 1] = after(part, arrived[sweep_index - 1])
         args = (keep, part, far_sums, near_sums, *coarse)

time: 73.8 us -> 73.8 us (level)
  no operation moved by 1% of the time
where the time goes in v11:
time: 73.8 us; the launch traced here: 73.6 us
  waiting for transfers between devices  34.5 us (47%)
  starting transfers between devices  24.3 us (33%)
  Pallas kernels  12.7 us (17%)
  local copies, waits for them, and re-layouts  1.23 us (2%)
  between operations  0.9 us (1%)
    ppermute x13, waiting for transfers between devices, swap_far(): return lax.ppermute(x, ('grp', 'gx'), across)  32.6 us
    ppermute x13, starting transfers between devices, swap_far(): return lax.ppermute(x, ('grp', 'gx'), across)  22.9 us
    pallas_call x28, Pallas kernels, call(): pl.pallas_call(body, out_shape=shapes, in_specs=in_specs or [VMEM] * len(...  12.7 us
    ppermute x10, waiting for transfers between devices, swap_near(): return lax.ppermute(x, 'gx', on_chip)  1.81 us
  transfers between devices with their start and end apart: 23, of which 12 were waited for; matrix products, arithmetic and copies ran while one was open for 0% of the time, Pallas kernels for 14%

profile of v11, /device:TPU:1, one launch (start us, length us, event | category | flops | bytes accessed | tf_op | source)
XLA Modules:
  0.0 73.6 jit_solution(8124396149465693948)
XLA Ops:
  0.7 1.3 %take.1 = (f32[2,80,512]{2,1,0:T(8,128)S(1)}, f32[2,48,512]{2,1,0:T(8,128)S(1)}, f32[2,128,512]{2,1,0:T(8,128)S(1)}) custom-call(s32[1]{0:T(128)} %bitcast.where, f32[2,2,128,512]{3,2,1,0:T(8,128)} %warm.1), custom_call_target="tpu_custom_call" | custom-call | bytes 2097156 | tf_op jit(solution)/shard_map/take/pallas_call | solution.py:53
  2.0 0.1 collective-permute-start.1
  2.1 2.6 %collective-permute-start.2 = (f32[2,48,512]{2,1,0:T(8,128)S(1)}, f32[2,48,512]{2,1,0:T(8,128)S(1)}, u32[]{:S(2)}, u32[]{:S(2)}) collective-permute-start(f32[2,48,512]{2,1,0:T(8,128)S(1)} %get-tuple-element.54.refs_1_), channel_id=1, source_target_pairs={{1,2},{3,4},{5,6},{7,8},{9,10},{11,12},{13,14},{17,18},{19,20},{21... | collective-permute-start | bytes 589832 | tf_op jit(solution)/shard_map/ppermute | solution.py:454
  4.8 0.1 collective-permute-start
  4.8 1.2 %copy-done.2 = f32[2,2,128,512]{3,2,1,0:T(8,128)S(1)} copy-done((f32[2,2,128,512]{3,2,1,0:T(8,128)S(1)}, f32[2,2,128,512]{3,2,1,0:T(8,128)}, u32[]{:S(2)}) %copy-start.2) | copy-done | bytes 1048600
  6.1 0.2 setup.1
  6.3 0.9 %part.3 = (f32[2,128,512]{2,1,0:T(8,128)S(1)}, f32[2,128,512]{2,1,0:T(8,128)S(1)}) custom-call(f32[2,80,512]{2,1,0:T(8,128)S(1)} %get-tuple-element.53.refs_0_, f32[2,48,512]{2,1,0:T(8,128)S(1)} %get-tuple-element.54.refs_1_, f32[2,128,512]{2,1,0:T(8,128)S(1)} %get-tuple-element.55.refs_2_, f32[2,128,512]{2,1,0:T(8,128)S(1)} %get-tuple-element.52.refs_3_.gain.refs_2_, ...), custom_call_target="tpu_custom_call" | custom-call | bytes 3670016 | tf_op jit(solution)/shard_map/part/pallas_call | solution.py:53
  7.3 5.7 %collective-permute-done.2.halo = f32[2,48,512]{2,1,0:T(8,128)S(1)} collective-permute-done((f32[2,48,512]{2,1,0:T(8,128)S(1)}, f32[2,48,512]{2,1,0:T(8,128)S(1)}, u32[]{:S(2)}, u32[]{:S(2)}) %collective-permute-start.2) | collective-permute-done | bytes 196640 | tf_op jit(solution)/shard_map/ppermute | solution.py:454
  13.0 0.1 finish.5.refs_2_
  13.2 0.1 collective-permute-start.6
  13.2 3.3 %collective-permute-done.halo = f32[2,80,512]{2,1,0:T(8,128)S(1)} collective-permute-done((f32[2,80,512]{2,1,0:T(8,128)S(1)}, f32[2,80,512]{2,1,0:T(8,128)S(1)}, u32[]{:S(2)}, u32[]{:S(2)}) %collective-permute-start) | collective-permute-done | bytes 327712 | tf_op jit(solution)/shard_map/ppermute | solution.py:454
  16.5 0.1 finish.3.refs_0_
  16.6 2.5 %collective-permute-start.4 = (f32[2,80,512]{2,1,0:T(8,128)S(1)}, f32[2,80,512]{2,1,0:T(8,128)S(1)}, u32[]{:S(2)}, u32[]{:S(2)}) collective-permute-start(f32[2,80,512]{2,1,0:T(8,128)S(1)} %finish.3.refs_0_), channel_id=1, source_target_pairs={{1,2},{3,4},{5,6},{7,8},{9,10},{11,12},{13,14},{17,18},{19,20},{21... | collective-permute-start | bytes 983048 | tf_op jit(solution)/shard_map/ppermute | solution.py:454
  19.1 0.1 collective-permute-start.3
  19.2 0.9 %part.4 = (f32[2,128,512]{2,1,0:T(8,128)S(1)}, f32[2,128,512]{2,1,0:T(8,128)S(1)}) custom-call(f32[2,80,512]{2,1,0:T(8,128)S(1)} %finish.3.refs_0_, f32[2,48,512]{2,1,0:T(8,128)S(1)} %finish.4.refs_1_, f32[2,128,512]{2,1,0:T(8,128)S(1)} %finish.5.refs_2_, f32[2,128,512]{2,1,0:T(8,128)S(1)} %get-tuple-element.52.refs_3_.gain.refs_2_, ...), custom_call_target="tpu_custom_call" | custom-call | bytes 3670016 | tf_op jit(solution)/shard_map/part/pallas_call | solution.py:53
  20.1 0.1 matrices.1
  20.2 6.8 %collective-permute-done.4.halo = f32[2,80,512]{2,1,0:T(8,128)S(1)} collective-permute-done((f32[2,80,512]{2,1,0:T(8,128)S(1)}, f32[2,80,512]{2,1,0:T(8,128)S(1)}, u32[]{:S(2)}, u32[]{:S(2)}) %collective-permute-start.4) | collective-permute-done | bytes 327712 | tf_op jit(solution)/shard_map/ppermute | solution.py:454
  27.1 0.3 finish_pool.3
  27.4 3.2 %collective-permute-done.3.halo = f32[2,48,512]{2,1,0:T(8,128)S(1)} collective-permute-done((f32[2,48,512]{2,1,0:T(8,128)S(1)}, f32[2,48,512]{2,1,0:T(8,128)S(1)}, u32[]{:S(2)}, u32[]{:S(2)}) %collective-permute-start.3) | collective-permute-done | bytes 196640 | tf_op jit(solution)/shard_map/ppermute | solution.py:454
  30.6 0.2 finish_pool.4
  30.8 2.5 %collective-permute-start.5 = (f32[2,64,256]{2,1,0:T(8,128)S(1)}, f32[2,64,256]{2,1,0:T(8,128)S(1)}, u32[]{:S(2)}, u32[]{:S(2)}) collective-permute-start(f32[2,64,256]{2,1,0:T(8,128)S(1)} %get-tuple-element.66), channel_id=1, source_target_pairs={{1,2},{3,4},{5,6},{7,8},{9,10},{11,12},{13,14},{17,18},{19,20},{21... | collective-permute-start | bytes 393224 | tf_op jit(solution)/shard_map/ppermute | solution.py:454
  33.4 0.0 collective-permute-done.6.halo
  33.4 0.4 finish_pool.5
  33.7 0.1 collective-permute-start.7
  33.8 0.3 coarse_setup.1.gain
  34.1 0.6 collective-permute-start.16
  34.7 1.5 %part_defect.1 = (f32[2,128,512]{2,1,0:T(8,128)S(1)}, f32[2,128,512]{2,1,0:T(8,128)S(1)}, f32[2,64,256]{2,1,0:T(8,128)S(1)}) custom-call(f32[2,80,512]{2,1,0:T(8,128)S(1)} %get-tuple-element.67.refs_0_, f32[2,48,512]{2,1,0:T(8,128)S(1)} %get-tuple-element.68.refs_1_, f32[2,128,512]{2,1,0:T(8,128)S(1)} %get-tuple-element.70.refs_2_, ...), custom_call_target="tpu_custom_call" | custom-call | bytes 3932160 | tf_op jit(solution)/shard_map/part_defect/pallas_call | solution.py:53
  36.2 0.0 collective-permute-done.7.near
  36.2 1.6 %collective-permute-start.8 = (f32[2,64,256]{2,1,0:T(8,128)S(1)}, f32[2,64,256]{2,1,0:T(8,128)S(1)}, u32[]{:S(2)}, u32[]{:S(2)}) collective-permute-start(f32[2,64,256]{2,1,0:T(8,128)S(1)} %coarse_first.1.fix.own), channel_id=1, source_target_pairs={{1,2},{3,4},{5,6},{7,8},{9,10},{11,12},{13,14},{17,18},{19,20},{21... | collective-permute-start | bytes 393224 | tf_op jit(solution)/shard_map/ppermute | solution.py:454
  37.9 0.0 collective-permute-start.9
  37.9 0.5 three.1
  38.4 1.3 %collective-permute-start.10 = (f32[2,64,256]{2,1,0:T(8,128)S(1)}, f32[2,64,256]{2,1,0:T(8,128)S(1)}, u32[]{:S(2)}, u32[]{:S(2)}) collective-permute-start(f32[2,64,256]{2,1,0:T(8,128)S(1)} %get-tuple-element.81), channel_id=1, source_target_pairs={{1,2},{3,4},{5,6},{7,8},{9,10},{11,12},{13,14},{17,18},{19,20},{21... | collective-permute-start | bytes 393224 | tf_op jit(solution)/shard_map/ppermute | solution.py:454
  39.6 0.1 coarse_part.3.part
  39.8 1.1 %collective-permute-done.8.far = f32[2,64,256]{2,1,0:T(8,128)S(1)} collective-permute-done((f32[2,64,256]{2,1,0:T(8,128)S(1)}, f32[2,64,256]{2,1,0:T(8,128)S(1)}, u32[]{:S(2)}, u32[]{:S(2)}) %collective-permute-start.8) | collective-permute-done | bytes 131104 | tf_op jit(solution)/shard_map/ppermute | solution.py:454
  40.9 0.0 collective-permute-done.9.near
  41.0 2.5 %collective-permute-start.11 = (f32[2,64,256]{2,1,0:T(8,128)S(1)}, f32[2,64,256]{2,1,0:T(8,128)S(1)}, u32[]{:S(2)}, u32[]{:S(2)}) collective-permute-start(f32[2,64,256]{2,1,0:T(8,128)S(1)} %coarse_finish.3.fix), channel_id=1, source_target_pairs={{1,2},{3,4},{5,6},{7,8},{9,10},{11,12},{13,14},{17,18},{19,20},{21... | collective-permute-start | bytes 393224 | tf_op jit(solution)/shard_map/ppermute | solution.py:454
  43.4 0.0 collective-permute-start.12
  43.4 1.2 %collective-permute-start.13 = (f32[2,64,256]{2,1,0:T(8,128)S(1)}, f32[2,64,256]{2,1,0:T(8,128)S(1)}, u32[]{:S(2)}, u32[]{:S(2)}) collective-permute-start(f32[2,64,256]{2,1,0:T(8,128)S(1)} %get-tuple-element.83), channel_id=1, source_target_pairs={{1,2},{3,4},{5,6},{7,8},{9,10},{11,12},{13,14},{17,18},{19,20},{21... | collective-permute-start | bytes 393224 | tf_op jit(solution)/shard_map/ppermute | solution.py:454
  44.6 0.2 coarse_part.4.part
  44.8 1.7 %collective-permute-done.11.far = f32[2,64,256]{2,1,0:T(8,128)S(1)} collective-permute-done((f32[2,64,256]{2,1,0:T(8,128)S(1)}, f32[2,64,256]{2,1,0:T(8,128)S(1)}, u32[]{:S(2)}, u32[]{:S(2)}) %collective-permute-start.11) | collective-permute-done | bytes 131104 | tf_op jit(solution)/shard_map/ppermute | solution.py:454
  46.5 3.9 %collective-permute-start.14 = (f32[2,64,256]{2,1,0:T(8,128)S(1)}, f32[2,64,256]{2,1,0:T(8,128)S(1)}, u32[]{:S(2)}, u32[]{:S(2)}) collective-permute-start(f32[2,64,256]{2,1,0:T(8,128)S(1)} %coarse_finish.4.fix), channel_id=1, source_target_pairs={{1,2},{3,4},{5,6},{7,8},{9,10},{11,12},{13,14},{17,18},{19,20},{21... | collective-permute-start | bytes 393224 | tf_op jit(solution)/shard_map/ppermute | solution.py:454
  50.5 0.0 collective-permute-start.15
  50.5 0.2 collective-permute-start.18
  50.6 0.2 coarse_part.5.part
  50.8 2.3 %collective-permute-done.14.far = f32[2,64,256]{2,1,0:T(8,128)S(1)} collective-permute-done((f32[2,64,256]{2,1,0:T(8,128)S(1)}, f32[2,64,256]{2,1,0:T(8,128)S(1)}, u32[]{:S(2)}, u32[]{:S(2)}) %collective-permute-start.14) | collective-permute-done | bytes 131104 | tf_op jit(solution)/shard_map/ppermute | solution.py:454
  53.1 0.0 collective-permute-done.15.near
  53.2 1.8 %collective-permute-start.17 = (f32[2,64,256]{2,1,0:T(8,128)S(1)}, f32[2,64,256]{2,1,0:T(8,128)S(1)}, u32[]{:S(2)}, u32[]{:S(2)}) collective-permute-start(f32[2,64,256]{2,1,0:T(8,128)S(1)} %coarse_finish.5.fix), channel_id=1, source_target_pairs={{1,2},{3,4},{5,6},{7,8},{9,10},{11,12},{13,14},{17,18},{19,20},{21... | collective-permute-start | bytes 393224 | tf_op jit(solution)/shard_map/ppermute | solution.py:454
  55.0 1.0 %third.1 = (f32[2,128,512]{2,1,0:T(8,128)S(1)}, f32[2,128,512]{2,1,0:T(8,128)S(1)}) custom-call(f32[2,128,512]{2,1,0:T(8,128)S(1)} %get-tuple-element.71.far, f32[2,128,512]{2,1,0:T(8,128)S(1)} %get-tuple-element.72.near, f32[2,64,256]{2,1,0:T(8,128)S(1)} %coarse_finish.5.fix, f32[2,128,512]{2,1,0:T(8,128)S(1)} %collective-permute-done.16.near_halo, ...), custom_call_target="tpu_custom_call" | custom-call | bytes 3407872 | tf_op jit(solution)/shard_map/third/pallas_call | solution.py:53
  56.0 0.0 collective-permute-done.18.refs_2_
  56.0 0.6 rebuild.1.state_nb
  56.6 1.7 %collective-permute-done.17.halo = f32[2,64,256]{2,1,0:T(8,128)S(1)} collective-permute-done((f32[2,64,256]{2,1,0:T(8,128)S(1)}, f32[2,64,256]{2,1,0:T(8,128)S(1)}, u32[]{:S(2)}, u32[]{:S(2)}) %collective-permute-start.17) | collective-permute-done | bytes 131104 | tf_op jit(solution)/shard_map/ppermute | solution.py:454
  58.3 0.3 fix_far.1.refs_0_
  58.6 2.5 %collective-permute-start.20 = (f32[2,128,512]{2,1,0:T(8,128)S(1)}, f32[2,128,512]{2,1,0:T(8,128)S(1)}, u32[]{:S(2)}, u32[]{:S(2)}) collective-permute-start(f32[2,128,512]{2,1,0:T(8,128)S(1)} %fix_far.1.refs_0_), channel_id=1, source_target_pairs={{1,2},{3,4},{5,6},{7,8},{9,10},{11,12},{13,14},{17,18},{19,20},{21... | collective-permute-start | bytes 1572872 | tf_op jit(solution)/shard_map/ppermute | solution.py:454
  61.2 0.0 collective-permute-start.19
  61.2 1.3 %collective-permute-done.19.halo = f32[2,64,256]{2,1,0:T(8,128)S(1)} collective-permute-done((f32[2,64,256]{2,1,0:T(8,128)S(1)}, f32[2,64,256]{2,1,0:T(8,128)S(1)}, u32[]{:S(2)}, u32[]{:S(2)}) %collective-permute-start.19) | collective-permute-done | bytes 131104 | tf_op jit(solution)/shard_map/ppermute | solution.py:457
  62.5 0.3 fix_near.1
  62.9 0.2 collective-permute-start.21
  63.1 0.4 collective-permute-start.22
  63.4 0.9 %part.5 = (f32[2,128,512]{2,1,0:T(8,128)S(1)}, f32[2,128,512]{2,1,0:T(8,128)S(1)}) custom-call(f32[2,128,512]{2,1,0:T(8,128)S(1)} %fix_far.1.refs_0_, f32[2,128,512]{2,1,0:T(8,128)S(1)} %get-tuple-element.95.refs_1_, f32[2,128,512]{2,1,0:T(8,128)S(1)} %get-tuple-element.52.refs_3_.gain.refs_2_, f32[2,2,128,512]{3,2,1,0:T(8,128)S(1)} %get-tuple-element.56.refs_4_.refs_3_), custom_call_target="tpu_custom_call" | custom-call | bytes 3670016 | tf_op jit(solution)/shard_map/part/pallas_call | solution.py:53
  64.4 0.1 collective-permute-done.21.refs_1_
  64.5 0.4 collective-permute-done.22.refs_3_
  64.8 1.0 %final.2 = (f32[2,2,128,512]{3,2,1,0:T(8,128)}, f32[2,128,512]{2,1,0:T(8,128)}) custom-call(s32[1]{0:T(128)} %bitcast.where, f32[1]{0:T(128)} %bitcast.1.keep, f32[2,128,512]{2,1,0:T(8,128)S(1)} %get-tuple-element.52.refs_3_.gain.refs_2_, f32[2,128,512]{2,1,0:T(8,128)S(1)} %copy-done, f32[2,128,512]{2,1,0:T(8,128)S(1)} %copy-done.1, ...), custom_call_target="tpu_custom_call" | custom-call | bytes 4718600 | tf_op jit(solution)/shard_map/final/pallas_call | solution.py:53
  65.9 6.8 %collective-permute-done.20.refs_1_ = f32[2,128,512]{2,1,0:T(8,128)S(1)} collective-permute-done((f32[2,128,512]{2,1,0:T(8,128)S(1)}, f32[2,128,512]{2,1,0:T(8,128)S(1)}, u32[]{:S(2)}, u32[]{:S(2)}) %collective-permute-start.20) | collective-permute-done | bytes 524320 | tf_op jit(solution)/shard_map/ppermute | solution.py:454
  72.7 1.0 %final.3 = (f32[2,2,128,512]{3,2,1,0:T(8,128)}, f32[2,128,512]{2,1,0:T(8,128)}) custom-call(s32[1]{0:T(128)} %bitcast.where, f32[1]{0:T(128)} %bitcast.1.keep, f32[2,128,512]{2,1,0:T(8,128)S(1)} %get-tuple-element.52.refs_3_.gain.refs_2_, f32[2,128,512]{2,1,0:T(8,128)S(1)} %copy-done, ...), custom_call_target="tpu_custom_call", output_to_operand_aliasing={{0}: (7, {}), {1}: (8, {})} | custom-call | bytes 5767176 | tf_op jit(solution)/shard_map/final/pallas_call | solution.py:53
  (16 shorter events, 0.3 us)
Async XLA Ops:
  0.6 4.2 %copy-start = (f32[2,128,512]{2,1,0:T(8,128)S(1)}, f32[2,128,512]{2,1,0:T(8,128)}, u32[]{:S(2)}) copy-start(f32[2,128,512]{2,1,0:T(8,128)} %phi.7) | copy-start | bytes 1572868
  2.0 11.1 %collective-permute-start.1 = (f32[2,128,512]{2,1,0:T(8,128)S(1)}, f32[2,128,512]{2,1,0:T(8,128)S(1)}, u32[]{:S(2)}, u32[]{:S(2)}) collective-permute-start(f32[2,128,512]{2,1,0:T(8,128)S(1)} %get-tuple-element.55.refs_2_), channel_id=1, source_target_pairs={{0,1},{1,0},{2,3},{3,2},{4,5},{5,4},{6,7},{7,6},{8,9},{9,8},{10,11... | collective-permute-start | bytes 1572872 | tf_op jit(solution)/shard_map/ppermute | solution.py:457
  2.1 10.9 %collective-permute-start.2 = (f32[2,48,512]{2,1,0:T(8,128)S(1)}, f32[2,48,512]{2,1,0:T(8,128)S(1)}, u32[]{:S(2)}, u32[]{:S(2)}) collective-permute-start(f32[2,48,512]{2,1,0:T(8,128)S(1)} %get-tuple-element.54.refs_1_), channel_id=1, source_target_pairs={{1,2},{3,4},{5,6},{7,8},{9,10},{11,12},{13,14},{17,18},{19,20},{21... | collective-permute-start | bytes 589832 | tf_op jit(solution)/shard_map/ppermute | solution.py:454
  4.8 11.7 %collective-permute-start = (f32[2,80,512]{2,1,0:T(8,128)S(1)}, f32[2,80,512]{2,1,0:T(8,128)S(1)}, u32[]{:S(2)}, u32[]{:S(2)}) collective-permute-start(f32[2,80,512]{2,1,0:T(8,128)S(1)} %get-tuple-element.53.refs_0_), channel_id=1, source_target_pairs={{1,2},{3,4},{5,6},{7,8},{9,10},{11,12},{13,14},{17,18},{19,20},{21... | collective-permute-start | bytes 983048 | tf_op jit(solution)/shard_map/ppermute | solution.py:454
  4.8 1.2 %copy-start.2 = (f32[2,2,128,512]{3,2,1,0:T(8,128)S(1)}, f32[2,2,128,512]{3,2,1,0:T(8,128)}, u32[]{:S(2)}) copy-start(f32[2,2,128,512]{3,2,1,0:T(8,128)} %cot.1) | copy-start | bytes 3145732
  13.2 20.2 %collective-permute-start.6 = (f32[2,128,512]{2,1,0:T(8,128)S(1)}, f32[2,128,512]{2,1,0:T(8,128)S(1)}, u32[]{:S(2)}, u32[]{:S(2)}) collective-permute-start(f32[2,128,512]{2,1,0:T(8,128)S(1)} %finish.5.refs_2_), channel_id=1, source_target_pairs={{0,1},{1,0},{2,3},{3,2},{4,5},{5,4},{6,7},{7,6},{8,9},{9,8},{10,11... | collective-permute-start | bytes 1572872 | tf_op jit(solution)/shard_map/ppermute | solution.py:457
  16.6 10.5 %collective-permute-start.4 = (f32[2,80,512]{2,1,0:T(8,128)S(1)}, f32[2,80,512]{2,1,0:T(8,128)S(1)}, u32[]{:S(2)}, u32[]{:S(2)}) collective-permute-start(f32[2,80,512]{2,1,0:T(8,128)S(1)} %finish.3.refs_0_), channel_id=1, source_target_pairs={{1,2},{3,4},{5,6},{7,8},{9,10},{11,12},{13,14},{17,18},{19,20},{21... | collective-permute-start | bytes 983048 | tf_op jit(solution)/shard_map/ppermute | solution.py:454
  19.1 11.5 %collective-permute-start.3 = (f32[2,48,512]{2,1,0:T(8,128)S(1)}, f32[2,48,512]{2,1,0:T(8,128)S(1)}, u32[]{:S(2)}, u32[]{:S(2)}) collective-permute-start(f32[2,48,512]{2,1,0:T(8,128)S(1)} %finish.4.refs_1_), channel_id=1, source_target_pairs={{1,2},{3,4},{5,6},{7,8},{9,10},{11,12},{13,14},{17,18},{19,20},{21... | collective-permute-start | bytes 589832 | tf_op jit(solution)/shard_map/ppermute | solution.py:454
  30.8 5.4 %collective-permute-start.5 = (f32[2,64,256]{2,1,0:T(8,128)S(1)}, f32[2,64,256]{2,1,0:T(8,128)S(1)}, u32[]{:S(2)}, u32[]{:S(2)}) collective-permute-start(f32[2,64,256]{2,1,0:T(8,128)S(1)} %get-tuple-element.66), channel_id=1, source_target_pairs={{1,2},{3,4},{5,6},{7,8},{9,10},{11,12},{13,14},{17,18},{19,20},{21... | collective-permute-start | bytes 393224 | tf_op jit(solution)/shard_map/ppermute | solution.py:454
  33.7 2.5 %collective-permute-start.7 = (f32[2,64,256]{2,1,0:T(8,128)S(1)}, f32[2,64,256]{2,1,0:T(8,128)S(1)}, u32[]{:S(2)}, u32[]{:S(2)}) collective-permute-start(f32[2,64,256]{2,1,0:T(8,128)S(1)} %get-tuple-element.78), channel_id=1, source_target_pairs={{0,1},{1,0},{2,3},{3,2},{4,5},{5,4},{6,7},{7,6},{8,9},{9,8},{10,11... | collective-permute-start | bytes 393224 | tf_op jit(solution)/shard_map/ppermute | solution.py:457
  34.1 20.9 %collective-permute-start.16 = (f32[2,128,512]{2,1,0:T(8,128)S(1)}, f32[2,128,512]{2,1,0:T(8,128)S(1)}, u32[]{:S(2)}, u32[]{:S(2)}) collective-permute-start(f32[2,128,512]{2,1,0:T(8,128)S(1)} %get-tuple-element.70.refs_2_), channel_id=1, source_target_pairs={{0,1},{1,0},{2,3},{3,2},{4,5},{5,4},{6,7},{7,6},{8,9},{9,8},{10,11... | collective-permute-start | bytes 1572872 | tf_op jit(solution)/shard_map/ppermute | solution.py:457
  36.2 4.7 %collective-permute-start.8 = (f32[2,64,256]{2,1,0:T(8,128)S(1)}, f32[2,64,256]{2,1,0:T(8,128)S(1)}, u32[]{:S(2)}, u32[]{:S(2)}) collective-permute-start(f32[2,64,256]{2,1,0:T(8,128)S(1)} %coarse_first.1.fix.own), channel_id=1, source_target_pairs={{1,2},{3,4},{5,6},{7,8},{9,10},{11,12},{13,14},{17,18},{19,20},{21... | collective-permute-start | bytes 393224 | tf_op jit(solution)/shard_map/ppermute | solution.py:454
  37.9 3.0 %collective-permute-start.9 = (f32[2,64,256]{2,1,0:T(8,128)S(1)}, f32[2,64,256]{2,1,0:T(8,128)S(1)}, u32[]{:S(2)}, u32[]{:S(2)}) collective-permute-start(f32[2,64,256]{2,1,0:T(8,128)S(1)} %coarse_first.1.fix.own), channel_id=1, source_target_pairs={{0,1},{1,0},{2,3},{3,2},{4,5},{5,4},{6,7},{7,6},{8,9},{9,8},{10,11... | collective-permute-start | bytes 393224 | tf_op jit(solution)/shard_map/ppermute | solution.py:457
  38.4 6.4 %collective-permute-start.10 = (f32[2,64,256]{2,1,0:T(8,128)S(1)}, f32[2,64,256]{2,1,0:T(8,128)S(1)}, u32[]{:S(2)}, u32[]{:S(2)}) collective-permute-start(f32[2,64,256]{2,1,0:T(8,128)S(1)} %get-tuple-element.81), channel_id=1, source_target_pairs={{1,2},{3,4},{5,6},{7,8},{9,10},{11,12},{13,14},{17,18},{19,20},{21... | collective-permute-start | bytes 393224 | tf_op jit(solution)/shard_map/ppermute | solution.py:454
  41.0 5.5 %collective-permute-start.11 = (f32[2,64,256]{2,1,0:T(8,128)S(1)}, f32[2,64,256]{2,1,0:T(8,128)S(1)}, u32[]{:S(2)}, u32[]{:S(2)}) collective-permute-start(f32[2,64,256]{2,1,0:T(8,128)S(1)} %coarse_finish.3.fix), channel_id=1, source_target_pairs={{1,2},{3,4},{5,6},{7,8},{9,10},{11,12},{13,14},{17,18},{19,20},{21... | collective-permute-start | bytes 393224 | tf_op jit(solution)/shard_map/ppermute | solution.py:454
  43.4 3.0 %collective-permute-start.12 = (f32[2,64,256]{2,1,0:T(8,128)S(1)}, f32[2,64,256]{2,1,0:T(8,128)S(1)}, u32[]{:S(2)}, u32[]{:S(2)}) collective-permute-start(f32[2,64,256]{2,1,0:T(8,128)S(1)} %coarse_finish.3.fix), channel_id=1, source_target_pairs={{0,1},{1,0},{2,3},{3,2},{4,5},{5,4},{6,7},{7,6},{8,9},{9,8},{10,11... | collective-permute-start | bytes 393224 | tf_op jit(solution)/shard_map/ppermute | solution.py:457
  43.4 7.3 %collective-permute-start.13 = (f32[2,64,256]{2,1,0:T(8,128)S(1)}, f32[2,64,256]{2,1,0:T(8,128)S(1)}, u32[]{:S(2)}, u32[]{:S(2)}) collective-permute-start(f32[2,64,256]{2,1,0:T(8,128)S(1)} %get-tuple-element.83), channel_id=1, source_target_pairs={{1,2},{3,4},{5,6},{7,8},{9,10},{11,12},{13,14},{17,18},{19,20},{21... | collective-permute-start | bytes 393224 | tf_op jit(solution)/shard_map/ppermute | solution.py:454
  46.5 6.6 %collective-permute-start.14 = (f32[2,64,256]{2,1,0:T(8,128)S(1)}, f32[2,64,256]{2,1,0:T(8,128)S(1)}, u32[]{:S(2)}, u32[]{:S(2)}) collective-permute-start(f32[2,64,256]{2,1,0:T(8,128)S(1)} %coarse_finish.4.fix), channel_id=1, source_target_pairs={{1,2},{3,4},{5,6},{7,8},{9,10},{11,12},{13,14},{17,18},{19,20},{21... | collective-permute-start | bytes 393224 | tf_op jit(solution)/shard_map/ppermute | solution.py:454
  50.5 2.7 %collective-permute-start.15 = (f32[2,64,256]{2,1,0:T(8,128)S(1)}, f32[2,64,256]{2,1,0:T(8,128)S(1)}, u32[]{:S(2)}, u32[]{:S(2)}) collective-permute-start(f32[2,64,256]{2,1,0:T(8,128)S(1)} %coarse_finish.4.fix), channel_id=1, source_target_pairs={{0,1},{1,0},{2,3},{3,2},{4,5},{5,4},{6,7},{7,6},{8,9},{9,8},{10,11... | collective-permute-start | bytes 393224 | tf_op jit(solution)/shard_map/ppermute | solution.py:457
  50.5 5.6 %collective-permute-start.18 = (f32[2,64,256]{2,1,0:T(8,128)S(1)}, f32[2,64,256]{2,1,0:T(8,128)S(1)}, u32[]{:S(2)}, u32[]{:S(2)}) collective-permute-start(f32[2,64,256]{2,1,0:T(8,128)S(1)} %get-tuple-element.91), channel_id=1, source_target_pairs={{1,2},{3,4},{5,6},{7,8},{9,10},{11,12},{13,14},{17,18},{19,20},{21... | collective-permute-start | bytes 393224 | tf_op jit(solution)/shard_map/ppermute | solution.py:454
  53.2 5.1 %collective-permute-start.17 = (f32[2,64,256]{2,1,0:T(8,128)S(1)}, f32[2,64,256]{2,1,0:T(8,128)S(1)}, u32[]{:S(2)}, u32[]{:S(2)}) collective-permute-start(f32[2,64,256]{2,1,0:T(8,128)S(1)} %coarse_finish.5.fix), channel_id=1, source_target_pairs={{1,2},{3,4},{5,6},{7,8},{9,10},{11,12},{13,14},{17,18},{19,20},{21... | collective-permute-start | bytes 393224 | tf_op jit(solution)/shard_map/ppermute | solution.py:454
  58.6 14.0 %collective-permute-start.20 = (f32[2,128,512]{2,1,0:T(8,128)S(1)}, f32[2,128,512]{2,1,0:T(8,128)S(1)}, u32[]{:S(2)}, u32[]{:S(2)}) collective-permute-start(f32[2,128,512]{2,1,0:T(8,128)S(1)} %fix_far.1.refs_0_), channel_id=1, source_target_pairs={{1,2},{3,4},{5,6},{7,8},{9,10},{11,12},{13,14},{17,18},{19,20},{21... | collective-permute-start | bytes 1572872 | tf_op jit(solution)/shard_map/ppermute | solution.py:454
  61.2 1.3 %collective-permute-start.19 = (f32[2,64,256]{2,1,0:T(8,128)S(1)}, f32[2,64,256]{2,1,0:T(8,128)S(1)}, u32[]{:S(2)}, u32[]{:S(2)}) collective-permute-start(f32[2,64,256]{2,1,0:T(8,128)S(1)} %coarse_finish.5.fix), channel_id=1, source_target_pairs={{0,1},{1,0},{2,3},{3,2},{4,5},{5,4},{6,7},{7,6},{8,9},{9,8},{10,11... | collective-permute-start | bytes 393224 | tf_op jit(solution)/shard_map/ppermute | solution.py:457
  62.9 1.6 %collective-permute-start.21 = (f32[2,64,512]{2,1,0:T(8,128)S(1)}, f32[2,64,512]{2,1,0:T(8,128)S(1)}, u32[]{:S(2)}, u32[]{:S(2)}) collective-permute-start(f32[2,64,512]{2,1,0:T(8,128)S(1)} %get-tuple-element.98), channel_id=1, source_target_pairs={{0,1},{1,0},{2,3},{3,2},{4,5},{5,4},{6,7},{7,6},{8,9},{9,8},{10,11... | collective-permute-start | bytes 786440 | tf_op jit(solution)/shard_map/ppermute | solution.py:457
  63.1 1.8 %collective-permute-start.22 = (f32[2,64,512]{2,1,0:T(8,128)S(1)}, f32[2,64,512]{2,1,0:T(8,128)S(1)}, u32[]{:S(2)}, u32[]{:S(2)}) collective-permute-start(f32[2,64,512]{2,1,0:T(8,128)S(1)} %get-tuple-element.99), channel_id=1, source_target_pairs={{0,1},{1,0},{2,3},{3,2},{4,5},{5,4},{6,7},{7,6},{8,9},{9,8},{10,11... | collective-permute-start | bytes 786440 | tf_op jit(solution)/shard_map/ppermute | solution.py:457
  63.4 1.4 %copy-start.1 = (f32[2,128,512]{2,1,0:T(8,128)S(1)}, f32[2,128,512]{2,1,0:T(8,128)}, u32[]{:S(2)}) copy-start(f32[2,128,512]{2,1,0:T(8,128)} %psi.3) | copy-start | bytes 1572868
